TPU v7x, 512 devices: a whole 4x8x8 slice. The times are simulated.
512 devices in a mesh: row: 8 (over z_hi, core), col: 8 (over x, z_lo), dep: 8 (over y).
Axes of the slice: x: 4, y: 8, z: 8 (z_hi: 4, z_lo: 2; z = z_hi * 2 + z_lo), core: 2. Of those that a mesh axis runs over, the one named last changes fastest.
Arguments:
- tokens: bfloat16 [1024, 8192], P('row', ('dep', 'col')), may hold values from -30 to 30
- w_gate: bfloat16 [8192, 16384], P('dep', ('col', 'row')), may hold values from -0.0625 to 0.0625
- w_up: bfloat16 [8192, 16384], P('dep', ('col', 'row')), may hold values from -0.0625 to 0.0625
- upstream: bfloat16 [1024, 16384], P('row', ('col', 'dep')), may hold values from -6 to 6
- history: float32 [16, 3], replicated, may hold values from 2 to 24
Outputs:
- hidden: bfloat16 [1024, 16384], P('row', ('col', 'dep'))
- input_grad: bfloat16 [1024, 8192], P('row', ('dep', 'col'))
- gate_grad: bfloat16 [8192, 16384], P('dep', ('col', 'row'))
- upper_grad: bfloat16 [8192, 16384], P('dep', ('col', 'row'))
- new_history: float32 [16, 3], replicated
All inputs are finite; a program needn't handle non-finite values.
Results may differ from a plain program's by a relative error of at most 0.0085.
Values may be sent and summed in bfloat16 or wider, within the bound.
No kernel may reach another device: no remote copies, remote signals or barrier semaphores. Data moves between devices by JAX's collectives and lax.ppermute only.
A program may use at most 64 MiB of HBM per device.

v0:
```python
import jax
import jax.numpy as jnp
from jax import lax
from jax.sharding import PartitionSpec as P


def quantize(values, factor):
    return jnp.clip(values * factor, -448.0, 448.0).astype(jnp.bfloat16)


def backward_parts(gate_sum, lift_sum, grad_in):
    sigmoid_gate = jax.nn.sigmoid(gate_sum)
    activated = gate_sum * sigmoid_gate
    grad_gate = grad_in * lift_sum * sigmoid_gate * (1.0 + gate_sum * (1.0 - sigmoid_gate))
    grad_lift = grad_in * activated
    return (activated, grad_gate, grad_lift)


def per_device(tokens, w_gate, w_up, upstream, history):
    tops = jnp.max(history, axis=0)
    scale_in = 448.0 / tops[0]
    scale_grad = 448.0 / tops[2]
    tok_float = tokens.astype(jnp.float32)
    quant_in = quantize(tok_float, scale_in)
    peak_in = jnp.max(jnp.abs(tok_float))
    peak_in = lax.pmax(peak_in, ("row", "col", "dep"))
    x_block = lax.all_gather(quant_in, "col", axis=1, tiled=True)
    gate_block, lift_block = (
        lax.all_gather(w_gate, "row", axis=1, tiled=True),
        lax.all_gather(w_up, "row", axis=1, tiled=True),
    )
    gate_part = jnp.dot(x_block, gate_block, preferred_element_type=jnp.float32)
    lift_part = jnp.dot(x_block, lift_block, preferred_element_type=jnp.float32)
    gate_sum, lift_sum = (
        lax.psum_scatter(gate_part, "dep", scatter_dimension=1, tiled=True),
        lax.psum_scatter(lift_part, "dep", scatter_dimension=1, tiled=True),
    )
    gate_sum = gate_sum / scale_in
    lift_sum = lift_sum / scale_in
    activated, grad_gate, grad_lift = backward_parts(
        gate_sum, lift_sum, upstream.astype(jnp.float32)
    )
    hidden = (activated * lift_sum).astype(jnp.bfloat16)
    peak_grad = jnp.maximum(jnp.max(jnp.abs(grad_gate)), jnp.max(jnp.abs(grad_lift)))
    quant_gate, quant_lift = (
        lax.all_gather(quantize(grad_gate, scale_grad), "dep", axis=1, tiled=True),
        lax.all_gather(quantize(grad_lift, scale_grad), "dep", axis=1, tiled=True),
    )
    peak_hidden = jnp.max(jnp.abs(hidden.astype(jnp.float32)))
    peak_hidden = lax.pmax(peak_hidden, ("row", "col", "dep"))
    peak_grad = lax.pmax(peak_grad, ("row", "col", "dep"))
    back_part = jnp.dot(quant_gate, gate_block.T, preferred_element_type=jnp.float32) + jnp.dot(
        quant_lift, lift_block.T, preferred_element_type=jnp.float32
    )
    back_sum = lax.psum_scatter(back_part, "col", scatter_dimension=1, tiled=True)
    input_grad = (back_sum / scale_grad).astype(jnp.bfloat16)
    rows_gate, rows_lift = (
        lax.all_to_all(quant_gate, "row", split_axis=1, concat_axis=0, tiled=True),
        lax.all_to_all(quant_lift, "row", split_axis=1, concat_axis=0, tiled=True),
    )
    piece = lax.all_gather(x_block, "row", axis=0, tiled=True)
    contract = (((0,), (0,)), ((), ()))
    new_gate = lax.dot_general(piece, rows_gate, contract, preferred_element_type=jnp.float32)
    new_lift = lax.dot_general(piece, rows_lift, contract, preferred_element_type=jnp.float32)
    divisor = scale_in * scale_grad * rows_gate.shape[0]
    gate_grad = (new_gate / divisor).astype(jnp.bfloat16)
    upper_grad = (new_lift / divisor).astype(jnp.bfloat16)
    peaks = jnp.stack([peak_in, peak_hidden, peak_grad])
    new_history = jnp.concatenate([history[1:], peaks[None, :]], axis=0)
    return (hidden, input_grad, gate_grad, upper_grad, new_history)


def solution(mesh):
    placed = (
        P("row", ("dep", "col")),
        P("dep", ("col", "row")),
        P("dep", ("col", "row")),
        P("row", ("col", "dep")),
        P(),
    )
    return jax.shard_map(
        per_device,
        mesh=mesh,
        in_specs=placed,
        out_specs=(
            P("row", ("col", "dep")),
            P("row", ("dep", "col")),
            P("dep", ("col", "row")),
            P("dep", ("col", "row")),
            P(),
        ),
        check_vma=False,
    )
```

profile of v0, /device:TPU:1, one launch (start us, length us, event | category | flops | bytes accessed | tf_op | source)
XLA Modules:
  0.0 419.3 jit_solution(603989787466451865)
XLA Ops:
  7.2 0.0 all-gather.4.cloned.1.call-start
  7.2 0.7 all-gather.4.cloned.1.call-update
  7.9 0.0 all-gather.6.cloned.1.call-start
  7.9 0.7 all-gather.6.cloned.1.call-update
  8.6 0.0 reduce-scatter.4.cloned.1.call-start
  8.7 0.8 reduce_max.45
  9.5 0.6 fusion.9
  10.8 1.5 fusion.7
  12.2 21.5 %all_gather.18 = bf16[128,1024]{1,0:T(8,128)(2,1)S(1)} all-gather(bf16[128,128]{1,0:T(8,128)(2,1)S(1)} %get-tuple-element.21), channel_id=1, replica_groups=mesh['row'=8,'col'=8,'dep'=8] {'col'}, dimensions={1}, use_global_device_ids=true | all-gather | bytes 294912 | tf_op jit(solution)/shard_map/all_gather | solution.py:27
  33.7 0.0 copy-start
  33.7 43.9 %all-gather.4.cloned.1.call-done = bf16[1024,2048]{1,0:T(8,128)(2,1)} async-done(((bf16[1024,256]{1,0:T(8,128)(2,1)}), bf16[1024,2048]{1,0:T(8,128)(2,1)}) %all-gather.4.cloned.1.call-update) | async-done | bytes 4194320 | tf_op jit(solution)/shard_map/all_gather | solution.py:29
  77.6 3.9 fusion.10
  81.5 0.0 copy-start.1
  81.5 0.0 reduce-scatter.4.cloned.1.call-update
  81.5 0.0 reduce-scatter.6.cloned.1.call-start
  81.6 59.7 %all-gather.6.cloned.1.call-done = bf16[1024,2048]{1,0:T(8,128)(2,1)} async-done(((bf16[1024,256]{1,0:T(8,128)(2,1)}), bf16[1024,2048]{1,0:T(8,128)(2,1)}) %all-gather.6.cloned.1.call-update) | async-done | bytes 4194320 | tf_op jit(solution)/shard_map/all_gather | solution.py:30
  141.3 3.9 fusion.11
  145.1 0.0 copy-done
  145.2 0.0 reduce-scatter.6.cloned.1.call-update
  145.2 0.0 all-gather.8.cloned.1.call-start
  145.2 0.5 all-gather.8.cloned.1.call-update
  146.5 31.5 %reduce-scatter.4.cloned.1.call-done = f32[128,256]{1,0:T(8,128)} async-done(((f32[128,2048]{1,0:T(8,128)}), f32[128,256]{1,0:T(8,128)}) %reduce-scatter.4.cloned.1.call-update) | async-done | bytes 131088 | tf_op jit(solution)/shard_map/reduce_scatter | solution.py:35
  178.0 42.8 %reduce-scatter.6.cloned.1.call-done = f32[128,256]{1,0:T(8,128)} async-done(((f32[128,2048]{1,0:T(8,128)}), f32[128,256]{1,0:T(8,128)}) %reduce-scatter.6.cloned.1.call-update) | async-done | bytes 131088 | tf_op jit(solution)/shard_map/reduce_scatter | solution.py:36
  220.8 0.0 copy-done.1
  220.8 2.3 abs_reduce_fusion
  223.2 19.8 %all_gather.21 = bf16[128,2048]{1,0:T(8,128)(2,1)S(1)} all-gather(bf16[128,256]{1,0:T(8,128)(2,1)S(1)} %clamp_convert_fusion.1), channel_id=1, replica_groups=mesh['row'=8,'col'=8,'dep'=8] {'dep'}, dimensions={1}, use_global_device_ids=true | all-gather | bytes 589824 | tf_op jit(solution)/shard_map/all_gather | solution.py:46
  243.0 0.8 copy.19
  243.8 18.1 %all-to-all-start = ((bf16[128,8,256]{2,0,1:T(8,128)(2,1)}), bf16[128,8,256]{2,0,1:T(8,128)(2,1)S(1)}, u32[]{:S(2)}, u32[]{:S(2)}) async-start(bf16[128,8,256]{2,0,1:T(8,128)(2,1)} %bitcast.32), calls=%async_computation.3 | async-start | bytes 1048576 | tf_op jit(solution)/shard_map/all_to_all | solution.py:58
  261.9 21.0 %all_gather.22 = bf16[128,2048]{1,0:T(8,128)(2,1)S(1)} all-gather(bf16[128,256]{1,0:T(8,128)(2,1)S(1)} %get-tuple-element.15), channel_id=1, replica_groups=mesh['row'=8,'col'=8,'dep'=8] {'dep'}, dimensions={1}, use_global_device_ids=true | all-gather | bytes 589824 | tf_op jit(solution)/shard_map/all_gather | solution.py:47
  282.9 0.8 copy.18
  283.8 3.7 fusion.12
  287.5 0.0 copy-start.2
  287.5 0.0 all-to-all-done
  287.5 11.5 %all-to-all-start.1 = ((bf16[128,8,256]{2,0,1:T(8,128)(2,1)}), bf16[128,8,256]{2,0,1:T(8,128)(2,1)S(1)}, u32[]{:S(2)}, u32[]{:S(2)}) async-start(bf16[128,8,256]{2,0,1:T(8,128)(2,1)} %bitcast.31), calls=%async_computation.4 | async-start | bytes 1048576 | tf_op jit(solution)/shard_map/all_to_all | solution.py:59
  299.0 0.0 reduce-scatter.8.cloned.1.call-start
  299.0 4.5 %convolution_add_fusion = f32[128,1024]{1,0:T(8,128)} fusion(f32[128,1024]{1,0:T(8,128)S(1)} %fusion.12, bf16[128,2048]{1,0:T(8,128)(2,1)S(1)} %all_gather.22, bf16[1024,2048]{1,0:T(8,128)(2,1)} %all-gather.6.cloned.1.call-done), kind=kOutput, calls=%fused_computation.4 | convolution fusion | flops 537001984 | bytes 5767168 | tf_op jit(solution)/shard_map/dot_general | solution.py:52
  303.5 0.0 reduce-scatter.8.cloned.1.call-update
  303.5 0.0 copy-done.2
  303.5 0.1 slice.11
  304.9 98.5 %all-reduce = (f32[1]{0:T(128)}, f32[1]{0:T(128)}, f32[1]{0:T(128)}) all-reduce(f32[1]{0:T(128)} %bitcast.8, f32[1]{0:T(128)} %bitcast.7, f32[1]{0:T(128)} %bitcast.6), channel_id=1, replica_groups=mesh['row'=8,'col'=8,'dep'=8] {'row','col','dep'}, use_global_device_ids=true, to_apply=%region_10.11 | all-reduce | flops 3 | bytes 24 | tf_op jit(solution)/shard_map/pmax | solution.py:51
  403.4 2.0 maximum_bitcast_fusion
  405.4 0.1 copy.13
  405.5 0.7 pad_maximum_fusion
  406.2 0.0 all-gather.8.cloned.1.call-done
  406.2 0.0 copy-start.3
  406.2 3.3 fusion
  409.5 0.0 all-to-all-done.1
  409.5 0.0 copy-done.3
  409.5 1.6 fusion.1
  411.0 0.0 reduce-scatter.8.cloned.1.call-done
  411.0 1.5 divide_convert_fusion
  (1 shorter events, 0.0 us)
Async XLA Ops:
  7.2 70.4 %all-gather.4.cloned.1.call-start = ((), (), s32[]{:S(2)}) async-start(), calls=%async_computation.5 | async-start | bytes 4718592 | tf_op jit(solution)/shard_map/all_gather | solution.py:29
  7.9 133.4 %all-gather.6.cloned.1.call-start = ((), (), s32[]{:S(2)}) async-start(), calls=%async_computation.7 | async-start | bytes 4718592 | tf_op jit(solution)/shard_map/all_gather | solution.py:30
  8.6 169.3 %reduce-scatter.4.cloned.1.call-start = ((), (), s32[]{:S(2)}) async-start(), calls=%async_computation.6 | async-start | bytes 1179648 | tf_op jit(solution)/shard_map/reduce_scatter | solution.py:35
  33.7 111.5 %copy-start = (bf16[128,1024]{1,0:T(8,128)(2,1)}, bf16[128,1024]{1,0:T(8,128)(2,1)S(1)}, u32[]{:S(2)}) copy-start(bf16[128,1024]{1,0:T(8,128)(2,1)S(1)} %all_gather.18) | copy-start | bytes 786436
  81.5 139.3 %copy-start.1 = (bf16[128,256]{1,0:T(8,128)(2,1)S(1)}, bf16[128,256]{1,0:T(8,128)(2,1)}, u32[]{:S(2)}) copy-start(bf16[128,256]{1,0:T(8,128)(2,1)} %param.8) | copy-start | bytes 196612
  81.5 139.3 %reduce-scatter.6.cloned.1.call-start = ((), (), s32[]{:S(2)}) async-start(), calls=%async_computation.8 | async-start | bytes 1179648 | tf_op jit(solution)/shard_map/reduce_scatter | solution.py:36
  145.2 261.0 %all-gather.8.cloned.1.call-start = ((), (), s32[]{:S(2)}) async-start(), calls=%async_computation.10 | async-start | bytes 2359296 | tf_op jit(solution)/shard_map/all_gather | solution.py:61
  243.8 43.7 %all-to-all-start = ((bf16[128,8,256]{2,0,1:T(8,128)(2,1)}), bf16[128,8,256]{2,0,1:T(8,128)(2,1)S(1)}, u32[]{:S(2)}, u32[]{:S(2)}) async-start(bf16[128,8,256]{2,0,1:T(8,128)(2,1)} %bitcast.32), calls=%async_computation.3 | async-start | bytes 1048576 | tf_op jit(solution)/shard_map/all_to_all | solution.py:58
  287.5 16.0 %copy-start.2 = (f32[16,3]{0,1:T(4,128)S(1)}, f32[16,3]{0,1:T(4,128)}, u32[]{:S(2)}) copy-start(f32[16,3]{0,1:T(4,128)} %param.9) | copy-start | bytes 580
  287.5 122.0 %all-to-all-start.1 = ((bf16[128,8,256]{2,0,1:T(8,128)(2,1)}), bf16[128,8,256]{2,0,1:T(8,128)(2,1)S(1)}, u32[]{:S(2)}, u32[]{:S(2)}) async-start(bf16[128,8,256]{2,0,1:T(8,128)(2,1)} %bitcast.31), calls=%async_computation.4 | async-start | bytes 1048576 | tf_op jit(solution)/shard_map/all_to_all | solution.py:59
  299.0 112.1 %reduce-scatter.8.cloned.1.call-start = ((), (), s32[]{:S(2)}) async-start(), calls=%async_computation.9 | async-start | bytes 589824 | tf_op jit(solution)/shard_map/reduce_scatter | solution.py:55
  406.2 3.3 copy-start.3
Sparse Core Ops, SparseCore 0:
  10.1 67.4 all-gather.3
  79.7 61.4 all-gather.5
  144.1 33.8 reduce-scatter.3
  180.7 40.1 reduce-scatter.5
  223.4 44.0 all-gather.7
  303.6 37.4 reduce-scatter.7
where the time goes:
time: 420 us; the launch traced here: 419 us
  waiting for transfers between devices  180 us (43%)
  blocking collectives  161 us (38%)
  starting transfers between devices  29.8 us (7%)
  matrix products  20.8 us (5%)
  between operations  16.8 us (4%)
  other arithmetic  8.73 us (2%)
    pmax x1, blocking collectives, per_device(): peak_grad = lax.pmax(peak_grad, ('row', 'col', 'dep'))  98.5 us
    all_gather x1, waiting for transfers between devices, per_device(): lax.all_gather(w_up, 'row', axis=1, tiled=True)  59.7 us
    all_gather x1, waiting for transfers between devices, per_device(): lax.all_gather(w_gate, 'row', axis=1, tiled=True)  43.9 us
    reduce_scatter x1, waiting for transfers between devices, per_device(): lax.psum_scatter(lift_part, 'dep', scatter_dimension=1, tiled=True)  42.8 us
    reduce_scatter x1, waiting for transfers between devices, per_device(): lax.psum_scatter(gate_part, 'dep', scatter_dimension=1, tiled=True)  31.5 us
    all_gather x1, blocking collectives, per_device(): x_block = lax.all_gather(quant_in, 'col', axis=1, tiled=True)  21.5 us
    all_gather x1, blocking collectives, per_device(): lax.all_gather(quantize(grad_lift, scale_grad), 'dep', axis=1, tiled=True)  21 us
    all_gather x1, blocking collectives, per_device(): lax.all_gather(quantize(grad_gate, scale_grad), 'dep', axis=1, tiled=True)  19.8 us
  transfers between devices with their start and end apart: 8, of which 4 were waited for; matrix products, arithmetic and copies ran while one was open for 7% of the time, Pallas kernels for 0%

commit v1 on v0

v1 whole, which is shorter than its diff:
```python
import jax
import jax.numpy as jnp
from jax import lax
from jax.experimental import pallas as pl
from jax.experimental.pallas import tpu as pltpu
from jax.sharding import Mesh
from jax.sharding import PartitionSpec as P

F32 = jnp.float32
BF16 = jnp.bfloat16
VMEM = pl.BlockSpec(memory_space=pltpu.VMEM)
SMEM = pl.BlockSpec(memory_space=pltpu.SMEM)


def params():
    return pltpu.CompilerParams(vmem_limit_bytes=40 * 1024 * 1024)


def call(body, outs, args, flops=0, moved=0, scratch=()):
    return pl.pallas_call(
        body,
        out_shape=[jax.ShapeDtypeStruct(s, t) for s, t in outs],
        in_specs=[SMEM if a.dtype == jnp.int32 else VMEM for a in args],
        out_specs=[VMEM] * len(outs),
        scratch_shapes=list(scratch),
        compiler_params=params(),
        cost_estimate=pl.CostEstimate(flops=flops, bytes_accessed=moved, transcendentals=0),
    )(*args)


def top(values):
    return jnp.max(jnp.max(values, axis=0, keepdims=True), axis=1, keepdims=True)


def rows_of(*values):
    row = lax.broadcasted_iota(jnp.int32, (8, 128), 0)
    tile = jnp.zeros((8, 128), F32)
    for i, v in enumerate(values):
        tile = jnp.where(row == i, v, tile)
    return tile


def pack_peaks(peak_in, peak_hidden, peak_grad):
    high = peak_grad.astype(BF16).astype(F32)
    rest = peak_grad - high
    mid = rest.astype(BF16).astype(F32)
    return rows_of(peak_in, peak_hidden, high, mid, rest - mid).astype(BF16)


def unpack_peaks(packed):
    grads = packed[:, 2, :] + packed[:, 3, :] + packed[:, 4, :]
    return top(packed[:, 0, :]), top(packed[:, 1, :]), top(grads)


def scale_body(hist_ref, tok_ref, out_ref, scal_ref):
    tops = jnp.max(hist_ref[...], axis=0, keepdims=True)
    scale_in = 448.0 / tops[:, 0:1]
    scale_grad = 448.0 / tops[:, 2:3]
    tok = tok_ref[...].astype(F32)
    quant = jnp.clip(tok * scale_in, -448.0, 448.0).astype(BF16)
    for i in range(out_ref.shape[0]):
        out_ref[i] = quant
    scal_ref[...] = rows_of(scale_in, scale_grad, top(jnp.abs(tok)))


def forward_body(core_ref, x_ref, g0_ref, u0_ref, g1_ref, u1_ref, out_ref, xh_ref):
    groups, cols, rows = out_ref.shape[0] // 2, x_ref.shape[0] // (out_ref.shape[0] // 2), x_ref.shape[1]
    core = core_ref[0]
    for g in range(groups):
        for k in range(cols):
            xh_ref[g * rows : (g + 1) * rows, k * 128 : (k + 1) * 128] = x_ref[g * cols + k]
    x = xh_ref[...]
    for which, pair in enumerate(((g0_ref, u0_ref), (g1_ref, u1_ref))):
        place = core if which == 0 else 1 - core
        for half, w_ref in enumerate(pair):
            part = jnp.dot(x, w_ref[...], preferred_element_type=F32).astype(BF16)
            for g in range(groups):
                out_ref[2 * g + place, half * rows : (half + 1) * rows, :] = part[g * rows : (g + 1) * rows]


def middle_body(in_ref, up_ref, scal_ref, hidden_ref, q_ref):
    rows = up_ref.shape[0]
    scale_in = scal_ref[0:1, 0:1]
    scale_grad = scal_ref[1:2, 0:1]
    gate_sum = jnp.sum(in_ref[:, :rows, :].astype(F32), axis=0) / scale_in
    lift_sum = jnp.sum(in_ref[:, rows:, :].astype(F32), axis=0) / scale_in
    sigmoid_gate = 1.0 / (1.0 + jnp.exp(-gate_sum))
    activated = gate_sum * sigmoid_gate
    hidden = (activated * lift_sum).astype(BF16)
    hidden_ref[...] = hidden
    grad_in = up_ref[...].astype(F32)
    grad_gate = grad_in * lift_sum * sigmoid_gate * (1.0 + gate_sum * (1.0 - sigmoid_gate))
    grad_lift = grad_in * activated
    quant_gate = jnp.clip(grad_gate * scale_grad, -448.0, 448.0).astype(BF16)
    quant_lift = jnp.clip(grad_lift * scale_grad, -448.0, 448.0).astype(BF16)
    peak_grad = jnp.maximum(top(jnp.abs(grad_gate)), top(jnp.abs(grad_lift)))
    peaks = pack_peaks(scal_ref[2:3, 0:1], top(jnp.abs(hidden.astype(F32))), peak_grad)
    wide = jnp.concatenate([peaks, peaks], axis=1)
    wide = jnp.concatenate([wide, wide], axis=0)
    for i in range(q_ref.shape[0]):
        q_ref[i, :rows, :] = quant_gate
        q_ref[i, rows : 2 * rows, :] = quant_lift
        q_ref[i, 2 * rows :, :] = wide


def backward_body(core_ref, q_ref, g0_ref, u0_ref, g1_ref, u1_ref, out_ref, mine_ref, send_ref):
    groups = q_ref.shape[0] // 2
    rows = (q_ref.shape[1] - 16) // 2
    cols = out_ref.shape[0] // groups
    core = core_ref[0]
    contract = (((1,), (1,)), ((), ()))
    total = None
    for which, pair in enumerate(((g0_ref, u0_ref), (g1_ref, u1_ref))):
        place = core if which == 0 else 1 - core
        kept = mine_ref if which == 0 else send_ref
        for half, w_ref in enumerate(pair):
            for g in range(groups):
                kept[half, g * rows : (g + 1) * rows, :] = q_ref[2 * g + place, half * rows : (half + 1) * rows, :]
            part = lax.dot_general(kept[half], w_ref[...], contract, preferred_element_type=F32)
            total = part if total is None else total + part
    packed = pack_peaks(*unpack_peaks(q_ref[:, 2 * rows : 2 * rows + 16, 0:128].astype(F32)[:, 0:8, :]))
    for g in range(groups):
        for k in range(cols):
            out_ref[g * cols + k, :rows, :] = total[g * rows : (g + 1) * rows, k * 128 : (k + 1) * 128].astype(BF16)
            out_ref[g * cols + k, rows:, :] = packed


def last_body(in_ref, scal_ref, out_ref, peaks_ref):
    rows = out_ref.shape[0]
    out_ref[...] = (jnp.sum(in_ref[:, :rows, :].astype(F32), axis=0) / scal_ref[1:2, 0:1]).astype(BF16)
    peaks_ref[...] = rows_of(*unpack_peaks(in_ref[:, rows:, :].astype(F32)))


def history_body(hist_ref, mine_ref, other_ref, out_ref):
    peaks = jnp.maximum(mine_ref[...], other_ref[...])
    col = lax.broadcasted_iota(jnp.int32, (1, 3), 1)
    row = jnp.where(col == 0, peaks[0:1, 0:1], jnp.where(col == 1, peaks[1:2, 0:1], peaks[2:3, 0:1]))
    past = hist_ref.shape[0] - 1
    out_ref[0:past, :] = hist_ref[1:, :]
    out_ref[past:, :] = row


def per_device(sizes, tokens, w_gate, w_up, upstream, history):
    nh, nx, nw, ny = (sizes[a] for a in "hxwy")
    plane = ("h", "x", "w")
    count = nh * nx * nw
    rows, width = tokens.shape
    depth, units = w_gate.shape
    swap = [(0, 1), (1, 0)]
    turn = [(h * ny + y, (y // 2) * ny + h * 2 + y % 2) for h in range(nh) for y in range(ny)]
    core = lax.axis_index("c").reshape(1)

    copies, scal = call(scale_body, [((count, rows, width), BF16), ((8, 128), F32)], (history, tokens))
    up = lax.ppermute(upstream, ("h", "y"), turn)
    gate_other = lax.ppermute(w_gate, "c", swap)
    lift_other = lax.ppermute(w_up, "c", swap)
    weights = (w_gate, w_up, gate_other, lift_other)
    x_all = lax.all_to_all(copies, plane, 0, 0, tiled=True)

    work = 8 * nh * rows * depth * units
    parts, x_mine = call(
        forward_body,
        [((ny, 2 * rows, units), BF16), ((nh * rows, depth), BF16)],
        (core, x_all) + weights,
        flops=work,
        moved=6 * 2**20,
    )
    sums = lax.all_to_all(parts, "y", 0, 0, tiled=True)
    x_other = lax.ppermute(x_mine, "c", swap)
    hidden, quants = call(
        middle_body, [((rows, units), BF16), ((ny, 2 * rows + 16, units), BF16)], (sums, up, scal), moved=2**21
    )
    q_all = lax.all_to_all(quants, "y", 0, 0, tiled=True)
    hidden = lax.ppermute(hidden, ("h", "y"), turn)
    back, q_mine, q_send = call(
        backward_body,
        [((count, rows + 8, width), BF16), ((2, nh * rows, units), BF16), ((2, nh * rows, units), BF16)],
        (core, q_all) + weights,
        flops=work,
        moved=6 * 2**20,
    )
    back_all = lax.all_to_all(back, plane, 0, 0, tiled=True)
    q_other = lax.ppermute(q_send, "c", swap)
    divisor = scal[0, 0] * scal[1, 0] * (2 * nh * rows)
    contract = (((0,), (0,)), ((), ()))
    grads = []
    for i in range(2):
        total = lax.dot_general(x_mine, q_mine[i], contract, preferred_element_type=F32) + lax.dot_general(
            x_other, q_other[i], contract, preferred_element_type=F32
        )
        grads.append((total / divisor).astype(BF16))
    input_grad, peaks = call(last_body, [((rows, width), BF16), ((8, 128), F32)], (back_all, scal), moved=2**21)
    peaks_other = lax.ppermute(peaks, "c", swap)
    (new_history,) = call(history_body, [(history.shape, F32)], (history, peaks, peaks_other))
    return (hidden, input_grad, grads[0], grads[1], new_history)


def solution(mesh):
    sizes = dict(h=mesh.shape["row"] // 2, c=2, x=mesh.shape["col"] // 2, w=2, y=mesh.shape["dep"])
    fine = Mesh(mesh.devices.reshape(tuple(sizes.values())), tuple(sizes))
    row, col = ("h", "c"), ("x", "w")
    placed = (
        P(row, ("y",) + col),
        P("y", col + row),
        P("y", col + row),
        P(row, col + ("y",)),
        P(),
    )

    def step(*args):
        return per_device(sizes, *args)

    return jax.shard_map(
        step,
        mesh=fine,
        in_specs=placed,
        out_specs=(P(row, col + ("y",)), P(row, ("y",) + col), P("y", col + row), P("y", col + row), P()),
        check_vma=False,
    )
```

time: 420 us -> 167 us (0.40)
  blocking collectives: 161 us -> 29.5 us
  waiting for transfers between devices: 180 us -> 63.2 us
  starting transfers between devices: 29.8 us -> 50.4 us
  matrix products: 20.8 us -> 4.51 us
  between operations: 16.8 us -> 2.14 us
  other arithmetic: 8.73 us -> 0 us
  Pallas kernels: 0 us -> 6.98 us
  local copies, waits for them, and re-layouts: 2.44 us -> 8.6 us
    all_gather x3 -> x0, waiting for transfers between devices: 104 us -> none  [the longest x1 59.7 us: per_device(): lax.all_gather(w_up, 'row', axis=1, tiled=True)]
    pmax x1 -> x0, blocking collectives: 98.5 us -> none  [per_device(): peak_grad = lax.pmax(peak_grad, ('row', 'col', 'dep'))]
    reduce_scatter x3 -> x0, waiting for transfers between devices: 74.4 us -> none  [the longest x1 42.8 us: per_device(): lax.psum_scatter(lift_part, 'dep', scatter_dimension=1, tiled=True)]
    all_gather x3 -> x0, blocking collectives: 62.3 us -> none  [the longest x1 21.5 us: per_device(): x_block = lax.all_gather(quant_in, 'col', axis=1, tiled=True)]
    all_to_all x2 -> x3, waiting for transfers between devices: 0.01 us -> 62.1 us  [the longest x1 28.5 us: per_device(): sums = lax.all_to_all(parts, 'y', 0, 0, tiled=True)]
    all_to_all x0 -> x1, blocking collectives: none -> 29.5 us  [per_device(): q_all = lax.all_to_all(quants, 'y', 0, 0, tiled=True)]
    ppermute x0 -> x7, starting transfers between devices: none -> 18.5 us  [the longest x1 5.49 us: per_device(): peaks_other = lax.ppermute(peaks, 'c', swap)]
    dot_general x6 -> x4, matrix products: 20.8 us -> 4.51 us  [the longest x2 2.58 us: per_device(): lax.dot_general(x_mine, q_mine[i], contract, preferred_element_type=F32)]
  transfers between devices with their start and end apart: 8 -> 10, of which waited for: 4 -> 4; matrix products, arithmetic and copies ran while one was open for 7% -> 3% of each run, Pallas kernels for 0% -> 0%
where the time goes in v1:
time: 167 us; the launch traced here: 165 us
  waiting for transfers between devices  63.2 us (38%)
  starting transfers between devices  50.4 us (30%)
  blocking collectives  29.5 us (18%)
  local copies, waits for them, and re-layouts  8.6 us (5%)
  Pallas kernels  6.98 us (4%)
  matrix products  4.51 us (3%)
  between operations  2.14 us (1%)
    all_to_all x1, blocking collectives, per_device(): q_all = lax.all_to_all(quants, 'y', 0, 0, tiled=True)  29.5 us
    all_to_all x1, waiting for transfers between devices, per_device(): sums = lax.all_to_all(parts, 'y', 0, 0, tiled=True)  28.5 us
    all_to_all x1, waiting for transfers between devices, per_device(): x_all = lax.all_to_all(copies, plane, 0, 0, tiled=True)  19.4 us
    all_to_all x1, waiting for transfers between devices, per_device(): back_all = lax.all_to_all(back, plane, 0, 0, tiled=True)  14.1 us
    all_to_all x1, starting transfers between devices, per_device(): x_all = lax.all_to_all(copies, plane, 0, 0, tiled=True)  13.7 us
    all_to_all x1, starting transfers between devices, per_device(): back_all = lax.all_to_all(back, plane, 0, 0, tiled=True)  11.2 us
    unnamed x33, local copies, waits for them, and re-layouts  8.09 us
    pallas_call x6, Pallas kernels, call(): pl.pallas_call(body, out_shape=[jax.ShapeDtypeStruct(s, t) for s, t in ou...  6.98 us
  transfers between devices with their start and end apart: 10, of which 4 were waited for; matrix products, arithmetic and copies ran while one was open for 3% of the time, Pallas kernels for 0%

profile of v1, /device:TPU:1, one launch (start us, length us, event | category | flops | bytes accessed | tf_op | source)
XLA Modules:
  0.0 165.3 jit_solution(13683739653019473873)
XLA Ops:
  0.6 0.8 copy.10.hist_ref
  1.4 0.0 copy-start
  1.4 0.8 copy-done
  2.1 0.0 copy-start.1
  2.2 0.0 copy-start.2
  2.2 1.1 shard_map.92
  3.3 13.7 %all-to-all-start = ((bf16[32,128,128]{2,1,0:T(8,128)(2,1)}), bf16[32,128,128]{2,1,0:T(8,128)(2,1)S(1)}, u32[]{:S(2)}, u32[]{:S(2)}) async-start(bf16[32,128,128]{2,1,0:T(8,128)(2,1)} %get-tuple-element.16), calls=%async_computation | async-start | bytes 2097152 | tf_op jit(solution)/shard_map/all_to_all | solution.py:158
  17.0 0.0 copy-done.1
  17.0 2.9 %collective-permute-start = (bf16[1024,256]{1,0:T(8,128)(2,1)S(1)}, bf16[1024,256]{1,0:T(8,128)(2,1)S(1)}, u32[]{:S(2)}, u32[]{:S(2)}) collective-permute-start(bf16[1024,256]{1,0:T(8,128)(2,1)S(1)} %copy-done.1), channel_id=1, source_target_pairs={{0,64},{64,0},{1,65},{65,1},{2,66},{66,2},{3,67},{67,3},{4,68},{68... | collective-permute-start | bytes 1572872 | tf_op jit(solution)/shard_map/ppermute | solution.py:155
  19.9 0.0 copy-done.2
  19.9 1.9 %collective-permute-start.1 = (bf16[1024,256]{1,0:T(8,128)(2,1)S(1)}, bf16[1024,256]{1,0:T(8,128)(2,1)S(1)}, u32[]{:S(2)}, u32[]{:S(2)}) collective-permute-start(bf16[1024,256]{1,0:T(8,128)(2,1)S(1)} %copy-done.2), channel_id=1, source_target_pairs={{0,64},{64,0},{1,65},{65,1},{2,66},{66,2},{3,67},{67,3},{4,68},{68... | collective-permute-start | bytes 1572872 | tf_op jit(solution)/shard_map/ppermute | solution.py:156
  21.8 0.0 collective-permute-done.g1_ref
  21.9 0.0 copy-start.3
  21.9 0.8 copy-done.3
  22.6 1.1 collective-permute-done.1.u1_ref
  23.7 0.0 copy-start.6
  23.7 0.8 copy-done.6
  24.5 19.4 %all-to-all-done.x_ref = bf16[32,128,128]{2,1,0:T(8,128)(2,1)S(1)} async-done(((bf16[32,128,128]{2,1,0:T(8,128)(2,1)}), bf16[32,128,128]{2,1,0:T(8,128)(2,1)S(1)}, u32[]{:S(2)}, u32[]{:S(2)}) %all-to-all-start) | async-done | bytes 1048608 | tf_op jit(solution)/shard_map/all_to_all | solution.py:158
  43.9 0.0 copy-start.4
  43.9 1.0 copy-done.4
  45.0 0.0 copy-start.7
  45.0 1.0 copy-done.7
  46.0 2.3 %shard_map.93 = (bf16[8,256,256]{2,1,0:T(8,128)(2,1)}, bf16[512,1024]{1,0:T(8,128)(2,1)S(1)}) custom-call(s32[1]{0:T(128)} %bitcast.core_ref, bf16[32,128,128]{2,1,0:T(8,128)(2,1)S(1)} %all-to-all-done.x_ref, bf16[1024,256]{1,0:T(8,128)(2,1)S(1)} %copy-done.1, bf16[1024,256]{1,0:T(8,128)(2,1)S(1)} %copy-done.2, bf16[1024,256]{1,0:T(8,128)(2,1)S(1)} %copy-done.4, ...), custom_call_target="tpu_custom_call" | custom-call | flops 1073741824 | bytes 6291456 | tf_op jit(solution)/shard_map/pallas_call | solution.py:20
  48.3 0.0 copy-start.14
  48.3 7.0 %all-to-all-start.1 = ((bf16[8,256,256]{2,1,0:T(8,128)(2,1)}), bf16[8,256,256]{2,1,0:T(8,128)(2,1)S(1)}, u32[]{:S(2)}, u32[]{:S(2)}) async-start(bf16[8,256,256]{2,1,0:T(8,128)(2,1)} %get-tuple-element.17), calls=%async_computation.1 | async-start | bytes 2097152 | tf_op jit(solution)/shard_map/all_to_all | solution.py:168
  55.2 0.0 copy-done.14
  55.2 0.7 collective-permute-start.2
  55.9 0.0 collective-permute-done.2.up_ref
  55.9 28.5 %all-to-all-done.1.in_ref = bf16[8,256,256]{2,1,0:T(8,128)(2,1)S(1)} async-done(((bf16[8,256,256]{2,1,0:T(8,128)(2,1)}), bf16[8,256,256]{2,1,0:T(8,128)(2,1)S(1)}, u32[]{:S(2)}, u32[]{:S(2)}) %all-to-all-start.1) | async-done | bytes 1048608 | tf_op jit(solution)/shard_map/all_to_all | solution.py:168
  84.4 0.4 shard_map.94
  84.8 0.0 copy-start.5
  84.8 0.0 copy-start.8
  84.8 29.5 %all_to_all.20.q_ref = bf16[8,272,256]{2,1,0:T(8,128)(2,1)S(1)} all-to-all(bf16[8,272,256]{2,1,0:T(8,128)(2,1)S(1)} %get-tuple-element.20), channel_id=1, replica_groups=mesh['h'=4,'c'=2,'x'=4,'w'=2,'y'=8] {'y'}, dimensions={0} | all-to-all | bytes 2228224 | tf_op jit(solution)/shard_map/all_to_all | solution.py:173
  114.3 0.0 copy-done.5
  114.3 0.0 copy-done.8
  114.3 2.3 %shard_map.95 = (bf16[32,136,128]{2,1,0:T(8,128)(2,1)}, bf16[2,512,256]{2,1,0:T(8,128)(2,1)S(1)}, bf16[2,512,256]{2,1,0:T(8,128)(2,1)S(1)}) custom-call(s32[1]{0:T(128)} %bitcast.core_ref, bf16[8,272,256]{2,1,0:T(8,128)(2,1)S(1)} %all_to_all.20.q_ref, bf16[1024,256]{1,0:T(8,128)(2,1)S(1)} %copy-done.1, bf16[1024,256]{1,0:T(8,128)(2,1)S(1)} %copy-done.2, ...), custom_call_target="tpu_custom_call" | custom-call | flops 1073741824 | bytes 6291456 | tf_op jit(solution)/shard_map/pallas_call | solution.py:20
  116.6 0.0 copy-start.9
  116.6 0.8 copy-done.9
  117.4 0.0 copy-start.11
  117.4 0.8 copy-done.11
  118.2 0.0 copy-start.10
  118.2 11.2 %all-to-all-start.3 = ((bf16[32,136,128]{2,1,0:T(8,128)(2,1)}), bf16[32,136,128]{2,1,0:T(8,128)(2,1)S(1)}, u32[]{:S(2)}, u32[]{:S(2)}) async-start(bf16[32,136,128]{2,1,0:T(8,128)(2,1)} %get-tuple-element.21), calls=%async_computation.3 | async-start | bytes 2228224 | tf_op jit(solution)/shard_map/all_to_all | solution.py:182
  129.4 5.0 %collective-permute-start.4 = (bf16[512,1024]{1,0:T(8,128)(2,1)S(1)}, bf16[512,1024]{1,0:T(8,128)(2,1)S(1)}, u32[]{:S(2)}, u32[]{:S(2)}) collective-permute-start(bf16[512,1024]{1,0:T(8,128)(2,1)S(1)} %get-tuple-element.23), channel_id=1, source_target_pairs={{0,64},{64,0},{1,65},{65,1},{2,66},{66,2},{3,67},{67,3},{4,68},{68... | collective-permute-start | bytes 3145736 | tf_op jit(solution)/shard_map/ppermute | solution.py:169
  134.4 0.0 copy-done.10
  134.4 1.9 %collective-permute-start.5 = (bf16[2,512,256]{2,1,0:T(8,128)(2,1)S(1)}, bf16[2,512,256]{2,1,0:T(8,128)(2,1)S(1)}, u32[]{:S(2)}, u32[]{:S(2)}) collective-permute-start(bf16[2,512,256]{2,1,0:T(8,128)(2,1)S(1)} %copy-done.10), channel_id=1, source_target_pairs={{0,64},{64,0},{1,65},{65,1},{2,66},{66,2},{3,67},{67,3},{4,68},{68... | collective-permute-start | bytes 1572872 | tf_op jit(solution)/shard_map/ppermute | solution.py:183
  136.4 0.7 collective-permute-start.3
  137.0 0.5 fusion.10
  138.9 0.0 collective-permute-done.3
  138.9 0.0 collective-permute-done.4
  138.9 0.0 collective-permute-done.5
  138.9 0.5 fusion.5
  139.4 0.0 copy-start.12
  139.4 1.4 fusion.4
  140.8 0.0 copy-done.12
  140.8 1.3 fusion.2
  142.1 14.1 %all-to-all-done.3.in_ref = bf16[32,136,128]{2,1,0:T(8,128)(2,1)S(1)} async-done(((bf16[32,136,128]{2,1,0:T(8,128)(2,1)}), bf16[32,136,128]{2,1,0:T(8,128)(2,1)S(1)}, u32[]{:S(2)}, u32[]{:S(2)}) %all-to-all-start.3) | async-done | bytes 1114144 | tf_op jit(solution)/shard_map/all_to_all | solution.py:182
  156.3 0.9 shard_map.96
  157.1 5.5 %collective-permute-start.6 = (f32[8,128]{1,0:T(8,128)S(1)}, f32[8,128]{1,0:T(8,128)S(1)}, u32[]{:S(2)}, u32[]{:S(2)}) collective-permute-start(f32[8,128]{1,0:T(8,128)S(1)} %get-tuple-element.26.mine_ref), channel_id=1, source_target_pairs={{0,64},{64,0},{1,65},{65,1},{2,66},{66,2},{3,67},{67,3},{4,68},{68... | collective-permute-start | bytes 12296 | tf_op jit(solution)/shard_map/ppermute | solution.py:193
  162.6 0.0 copy-done.13
  162.6 1.3 fusion.3
  163.9 0.0 collective-permute-done.6.other_ref
  163.9 0.1 shard_map.97
  164.0 0.7 copy.12
  164.7 0.6 copy.14
  (1 shorter events, 0.0 us)
Async XLA Ops:
  1.4 0.8 copy-start
  2.1 14.9 %copy-start.1 = (bf16[1024,256]{1,0:T(8,128)(2,1)S(1)}, bf16[1024,256]{1,0:T(8,128)(2,1)}, u32[]{:S(2)}) copy-start(bf16[1024,256]{1,0:T(8,128)(2,1)} %g0_ref.3) | copy-start | bytes 1572868
  2.2 17.8 %copy-start.2 = (bf16[1024,256]{1,0:T(8,128)(2,1)S(1)}, bf16[1024,256]{1,0:T(8,128)(2,1)}, u32[]{:S(2)}) copy-start(bf16[1024,256]{1,0:T(8,128)(2,1)} %u0_ref.3) | copy-start | bytes 1572868
  3.3 40.6 %all-to-all-start = ((bf16[32,128,128]{2,1,0:T(8,128)(2,1)}), bf16[32,128,128]{2,1,0:T(8,128)(2,1)S(1)}, u32[]{:S(2)}, u32[]{:S(2)}) async-start(bf16[32,128,128]{2,1,0:T(8,128)(2,1)} %get-tuple-element.16), calls=%async_computation | async-start | bytes 2097152 | tf_op jit(solution)/shard_map/all_to_all | solution.py:158
  17.0 4.8 %collective-permute-start = (bf16[1024,256]{1,0:T(8,128)(2,1)S(1)}, bf16[1024,256]{1,0:T(8,128)(2,1)S(1)}, u32[]{:S(2)}, u32[]{:S(2)}) collective-permute-start(bf16[1024,256]{1,0:T(8,128)(2,1)S(1)} %copy-done.1), channel_id=1, source_target_pairs={{0,64},{64,0},{1,65},{65,1},{2,66},{66,2},{3,67},{67,3},{4,68},{68... | collective-permute-start | bytes 1572872 | tf_op jit(solution)/shard_map/ppermute | solution.py:155
  19.9 3.8 %collective-permute-start.1 = (bf16[1024,256]{1,0:T(8,128)(2,1)S(1)}, bf16[1024,256]{1,0:T(8,128)(2,1)S(1)}, u32[]{:S(2)}, u32[]{:S(2)}) collective-permute-start(bf16[1024,256]{1,0:T(8,128)(2,1)S(1)} %copy-done.2), channel_id=1, source_target_pairs={{0,64},{64,0},{1,65},{65,1},{2,66},{66,2},{3,67},{67,3},{4,68},{68... | collective-permute-start | bytes 1572872 | tf_op jit(solution)/shard_map/ppermute | solution.py:156
  21.9 0.8 copy-start.3
  23.7 0.8 copy-start.6
  43.9 1.0 copy-start.4
  45.0 1.0 copy-start.7
  48.3 7.0 %copy-start.14 = (bf16[128,256]{1,0:T(8,128)(2,1)S(1)}, bf16[128,256]{1,0:T(8,128)(2,1)}, u32[]{:S(2)}) copy-start(bf16[128,256]{1,0:T(8,128)(2,1)} %param.8) | copy-start | bytes 196612
  48.3 36.1 %all-to-all-start.1 = ((bf16[8,256,256]{2,1,0:T(8,128)(2,1)}), bf16[8,256,256]{2,1,0:T(8,128)(2,1)S(1)}, u32[]{:S(2)}, u32[]{:S(2)}) async-start(bf16[8,256,256]{2,1,0:T(8,128)(2,1)} %get-tuple-element.17), calls=%async_computation.1 | async-start | bytes 2097152 | tf_op jit(solution)/shard_map/all_to_all | solution.py:168
  55.2 0.7 collective-permute-start.2
  84.8 29.5 %copy-start.5 = (bf16[1024,256]{1,0:T(8,128)(2,1)S(1)}, bf16[1024,256]{1,0:T(8,128)(2,1)}, u32[]{:S(2)}) copy-start(bf16[1024,256]{1,0:T(8,128)(2,1)} %copy-done.3) | copy-start | bytes 1572868
  84.8 29.5 %copy-start.8 = (bf16[1024,256]{1,0:T(8,128)(2,1)S(1)}, bf16[1024,256]{1,0:T(8,128)(2,1)}, u32[]{:S(2)}) copy-start(bf16[1024,256]{1,0:T(8,128)(2,1)} %copy-done.6) | copy-start | bytes 1572868
  116.6 0.8 copy-start.9
  117.4 0.8 copy-start.11
  118.2 16.2 %copy-start.10 = (bf16[2,512,256]{2,1,0:T(8,128)(2,1)S(1)}, bf16[2,512,256]{2,1,0:T(8,128)(2,1)}, u32[]{:S(2)}) copy-start(bf16[2,512,256]{2,1,0:T(8,128)(2,1)} %copy-done.9) | copy-start | bytes 1572868
  118.2 38.1 %all-to-all-start.3 = ((bf16[32,136,128]{2,1,0:T(8,128)(2,1)}), bf16[32,136,128]{2,1,0:T(8,128)(2,1)S(1)}, u32[]{:S(2)}, u32[]{:S(2)}) async-start(bf16[32,136,128]{2,1,0:T(8,128)(2,1)} %get-tuple-element.21), calls=%async_computation.3 | async-start | bytes 2228224 | tf_op jit(solution)/shard_map/all_to_all | solution.py:182
  129.4 9.4 %collective-permute-start.4 = (bf16[512,1024]{1,0:T(8,128)(2,1)S(1)}, bf16[512,1024]{1,0:T(8,128)(2,1)S(1)}, u32[]{:S(2)}, u32[]{:S(2)}) collective-permute-start(bf16[512,1024]{1,0:T(8,128)(2,1)S(1)} %get-tuple-element.23), channel_id=1, source_target_pairs={{0,64},{64,0},{1,65},{65,1},{2,66},{66,2},{3,67},{67,3},{4,68},{68... | collective-permute-start | bytes 3145736 | tf_op jit(solution)/shard_map/ppermute | solution.py:169
  134.4 4.4 %collective-permute-start.5 = (bf16[2,512,256]{2,1,0:T(8,128)(2,1)S(1)}, bf16[2,512,256]{2,1,0:T(8,128)(2,1)S(1)}, u32[]{:S(2)}, u32[]{:S(2)}) collective-permute-start(bf16[2,512,256]{2,1,0:T(8,128)(2,1)S(1)} %copy-done.10), channel_id=1, source_target_pairs={{0,64},{64,0},{1,65},{65,1},{2,66},{66,2},{3,67},{67,3},{4,68},{68... | collective-permute-start | bytes 1572872 | tf_op jit(solution)/shard_map/ppermute | solution.py:183
  136.4 2.5 %collective-permute-start.3 = (bf16[128,256]{1,0:T(8,128)(2,1)S(1)}, bf16[128,256]{1,0:T(8,128)(2,1)S(1)}, u32[]{:S(2)}, u32[]{:S(2)}) collective-permute-start(bf16[128,256]{1,0:T(8,128)(2,1)S(1)} %get-tuple-element.19), channel_id=1, source_target_pairs={{0,0},{1,1},{2,128},{3,129},{4,256},{5,257},{6,384},{7,385},{128,2... | collective-permute-start | bytes 196616 | tf_op jit(solution)/shard_map/ppermute | solution.py:174
  139.4 1.5 copy-start.12
  156.3 6.4 %copy-start.13 = (f32[1024,256]{1,0:T(8,128)S(1)}, f32[1024,256]{1,0:T(8,128)}, u32[]{:S(2)}) copy-start(f32[1024,256]{1,0:T(8,128)} %fusion.4) | copy-start | bytes 3145732
  157.1 6.8 %collective-permute-start.6 = (f32[8,128]{1,0:T(8,128)S(1)}, f32[8,128]{1,0:T(8,128)S(1)}, u32[]{:S(2)}, u32[]{:S(2)}) collective-permute-start(f32[8,128]{1,0:T(8,128)S(1)} %get-tuple-element.26.mine_ref), channel_id=1, source_target_pairs={{0,64},{64,0},{1,65},{65,1},{2,66},{66,2},{3,67},{67,3},{4,68},{68... | collective-permute-start | bytes 12296 | tf_op jit(solution)/shard_map/ppermute | solution.py:193

commit v2 on v1

v2 whole, which is shorter than its diff:
```python
import jax
import jax.numpy as jnp
from jax import lax
from jax.experimental import pallas as pl
from jax.experimental.pallas import tpu as pltpu
from jax.sharding import Mesh
from jax.sharding import PartitionSpec as P

F32 = jnp.float32
BF16 = jnp.bfloat16
VMEM = pl.BlockSpec(memory_space=pltpu.VMEM)
HBM = pl.BlockSpec(memory_space=pltpu.HBM)
SMEM = pl.BlockSpec(memory_space=pltpu.SMEM)


def params():
    return pltpu.CompilerParams(vmem_limit_bytes=16 * 1024 * 1024)


def call(body, outs, args, flops=0, moved=0, scratch=(), far=(), far_outs=()):
    return pl.pallas_call(
        body,
        out_shape=[jax.ShapeDtypeStruct(s, t) for s, t in outs],
        in_specs=[SMEM if a.dtype == jnp.int32 else HBM if i in far else VMEM for i, a in enumerate(args)],
        out_specs=[HBM if i in far_outs else VMEM for i in range(len(outs))],
        scratch_shapes=list(scratch),
        compiler_params=params(),
        cost_estimate=pl.CostEstimate(flops=flops, bytes_accessed=moved, transcendentals=0),
    )(*args)


def fetched(sources, held_ref, sems):
    copies = [pltpu.make_async_copy(ref, held_ref.at[i], sems.at[i]) for i, ref in enumerate(sources)]
    for copy in copies:
        copy.start()
    return copies


def top(values):
    return jnp.max(jnp.max(values, axis=0, keepdims=True), axis=1, keepdims=True)


def rows_of(*values):
    row = lax.broadcasted_iota(jnp.int32, (8, 128), 0)
    tile = jnp.zeros((8, 128), F32)
    for i, v in enumerate(values):
        tile = jnp.where(row == i, v, tile)
    return tile


def scale_body(hist_ref, tok_ref, out_ref, scal_ref):
    tops = jnp.max(hist_ref[...], axis=0, keepdims=True)
    scale_in = 448.0 / tops[:, 0:1]
    scale_grad = 448.0 / tops[:, 2:3]
    tok = tok_ref[...].astype(F32)
    quant = jnp.clip(tok * scale_in, -448.0, 448.0).astype(BF16)
    for i in range(out_ref.shape[0]):
        out_ref[i] = quant
    scal_ref[...] = rows_of(scale_in, scale_grad, top(jnp.abs(tok)))


def forward_body(place_ref, x_ref, g0_ref, u0_ref, g1_ref, u1_ref, out_ref, xh_ref, held_ref, sems):
    groups, cols, rows = out_ref.shape[0] // 2, x_ref.shape[0] // (out_ref.shape[0] // 2), x_ref.shape[1]
    copies = fetched((g0_ref, u0_ref, g1_ref, u1_ref), held_ref, sems)
    core, turned = place_ref[0], place_ref[1]
    for g in range(groups):
        for k in range(cols):
            xh_ref[g * rows : (g + 1) * rows, k * 128 : (k + 1) * 128] = x_ref[g * cols + k]
    x = xh_ref[...]
    for i, copy in enumerate(copies):
        place, half = (core if i < 2 else 1 - core), i % 2
        copy.wait()
        part = jnp.dot(x, held_ref[i], preferred_element_type=F32).astype(BF16)
        for g in range(groups):
            piece = 2 * lax.rem(turned + g, groups) + place
            out_ref[piece, half * rows : (half + 1) * rows, :] = part[g * rows : (g + 1) * rows]


def middle_body(in_ref, up_ref, scal_ref, hidden_ref, q_ref, peaks_ref):
    rows = up_ref.shape[0]
    scale_in = scal_ref[0:1, 0:1]
    scale_grad = scal_ref[1:2, 0:1]
    gate_sum = jnp.sum(in_ref[:, :rows, :].astype(F32), axis=0) / scale_in
    lift_sum = jnp.sum(in_ref[:, rows:, :].astype(F32), axis=0) / scale_in
    sigmoid_gate = 1.0 / (1.0 + jnp.exp(-gate_sum))
    activated = gate_sum * sigmoid_gate
    hidden = (activated * lift_sum).astype(BF16)
    hidden_ref[...] = hidden
    grad_in = up_ref[...].astype(F32)
    grad_gate = grad_in * lift_sum * sigmoid_gate * (1.0 + gate_sum * (1.0 - sigmoid_gate))
    grad_lift = grad_in * activated
    quant_gate = jnp.clip(grad_gate * scale_grad, -448.0, 448.0).astype(BF16)
    quant_lift = jnp.clip(grad_lift * scale_grad, -448.0, 448.0).astype(BF16)
    peak_grad = jnp.maximum(top(jnp.abs(grad_gate)), top(jnp.abs(grad_lift)))
    peaks_ref[...] = rows_of(scal_ref[2:3, 0:1], top(jnp.abs(hidden.astype(F32))), peak_grad)
    for i in range(q_ref.shape[0]):
        q_ref[i, :rows, :] = quant_gate
        q_ref[i, rows:, :] = quant_lift


def backward_body(
    place_ref, q_ref, g0_ref, u0_ref, g1_ref, u1_ref, out_ref, mine_ref, send_ref, held_ref, sems, kept_ref, out_sems
):
    groups = q_ref.shape[0] // 2
    rows = q_ref.shape[1] // 2
    cols = out_ref.shape[0] // groups
    copies = fetched((g0_ref, u0_ref, g1_ref, u1_ref), held_ref, sems)
    core, turned = place_ref[0], place_ref[1]
    contract = (((1,), (1,)), ((), ()))
    for i in range(4):
        which, half = i // 2, i % 2
        place = core if which == 0 else 1 - core
        for g in range(groups):
            piece = 2 * lax.rem(turned + g, groups) + place
            kept_ref[which, half, g * rows : (g + 1) * rows, :] = q_ref[piece, half * rows : (half + 1) * rows, :]
    sends = [
        pltpu.make_async_copy(kept_ref.at[which], far_ref, out_sems.at[which])
        for which, far_ref in ((1, send_ref), (0, mine_ref))
    ]
    for send in sends:
        send.start()
    total = None
    for i, copy in enumerate(copies):
        copy.wait()
        part = lax.dot_general(kept_ref[i // 2, i % 2], held_ref[i], contract, preferred_element_type=F32)
        total = part if total is None else total + part
    for g in range(groups):
        for k in range(cols):
            out_ref[g * cols + k] = total[g * rows : (g + 1) * rows, k * 128 : (k + 1) * 128].astype(BF16)
    for send in sends:
        send.wait()


def last_body(in_ref, scal_ref, hist_ref, peaks_ref, hidden_ref, out_ref, next_ref, hidden_out_ref):
    out_ref[...] = (jnp.sum(in_ref[...].astype(F32), axis=0) / scal_ref[1:2, 0:1]).astype(BF16)
    col = lax.broadcasted_iota(jnp.int32, (1, 3), 1)
    peaks = [peaks_ref[i : i + 1, 0:1] for i in range(3)]
    past = hist_ref.shape[0] - 1
    next_ref[0:past, :] = hist_ref[1:, :]
    next_ref[past:, :] = jnp.where(col == 0, peaks[0], jnp.where(col == 1, peaks[1], peaks[2]))
    hidden_out_ref[...] = hidden_ref[...]


def flips(n):
    bits = [1 << b for b in range(n.bit_length() - 1)]
    return [[(i, i ^ b) for i in range(n)] for b in bits]


def merged(peaks, axis, n):
    for perm in flips(n):
        peaks = jnp.maximum(peaks, lax.ppermute(peaks, axis, perm))
    return peaks


def per_device(sizes, tokens, w_gate, w_up, upstream, history):
    nh, nx, nw, ny = (sizes[a] for a in "hxwy")
    plane = ("h", "x", "w")
    count = nh * nx * nw
    rows, width = tokens.shape
    depth, units = w_gate.shape
    swap = [(0, 1), (1, 0)]
    spots = [(h, a, b) for h in range(nh) for a in range(nh) for b in range(2)]
    at = lambda h, a, b: h * ny + 2 * (a % nh) + b
    along_y = [(at(h, a, b), at(h, a + h, b)) for h, a, b in spots]
    along_z = [(at(h, a, b), at((a - h) % nh, a, b)) for h, a, b in spots]
    back_y = [(j, i) for i, j in along_y]
    place = jnp.stack([lax.axis_index("c"), lax.axis_index("h")])

    copies, scal = call(scale_body, [((count, rows, width), BF16), ((8, 128), F32)], (history, tokens))
    x_all = lax.all_to_all(copies, plane, 0, 0, tiled=True)
    gate_other = lax.ppermute(w_gate, "c", swap)
    lift_other = lax.ppermute(w_up, "c", swap)
    up = lax.ppermute(upstream, ("h", "y"), along_y)
    x_all, gate_other, lift_other, up = lax.optimization_barrier((x_all, gate_other, lift_other, up))
    weights = (w_gate, w_up, gate_other, lift_other)

    held = [pltpu.VMEM((4, depth, units), BF16), pltpu.SemaphoreType.DMA((4,))]
    work = 8 * nh * rows * depth * units
    parts, x_mine = call(
        forward_body,
        [((ny, 2 * rows, units), BF16), ((nh * rows, depth), BF16)],
        (place, x_all) + weights,
        flops=work,
        moved=6 * 2**20,
        scratch=held,
        far=range(2, 6),
    )
    parts, x_mine, up = lax.optimization_barrier((parts, x_mine, up))
    sums = lax.all_to_all(parts, "y", 0, 0, tiled=True)
    up = lax.ppermute(up, ("h", "y"), along_z)
    x_other = lax.ppermute(x_mine, "c", swap)
    sums, up, x_other = lax.optimization_barrier((sums, up, x_other))
    hidden, quants, peaks = call(
        middle_body,
        [((rows, units), BF16), ((ny, 2 * rows, units), BF16), ((8, 128), F32)],
        (sums, up, scal),
        moved=2**21,
    )
    q_all = lax.all_to_all(quants, "y", 0, 0, tiled=True)
    hidden = lax.ppermute(hidden, ("h", "y"), along_z)
    peaks = merged(merged(merged(peaks, "c", 2), "x", nx), ("h", "w"), nh * nw)
    q_all, hidden, peaks = lax.optimization_barrier((q_all, hidden, peaks))
    back, q_mine, q_send = call(
        backward_body,
        [((count, rows, width), BF16), ((2, nh * rows, units), BF16), ((2, nh * rows, units), BF16)],
        (place, q_all) + weights,
        flops=work,
        moved=6 * 2**20,
        scratch=held + [pltpu.VMEM((2, 2, nh * rows, units), BF16), pltpu.SemaphoreType.DMA((2,))],
        far=range(2, 6),
        far_outs=(1, 2),
    )
    back, q_send, hidden, peaks = lax.optimization_barrier((back, q_send, hidden, peaks))
    back_all = lax.all_to_all(back, plane, 0, 0, tiled=True)
    q_other = lax.ppermute(q_send, "c", swap)
    hidden = lax.ppermute(hidden, ("h", "y"), back_y)
    peaks = merged(peaks, "y", ny)
    divisor = scal[0, 0] * scal[1, 0] * (2 * nh * rows)
    contract = (((0,), (0,)), ((), ()))
    grads = []
    for i in range(2):
        total = lax.dot_general(x_mine, q_mine[i], contract, preferred_element_type=F32) + lax.dot_general(
            x_other, q_other[i], contract, preferred_element_type=F32
        )
        grads.append((total / divisor).astype(BF16))
    back_all, grads = lax.optimization_barrier((back_all, grads))
    input_grad, new_history, hidden = call(
        last_body,
        [((rows, width), BF16), (history.shape, F32), ((rows, units), BF16)],
        (back_all, scal, history, peaks, hidden),
        moved=2**21,
    )
    return (hidden, input_grad, grads[0], grads[1], new_history)


def solution(mesh):
    sizes = dict(h=mesh.shape["row"] // 2, c=2, x=mesh.shape["col"] // 2, w=2, y=mesh.shape["dep"])
    fine = Mesh(mesh.devices.reshape(tuple(sizes.values())), tuple(sizes))
    row, col = ("h", "c"), ("x", "w")
    placed = (
        P(row, ("y",) + col),
        P("y", col + row),
        P("y", col + row),
        P(row, col + ("y",)),
        P(),
    )

    def step(*args):
        return per_device(sizes, *args)

    return jax.shard_map(
        step,
        mesh=fine,
        in_specs=placed,
        out_specs=(P(row, col + ("y",)), P(row, ("y",) + col), P("y", col + row), P("y", col + row), P()),
        check_vma=False,
    )
```

time: 167 us -> 178 us (1.066)
  starting transfers between devices: 50.4 us -> 87.4 us
  blocking collectives: 29.5 us -> 0 us
  waiting for transfers between devices: 63.2 us -> 58 us
  Pallas kernels: 6.98 us -> 11.4 us
    ppermute x3 -> x13, starting transfers between devices: 6.82 us -> 40.4 us  [the longest x9 37.7 us: merged(): peaks = jnp.maximum(peaks, lax.ppermute(peaks, axis, perm))]
    all_to_all x1 -> x0, blocking collectives: 29.5 us -> none  [per_device(): q_all = lax.all_to_all(quants, 'y', 0, 0, tiled=True)]
    all_to_all x1, waiting for transfers between devices: 14.1 us -> 0.01 us  [per_device(): back_all = lax.all_to_all(back, plane, 0, 0, tiled=True)]
    ppermute x3 -> x13, waiting for transfers between devices: 0.01 us -> 13.5 us  [the longest x9 13.4 us: merged(): peaks = jnp.maximum(peaks, lax.ppermute(peaks, axis, perm))]
    ppermute x1, starting transfers between devices: 1.92 us -> 7.67 us  [per_device(): q_other = lax.ppermute(q_send, 'c', swap)]
    all_to_all x1, waiting for transfers between devices: 28.5 us -> 23 us  [per_device(): sums = lax.all_to_all(parts, 'y', 0, 0, tiled=True)]
    all_to_all x1, starting transfers between devices: 11.2 us -> 6.61 us  [per_device(): back_all = lax.all_to_all(back, plane, 0, 0, tiled=True)]
    pallas_call x6 -> x5, Pallas kernels: 6.98 us -> 11.4 us  [call(): pl.pallas_call(body, out_shape=[jax.ShapeDtypeStruct(s, t) for s, t in ou...]
  transfers between devices with their start and end apart: 10 -> 21, of which waited for: 4 -> 11; matrix products, arithmetic and copies ran while one was open for 3% -> 4% of each run, Pallas kernels for 0% -> 0%
where the time goes in v2:
time: 178 us; the launch traced here: 175 us
  starting transfers between devices  87.4 us (49%)
  waiting for transfers between devices  58 us (33%)
  Pallas kernels  11.4 us (6%)
  local copies, waits for them, and re-layouts  10.3 us (6%)
  matrix products  5.95 us (3%)
  between operations  2.25 us (1%)
    ppermute x9, starting transfers between devices, merged(): peaks = jnp.maximum(peaks, lax.ppermute(peaks, axis, perm))  37.7 us
    all_to_all x1, waiting for transfers between devices, per_device(): sums = lax.all_to_all(parts, 'y', 0, 0, tiled=True)  23 us
    all_to_all x1, waiting for transfers between devices, per_device(): x_all = lax.all_to_all(copies, plane, 0, 0, tiled=True)  19.4 us
    all_to_all x1, starting transfers between devices, per_device(): x_all = lax.all_to_all(copies, plane, 0, 0, tiled=True)  13.8 us
    ppermute x9, waiting for transfers between devices, merged(): peaks = jnp.maximum(peaks, lax.ppermute(peaks, axis, perm))  13.4 us
    pallas_call x5, Pallas kernels, call(): pl.pallas_call(body, out_shape=[jax.ShapeDtypeStruct(s, t) for s, t in ou...  11.4 us
    unnamed x28, local copies, waits for them, and re-layouts  9.76 us
    ppermute x1, starting transfers between devices, per_device(): q_other = lax.ppermute(q_send, 'c', swap)  7.67 us
  transfers between devices with their start and end apart: 21, of which 11 were waited for; matrix products, arithmetic and copies ran while one was open for 4% of the time, Pallas kernels for 0%

profile of v2, /device:TPU:1, one launch (start us, length us, event | category | flops | bytes accessed | tf_op | source)
XLA Modules:
  0.0 175.4 jit_solution(10951160775235244489)
XLA Ops:
  0.6 0.8 copy.10.hist_ref
  1.4 0.8 copy-done
  2.1 1.2 shard_map.92
  3.3 13.8 %all-to-all-start = ((bf16[32,128,128]{2,1,0:T(8,128)(2,1)}), bf16[32,128,128]{2,1,0:T(8,128)(2,1)S(1)}, u32[]{:S(2)}, u32[]{:S(2)}) async-start(bf16[32,128,128]{2,1,0:T(8,128)(2,1)} %get-tuple-element.38), calls=%async_computation | async-start | bytes 2097152 | tf_op jit(solution)/shard_map/all_to_all | solution.py:170
  17.2 2.9 %collective-permute-start = (bf16[1024,256]{1,0:T(8,128)(2,1)S(1)}, bf16[1024,256]{1,0:T(8,128)(2,1)S(1)}, u32[]{:S(2)}, u32[]{:S(2)}) collective-permute-start(bf16[1024,256]{1,0:T(8,128)(2,1)S(1)} %copy-done.1), channel_id=1, source_target_pairs={{0,64},{64,0},{1,65},{65,1},{2,66},{66,2},{3,67},{67,3},{4,68},{68... | collective-permute-start | bytes 1572872 | tf_op jit(solution)/shard_map/ppermute | solution.py:171
  20.1 1.9 %collective-permute-start.1 = (bf16[1024,256]{1,0:T(8,128)(2,1)S(1)}, bf16[1024,256]{1,0:T(8,128)(2,1)S(1)}, u32[]{:S(2)}, u32[]{:S(2)}) collective-permute-start(bf16[1024,256]{1,0:T(8,128)(2,1)S(1)} %copy-done.2), channel_id=1, source_target_pairs={{0,64},{64,0},{1,65},{65,1},{2,66},{66,2},{3,67},{67,3},{4,68},{68... | collective-permute-start | bytes 1572872 | tf_op jit(solution)/shard_map/ppermute | solution.py:172
  22.0 0.7 collective-permute-start.2
  22.7 0.1 pad_add_fusion.place_ref
  22.8 0.0 collective-permute-done.2
  22.8 0.0 collective-permute-done.g1_ref
  22.8 0.8 copy-done.4
  23.6 0.3 collective-permute-done.1.u1_ref
  23.9 0.8 copy-done.7
  24.7 19.4 %all-to-all-done.x_ref = bf16[32,128,128]{2,1,0:T(8,128)(2,1)S(1)} async-done(((bf16[32,128,128]{2,1,0:T(8,128)(2,1)}), bf16[32,128,128]{2,1,0:T(8,128)(2,1)S(1)}, u32[]{:S(2)}, u32[]{:S(2)}) %all-to-all-start) | async-done | bytes 1048608 | tf_op jit(solution)/shard_map/all_to_all | solution.py:170
  44.1 1.0 copy-done.5
  45.1 1.0 copy-done.8
  46.2 4.8 %shard_map.93 = (bf16[8,256,256]{2,1,0:T(8,128)(2,1)}, bf16[512,1024]{1,0:T(8,128)(2,1)S(1)}) custom-call(s32[2]{0:T(128)S(1)} %pad_add_fusion.place_ref, bf16[32,128,128]{2,1,0:T(8,128)(2,1)S(1)} %all-to-all-done.x_ref, bf16[1024,256]{1,0:T(8,128)(2,1)S(1)} %copy-done.1, bf16[1024,256]{1,0:T(8,128)(2,1)S(1)} %copy-done.2, bf16[1024,256]{1,0:T(8,128)(2,1)S(1)} %copy-done.5, ...), custom_call_target="tpu_custom_call" | custom-call | flops 1073741824 | bytes 6291456 | tf_op jit(solution)/shard_map/pallas_call | solution.py:21
  51.0 6.8 %all-to-all-start.1 = ((bf16[8,256,256]{2,1,0:T(8,128)(2,1)}), bf16[8,256,256]{2,1,0:T(8,128)(2,1)S(1)}, u32[]{:S(2)}, u32[]{:S(2)}) async-start(bf16[8,256,256]{2,1,0:T(8,128)(2,1)} %get-tuple-element.45), calls=%async_computation.1 | async-start | bytes 2097152 | tf_op jit(solution)/shard_map/all_to_all | solution.py:189
  57.8 3.7 %collective-permute-start.4 = (bf16[512,1024]{1,0:T(8,128)(2,1)S(1)}, bf16[512,1024]{1,0:T(8,128)(2,1)}, u32[]{:S(2)}, u32[]{:S(2)}) collective-permute-start(bf16[512,1024]{1,0:T(8,128)(2,1)S(1)} %get-tuple-element.47), channel_id=1, source_target_pairs={{0,64},{64,0},{1,65},{65,1},{2,66},{66,2},{3,67},{67,3},{4,68},{68... | collective-permute-start | bytes 3145736 | tf_op jit(solution)/shard_map/ppermute | solution.py:191
  61.5 0.7 collective-permute-start.3
  62.2 0.0 collective-permute-done.3.up_ref
  62.2 1.7 collective-permute-done.4
  63.9 23.0 %all-to-all-done.1.in_ref = bf16[8,256,256]{2,1,0:T(8,128)(2,1)S(1)} async-done(((bf16[8,256,256]{2,1,0:T(8,128)(2,1)}), bf16[8,256,256]{2,1,0:T(8,128)(2,1)S(1)}, u32[]{:S(2)}, u32[]{:S(2)}) %all-to-all-start.1) | async-done | bytes 1048608 | tf_op jit(solution)/shard_map/all_to_all | solution.py:189
  87.0 1.3 shard_map.94
  88.3 3.6 %all-to-all-start.2 = ((bf16[8,256,256]{2,1,0:T(8,128)(2,1)}), bf16[8,256,256]{2,1,0:T(8,128)(2,1)S(1)}, u32[]{:S(2)}, u32[]{:S(2)}) async-start(bf16[8,256,256]{2,1,0:T(8,128)(2,1)} %get-tuple-element.51), calls=%async_computation.2 | async-start | bytes 2097152 | tf_op jit(solution)/shard_map/all_to_all | solution.py:199
  91.8 0.7 collective-permute-start.5
  92.5 2.4 %collective-permute-start.6 = (f32[8,128]{1,0:T(8,128)S(1)}, f32[8,128]{1,0:T(8,128)S(1)}, u32[]{:S(2)}, u32[]{:S(2)}) collective-permute-start(f32[8,128]{1,0:T(8,128)S(1)} %get-tuple-element.53), channel_id=1, source_target_pairs={{0,64},{64,0},{1,65},{65,1},{2,66},{66,2},{3,67},{67,3},{4,68},{68... | collective-permute-start | bytes 12296 | tf_op jit(solution)/shard_map/ppermute | solution.py:151
  94.9 0.8 collective-permute-done.6
  95.7 2.4 %collective-permute-start.7 = (f32[8,128]{1,0:T(8,128)S(1)}, f32[8,128]{1,0:T(8,128)S(1)}, u32[]{:S(2)}, u32[]{:S(2)}) collective-permute-start(f32[8,128]{1,0:T(8,128)S(1)} %max.27), channel_id=1, source_target_pairs={{0,16},{16,0},{32,48},{48,32},{1,17},{17,1},{33,49},{49,33},{2,18}... | collective-permute-start | bytes 12296 | tf_op jit(solution)/shard_map/ppermute | solution.py:151
  98.1 2.2 %collective-permute-done.7 = f32[8,128]{1,0:T(8,128)S(1)} collective-permute-done((f32[8,128]{1,0:T(8,128)S(1)}, f32[8,128]{1,0:T(8,128)S(1)}, u32[]{:S(2)}, u32[]{:S(2)}) %collective-permute-start.7) | collective-permute-done | bytes 4128 | tf_op jit(solution)/shard_map/ppermute | solution.py:151
  100.4 4.5 %collective-permute-start.8 = (f32[8,128]{1,0:T(8,128)S(1)}, f32[8,128]{1,0:T(8,128)S(1)}, u32[]{:S(2)}, u32[]{:S(2)}) collective-permute-start(f32[8,128]{1,0:T(8,128)S(1)} %max.28), channel_id=1, source_target_pairs={{0,32},{16,48},{32,0},{48,16},{1,33},{17,49},{33,1},{49,17},{2,34}... | collective-permute-start | bytes 12296 | tf_op jit(solution)/shard_map/ppermute | solution.py:151
  104.8 1.5 collective-permute-done.8
  106.3 2.4 %collective-permute-start.9 = (f32[8,128]{1,0:T(8,128)S(1)}, f32[8,128]{1,0:T(8,128)S(1)}, u32[]{:S(2)}, u32[]{:S(2)}) collective-permute-start(f32[8,128]{1,0:T(8,128)S(1)} %max.29), channel_id=1, source_target_pairs={{0,8},{8,0},{128,136},{136,128},{256,264},{264,256},{384,392},{392... | collective-permute-start | bytes 12296 | tf_op jit(solution)/shard_map/ppermute | solution.py:151
  108.8 2.2 %collective-permute-done.9 = f32[8,128]{1,0:T(8,128)S(1)} collective-permute-done((f32[8,128]{1,0:T(8,128)S(1)}, f32[8,128]{1,0:T(8,128)S(1)}, u32[]{:S(2)}, u32[]{:S(2)}) %collective-permute-start.9) | collective-permute-done | bytes 4128 | tf_op jit(solution)/shard_map/ppermute | solution.py:151
  111.0 6.8 %collective-permute-start.10 = (f32[8,128]{1,0:T(8,128)S(1)}, f32[8,128]{1,0:T(8,128)S(1)}, u32[]{:S(2)}, u32[]{:S(2)}) collective-permute-start(f32[8,128]{1,0:T(8,128)S(1)} %max.30), channel_id=1, source_target_pairs={{0,128},{8,136},{128,0},{136,8},{256,384},{264,392},{384,256},{392... | collective-permute-start | bytes 12296 | tf_op jit(solution)/shard_map/ppermute | solution.py:151
  117.8 1.3 collective-permute-done.10
  119.1 3.9 %collective-permute-start.11 = (f32[8,128]{1,0:T(8,128)S(1)}, f32[8,128]{1,0:T(8,128)S(1)}, u32[]{:S(2)}, u32[]{:S(2)}) collective-permute-start(f32[8,128]{1,0:T(8,128)S(1)} %max.31), channel_id=1, source_target_pairs={{0,256},{8,264},{128,384},{136,392},{256,0},{264,8},{384,128},{392... | collective-permute-start | bytes 12296 | tf_op jit(solution)/shard_map/ppermute | solution.py:151
  123.0 4.3 %collective-permute-done.11 = f32[8,128]{1,0:T(8,128)S(1)} collective-permute-done((f32[8,128]{1,0:T(8,128)S(1)}, f32[8,128]{1,0:T(8,128)S(1)}, u32[]{:S(2)}, u32[]{:S(2)}) %collective-permute-start.11) | collective-permute-done | bytes 4128 | tf_op jit(solution)/shard_map/ppermute | solution.py:151
  127.4 0.0 collective-permute-done.5
  127.4 0.0 all-to-all-done.2.q_ref
  127.4 0.0 copy-start.3
  127.4 1.0 copy-done.3
  128.4 1.0 copy-done.6
  129.5 1.0 copy-done.9
  130.5 3.4 %shard_map.95 = (bf16[32,128,128]{2,1,0:T(8,128)(2,1)}, bf16[2,512,256]{2,1,0:T(8,128)(2,1)S(1)}, bf16[2,512,256]{2,1,0:T(8,128)(2,1)S(1)}) custom-call(s32[2]{0:T(128)S(1)} %pad_add_fusion.place_ref, bf16[8,256,256]{2,1,0:T(8,128)(2,1)S(1)} %all-to-all-done.2.q_ref, bf16[1024,256]{1,0:T(8,128)(2,1)S(1)} %copy-done.1, bf16[1024,256]{1,0:T(8,128)(2,1)S(1)} %copy-done.3, ...), custom_call_target="tpu_custom_call" | custom-call | flops 1073741824 | bytes 6291456 | tf_op jit(solution)/shard_map/pallas_call | solution.py:21
  133.9 0.0 copy-start.10
  133.9 0.8 copy-done.10
  134.7 6.6 %all-to-all-start.3 = ((bf16[32,128,128]{2,1,0:T(8,128)(2,1)}), bf16[32,128,128]{2,1,0:T(8,128)(2,1)S(1)}, u32[]{:S(2)}, u32[]{:S(2)}) async-start(bf16[32,128,128]{2,1,0:T(8,128)(2,1)} %get-tuple-element.59), calls=%async_computation.3 | async-start | bytes 2097152 | tf_op jit(solution)/shard_map/all_to_all | solution.py:214
  141.3 3.7 %collective-permute-start.13 = (f32[8,128]{1,0:T(8,128)S(1)}, f32[8,128]{1,0:T(8,128)S(1)}, u32[]{:S(2)}, u32[]{:S(2)}) collective-permute-start(f32[8,128]{1,0:T(8,128)S(1)} %max.32), channel_id=1, source_target_pairs={{0,1},{1,0},{2,3},{3,2},{4,5},{5,4},{6,7},{7,6},{8,9},{9,8},{10,11... | collective-permute-start | bytes 12296 | tf_op jit(solution)/shard_map/ppermute | solution.py:151
  145.0 0.5 fusion.10
  146.9 7.7 %collective-permute-start.12 = (bf16[2,512,256]{2,1,0:T(8,128)(2,1)S(1)}, bf16[2,512,256]{2,1,0:T(8,128)(2,1)S(1)}, u32[]{:S(2)}, u32[]{:S(2)}) collective-permute-start(bf16[2,512,256]{2,1,0:T(8,128)(2,1)S(1)} %copy-done.11), channel_id=1, source_target_pairs={{0,64},{64,0},{1,65},{65,1},{2,66},{66,2},{3,67},{67,3},{4,68},{68... | collective-permute-start | bytes 1572872 | tf_op jit(solution)/shard_map/ppermute | solution.py:215
  154.5 0.0 collective-permute-done.13
  154.6 4.0 %collective-permute-start.14 = (f32[8,128]{1,0:T(8,128)S(1)}, f32[8,128]{1,0:T(8,128)S(1)}, u32[]{:S(2)}, u32[]{:S(2)}) collective-permute-start(f32[8,128]{1,0:T(8,128)S(1)} %max.33), channel_id=1, source_target_pairs={{0,2},{1,3},{2,0},{3,1},{4,6},{5,7},{6,4},{7,5},{8,10},{9,11},{10,... | collective-permute-start | bytes 12296 | tf_op jit(solution)/shard_map/ppermute | solution.py:151
  158.6 0.5 fusion.4
  159.0 1.1 collective-permute-done.14
  160.1 7.6 %collective-permute-start.15 = (f32[8,128]{1,0:T(8,128)S(1)}, f32[8,128]{1,0:T(8,128)S(1)}, u32[]{:S(2)}, u32[]{:S(2)}) collective-permute-start(f32[8,128]{1,0:T(8,128)S(1)} %max.34), channel_id=1, source_target_pairs={{0,4},{1,5},{2,6},{3,7},{4,0},{5,1},{6,2},{7,3},{8,12},{9,13},{10,... | collective-permute-start | bytes 12296 | tf_op jit(solution)/shard_map/ppermute | solution.py:151
  167.7 0.5 fusion.6
  168.2 0.7 collective-permute-start.16
  168.8 0.0 collective-permute-done.15
  168.9 0.0 collective-permute-done.12
  168.9 2.5 %fusion.3 = bf16[1024,256]{1,0:T(8,128)(2,1)} fusion(f32[1024,256]{1,0:T(8,128)S(1)} %fusion.4, bf16[512,1024]{1,0:T(8,128)(2,1)} %collective-permute-done.4, f32[]{:T(128)} %bitcast.4, bf16[2,512,256]{2,1,0:T(8,128)(2,1)S(1)} %collective-permute-done.12), kind=kOutput, calls=%fused_computation.5 | convolution fusion | flops 269221888 | bytes 2883588 | tf_op jit(solution)/shard_map/dot_general | solution.py:222
  171.4 2.5 %fusion.2 = bf16[1024,256]{1,0:T(8,128)(2,1)} fusion(f32[1024,256]{1,0:T(8,128)S(1)} %fusion.6, bf16[512,1024]{1,0:T(8,128)(2,1)} %collective-permute-done.4, f32[]{:T(128)} %bitcast.4, bf16[2,512,256]{2,1,0:T(8,128)(2,1)S(1)} %collective-permute-done.12), kind=kOutput, calls=%fused_computation.4 | convolution fusion | flops 269221888 | bytes 2883588 | tf_op jit(solution)/shard_map/dot_general | solution.py:222
  173.9 0.8 shard_map.96
  174.7 0.7 copy.12
  (26 shorter events, 0.1 us)
Async XLA Ops:
  1.4 0.8 copy-start
  3.3 13.9 %copy-start.1 = (bf16[1024,256]{1,0:T(8,128)(2,1)S(1)}, bf16[1024,256]{1,0:T(8,128)(2,1)}, u32[]{:S(2)}) copy-start(bf16[1024,256]{1,0:T(8,128)(2,1)} %g0_ref.3) | copy-start | bytes 1572868
  3.3 16.7 %copy-start.2 = (bf16[1024,256]{1,0:T(8,128)(2,1)S(1)}, bf16[1024,256]{1,0:T(8,128)(2,1)}, u32[]{:S(2)}) copy-start(bf16[1024,256]{1,0:T(8,128)(2,1)} %u0_ref.3) | copy-start | bytes 1572868
  3.3 18.7 %copy-start.12 = (bf16[128,256]{1,0:T(8,128)(2,1)S(1)}, bf16[128,256]{1,0:T(8,128)(2,1)}, u32[]{:S(2)}) copy-start(bf16[128,256]{1,0:T(8,128)(2,1)} %param.8) | copy-start | bytes 196612
  3.3 40.8 %all-to-all-start = ((bf16[32,128,128]{2,1,0:T(8,128)(2,1)}), bf16[32,128,128]{2,1,0:T(8,128)(2,1)S(1)}, u32[]{:S(2)}, u32[]{:S(2)}) async-start(bf16[32,128,128]{2,1,0:T(8,128)(2,1)} %get-tuple-element.38), calls=%async_computation | async-start | bytes 2097152 | tf_op jit(solution)/shard_map/all_to_all | solution.py:170
  17.2 5.6 %collective-permute-start = (bf16[1024,256]{1,0:T(8,128)(2,1)S(1)}, bf16[1024,256]{1,0:T(8,128)(2,1)S(1)}, u32[]{:S(2)}, u32[]{:S(2)}) collective-permute-start(bf16[1024,256]{1,0:T(8,128)(2,1)S(1)} %copy-done.1), channel_id=1, source_target_pairs={{0,64},{64,0},{1,65},{65,1},{2,66},{66,2},{3,67},{67,3},{4,68},{68... | collective-permute-start | bytes 1572872 | tf_op jit(solution)/shard_map/ppermute | solution.py:171
  20.1 3.8 %collective-permute-start.1 = (bf16[1024,256]{1,0:T(8,128)(2,1)S(1)}, bf16[1024,256]{1,0:T(8,128)(2,1)S(1)}, u32[]{:S(2)}, u32[]{:S(2)}) collective-permute-start(bf16[1024,256]{1,0:T(8,128)(2,1)S(1)} %copy-done.2), channel_id=1, source_target_pairs={{0,64},{64,0},{1,65},{65,1},{2,66},{66,2},{3,67},{67,3},{4,68},{68... | collective-permute-start | bytes 1572872 | tf_op jit(solution)/shard_map/ppermute | solution.py:172
  22.0 0.8 collective-permute-start.2
  22.8 0.8 copy-start.4
  23.9 0.8 copy-start.7
  44.1 1.0 copy-start.5
  45.1 1.0 copy-start.8
  51.0 36.0 %all-to-all-start.1 = ((bf16[8,256,256]{2,1,0:T(8,128)(2,1)}), bf16[8,256,256]{2,1,0:T(8,128)(2,1)S(1)}, u32[]{:S(2)}, u32[]{:S(2)}) async-start(bf16[8,256,256]{2,1,0:T(8,128)(2,1)} %get-tuple-element.45), calls=%async_computation.1 | async-start | bytes 2097152 | tf_op jit(solution)/shard_map/all_to_all | solution.py:189
  57.8 6.1 %collective-permute-start.4 = (bf16[512,1024]{1,0:T(8,128)(2,1)S(1)}, bf16[512,1024]{1,0:T(8,128)(2,1)}, u32[]{:S(2)}, u32[]{:S(2)}) collective-permute-start(bf16[512,1024]{1,0:T(8,128)(2,1)S(1)} %get-tuple-element.47), channel_id=1, source_target_pairs={{0,64},{64,0},{1,65},{65,1},{2,66},{66,2},{3,67},{67,3},{4,68},{68... | collective-permute-start | bytes 3145736 | tf_op jit(solution)/shard_map/ppermute | solution.py:191
  61.5 0.7 collective-permute-start.3
  88.3 39.1 %all-to-all-start.2 = ((bf16[8,256,256]{2,1,0:T(8,128)(2,1)}), bf16[8,256,256]{2,1,0:T(8,128)(2,1)S(1)}, u32[]{:S(2)}, u32[]{:S(2)}) async-start(bf16[8,256,256]{2,1,0:T(8,128)(2,1)} %get-tuple-element.51), calls=%async_computation.2 | async-start | bytes 2097152 | tf_op jit(solution)/shard_map/all_to_all | solution.py:199
  91.8 35.5 %collective-permute-start.5 = (bf16[128,256]{1,0:T(8,128)(2,1)S(1)}, bf16[128,256]{1,0:T(8,128)(2,1)S(1)}, u32[]{:S(2)}, u32[]{:S(2)}) collective-permute-start(bf16[128,256]{1,0:T(8,128)(2,1)S(1)} %get-tuple-element.52), channel_id=1, source_target_pairs={{0,0},{1,1},{2,130},{3,131},{4,260},{5,261},{6,390},{7,391},{128,3... | collective-permute-start | bytes 196616 | tf_op jit(solution)/shard_map/ppermute | solution.py:200
  92.5 3.2 %collective-permute-start.6 = (f32[8,128]{1,0:T(8,128)S(1)}, f32[8,128]{1,0:T(8,128)S(1)}, u32[]{:S(2)}, u32[]{:S(2)}) collective-permute-start(f32[8,128]{1,0:T(8,128)S(1)} %get-tuple-element.53), channel_id=1, source_target_pairs={{0,64},{64,0},{1,65},{65,1},{2,66},{66,2},{3,67},{67,3},{4,68},{68... | collective-permute-start | bytes 12296 | tf_op jit(solution)/shard_map/ppermute | solution.py:151
  95.7 4.6 %collective-permute-start.7 = (f32[8,128]{1,0:T(8,128)S(1)}, f32[8,128]{1,0:T(8,128)S(1)}, u32[]{:S(2)}, u32[]{:S(2)}) collective-permute-start(f32[8,128]{1,0:T(8,128)S(1)} %max.27), channel_id=1, source_target_pairs={{0,16},{16,0},{32,48},{48,32},{1,17},{17,1},{33,49},{49,33},{2,18}... | collective-permute-start | bytes 12296 | tf_op jit(solution)/shard_map/ppermute | solution.py:151
  100.4 6.0 %collective-permute-start.8 = (f32[8,128]{1,0:T(8,128)S(1)}, f32[8,128]{1,0:T(8,128)S(1)}, u32[]{:S(2)}, u32[]{:S(2)}) collective-permute-start(f32[8,128]{1,0:T(8,128)S(1)} %max.28), channel_id=1, source_target_pairs={{0,32},{16,48},{32,0},{48,16},{1,33},{17,49},{33,1},{49,17},{2,34}... | collective-permute-start | bytes 12296 | tf_op jit(solution)/shard_map/ppermute | solution.py:151
  106.3 4.6 %collective-permute-start.9 = (f32[8,128]{1,0:T(8,128)S(1)}, f32[8,128]{1,0:T(8,128)S(1)}, u32[]{:S(2)}, u32[]{:S(2)}) collective-permute-start(f32[8,128]{1,0:T(8,128)S(1)} %max.29), channel_id=1, source_target_pairs={{0,8},{8,0},{128,136},{136,128},{256,264},{264,256},{384,392},{392... | collective-permute-start | bytes 12296 | tf_op jit(solution)/shard_map/ppermute | solution.py:151
  111.0 8.1 %collective-permute-start.10 = (f32[8,128]{1,0:T(8,128)S(1)}, f32[8,128]{1,0:T(8,128)S(1)}, u32[]{:S(2)}, u32[]{:S(2)}) collective-permute-start(f32[8,128]{1,0:T(8,128)S(1)} %max.30), channel_id=1, source_target_pairs={{0,128},{8,136},{128,0},{136,8},{256,384},{264,392},{384,256},{392... | collective-permute-start | bytes 12296 | tf_op jit(solution)/shard_map/ppermute | solution.py:151
  119.1 8.3 %collective-permute-start.11 = (f32[8,128]{1,0:T(8,128)S(1)}, f32[8,128]{1,0:T(8,128)S(1)}, u32[]{:S(2)}, u32[]{:S(2)}) collective-permute-start(f32[8,128]{1,0:T(8,128)S(1)} %max.31), channel_id=1, source_target_pairs={{0,256},{8,264},{128,384},{136,392},{256,0},{264,8},{384,128},{392... | collective-permute-start | bytes 12296 | tf_op jit(solution)/shard_map/ppermute | solution.py:151
  127.4 1.0 copy-start.3
  128.4 1.0 copy-start.6
  129.5 1.0 copy-start.9
  133.9 0.8 copy-start.10
  134.7 12.2 %copy-start.11 = (bf16[2,512,256]{2,1,0:T(8,128)(2,1)S(1)}, bf16[2,512,256]{2,1,0:T(8,128)(2,1)}, u32[]{:S(2)}) copy-start(bf16[2,512,256]{2,1,0:T(8,128)(2,1)} %copy-done.10) | copy-start | bytes 1572868
  134.7 39.2 %all-to-all-start.3 = ((bf16[32,128,128]{2,1,0:T(8,128)(2,1)}), bf16[32,128,128]{2,1,0:T(8,128)(2,1)S(1)}, u32[]{:S(2)}, u32[]{:S(2)}) async-start(bf16[32,128,128]{2,1,0:T(8,128)(2,1)} %get-tuple-element.59), calls=%async_computation.3 | async-start | bytes 2097152 | tf_op jit(solution)/shard_map/all_to_all | solution.py:214
  141.3 13.3 %collective-permute-start.13 = (f32[8,128]{1,0:T(8,128)S(1)}, f32[8,128]{1,0:T(8,128)S(1)}, u32[]{:S(2)}, u32[]{:S(2)}) collective-permute-start(f32[8,128]{1,0:T(8,128)S(1)} %max.32), channel_id=1, source_target_pairs={{0,1},{1,0},{2,3},{3,2},{4,5},{5,4},{6,7},{7,6},{8,9},{9,8},{10,11... | collective-permute-start | bytes 12296 | tf_op jit(solution)/shard_map/ppermute | solution.py:151
  146.9 22.0 %collective-permute-start.12 = (bf16[2,512,256]{2,1,0:T(8,128)(2,1)S(1)}, bf16[2,512,256]{2,1,0:T(8,128)(2,1)S(1)}, u32[]{:S(2)}, u32[]{:S(2)}) collective-permute-start(bf16[2,512,256]{2,1,0:T(8,128)(2,1)S(1)} %copy-done.11), channel_id=1, source_target_pairs={{0,64},{64,0},{1,65},{65,1},{2,66},{66,2},{3,67},{67,3},{4,68},{68... | collective-permute-start | bytes 1572872 | tf_op jit(solution)/shard_map/ppermute | solution.py:215
  154.6 5.6 %collective-permute-start.14 = (f32[8,128]{1,0:T(8,128)S(1)}, f32[8,128]{1,0:T(8,128)S(1)}, u32[]{:S(2)}, u32[]{:S(2)}) collective-permute-start(f32[8,128]{1,0:T(8,128)S(1)} %max.33), channel_id=1, source_target_pairs={{0,2},{1,3},{2,0},{3,1},{4,6},{5,7},{6,4},{7,5},{8,10},{9,11},{10,... | collective-permute-start | bytes 12296 | tf_op jit(solution)/shard_map/ppermute | solution.py:151
  160.1 8.7 %collective-permute-start.15 = (f32[8,128]{1,0:T(8,128)S(1)}, f32[8,128]{1,0:T(8,128)S(1)}, u32[]{:S(2)}, u32[]{:S(2)}) collective-permute-start(f32[8,128]{1,0:T(8,128)S(1)} %max.34), channel_id=1, source_target_pairs={{0,4},{1,5},{2,6},{3,7},{4,0},{5,1},{6,2},{7,3},{8,12},{9,13},{10,... | collective-permute-start | bytes 12296 | tf_op jit(solution)/shard_map/ppermute | solution.py:151
  168.2 5.7 %collective-permute-start.16 = (bf16[128,256]{1,0:T(8,128)(2,1)S(1)}, bf16[128,256]{1,0:T(8,128)(2,1)S(1)}, u32[]{:S(2)}, u32[]{:S(2)}) collective-permute-start(bf16[128,256]{1,0:T(8,128)(2,1)S(1)} %collective-permute-done.5), channel_id=1, source_target_pairs={{0,0},{1,1},{2,2},{3,3},{4,4},{5,5},{6,6},{7,7},{130,128},{131,129... | collective-permute-start | bytes 196616 | tf_op jit(solution)/shard_map/ppermute | solution.py:216

commit v3 on v1

--- a/solution.py
+++ b/solution.py
@@ -13,7 +13,7 @@
 
 
 def params():
-    return pltpu.CompilerParams(vmem_limit_bytes=40 * 1024 * 1024)
+    return pltpu.CompilerParams(vmem_limit_bytes=16 * 1024 * 1024)
 
 
 def call(body, outs, args, flops=0, moved=0, scratch=()):
@@ -63,12 +63,13 @@
     scal_ref[...] = rows_of(scale_in, scale_grad, top(jnp.abs(tok)))
 
 
-def forward_body(core_ref, x_ref, g0_ref, u0_ref, g1_ref, u1_ref, out_ref, xh_ref):
+def forward_body(place_ref, x_ref, g0_ref, u0_ref, g1_ref, u1_ref, out_ref, xh_ref):
     groups, cols, rows = out_ref.shape[0] // 2, x_ref.shape[0] // (out_ref.shape[0] // 2), x_ref.shape[1]
-    core = core_ref[0]
+    core, turned = place_ref[0], place_ref[1]
     for g in range(groups):
+        spot = pl.ds(pl.multiple_of(lax.rem(turned + g, groups) * rows, rows), rows)
         for k in range(cols):
-            xh_ref[g * rows : (g + 1) * rows, k * 128 : (k + 1) * 128] = x_ref[g * cols + k]
+            xh_ref[spot, k * 128 : (k + 1) * 128] = x_ref[g * cols + k]
     x = xh_ref[...]
     for which, pair in enumerate(((g0_ref, u0_ref), (g1_ref, u1_ref))):
         place = core if which == 0 else 1 - core
@@ -96,39 +97,39 @@
     peak_grad = jnp.maximum(top(jnp.abs(grad_gate)), top(jnp.abs(grad_lift)))
     peaks = pack_peaks(scal_ref[2:3, 0:1], top(jnp.abs(hidden.astype(F32))), peak_grad)
     wide = jnp.concatenate([peaks, peaks], axis=1)
-    wide = jnp.concatenate([wide, wide], axis=0)
     for i in range(q_ref.shape[0]):
         q_ref[i, :rows, :] = quant_gate
         q_ref[i, rows : 2 * rows, :] = quant_lift
         q_ref[i, 2 * rows :, :] = wide
 
 
-def backward_body(core_ref, q_ref, g0_ref, u0_ref, g1_ref, u1_ref, out_ref, mine_ref, send_ref):
+def backward_body(place_ref, q_ref, g0_ref, u0_ref, g1_ref, u1_ref, out_ref, kept_ref):
     groups = q_ref.shape[0] // 2
-    rows = (q_ref.shape[1] - 16) // 2
+    rows = (q_ref.shape[1] - 8) // 2
     cols = out_ref.shape[0] // groups
-    core = core_ref[0]
+    core, turned = place_ref[0], place_ref[1]
     contract = (((1,), (1,)), ((), ()))
     total = None
     for which, pair in enumerate(((g0_ref, u0_ref), (g1_ref, u1_ref))):
         place = core if which == 0 else 1 - core
-        kept = mine_ref if which == 0 else send_ref
         for half, w_ref in enumerate(pair):
             for g in range(groups):
-                kept[half, g * rows : (g + 1) * rows, :] = q_ref[2 * g + place, half * rows : (half + 1) * rows, :]
-            part = lax.dot_general(kept[half], w_ref[...], contract, preferred_element_type=F32)
+                kept_ref[g * rows : (g + 1) * rows, :] = q_ref[2 * g + place, half * rows : (half + 1) * rows, :]
+            part = lax.dot_general(kept_ref[...], w_ref[...], contract, preferred_element_type=F32)
             total = part if total is None else total + part
-    packed = pack_peaks(*unpack_peaks(q_ref[:, 2 * rows : 2 * rows + 16, 0:128].astype(F32)[:, 0:8, :]))
+    packed = pack_peaks(*unpack_peaks(q_ref[:, 2 * rows :, 0:128].astype(F32)))
     for g in range(groups):
+        first = lax.rem(groups + g - turned, groups) * cols
         for k in range(cols):
-            out_ref[g * cols + k, :rows, :] = total[g * rows : (g + 1) * rows, k * 128 : (k + 1) * 128].astype(BF16)
-            out_ref[g * cols + k, rows:, :] = packed
-
-
-def last_body(in_ref, scal_ref, out_ref, peaks_ref):
+            out_ref[first + k, :rows, :] = total[g * rows : (g + 1) * rows, k * 128 : (k + 1) * 128].astype(BF16)
+            out_ref[first + k, rows:, :] = packed
+
+
+def last_body(in_ref, scal_ref, hidden_ref, out_ref, peaks_ref, hidden_out_ref):
     rows = out_ref.shape[0]
     out_ref[...] = (jnp.sum(in_ref[:, :rows, :].astype(F32), axis=0) / scal_ref[1:2, 0:1]).astype(BF16)
     peaks_ref[...] = rows_of(*unpack_peaks(in_ref[:, rows:, :].astype(F32)))
+    hidden_out_ref[...] = hidden_ref[...]
 
 
 def history_body(hist_ref, mine_ref, other_ref, out_ref):
@@ -147,40 +148,60 @@
     rows, width = tokens.shape
     depth, units = w_gate.shape
     swap = [(0, 1), (1, 0)]
-    turn = [(h * ny + y, (y // 2) * ny + h * 2 + y % 2) for h in range(nh) for y in range(ny)]
-    core = lax.axis_index("c").reshape(1)
+    spots = [(h, a, b) for h in range(nh) for a in range(nh) for b in range(2)]
+    at = lambda h, a, b: h * ny + 2 * (a % nh) + b
+    along_y = [(at(h, a, b), at(h, a + h, b)) for h, a, b in spots]
+    along_z = [(at(h, a, b), at((a - h) % nh, a, b)) for h, a, b in spots]
+    back_y = [(j, i) for i, j in along_y]
+    core = lax.axis_index("c")
+    place = jnp.stack([core, lax.axis_index("h")])
 
     copies, scal = call(scale_body, [((count, rows, width), BF16), ((8, 128), F32)], (history, tokens))
-    up = lax.ppermute(upstream, ("h", "y"), turn)
+    x_all = lax.all_to_all(copies, plane, 0, 0, tiled=True)
     gate_other = lax.ppermute(w_gate, "c", swap)
     lift_other = lax.ppermute(w_up, "c", swap)
-    weights = (w_gate, w_up, gate_other, lift_other)
-    x_all = lax.all_to_all(copies, plane, 0, 0, tiled=True)
+    up = lax.ppermute(upstream, ("h", "y"), along_y)
+    x_all, gate_other, lift_other, up = lax.optimization_barrier((x_all, gate_other, lift_other, up))
 
     work = 8 * nh * rows * depth * units
     parts, x_mine = call(
         forward_body,
         [((ny, 2 * rows, units), BF16), ((nh * rows, depth), BF16)],
-        (core, x_all) + weights,
+        (place, x_all, w_gate, w_up, gate_other, lift_other),
         flops=work,
         moved=6 * 2**20,
     )
+    parts, x_mine, up = lax.optimization_barrier((parts, x_mine, up))
     sums = lax.all_to_all(parts, "y", 0, 0, tiled=True)
+    up = lax.ppermute(up, ("h", "y"), along_z)
+    sums, up = lax.optimization_barrier((sums, up))
+    hidden, quants = call(
+        middle_body, [((rows, units), BF16), ((ny, 2 * rows + 8, units), BF16)], (sums, up, scal), moved=2**21
+    )
+    quants, x_mine = lax.optimization_barrier((quants, x_mine))
+    q_all = lax.all_to_all(quants, "y", 0, 0, tiled=True)
+    hidden = lax.ppermute(hidden, ("h", "y"), along_z)
     x_other = lax.ppermute(x_mine, "c", swap)
-    hidden, quants = call(
-        middle_body, [((rows, units), BF16), ((ny, 2 * rows + 16, units), BF16)], (sums, up, scal), moved=2**21
-    )
-    q_all = lax.all_to_all(quants, "y", 0, 0, tiled=True)
-    hidden = lax.ppermute(hidden, ("h", "y"), turn)
-    back, q_mine, q_send = call(
+    q_all, hidden, x_other = lax.optimization_barrier((q_all, hidden, x_other))
+    (back,) = call(
         backward_body,
-        [((count, rows + 8, width), BF16), ((2, nh * rows, units), BF16), ((2, nh * rows, units), BF16)],
-        (core, q_all) + weights,
+        [((count, rows + 8, width), BF16)],
+        (place, q_all, w_gate, w_up, gate_other, lift_other),
         flops=work,
         moved=6 * 2**20,
-    )
+        scratch=[pltpu.VMEM((nh * rows, units), BF16)],
+    )
+    back, q_all, hidden = lax.optimization_barrier((back, q_all, hidden))
     back_all = lax.all_to_all(back, plane, 0, 0, tiled=True)
-    q_other = lax.ppermute(q_send, "c", swap)
+    hidden = lax.ppermute(hidden, ("h", "y"), back_y)
+    q_parts = q_all[:, : 2 * rows].reshape(nh, 2, 2, rows, units)
+
+    def chosen(which):
+        part = lax.dynamic_index_in_dim(q_parts, which, 1, keepdims=False)
+        return part.transpose(1, 0, 2, 3).reshape(2, nh * rows, units)
+
+    q_other = lax.ppermute(chosen(1 - core), "c", swap)
+    q_mine = chosen(core)
     divisor = scal[0, 0] * scal[1, 0] * (2 * nh * rows)
     contract = (((0,), (0,)), ((), ()))
     grads = []
@@ -189,7 +210,13 @@
             x_other, q_other[i], contract, preferred_element_type=F32
         )
         grads.append((total / divisor).astype(BF16))
-    input_grad, peaks = call(last_body, [((rows, width), BF16), ((8, 128), F32)], (back_all, scal), moved=2**21)
+    back_all, grads, hidden = lax.optimization_barrier((back_all, grads, hidden))
+    input_grad, peaks, hidden = call(
+        last_body,
+        [((rows, width), BF16), ((8, 128), F32), ((rows, units), BF16)],
+        (back_all, scal, hidden),
+        moved=2**21,
+    )
     peaks_other = lax.ppermute(peaks, "c", swap)
     (new_history,) = call(history_body, [(history.shape, F32)], (history, peaks, peaks_other))
     return (hidden, input_grad, grads[0], grads[1], new_history)

time: 167 us -> 166 us (level)
  waiting for transfers between devices: 63.2 us -> 92.9 us
  blocking collectives: 29.5 us -> 0 us
  starting transfers between devices: 50.4 us -> 45.7 us
  Pallas kernels: 6.98 us -> 9.13 us
    all_to_all x1 -> x0, blocking collectives: 29.5 us -> none  [per_device(): q_all = lax.all_to_all(quants, 'y', 0, 0, tiled=True)]
    all_to_all x0 -> x1, waiting for transfers between devices: none -> 25.1 us  [per_device(): q_all = lax.all_to_all(quants, 'y', 0, 0, tiled=True)]
    all_to_all x1, starting transfers between devices: 11.2 us -> 5.8 us  [per_device(): back_all = lax.all_to_all(back, plane, 0, 0, tiled=True)]
    all_to_all x0 -> x1, starting transfers between devices: none -> 3.56 us  [per_device(): q_all = lax.all_to_all(quants, 'y', 0, 0, tiled=True)]
    dot_general x2, matrix products: 1.93 us -> 5 us  [per_device(): lax.dot_general(x_other, q_other[i], contract, preferred_element_type=F32)]
    ppermute x1, starting transfers between devices: 4.97 us -> 2.4 us  [per_device(): x_other = lax.ppermute(x_mine, 'c', swap)]
    all_to_all x1, waiting for transfers between devices: 14.1 us -> 16.5 us  [per_device(): back_all = lax.all_to_all(back, plane, 0, 0, tiled=True)]
    pallas_call x6, Pallas kernels: 6.98 us -> 9.13 us  [call(): pl.pallas_call(body, out_shape=[jax.ShapeDtypeStruct(s, t) for s, t in ou...]
  transfers between devices with their start and end apart: 10 -> 13, of which waited for: 4 -> 8; matrix products, arithmetic and copies ran while one was open for 3% -> 4% of each run, Pallas kernels for 0% -> 0%
where the time goes in v3:
time: 166 us; the launch traced here: 165 us
  waiting for transfers between devices  92.9 us (56%)
  starting transfers between devices  45.7 us (28%)
  Pallas kernels  9.13 us (6%)
  local copies, waits for them, and re-layouts  8.78 us (5%)
  matrix products  5.94 us (4%)
  between operations  2.16 us (1%)
    all_to_all x1, waiting for transfers between devices, per_device(): sums = lax.all_to_all(parts, 'y', 0, 0, tiled=True)  28.5 us
    all_to_all x1, waiting for transfers between devices, per_device(): q_all = lax.all_to_all(quants, 'y', 0, 0, tiled=True)  25.1 us
    all_to_all x1, waiting for transfers between devices, per_device(): x_all = lax.all_to_all(copies, plane, 0, 0, tiled=True)  19.4 us
    all_to_all x1, waiting for transfers between devices, per_device(): back_all = lax.all_to_all(back, plane, 0, 0, tiled=True)  16.5 us
    all_to_all x1, starting transfers between devices, per_device(): x_all = lax.all_to_all(copies, plane, 0, 0, tiled=True)  13.7 us
    pallas_call x6, Pallas kernels, call(): pl.pallas_call(body, out_shape=[jax.ShapeDtypeStruct(s, t) for s, t in ou...  9.13 us
    unnamed x22, local copies, waits for them, and re-layouts  8.02 us
    all_to_all x1, starting transfers between devices, per_device(): sums = lax.all_to_all(parts, 'y', 0, 0, tiled=True)  6.8 us
  transfers between devices with their start and end apart: 13, of which 8 were waited for; matrix products, arithmetic and copies ran while one was open for 4% of the time, Pallas kernels for 0%

profile of v3, /device:TPU:1, one launch (start us, length us, event | category | flops | bytes accessed | tf_op | source)
XLA Modules:
  0.0 164.7 jit_solution(1029019504044873408)
XLA Ops:
  0.6 0.0 copy-start
  0.6 0.0 copy-start.1
  0.7 0.8 copy.13.hist_ref
  1.5 0.0 copy-start.8
  1.5 0.8 copy-done.8
  2.3 0.0 copy-start.9
  2.3 1.1 shard_map.92
  3.4 13.7 %all-to-all-start = ((bf16[32,128,128]{2,1,0:T(8,128)(2,1)}), bf16[32,128,128]{2,1,0:T(8,128)(2,1)S(1)}, u32[]{:S(2)}, u32[]{:S(2)}) async-start(bf16[32,128,128]{2,1,0:T(8,128)(2,1)} %get-tuple-element.35), calls=%async_computation | async-start | bytes 2097152 | tf_op jit(solution)/shard_map/all_to_all | solution.py:160
  17.1 0.0 copy-done
  17.1 2.9 %collective-permute-start = (bf16[1024,256]{1,0:T(8,128)(2,1)S(1)}, bf16[1024,256]{1,0:T(8,128)(2,1)S(1)}, u32[]{:S(2)}, u32[]{:S(2)}) collective-permute-start(bf16[1024,256]{1,0:T(8,128)(2,1)S(1)} %copy-done), channel_id=1, source_target_pairs={{0,64},{64,0},{1,65},{65,1},{2,66},{66,2},{3,67},{67,3},{4,68},{68... | collective-permute-start | bytes 1572872 | tf_op jit(solution)/shard_map/ppermute | solution.py:161
  20.0 0.0 copy-done.1
  20.0 1.9 %collective-permute-start.1 = (bf16[1024,256]{1,0:T(8,128)(2,1)S(1)}, bf16[1024,256]{1,0:T(8,128)(2,1)S(1)}, u32[]{:S(2)}, u32[]{:S(2)}) collective-permute-start(bf16[1024,256]{1,0:T(8,128)(2,1)S(1)} %copy-done.1), channel_id=1, source_target_pairs={{0,64},{64,0},{1,65},{65,1},{2,66},{66,2},{3,67},{67,3},{4,68},{68... | collective-permute-start | bytes 1572872 | tf_op jit(solution)/shard_map/ppermute | solution.py:162
  21.9 0.0 copy-done.9
  22.0 0.7 collective-permute-start.2
  22.6 0.1 pad_add_fusion.place_ref
  22.7 0.0 collective-permute-done.2
  22.7 0.0 collective-permute-done.g1_ref
  22.7 0.0 copy-start.2
  22.7 0.8 copy-done.2
  23.5 0.3 collective-permute-done.1.u1_ref
  23.8 0.0 copy-start.5
  23.8 0.8 copy-done.5
  24.6 19.4 %all-to-all-done.x_ref = bf16[32,128,128]{2,1,0:T(8,128)(2,1)S(1)} async-done(((bf16[32,128,128]{2,1,0:T(8,128)(2,1)}), bf16[32,128,128]{2,1,0:T(8,128)(2,1)S(1)}, u32[]{:S(2)}, u32[]{:S(2)}) %all-to-all-start) | async-done | bytes 1048608 | tf_op jit(solution)/shard_map/all_to_all | solution.py:160
  44.0 0.0 copy-start.3
  44.0 1.0 copy-done.3
  45.1 0.0 copy-start.6
  45.1 1.0 copy-done.6
  46.1 2.9 %shard_map.93 = (bf16[8,256,256]{2,1,0:T(8,128)(2,1)}, bf16[512,1024]{1,0:T(8,128)(2,1)S(1)}) custom-call(s32[2]{0:T(128)S(1)} %pad_add_fusion.place_ref, bf16[32,128,128]{2,1,0:T(8,128)(2,1)S(1)} %all-to-all-done.x_ref, bf16[1024,256]{1,0:T(8,128)(2,1)S(1)} %copy-done, bf16[1024,256]{1,0:T(8,128)(2,1)S(1)} %copy-done.1, bf16[1024,256]{1,0:T(8,128)(2,1)S(1)} %copy-done.3, ...), custom_call_target="tpu_custom_call" | custom-call | flops 1073741824 | bytes 6291456 | tf_op jit(solution)/shard_map/pallas_call | solution.py:20
  49.0 6.8 %all-to-all-start.1 = ((bf16[8,256,256]{2,1,0:T(8,128)(2,1)}), bf16[8,256,256]{2,1,0:T(8,128)(2,1)S(1)}, u32[]{:S(2)}, u32[]{:S(2)}) async-start(bf16[8,256,256]{2,1,0:T(8,128)(2,1)} %get-tuple-element.42), calls=%async_computation.1 | async-start | bytes 2097152 | tf_op jit(solution)/shard_map/all_to_all | solution.py:175
  55.8 0.7 collective-permute-start.3
  56.5 0.0 collective-permute-done.3.up_ref
  56.5 28.5 %all-to-all-done.1.in_ref = bf16[8,256,256]{2,1,0:T(8,128)(2,1)S(1)} async-done(((bf16[8,256,256]{2,1,0:T(8,128)(2,1)}), bf16[8,256,256]{2,1,0:T(8,128)(2,1)S(1)}, u32[]{:S(2)}, u32[]{:S(2)}) %all-to-all-start.1) | async-done | bytes 1048608 | tf_op jit(solution)/shard_map/all_to_all | solution.py:175
  85.0 1.4 shard_map.94
  86.4 3.6 %all-to-all-start.2 = ((bf16[8,264,256]{2,1,0:T(8,128)(2,1)}), bf16[8,264,256]{2,1,0:T(8,128)(2,1)S(1)}, u32[]{:S(2)}, u32[]{:S(2)}) async-start(bf16[8,264,256]{2,1,0:T(8,128)(2,1)} %get-tuple-element.49), calls=%async_computation.2 | async-start | bytes 2162688 | tf_op jit(solution)/shard_map/all_to_all | solution.py:182
  89.9 2.4 %collective-permute-start.5 = (bf16[512,1024]{1,0:T(8,128)(2,1)S(1)}, bf16[512,1024]{1,0:T(8,128)(2,1)}, u32[]{:S(2)}, u32[]{:S(2)}) collective-permute-start(bf16[512,1024]{1,0:T(8,128)(2,1)S(1)} %get-tuple-element.51), channel_id=1, source_target_pairs={{0,64},{64,0},{1,65},{65,1},{2,66},{66,2},{3,67},{67,3},{4,68},{68... | collective-permute-start | bytes 3145736 | tf_op jit(solution)/shard_map/ppermute | solution.py:184
  92.3 0.7 collective-permute-start.4
  93.0 0.0 collective-permute-done.4
  93.0 1.7 %collective-permute-done.5 = bf16[512,1024]{1,0:T(8,128)(2,1)} collective-permute-done((bf16[512,1024]{1,0:T(8,128)(2,1)S(1)}, bf16[512,1024]{1,0:T(8,128)(2,1)}, u32[]{:S(2)}, u32[]{:S(2)}) %collective-permute-start.5) | collective-permute-done | bytes 1048608 | tf_op jit(solution)/shard_map/ppermute | solution.py:184
  94.7 25.1 %all-to-all-done.2.q_ref = bf16[8,264,256]{2,1,0:T(8,128)(2,1)S(1)} async-done(((bf16[8,264,256]{2,1,0:T(8,128)(2,1)}), bf16[8,264,256]{2,1,0:T(8,128)(2,1)S(1)}, u32[]{:S(2)}, u32[]{:S(2)}) %all-to-all-start.2) | async-done | bytes 1081376 | tf_op jit(solution)/shard_map/all_to_all | solution.py:182
  119.8 0.0 copy-start.4
  119.8 1.0 copy-done.4
  120.9 0.0 copy-start.7
  120.9 1.0 copy-done.7
  121.9 2.8 %shard_map.95 = bf16[32,136,128]{2,1,0:T(8,128)(2,1)} custom-call(s32[2]{0:T(128)S(1)} %pad_add_fusion.place_ref, bf16[8,264,256]{2,1,0:T(8,128)(2,1)S(1)} %all-to-all-done.2.q_ref, bf16[1024,256]{1,0:T(8,128)(2,1)S(1)} %copy-done, bf16[1024,256]{1,0:T(8,128)(2,1)S(1)} %copy-done.1, bf16[1024,256]{1,0:T(8,128)(2,1)S(1)} %copy-done.4, ...), custom_call_target="tpu_custom_call" | custom-call | flops 1073741824 | bytes 6291456 | tf_op jit(solution)/shard_map/pallas_call | solution.py:20
  124.7 5.8 %all-to-all-start.3 = ((bf16[32,136,128]{2,1,0:T(8,128)(2,1)}), bf16[32,136,128]{2,1,0:T(8,128)(2,1)S(1)}, u32[]{:S(2)}, u32[]{:S(2)}) async-start(bf16[32,136,128]{2,1,0:T(8,128)(2,1)} %shard_map.95), calls=%async_computation.3 | async-start | bytes 2228224 | tf_op jit(solution)/shard_map/all_to_all | solution.py:195
  130.5 0.5 fusion.5
  132.4 0.7 collective-permute-start.7
  133.0 0.1 slice.23
  133.1 0.1 constant_dynamic-slice_fusion
  133.3 2.7 %collective-permute-start.6 = (bf16[2,512,256]{2,1,0:T(8,128)(2,1)S(1)}, bf16[2,512,256]{2,1,0:T(8,128)(2,1)S(1)}, u32[]{:S(2)}, u32[]{:S(2)}) collective-permute-start(bf16[2,512,256]{2,1,0:T(8,128)(2,1)S(1)} %bitcast.30), channel_id=1, source_target_pairs={{0,64},{64,0},{1,65},{65,1},{2,66},{66,2},{3,67},{67,3},{4,68},{68... | collective-permute-start | bytes 1572872 | tf_op jit(solution)/shard_map/ppermute | solution.py:203
  136.0 0.5 fusion.6
  136.5 0.5 fusion.7
  136.9 0.5 collective-permute-done.6
  137.5 2.5 %fusion.2 = bf16[1024,256]{1,0:T(8,128)(2,1)} fusion(f32[1024,256]{1,0:T(8,128)S(1)} %fusion.6, bf16[512,1024]{1,0:T(8,128)(2,1)} %collective-permute-done.5, f32[]{:T(128)} %bitcast.10, bf16[2,512,256]{2,1,0:T(8,128)(2,1)S(1)} %collective-permute-done.6), kind=kOutput, calls=%fused_computation.4 | convolution fusion | flops 269221888 | bytes 2883588 | tf_op jit(solution)/shard_map/dot_general | solution.py:209
  140.0 2.5 %fusion.3 = bf16[1024,256]{1,0:T(8,128)(2,1)} fusion(f32[1024,256]{1,0:T(8,128)S(1)} %fusion.7, bf16[512,1024]{1,0:T(8,128)(2,1)} %collective-permute-done.5, f32[]{:T(128)} %bitcast.10, bf16[2,512,256]{2,1,0:T(8,128)(2,1)S(1)} %collective-permute-done.6), kind=kOutput, calls=%fused_computation.5 | convolution fusion | flops 269221888 | bytes 2883588 | tf_op jit(solution)/shard_map/dot_general | solution.py:209
  142.5 0.0 collective-permute-done.7.hidden_ref
  142.5 16.5 %all-to-all-done.3.in_ref = bf16[32,136,128]{2,1,0:T(8,128)(2,1)S(1)} async-done(((bf16[32,136,128]{2,1,0:T(8,128)(2,1)}), bf16[32,136,128]{2,1,0:T(8,128)(2,1)S(1)}, u32[]{:S(2)}, u32[]{:S(2)}) %all-to-all-start.3) | async-done | bytes 1114144 | tf_op jit(solution)/shard_map/all_to_all | solution.py:195
  158.9 0.9 shard_map.96
  159.8 3.3 %collective-permute-start.8 = (f32[8,128]{1,0:T(8,128)S(1)}, f32[8,128]{1,0:T(8,128)S(1)}, u32[]{:S(2)}, u32[]{:S(2)}) collective-permute-start(f32[8,128]{1,0:T(8,128)S(1)} %get-tuple-element.64.mine_ref), channel_id=1, source_target_pairs={{0,64},{64,0},{1,65},{65,1},{2,66},{66,2},{3,67},{67,3},{4,68},{68... | collective-permute-start | bytes 12296 | tf_op jit(solution)/shard_map/ppermute | solution.py:220
  163.1 0.8 collective-permute-done.8.other_ref
  163.9 0.1 shard_map.97
  164.0 0.7 copy.16
  (2 shorter events, 0.1 us)
Async XLA Ops:
  0.6 16.5 %copy-start = (bf16[1024,256]{1,0:T(8,128)(2,1)S(1)}, bf16[1024,256]{1,0:T(8,128)(2,1)}, u32[]{:S(2)}) copy-start(bf16[1024,256]{1,0:T(8,128)(2,1)} %g0_ref.3) | copy-start | bytes 1572868
  0.6 19.4 %copy-start.1 = (bf16[1024,256]{1,0:T(8,128)(2,1)S(1)}, bf16[1024,256]{1,0:T(8,128)(2,1)}, u32[]{:S(2)}) copy-start(bf16[1024,256]{1,0:T(8,128)(2,1)} %u0_ref.3) | copy-start | bytes 1572868
  1.5 0.8 copy-start.8
  2.3 19.7 %copy-start.9 = (bf16[128,256]{1,0:T(8,128)(2,1)S(1)}, bf16[128,256]{1,0:T(8,128)(2,1)}, u32[]{:S(2)}) copy-start(bf16[128,256]{1,0:T(8,128)(2,1)} %param.8) | copy-start | bytes 196612
  3.4 40.6 %all-to-all-start = ((bf16[32,128,128]{2,1,0:T(8,128)(2,1)}), bf16[32,128,128]{2,1,0:T(8,128)(2,1)S(1)}, u32[]{:S(2)}, u32[]{:S(2)}) async-start(bf16[32,128,128]{2,1,0:T(8,128)(2,1)} %get-tuple-element.35), calls=%async_computation | async-start | bytes 2097152 | tf_op jit(solution)/shard_map/all_to_all | solution.py:160
  17.1 5.6 %collective-permute-start = (bf16[1024,256]{1,0:T(8,128)(2,1)S(1)}, bf16[1024,256]{1,0:T(8,128)(2,1)S(1)}, u32[]{:S(2)}, u32[]{:S(2)}) collective-permute-start(bf16[1024,256]{1,0:T(8,128)(2,1)S(1)} %copy-done), channel_id=1, source_target_pairs={{0,64},{64,0},{1,65},{65,1},{2,66},{66,2},{3,67},{67,3},{4,68},{68... | collective-permute-start | bytes 1572872 | tf_op jit(solution)/shard_map/ppermute | solution.py:161
  20.0 3.8 %collective-permute-start.1 = (bf16[1024,256]{1,0:T(8,128)(2,1)S(1)}, bf16[1024,256]{1,0:T(8,128)(2,1)S(1)}, u32[]{:S(2)}, u32[]{:S(2)}) collective-permute-start(bf16[1024,256]{1,0:T(8,128)(2,1)S(1)} %copy-done.1), channel_id=1, source_target_pairs={{0,64},{64,0},{1,65},{65,1},{2,66},{66,2},{3,67},{67,3},{4,68},{68... | collective-permute-start | bytes 1572872 | tf_op jit(solution)/shard_map/ppermute | solution.py:162
  22.0 0.8 collective-permute-start.2
  22.7 0.8 copy-start.2
  23.8 0.8 copy-start.5
  44.0 1.0 copy-start.3
  45.1 1.0 copy-start.6
  49.0 36.0 %all-to-all-start.1 = ((bf16[8,256,256]{2,1,0:T(8,128)(2,1)}), bf16[8,256,256]{2,1,0:T(8,128)(2,1)S(1)}, u32[]{:S(2)}, u32[]{:S(2)}) async-start(bf16[8,256,256]{2,1,0:T(8,128)(2,1)} %get-tuple-element.42), calls=%async_computation.1 | async-start | bytes 2097152 | tf_op jit(solution)/shard_map/all_to_all | solution.py:175
  55.8 0.7 collective-permute-start.3
  86.4 33.5 %all-to-all-start.2 = ((bf16[8,264,256]{2,1,0:T(8,128)(2,1)}), bf16[8,264,256]{2,1,0:T(8,128)(2,1)S(1)}, u32[]{:S(2)}, u32[]{:S(2)}) async-start(bf16[8,264,256]{2,1,0:T(8,128)(2,1)} %get-tuple-element.49), calls=%async_computation.2 | async-start | bytes 2162688 | tf_op jit(solution)/shard_map/all_to_all | solution.py:182
  89.9 4.8 %collective-permute-start.5 = (bf16[512,1024]{1,0:T(8,128)(2,1)S(1)}, bf16[512,1024]{1,0:T(8,128)(2,1)}, u32[]{:S(2)}, u32[]{:S(2)}) collective-permute-start(bf16[512,1024]{1,0:T(8,128)(2,1)S(1)} %get-tuple-element.51), channel_id=1, source_target_pairs={{0,64},{64,0},{1,65},{65,1},{2,66},{66,2},{3,67},{67,3},{4,68},{68... | collective-permute-start | bytes 3145736 | tf_op jit(solution)/shard_map/ppermute | solution.py:184
  92.3 0.7 collective-permute-start.4
  119.8 1.0 copy-start.4
  120.9 1.0 copy-start.7
  124.7 34.2 %all-to-all-start.3 = ((bf16[32,136,128]{2,1,0:T(8,128)(2,1)}), bf16[32,136,128]{2,1,0:T(8,128)(2,1)S(1)}, u32[]{:S(2)}, u32[]{:S(2)}) async-start(bf16[32,136,128]{2,1,0:T(8,128)(2,1)} %shard_map.95), calls=%async_computation.3 | async-start | bytes 2228224 | tf_op jit(solution)/shard_map/all_to_all | solution.py:195
  132.4 10.1 %collective-permute-start.7 = (bf16[128,256]{1,0:T(8,128)(2,1)S(1)}, bf16[128,256]{1,0:T(8,128)(2,1)S(1)}, u32[]{:S(2)}, u32[]{:S(2)}) collective-permute-start(bf16[128,256]{1,0:T(8,128)(2,1)S(1)} %collective-permute-done.4), channel_id=1, source_target_pairs={{0,0},{1,1},{2,2},{3,3},{4,4},{5,5},{6,6},{7,7},{130,128},{131,129... | collective-permute-start | bytes 196616 | tf_op jit(solution)/shard_map/ppermute | solution.py:196
  133.3 4.2 %collective-permute-start.6 = (bf16[2,512,256]{2,1,0:T(8,128)(2,1)S(1)}, bf16[2,512,256]{2,1,0:T(8,128)(2,1)S(1)}, u32[]{:S(2)}, u32[]{:S(2)}) collective-permute-start(bf16[2,512,256]{2,1,0:T(8,128)(2,1)S(1)} %bitcast.30), channel_id=1, source_target_pairs={{0,64},{64,0},{1,65},{65,1},{2,66},{66,2},{3,67},{67,3},{4,68},{68... | collective-permute-start | bytes 1572872 | tf_op jit(solution)/shard_map/ppermute | solution.py:203
  159.8 4.2 %collective-permute-start.8 = (f32[8,128]{1,0:T(8,128)S(1)}, f32[8,128]{1,0:T(8,128)S(1)}, u32[]{:S(2)}, u32[]{:S(2)}) collective-permute-start(f32[8,128]{1,0:T(8,128)S(1)} %get-tuple-element.64.mine_ref), channel_id=1, source_target_pairs={{0,64},{64,0},{1,65},{65,1},{2,66},{66,2},{3,67},{67,3},{4,68},{68... | collective-permute-start | bytes 12296 | tf_op jit(solution)/shard_map/ppermute | solution.py:220

commit v4 on v3

--- a/solution.py
+++ b/solution.py
@@ -97,32 +97,65 @@
     peak_grad = jnp.maximum(top(jnp.abs(grad_gate)), top(jnp.abs(grad_lift)))
     peaks = pack_peaks(scal_ref[2:3, 0:1], top(jnp.abs(hidden.astype(F32))), peak_grad)
     wide = jnp.concatenate([peaks, peaks], axis=1)
-    for i in range(q_ref.shape[0]):
-        q_ref[i, :rows, :] = quant_gate
-        q_ref[i, rows : 2 * rows, :] = quant_lift
-        q_ref[i, 2 * rows :, :] = wide
-
-
-def backward_body(place_ref, q_ref, g0_ref, u0_ref, g1_ref, u1_ref, out_ref, kept_ref):
-    groups = q_ref.shape[0] // 2
-    rows = (q_ref.shape[1] - 8) // 2
-    cols = out_ref.shape[0] // groups
-    core, turned = place_ref[0], place_ref[1]
+    q_ref[:rows, :] = quant_gate
+    q_ref[rows : 2 * rows, :] = quant_lift
+    q_ref[2 * rows :, :] = wide
+
+
+def gather(place_ref, piece_refs, kept_ref):
+    count = len(piece_refs)
+    rows = (piece_refs[0].shape[0] - 8) // 2
+    for offset, ref in zip(ring_offsets(count), piece_refs):
+        piece = lax.rem(place_ref[2] + (count + offset), count)
+        which = lax.rem(piece + place_ref[0], 2)
+        spot = pl.ds(pl.multiple_of(lax.div(piece, 2) * rows, rows), rows)
+        for half in range(2):
+            kept_ref[which, half, spot, :] = ref[half * rows : (half + 1) * rows, :]
+
+
+def backward_body(place_ref, *refs):
+    g0_ref, u0_ref, g1_ref, u1_ref, out_ref, kept_ref = refs[-6:]
+    pieces = refs[:-6]
+    rows = (pieces[0].shape[0] - 8) // 2
+    groups = len(pieces) // 2
+    cols = out_ref.shape[0]
+    turned = place_ref[1]
+    fine = (out_ref.shape[1] - 8) // (groups * rows)
     contract = (((1,), (1,)), ((), ()))
+    gather(place_ref, pieces, kept_ref)
     total = None
-    for which, pair in enumerate(((g0_ref, u0_ref), (g1_ref, u1_ref))):
-        place = core if which == 0 else 1 - core
-        for half, w_ref in enumerate(pair):
-            for g in range(groups):
-                kept_ref[g * rows : (g + 1) * rows, :] = q_ref[2 * g + place, half * rows : (half + 1) * rows, :]
-            part = lax.dot_general(kept_ref[...], w_ref[...], contract, preferred_element_type=F32)
-            total = part if total is None else total + part
-    packed = pack_peaks(*unpack_peaks(q_ref[:, 2 * rows :, 0:128].astype(F32)))
-    for g in range(groups):
-        first = lax.rem(groups + g - turned, groups) * cols
-        for k in range(cols):
-            out_ref[first + k, :rows, :] = total[g * rows : (g + 1) * rows, k * 128 : (k + 1) * 128].astype(BF16)
-            out_ref[first + k, rows:, :] = packed
+    for i, w_ref in enumerate((g0_ref, u0_ref, g1_ref, u1_ref)):
+        part = lax.dot_general(kept_ref[i // 2, i % 2], w_ref[...], contract, preferred_element_type=F32)
+        total = part if total is None else total + part
+    found = [unpack_peaks(ref[2 * rows :, 0:128].astype(F32)[None]) for ref in pieces]
+    peaks = found[0]
+    for other in found[1:]:
+        peaks = [jnp.maximum(a, b) for a, b in zip(peaks, other)]
+    packed = pack_peaks(*peaks)
+    for k in range(cols):
+        for g in range(groups):
+            first = lax.rem(groups + g - turned, groups) * (fine * rows)
+            for j in range(fine):
+                lane = (k * fine + j) * 128
+                spot = pl.ds(pl.multiple_of(first + j * rows, rows), rows)
+                out_ref[k, spot, :] = total[g * rows : (g + 1) * rows, lane : lane + 128].astype(BF16)
+        out_ref[k, groups * fine * rows :, :] = packed
+
+
+def pick_body(place_ref, *refs):
+    mine_ref, send_ref, kept_ref = refs[-3:]
+    gather(place_ref, refs[:-3], kept_ref)
+    mine_ref[...] = kept_ref[0]
+    send_ref[...] = kept_ref[1]
+
+
+def column_body(in_ref, out_ref):
+    blocks, rows = out_ref.shape[0], out_ref.shape[1] - 8
+    packed = pack_peaks(*unpack_peaks(in_ref[:, blocks * rows :, :].astype(F32)))
+    for i in range(blocks):
+        part = jnp.sum(in_ref[:, i * rows : (i + 1) * rows, :].astype(F32), axis=0)
+        out_ref[i, :rows, :] = part.astype(BF16)
+        out_ref[i, rows:, :] = packed
 
 
 def last_body(in_ref, scal_ref, hidden_ref, out_ref, peaks_ref, hidden_out_ref):
@@ -139,6 +172,24 @@
     past = hist_ref.shape[0] - 1
     out_ref[0:past, :] = hist_ref[1:, :]
     out_ref[past:, :] = row
+
+
+def ring_offsets(n):
+    offsets = [0]
+    for step in range(1, n // 2):
+        offsets += [step, -step]
+    return offsets + [n // 2]
+
+
+def ring(piece, axis, n):
+    ahead = [(i, (i - 1) % n) for i in range(n)]
+    behind = [(i, (i + 1) % n) for i in range(n)]
+    pieces, above, below = [piece], piece, piece
+    for step in range(1, n // 2):
+        above = lax.ppermute(above, axis, ahead)
+        below = lax.ppermute(below, axis, behind)
+        pieces += [above, below]
+    return pieces + [lax.ppermute(above, axis, ahead)]
 
 
 def per_device(sizes, tokens, w_gate, w_up, upstream, history):
@@ -154,7 +205,7 @@
     along_z = [(at(h, a, b), at((a - h) % nh, a, b)) for h, a, b in spots]
     back_y = [(j, i) for i, j in along_y]
     core = lax.axis_index("c")
-    place = jnp.stack([core, lax.axis_index("h")])
+    place = jnp.stack([core, lax.axis_index("h"), lax.axis_index("y")])
 
     copies, scal = call(scale_body, [((count, rows, width), BF16), ((8, 128), F32)], (history, tokens))
     x_all = lax.all_to_all(copies, plane, 0, 0, tiled=True)
@@ -174,34 +225,33 @@
     parts, x_mine, up = lax.optimization_barrier((parts, x_mine, up))
     sums = lax.all_to_all(parts, "y", 0, 0, tiled=True)
     up = lax.ppermute(up, ("h", "y"), along_z)
-    sums, up = lax.optimization_barrier((sums, up))
+    x_other = lax.ppermute(x_mine, "c", swap)
+    sums, up, x_other = lax.optimization_barrier((sums, up, x_other))
     hidden, quants = call(
-        middle_body, [((rows, units), BF16), ((ny, 2 * rows + 8, units), BF16)], (sums, up, scal), moved=2**21
-    )
-    quants, x_mine = lax.optimization_barrier((quants, x_mine))
-    q_all = lax.all_to_all(quants, "y", 0, 0, tiled=True)
+        middle_body, [((rows, units), BF16), ((2 * rows + 8, units), BF16)], (sums, up, scal), moved=2**21
+    )
+    pieces = ring(quants, "y", ny)
     hidden = lax.ppermute(hidden, ("h", "y"), along_z)
-    x_other = lax.ppermute(x_mine, "c", swap)
-    q_all, hidden, x_other = lax.optimization_barrier((q_all, hidden, x_other))
+    *pieces, hidden = lax.optimization_barrier((*pieces, hidden))
     (back,) = call(
         backward_body,
-        [((count, rows + 8, width), BF16)],
-        (place, q_all, w_gate, w_up, gate_other, lift_other),
+        [((nx, nh * nw * rows + 8, width), BF16)],
+        (place, *pieces, w_gate, w_up, gate_other, lift_other),
         flops=work,
         moved=6 * 2**20,
-        scratch=[pltpu.VMEM((nh * rows, units), BF16)],
-    )
-    back, q_all, hidden = lax.optimization_barrier((back, q_all, hidden))
-    back_all = lax.all_to_all(back, plane, 0, 0, tiled=True)
+        scratch=[pltpu.VMEM((2, 2, nh * rows, units), BF16)],
+    )
+    *pieces, back, hidden = lax.optimization_barrier((*pieces, back, hidden))
+    back_cols = lax.all_to_all(back, "x", 0, 0, tiled=True)
     hidden = lax.ppermute(hidden, ("h", "y"), back_y)
-    q_parts = q_all[:, : 2 * rows].reshape(nh, 2, 2, rows, units)
-
-    def chosen(which):
-        part = lax.dynamic_index_in_dim(q_parts, which, 1, keepdims=False)
-        return part.transpose(1, 0, 2, 3).reshape(2, nh * rows, units)
-
-    q_other = lax.ppermute(chosen(1 - core), "c", swap)
-    q_mine = chosen(core)
+    q_mine, q_send = call(
+        pick_body,
+        [((2, nh * rows, units), BF16)] * 2,
+        (place, *pieces),
+        moved=2**22,
+        scratch=[pltpu.VMEM((2, 2, nh * rows, units), BF16)],
+    )
+    q_other = lax.ppermute(q_send, "c", swap)
     divisor = scal[0, 0] * scal[1, 0] * (2 * nh * rows)
     contract = (((0,), (0,)), ((), ()))
     grads = []
@@ -210,7 +260,9 @@
             x_other, q_other[i], contract, preferred_element_type=F32
         )
         grads.append((total / divisor).astype(BF16))
-    back_all, grads, hidden = lax.optimization_barrier((back_all, grads, hidden))
+    (column,) = call(column_body, [((nh * nw, rows + 8, width), BF16)], (back_cols,), moved=2**21)
+    back_all = lax.all_to_all(column, ("h", "w"), 0, 0, tiled=True)
+    back_all, hidden, *grads = lax.optimization_barrier((back_all, hidden, *grads))
     input_grad, peaks, hidden = call(
         last_body,
         [((rows, width), BF16), ((8, 128), F32), ((rows, units), BF16)],

time: 166 us -> 170 us (1.024)
  starting transfers between devices: 45.7 us -> 83.1 us
  waiting for transfers between devices: 92.9 us -> 55.8 us
  local copies, waits for them, and re-layouts: 8.78 us -> 10.5 us
    all_to_all x2, waiting for transfers between devices: 41.6 us -> 7.59 us  [the longest x1 7.59 us: per_device(): back_all = lax.all_to_all(column, ('h', 'w'), 0, 0, tiled=True)]
    ppermute x1 -> x8, starting transfers between devices: 2.67 us -> 28.3 us  [the longest x3 10 us: ring(): above = lax.ppermute(above, axis, ahead)]
    all_to_all x2, starting transfers between devices: 9.36 us -> 20.6 us  [the longest x1 17.1 us: per_device(): back_all = lax.all_to_all(column, ('h', 'w'), 0, 0, tiled=True)]
    all_to_all x1, waiting for transfers between devices: 28.5 us -> 23 us  [per_device(): sums = lax.all_to_all(parts, 'y', 0, 0, tiled=True)]
    ppermute x1 -> x8, waiting for transfers between devices: 0.52 us -> 2.94 us  [the longest x3 1.64 us: ring(): above = lax.ppermute(above, axis, ahead)]
    unnamed x22 -> x28, local copies, waits for them, and re-layouts: 8.02 us -> 10 us
    pallas_call x6 -> x8, Pallas kernels: 9.13 us -> 10.4 us  [call(): pl.pallas_call(body, out_shape=[jax.ShapeDtypeStruct(s, t) for s, t in ou...]
  transfers between devices with their start and end apart: 13 -> 20, of which waited for: 8 -> 9; matrix products, arithmetic and copies ran while one was open for 4% -> 5% of each run, Pallas kernels for 0% -> 1%
where the time goes in v4:
time: 170 us; the launch traced here: 169 us
  starting transfers between devices  83.1 us (49%)
  waiting for transfers between devices  55.8 us (33%)
  local copies, waits for them, and re-layouts  10.5 us (6%)
  Pallas kernels  10.4 us (6%)
  matrix products  7.05 us (4%)
  between operations  2.2 us (1%)
    all_to_all x1, waiting for transfers between devices, per_device(): sums = lax.all_to_all(parts, 'y', 0, 0, tiled=True)  23 us
    all_to_all x1, waiting for transfers between devices, per_device(): x_all = lax.all_to_all(copies, plane, 0, 0, tiled=True)  19.4 us
    all_to_all x1, starting transfers between devices, per_device(): back_all = lax.all_to_all(column, ('h', 'w'), 0, 0, tiled=True)  17.1 us
    all_to_all x1, starting transfers between devices, per_device(): x_all = lax.all_to_all(copies, plane, 0, 0, tiled=True)  13.8 us
    pallas_call x8, Pallas kernels, call(): pl.pallas_call(body, out_shape=[jax.ShapeDtypeStruct(s, t) for s, t in ou...  10.4 us
    unnamed x28, local copies, waits for them, and re-layouts  10 us
    ppermute x3, starting transfers between devices, ring(): above = lax.ppermute(above, axis, ahead)  10 us
    all_to_all x1, waiting for transfers between devices, per_device(): back_all = lax.all_to_all(column, ('h', 'w'), 0, 0, tiled=True)  7.59 us
  transfers between devices with their start and end apart: 20, of which 9 were waited for; matrix products, arithmetic and copies ran while one was open for 5% of the time, Pallas kernels for 1%

profile of v4, /device:TPU:1, one launch (start us, length us, event | category | flops | bytes accessed | tf_op | source)
XLA Modules:
  0.0 169.2 jit_solution(6072839361827680476)
XLA Ops:
  0.6 0.8 copy.10.hist_ref
  1.4 0.8 copy-done.10
  2.1 1.2 shard_map.92
  3.3 13.8 %all-to-all-start = ((bf16[32,128,128]{2,1,0:T(8,128)(2,1)}), bf16[32,128,128]{2,1,0:T(8,128)(2,1)S(1)}, u32[]{:S(2)}, u32[]{:S(2)}) async-start(bf16[32,128,128]{2,1,0:T(8,128)(2,1)} %get-tuple-element.49), calls=%async_computation | async-start | bytes 2097152 | tf_op jit(solution)/shard_map/all_to_all | solution.py:211
  17.2 2.9 %collective-permute-start = (bf16[1024,256]{1,0:T(8,128)(2,1)S(1)}, bf16[1024,256]{1,0:T(8,128)(2,1)S(1)}, u32[]{:S(2)}, u32[]{:S(2)}) collective-permute-start(bf16[1024,256]{1,0:T(8,128)(2,1)S(1)} %copy-done), channel_id=1, source_target_pairs={{0,64},{64,0},{1,65},{65,1},{2,66},{66,2},{3,67},{67,3},{4,68},{68... | collective-permute-start | bytes 1572872 | tf_op jit(solution)/shard_map/ppermute | solution.py:212
  20.1 1.9 %collective-permute-start.1 = (bf16[1024,256]{1,0:T(8,128)(2,1)S(1)}, bf16[1024,256]{1,0:T(8,128)(2,1)S(1)}, u32[]{:S(2)}, u32[]{:S(2)}) collective-permute-start(bf16[1024,256]{1,0:T(8,128)(2,1)S(1)} %copy-done.2), channel_id=1, source_target_pairs={{0,64},{64,0},{1,65},{65,1},{2,66},{66,2},{3,67},{67,3},{4,68},{68... | collective-permute-start | bytes 1572872 | tf_op jit(solution)/shard_map/ppermute | solution.py:213
  22.0 0.7 collective-permute-start.2
  22.7 0.1 pad_add_fusion.place_ref
  22.8 0.0 collective-permute-done.2
  22.8 0.0 collective-permute-done.g1_ref.refs_10_
  22.8 0.8 copy-done.4
  23.6 0.3 collective-permute-done.1.u1_ref.refs_11_
  23.9 0.8 copy-done.7
  24.7 19.4 %all-to-all-done.x_ref = bf16[32,128,128]{2,1,0:T(8,128)(2,1)S(1)} async-done(((bf16[32,128,128]{2,1,0:T(8,128)(2,1)}), bf16[32,128,128]{2,1,0:T(8,128)(2,1)S(1)}, u32[]{:S(2)}, u32[]{:S(2)}) %all-to-all-start) | async-done | bytes 1048608 | tf_op jit(solution)/shard_map/all_to_all | solution.py:211
  44.1 1.0 copy-done.5
  45.1 1.0 copy-done.8
  46.2 2.9 %shard_map.93 = (bf16[8,256,256]{2,1,0:T(8,128)(2,1)}, bf16[512,1024]{1,0:T(8,128)(2,1)S(1)}) custom-call(s32[3]{0:T(128)S(1)} %pad_add_fusion.place_ref, bf16[32,128,128]{2,1,0:T(8,128)(2,1)S(1)} %all-to-all-done.x_ref, bf16[1024,256]{1,0:T(8,128)(2,1)S(1)} %copy-done, bf16[1024,256]{1,0:T(8,128)(2,1)S(1)} %copy-done.2, bf16[1024,256]{1,0:T(8,128)(2,1)S(1)} %copy-done.5, ...), custom_call_target="tpu_custom_call" | custom-call | flops 1073741824 | bytes 6291456 | tf_op jit(solution)/shard_map/pallas_call | solution.py:20
  49.1 6.8 %all-to-all-start.1 = ((bf16[8,256,256]{2,1,0:T(8,128)(2,1)}), bf16[8,256,256]{2,1,0:T(8,128)(2,1)S(1)}, u32[]{:S(2)}, u32[]{:S(2)}) async-start(bf16[8,256,256]{2,1,0:T(8,128)(2,1)} %get-tuple-element.56), calls=%async_computation.1 | async-start | bytes 2097152 | tf_op jit(solution)/shard_map/all_to_all | solution.py:226
  55.9 3.7 %collective-permute-start.4 = (bf16[512,1024]{1,0:T(8,128)(2,1)S(1)}, bf16[512,1024]{1,0:T(8,128)(2,1)}, u32[]{:S(2)}, u32[]{:S(2)}) collective-permute-start(bf16[512,1024]{1,0:T(8,128)(2,1)S(1)} %get-tuple-element.58), channel_id=1, source_target_pairs={{0,64},{64,0},{1,65},{65,1},{2,66},{66,2},{3,67},{67,3},{4,68},{68... | collective-permute-start | bytes 3145736 | tf_op jit(solution)/shard_map/ppermute | solution.py:228
  59.6 0.7 collective-permute-start.3
  60.3 0.0 collective-permute-done.3.up_ref
  60.3 1.7 %collective-permute-done.4 = bf16[512,1024]{1,0:T(8,128)(2,1)} collective-permute-done((bf16[512,1024]{1,0:T(8,128)(2,1)S(1)}, bf16[512,1024]{1,0:T(8,128)(2,1)}, u32[]{:S(2)}, u32[]{:S(2)}) %collective-permute-start.4) | collective-permute-done | bytes 1048608 | tf_op jit(solution)/shard_map/ppermute | solution.py:228
  62.0 23.0 %all-to-all-done.1.in_ref = bf16[8,256,256]{2,1,0:T(8,128)(2,1)S(1)} async-done(((bf16[8,256,256]{2,1,0:T(8,128)(2,1)}), bf16[8,256,256]{2,1,0:T(8,128)(2,1)S(1)}, u32[]{:S(2)}, u32[]{:S(2)}) %all-to-all-start.1) | async-done | bytes 1048608 | tf_op jit(solution)/shard_map/all_to_all | solution.py:226
  85.1 0.3 shard_map.94
  85.4 1.9 %collective-permute-start.5 = (bf16[264,256]{1,0:T(8,128)(2,1)S(1)}, bf16[264,256]{1,0:T(8,128)(2,1)S(1)}, u32[]{:S(2)}, u32[]{:S(2)}) collective-permute-start(bf16[264,256]{1,0:T(8,128)(2,1)S(1)} %get-tuple-element.75.refs_0_), channel_id=1, source_target_pairs={{0,7},{1,0},{2,1},{3,2},{4,3},{5,4},{6,5},{7,6},{8,15},{9,8},{10,9... | collective-permute-start | bytes 405512 | tf_op jit(solution)/shard_map/ppermute | solution.py:189
  87.4 3.4 %collective-permute-start.6 = (bf16[264,256]{1,0:T(8,128)(2,1)S(1)}, bf16[264,256]{1,0:T(8,128)(2,1)S(1)}, u32[]{:S(2)}, u32[]{:S(2)}) collective-permute-start(bf16[264,256]{1,0:T(8,128)(2,1)S(1)} %get-tuple-element.75.refs_0_), channel_id=1, source_target_pairs={{0,1},{1,2},{2,3},{3,4},{4,5},{5,6},{6,7},{7,0},{8,9},{9,10},{10,1... | collective-permute-start | bytes 405512 | tf_op jit(solution)/shard_map/ppermute | solution.py:190
  90.7 1.3 collective-permute-done.5.refs_1_
  92.0 3.4 %collective-permute-start.7 = (bf16[264,256]{1,0:T(8,128)(2,1)S(1)}, bf16[264,256]{1,0:T(8,128)(2,1)S(1)}, u32[]{:S(2)}, u32[]{:S(2)}) collective-permute-start(bf16[264,256]{1,0:T(8,128)(2,1)S(1)} %collective-permute-done.5.refs_1_), channel_id=1, source_target_pairs={{0,7},{1,0},{2,1},{3,2},{4,3},{5,4},{6,5},{7,6},{8,15},{9,8},{10,9... | collective-permute-start | bytes 405512 | tf_op jit(solution)/shard_map/ppermute | solution.py:189
  95.4 0.0 collective-permute-done.6.refs_2_
  95.4 1.9 %collective-permute-start.8 = (bf16[264,256]{1,0:T(8,128)(2,1)S(1)}, bf16[264,256]{1,0:T(8,128)(2,1)S(1)}, u32[]{:S(2)}, u32[]{:S(2)}) collective-permute-start(bf16[264,256]{1,0:T(8,128)(2,1)S(1)} %collective-permute-done.6.refs_2_), channel_id=1, source_target_pairs={{0,1},{1,2},{2,3},{3,4},{4,5},{5,6},{6,7},{7,0},{8,9},{9,10},{10,1... | collective-permute-start | bytes 405512 | tf_op jit(solution)/shard_map/ppermute | solution.py:190
  97.4 0.4 collective-permute-done.7.refs_3_
  97.7 4.6 %collective-permute-start.9 = (bf16[264,256]{1,0:T(8,128)(2,1)S(1)}, bf16[264,256]{1,0:T(8,128)(2,1)S(1)}, u32[]{:S(2)}, u32[]{:S(2)}) collective-permute-start(bf16[264,256]{1,0:T(8,128)(2,1)S(1)} %collective-permute-done.7.refs_3_), channel_id=1, source_target_pairs={{0,7},{1,0},{2,1},{3,2},{4,3},{5,4},{6,5},{7,6},{8,15},{9,8},{10,9... | collective-permute-start | bytes 405512 | tf_op jit(solution)/shard_map/ppermute | solution.py:189
  102.4 0.0 collective-permute-done.8.refs_4_
  102.4 1.9 %collective-permute-start.10 = (bf16[264,256]{1,0:T(8,128)(2,1)S(1)}, bf16[264,256]{1,0:T(8,128)(2,1)S(1)}, u32[]{:S(2)}, u32[]{:S(2)}) collective-permute-start(bf16[264,256]{1,0:T(8,128)(2,1)S(1)} %collective-permute-done.8.refs_4_), channel_id=1, source_target_pairs={{0,1},{1,2},{2,3},{3,4},{4,5},{5,6},{6,7},{7,0},{8,9},{9,10},{10,1... | collective-permute-start | bytes 405512 | tf_op jit(solution)/shard_map/ppermute | solution.py:190
  104.3 0.0 collective-permute-done.9.refs_5_
  104.3 5.0 %collective-permute-start.11 = (bf16[264,256]{1,0:T(8,128)(2,1)S(1)}, bf16[264,256]{1,0:T(8,128)(2,1)S(1)}, u32[]{:S(2)}, u32[]{:S(2)}) collective-permute-start(bf16[264,256]{1,0:T(8,128)(2,1)S(1)} %collective-permute-done.9.refs_5_), channel_id=1, source_target_pairs={{0,7},{1,0},{2,1},{3,2},{4,3},{5,4},{6,5},{7,6},{8,15},{9,8},{10,9... | collective-permute-start | bytes 405512 | tf_op jit(solution)/shard_map/ppermute | solution.py:192
  109.3 0.7 collective-permute-start.12
  110.0 0.0 collective-permute-done.12
  110.0 1.3 collective-permute-done.11.refs_7_
  111.3 1.0 copy-done.1
  112.3 1.0 copy-done.3
  113.4 1.0 copy-done.6
  114.4 1.0 copy-done.9
  115.5 2.9 %shard_map.95 = bf16[4,1032,128]{2,1,0:T(8,128)(2,1)} custom-call(s32[3]{0:T(128)S(1)} %pad_add_fusion.place_ref, bf16[264,256]{1,0:T(8,128)(2,1)S(1)} %get-tuple-element.75.refs_0_, bf16[264,256]{1,0:T(8,128)(2,1)S(1)} %collective-permute-done.5.refs_1_, bf16[264,256]{1,0:T(8,128)(2,1)S(1)} %collective-permute-done.6.refs_2_, ...), custom_call_target="tpu_custom_call" | custom-call | flops 1073741824 | bytes 6291456 | tf_op jit(solution)/shard_map/pallas_call | solution.py:20
  118.3 3.5 %all-to-all-start.2 = ((bf16[4,1032,128]{2,1,0:T(8,128)(2,1)}), bf16[4,1032,128]{2,1,0:T(8,128)(2,1)S(1)}, u32[]{:S(2)}, u32[]{:S(2)}) async-start(bf16[4,1032,128]{2,1,0:T(8,128)(2,1)} %shard_map.95), calls=%async_computation.2 | async-start | bytes 2113536 | tf_op jit(solution)/shard_map/all_to_all | solution.py:245
  121.9 0.5 fusion.10
  123.7 0.7 collective-permute-start.13
  124.3 1.5 shard_map.97
  125.8 6.1 %collective-permute-start.14 = (bf16[2,512,256]{2,1,0:T(8,128)(2,1)}, bf16[2,512,256]{2,1,0:T(8,128)(2,1)}, u32[]{:S(2)}, u32[]{:S(2)}) collective-permute-start(bf16[2,512,256]{2,1,0:T(8,128)(2,1)} %get-tuple-element.85), channel_id=1, source_target_pairs={{0,64},{64,0},{1,65},{65,1},{2,66},{66,2},{3,67},{67,3},{4,68},{68... | collective-permute-start | bytes 1572872 | tf_op jit(solution)/shard_map/ppermute | solution.py:254
  131.9 1.5 fusion.6
  133.4 0.5 fusion.4
  133.9 0.0 all-to-all-done.2.in_ref
  133.9 0.9 shard_map.96
  134.8 17.1 %all-to-all-start.3 = ((bf16[8,136,128]{2,1,0:T(8,128)(2,1)}), bf16[8,136,128]{2,1,0:T(8,128)(2,1)S(1)}, u32[]{:S(2)}, u32[]{:S(2)}) async-start(bf16[8,136,128]{2,1,0:T(8,128)(2,1)} %shard_map.96), calls=%async_computation.3 | async-start | bytes 557056 | tf_op jit(solution)/shard_map/all_to_all | solution.py:264
  151.9 0.0 collective-permute-done.14
  151.9 2.6 %fusion.2 = bf16[1024,256]{1,0:T(8,128)(2,1)} fusion(f32[1024,256]{1,0:T(8,128)S(1)} %copy-done.11, bf16[512,1024]{1,0:T(8,128)(2,1)} %collective-permute-done.4, f32[]{:T(128)} %bitcast.5, bf16[2,512,256]{2,1,0:T(8,128)(2,1)} %collective-permute-done.14), kind=kOutput, calls=%fused_computation.4 | convolution fusion | flops 269221888 | bytes 2884096 | tf_op jit(solution)/shard_map/dot_general | solution.py:259
  154.5 2.6 %fusion.3 = bf16[1024,256]{1,0:T(8,128)(2,1)} fusion(f32[1024,256]{1,0:T(8,128)S(1)} %fusion.4, bf16[512,1024]{1,0:T(8,128)(2,1)} %collective-permute-done.4, f32[]{:T(128)} %bitcast.5, bf16[2,512,256]{2,1,0:T(8,128)(2,1)} %collective-permute-done.14), kind=kOutput, calls=%fused_computation.5 | convolution fusion | flops 269221888 | bytes 2884096 | tf_op jit(solution)/shard_map/dot_general | solution.py:259
  157.0 0.0 collective-permute-done.13.hidden_ref
  157.0 7.6 %all-to-all-done.3.in_ref = bf16[8,136,128]{2,1,0:T(8,128)(2,1)S(1)} async-done(((bf16[8,136,128]{2,1,0:T(8,128)(2,1)}), bf16[8,136,128]{2,1,0:T(8,128)(2,1)S(1)}, u32[]{:S(2)}, u32[]{:S(2)}) %all-to-all-start.3) | async-done | bytes 278560 | tf_op jit(solution)/shard_map/all_to_all | solution.py:264
  164.6 0.7 shard_map.98
  165.3 2.4 %collective-permute-start.15 = (f32[8,128]{1,0:T(8,128)S(1)}, f32[8,128]{1,0:T(8,128)S(1)}, u32[]{:S(2)}, u32[]{:S(2)}) collective-permute-start(f32[8,128]{1,0:T(8,128)S(1)} %get-tuple-element.92.mine_ref), channel_id=1, source_target_pairs={{0,64},{64,0},{1,65},{65,1},{2,66},{66,2},{3,67},{67,3},{4,68},{68... | collective-permute-start | bytes 12296 | tf_op jit(solution)/shard_map/ppermute | solution.py:272
  167.7 0.8 collective-permute-done.15.other_ref
  168.5 0.1 shard_map.99
  168.5 0.7 copy.12
  (18 shorter events, 0.0 us)
Async XLA Ops:
  1.4 0.8 copy-start.10
  3.3 13.9 %copy-start = (bf16[1024,256]{1,0:T(8,128)(2,1)S(1)}, bf16[1024,256]{1,0:T(8,128)(2,1)}, u32[]{:S(2)}) copy-start(bf16[1024,256]{1,0:T(8,128)(2,1)} %refs_8_.1) | copy-start | bytes 1572868
  3.3 16.7 %copy-start.2 = (bf16[1024,256]{1,0:T(8,128)(2,1)S(1)}, bf16[1024,256]{1,0:T(8,128)(2,1)}, u32[]{:S(2)}) copy-start(bf16[1024,256]{1,0:T(8,128)(2,1)} %refs_9_.1) | copy-start | bytes 1572868
  3.3 18.7 %copy-start.12 = (bf16[128,256]{1,0:T(8,128)(2,1)S(1)}, bf16[128,256]{1,0:T(8,128)(2,1)}, u32[]{:S(2)}) copy-start(bf16[128,256]{1,0:T(8,128)(2,1)} %param.8) | copy-start | bytes 196612
  3.3 40.8 %all-to-all-start = ((bf16[32,128,128]{2,1,0:T(8,128)(2,1)}), bf16[32,128,128]{2,1,0:T(8,128)(2,1)S(1)}, u32[]{:S(2)}, u32[]{:S(2)}) async-start(bf16[32,128,128]{2,1,0:T(8,128)(2,1)} %get-tuple-element.49), calls=%async_computation | async-start | bytes 2097152 | tf_op jit(solution)/shard_map/all_to_all | solution.py:211
  17.2 5.6 %collective-permute-start = (bf16[1024,256]{1,0:T(8,128)(2,1)S(1)}, bf16[1024,256]{1,0:T(8,128)(2,1)S(1)}, u32[]{:S(2)}, u32[]{:S(2)}) collective-permute-start(bf16[1024,256]{1,0:T(8,128)(2,1)S(1)} %copy-done), channel_id=1, source_target_pairs={{0,64},{64,0},{1,65},{65,1},{2,66},{66,2},{3,67},{67,3},{4,68},{68... | collective-permute-start | bytes 1572872 | tf_op jit(solution)/shard_map/ppermute | solution.py:212
  20.1 3.8 %collective-permute-start.1 = (bf16[1024,256]{1,0:T(8,128)(2,1)S(1)}, bf16[1024,256]{1,0:T(8,128)(2,1)S(1)}, u32[]{:S(2)}, u32[]{:S(2)}) collective-permute-start(bf16[1024,256]{1,0:T(8,128)(2,1)S(1)} %copy-done.2), channel_id=1, source_target_pairs={{0,64},{64,0},{1,65},{65,1},{2,66},{66,2},{3,67},{67,3},{4,68},{68... | collective-permute-start | bytes 1572872 | tf_op jit(solution)/shard_map/ppermute | solution.py:213
  22.0 0.8 collective-permute-start.2
  22.8 0.8 copy-start.4
  23.9 0.8 copy-start.7
  44.1 1.0 copy-start.5
  45.1 1.0 copy-start.8
  49.1 36.0 %all-to-all-start.1 = ((bf16[8,256,256]{2,1,0:T(8,128)(2,1)}), bf16[8,256,256]{2,1,0:T(8,128)(2,1)S(1)}, u32[]{:S(2)}, u32[]{:S(2)}) async-start(bf16[8,256,256]{2,1,0:T(8,128)(2,1)} %get-tuple-element.56), calls=%async_computation.1 | async-start | bytes 2097152 | tf_op jit(solution)/shard_map/all_to_all | solution.py:226
  55.9 6.1 %collective-permute-start.4 = (bf16[512,1024]{1,0:T(8,128)(2,1)S(1)}, bf16[512,1024]{1,0:T(8,128)(2,1)}, u32[]{:S(2)}, u32[]{:S(2)}) collective-permute-start(bf16[512,1024]{1,0:T(8,128)(2,1)S(1)} %get-tuple-element.58), channel_id=1, source_target_pairs={{0,64},{64,0},{1,65},{65,1},{2,66},{66,2},{3,67},{67,3},{4,68},{68... | collective-permute-start | bytes 3145736 | tf_op jit(solution)/shard_map/ppermute | solution.py:228
  59.6 0.7 collective-permute-start.3
  85.4 6.5 %collective-permute-start.5 = (bf16[264,256]{1,0:T(8,128)(2,1)S(1)}, bf16[264,256]{1,0:T(8,128)(2,1)S(1)}, u32[]{:S(2)}, u32[]{:S(2)}) collective-permute-start(bf16[264,256]{1,0:T(8,128)(2,1)S(1)} %get-tuple-element.75.refs_0_), channel_id=1, source_target_pairs={{0,7},{1,0},{2,1},{3,2},{4,3},{5,4},{6,5},{7,6},{8,15},{9,8},{10,9... | collective-permute-start | bytes 405512 | tf_op jit(solution)/shard_map/ppermute | solution.py:189
  87.4 8.1 %collective-permute-start.6 = (bf16[264,256]{1,0:T(8,128)(2,1)S(1)}, bf16[264,256]{1,0:T(8,128)(2,1)S(1)}, u32[]{:S(2)}, u32[]{:S(2)}) collective-permute-start(bf16[264,256]{1,0:T(8,128)(2,1)S(1)} %get-tuple-element.75.refs_0_), channel_id=1, source_target_pairs={{0,1},{1,2},{2,3},{3,4},{4,5},{5,6},{6,7},{7,0},{8,9},{9,10},{10,1... | collective-permute-start | bytes 405512 | tf_op jit(solution)/shard_map/ppermute | solution.py:190
  92.0 5.7 %collective-permute-start.7 = (bf16[264,256]{1,0:T(8,128)(2,1)S(1)}, bf16[264,256]{1,0:T(8,128)(2,1)S(1)}, u32[]{:S(2)}, u32[]{:S(2)}) collective-permute-start(bf16[264,256]{1,0:T(8,128)(2,1)S(1)} %collective-permute-done.5.refs_1_), channel_id=1, source_target_pairs={{0,7},{1,0},{2,1},{3,2},{4,3},{5,4},{6,5},{7,6},{8,15},{9,8},{10,9... | collective-permute-start | bytes 405512 | tf_op jit(solution)/shard_map/ppermute | solution.py:189
  95.4 7.0 %collective-permute-start.8 = (bf16[264,256]{1,0:T(8,128)(2,1)S(1)}, bf16[264,256]{1,0:T(8,128)(2,1)S(1)}, u32[]{:S(2)}, u32[]{:S(2)}) collective-permute-start(bf16[264,256]{1,0:T(8,128)(2,1)S(1)} %collective-permute-done.6.refs_2_), channel_id=1, source_target_pairs={{0,1},{1,2},{2,3},{3,4},{4,5},{5,6},{6,7},{7,0},{8,9},{9,10},{10,1... | collective-permute-start | bytes 405512 | tf_op jit(solution)/shard_map/ppermute | solution.py:190
  97.7 6.6 %collective-permute-start.9 = (bf16[264,256]{1,0:T(8,128)(2,1)S(1)}, bf16[264,256]{1,0:T(8,128)(2,1)S(1)}, u32[]{:S(2)}, u32[]{:S(2)}) collective-permute-start(bf16[264,256]{1,0:T(8,128)(2,1)S(1)} %collective-permute-done.7.refs_3_), channel_id=1, source_target_pairs={{0,7},{1,0},{2,1},{3,2},{4,3},{5,4},{6,5},{7,6},{8,15},{9,8},{10,9... | collective-permute-start | bytes 405512 | tf_op jit(solution)/shard_map/ppermute | solution.py:189
  102.4 7.6 %collective-permute-start.10 = (bf16[264,256]{1,0:T(8,128)(2,1)S(1)}, bf16[264,256]{1,0:T(8,128)(2,1)S(1)}, u32[]{:S(2)}, u32[]{:S(2)}) collective-permute-start(bf16[264,256]{1,0:T(8,128)(2,1)S(1)} %collective-permute-done.8.refs_4_), channel_id=1, source_target_pairs={{0,1},{1,2},{2,3},{3,4},{4,5},{5,6},{6,7},{7,0},{8,9},{9,10},{10,1... | collective-permute-start | bytes 405512 | tf_op jit(solution)/shard_map/ppermute | solution.py:190
  104.3 7.0 %collective-permute-start.11 = (bf16[264,256]{1,0:T(8,128)(2,1)S(1)}, bf16[264,256]{1,0:T(8,128)(2,1)S(1)}, u32[]{:S(2)}, u32[]{:S(2)}) collective-permute-start(bf16[264,256]{1,0:T(8,128)(2,1)S(1)} %collective-permute-done.9.refs_5_), channel_id=1, source_target_pairs={{0,7},{1,0},{2,1},{3,2},{4,3},{5,4},{6,5},{7,6},{8,15},{9,8},{10,9... | collective-permute-start | bytes 405512 | tf_op jit(solution)/shard_map/ppermute | solution.py:192
  109.3 0.7 collective-permute-start.12
  111.3 1.0 copy-start.1
  112.3 1.0 copy-start.3
  113.4 1.0 copy-start.6
  114.4 1.0 copy-start.9
  118.3 15.6 %all-to-all-start.2 = ((bf16[4,1032,128]{2,1,0:T(8,128)(2,1)}), bf16[4,1032,128]{2,1,0:T(8,128)(2,1)S(1)}, u32[]{:S(2)}, u32[]{:S(2)}) async-start(bf16[4,1032,128]{2,1,0:T(8,128)(2,1)} %shard_map.95), calls=%async_computation.2 | async-start | bytes 2113536 | tf_op jit(solution)/shard_map/all_to_all | solution.py:245
  123.7 33.3 %collective-permute-start.13 = (bf16[128,256]{1,0:T(8,128)(2,1)S(1)}, bf16[128,256]{1,0:T(8,128)(2,1)S(1)}, u32[]{:S(2)}, u32[]{:S(2)}) collective-permute-start(bf16[128,256]{1,0:T(8,128)(2,1)S(1)} %collective-permute-done.12), channel_id=1, source_target_pairs={{0,0},{1,1},{2,2},{3,3},{4,4},{5,5},{6,6},{7,7},{130,128},{131,129... | collective-permute-start | bytes 196616 | tf_op jit(solution)/shard_map/ppermute | solution.py:246
  125.8 26.0 %collective-permute-start.14 = (bf16[2,512,256]{2,1,0:T(8,128)(2,1)}, bf16[2,512,256]{2,1,0:T(8,128)(2,1)}, u32[]{:S(2)}, u32[]{:S(2)}) collective-permute-start(bf16[2,512,256]{2,1,0:T(8,128)(2,1)} %get-tuple-element.85), channel_id=1, source_target_pairs={{0,64},{64,0},{1,65},{65,1},{2,66},{66,2},{3,67},{67,3},{4,68},{68... | collective-permute-start | bytes 1572872 | tf_op jit(solution)/shard_map/ppermute | solution.py:254
  133.9 18.0 %copy-start.11 = (f32[1024,256]{1,0:T(8,128)S(1)}, f32[1024,256]{1,0:T(8,128)}, u32[]{:S(2)}) copy-start(f32[1024,256]{1,0:T(8,128)} %fusion.6) | copy-start | bytes 3145732
  134.8 29.8 %all-to-all-start.3 = ((bf16[8,136,128]{2,1,0:T(8,128)(2,1)}), bf16[8,136,128]{2,1,0:T(8,128)(2,1)S(1)}, u32[]{:S(2)}, u32[]{:S(2)}) async-start(bf16[8,136,128]{2,1,0:T(8,128)(2,1)} %shard_map.96), calls=%async_computation.3 | async-start | bytes 557056 | tf_op jit(solution)/shard_map/all_to_all | solution.py:264
  165.3 3.2 %collective-permute-start.15 = (f32[8,128]{1,0:T(8,128)S(1)}, f32[8,128]{1,0:T(8,128)S(1)}, u32[]{:S(2)}, u32[]{:S(2)}) collective-permute-start(f32[8,128]{1,0:T(8,128)S(1)} %get-tuple-element.92.mine_ref), channel_id=1, source_target_pairs={{0,64},{64,0},{1,65},{65,1},{2,66},{66,2},{3,67},{67,3},{4,68},{68... | collective-permute-start | bytes 12296 | tf_op jit(solution)/shard_map/ppermute | solution.py:272

commit v5 on v4

--- a/solution.py
+++ b/solution.py
@@ -1,3 +1,5 @@
+import functools
+
 import jax
 import jax.numpy as jnp
 from jax import lax
@@ -63,9 +65,11 @@
     scal_ref[...] = rows_of(scale_in, scale_grad, top(jnp.abs(tok)))
 
 
-def forward_body(place_ref, x_ref, g0_ref, u0_ref, g1_ref, u1_ref, out_ref, xh_ref):
-    groups, cols, rows = out_ref.shape[0] // 2, x_ref.shape[0] // (out_ref.shape[0] // 2), x_ref.shape[1]
-    core, turned = place_ref[0], place_ref[1]
+def forward_body(place_ref, x_ref, g0_ref, u0_ref, g1_ref, u1_ref, out_ref, xh_ref, above_ref, below_ref):
+    count = out_ref.shape[0]
+    groups, rows = count // 2, x_ref.shape[1]
+    cols = x_ref.shape[0] // groups
+    core, turned, me = place_ref[0], place_ref[1], place_ref[2]
     for g in range(groups):
         spot = pl.ds(pl.multiple_of(lax.rem(turned + g, groups) * rows, rows), rows)
         for k in range(cols):
@@ -77,14 +81,23 @@
             part = jnp.dot(x, w_ref[...], preferred_element_type=F32).astype(BF16)
             for g in range(groups):
                 out_ref[2 * g + place, half * rows : (half + 1) * rows, :] = part[g * rows : (g + 1) * rows]
-
-
-def middle_body(in_ref, up_ref, scal_ref, hidden_ref, q_ref):
+    above_ref[...] = out_ref[lax.rem(me + count // 2, count)]
+    below_ref[...] = out_ref[lax.rem(me + count // 2 - 1, count)]
+
+
+def add_body(offset, place_ref, in_ref, parts_ref, out_ref):
+    count = parts_ref.shape[0]
+    own = parts_ref[lax.rem(place_ref[2] + (count + offset), count)]
+    out_ref[...] = (in_ref[...].astype(F32) + own.astype(F32)).astype(BF16)
+
+
+def middle_body(place_ref, above_ref, below_ref, parts_ref, up_ref, scal_ref, hidden_ref, q_ref):
     rows = up_ref.shape[0]
+    sums = above_ref[...].astype(F32) + below_ref[...].astype(F32) + parts_ref[place_ref[2]].astype(F32)
     scale_in = scal_ref[0:1, 0:1]
     scale_grad = scal_ref[1:2, 0:1]
-    gate_sum = jnp.sum(in_ref[:, :rows, :].astype(F32), axis=0) / scale_in
-    lift_sum = jnp.sum(in_ref[:, rows:, :].astype(F32), axis=0) / scale_in
+    gate_sum = sums[:rows] / scale_in
+    lift_sum = sums[rows:] / scale_in
     sigmoid_gate = 1.0 / (1.0 + jnp.exp(-gate_sum))
     activated = gate_sum * sigmoid_gate
     hidden = (activated * lift_sum).astype(BF16)
@@ -192,6 +205,21 @@
     return pieces + [lax.ppermute(above, axis, ahead)]
 
 
+def ring_sum(place, parts, above, below, axis, n):
+    down = [(i, (i - 1) % n) for i in range(n)]
+    onward = [(i, (i + 1) % n) for i in range(n)]
+    shape = [(above.shape, BF16)]
+    half = n // 2
+    for step in range(half):
+        above = lax.ppermute(above, axis, down)
+        if step < half - 1:
+            below = lax.ppermute(below, axis, onward)
+            (above,) = call(functools.partial(add_body, step + 1 - half), shape, (place, above, parts))
+        if step < half - 2:
+            (below,) = call(functools.partial(add_body, half - 2 - step), shape, (place, below, parts))
+    return above, below
+
+
 def per_device(sizes, tokens, w_gate, w_up, upstream, history):
     nh, nx, nw, ny = (sizes[a] for a in "hxwy")
     plane = ("h", "x", "w")
@@ -212,27 +240,26 @@
     gate_other = lax.ppermute(w_gate, "c", swap)
     lift_other = lax.ppermute(w_up, "c", swap)
     up = lax.ppermute(upstream, ("h", "y"), along_y)
+    up = lax.ppermute(up, ("h", "y"), along_z)
     x_all, gate_other, lift_other, up = lax.optimization_barrier((x_all, gate_other, lift_other, up))
 
     work = 8 * nh * rows * depth * units
-    parts, x_mine = call(
+    block = ((2 * rows, units), BF16)
+    parts, x_mine, above, below = call(
         forward_body,
-        [((ny, 2 * rows, units), BF16), ((nh * rows, depth), BF16)],
+        [((ny, 2 * rows, units), BF16), ((nh * rows, depth), BF16), block, block],
         (place, x_all, w_gate, w_up, gate_other, lift_other),
         flops=work,
         moved=6 * 2**20,
     )
-    parts, x_mine, up = lax.optimization_barrier((parts, x_mine, up))
-    sums = lax.all_to_all(parts, "y", 0, 0, tiled=True)
-    up = lax.ppermute(up, ("h", "y"), along_z)
-    x_other = lax.ppermute(x_mine, "c", swap)
-    sums, up, x_other = lax.optimization_barrier((sums, up, x_other))
+    above, below = ring_sum(place, parts, above, below, "y", ny)
     hidden, quants = call(
-        middle_body, [((rows, units), BF16), ((2 * rows + 8, units), BF16)], (sums, up, scal), moved=2**21
+        middle_body,
+        [((rows, units), BF16), ((2 * rows + 8, units), BF16)],
+        (place, above, below, parts, up, scal),
+        moved=2**21,
     )
     pieces = ring(quants, "y", ny)
-    hidden = lax.ppermute(hidden, ("h", "y"), along_z)
-    *pieces, hidden = lax.optimization_barrier((*pieces, hidden))
     (back,) = call(
         backward_body,
         [((nx, nh * nw * rows + 8, width), BF16)],
@@ -241,9 +268,10 @@
         moved=6 * 2**20,
         scratch=[pltpu.VMEM((2, 2, nh * rows, units), BF16)],
     )
-    *pieces, back, hidden = lax.optimization_barrier((*pieces, back, hidden))
+    *pieces, back, hidden, x_mine = lax.optimization_barrier((*pieces, back, hidden, x_mine))
     back_cols = lax.all_to_all(back, "x", 0, 0, tiled=True)
-    hidden = lax.ppermute(hidden, ("h", "y"), back_y)
+    hidden = lax.ppermute(hidden, ("h", "y"), along_z)
+    x_other = lax.ppermute(x_mine, "c", swap)
     q_mine, q_send = call(
         pick_body,
         [((2, nh * rows, units), BF16)] * 2,
@@ -252,6 +280,9 @@
         scratch=[pltpu.VMEM((2, 2, nh * rows, units), BF16)],
     )
     q_other = lax.ppermute(q_send, "c", swap)
+    back_cols, hidden, x_other, q_other = lax.optimization_barrier((back_cols, hidden, x_other, q_other))
+    (column,) = call(column_body, [((nh * nw, rows + 8, width), BF16)], (back_cols,), moved=2**21)
+    back_all = lax.all_to_all(column, ("h", "w"), 0, 0, tiled=True)
     divisor = scal[0, 0] * scal[1, 0] * (2 * nh * rows)
     contract = (((0,), (0,)), ((), ()))
     grads = []
@@ -260,8 +291,7 @@
             x_other, q_other[i], contract, preferred_element_type=F32
         )
         grads.append((total / divisor).astype(BF16))
-    (column,) = call(column_body, [((nh * nw, rows + 8, width), BF16)], (back_cols,), moved=2**21)
-    back_all = lax.all_to_all(column, ("h", "w"), 0, 0, tiled=True)
+    hidden = lax.ppermute(hidden, ("h", "y"), back_y)
     back_all, hidden, *grads = lax.optimization_barrier((back_all, hidden, *grads))
     input_grad, peaks, hidden = call(
         last_body,

time: 170 us -> 167 us (0.982)
  starting transfers between devices: 83.1 us -> 102 us
  waiting for transfers between devices: 55.8 us -> 38.1 us
  local copies, waits for them, and re-layouts: 10.5 us -> 2.72 us
    ppermute x0 -> x7, starting transfers between devices: none -> 25.1 us  [the longest x4 19.2 us: ring_sum(): above = lax.ppermute(above, axis, down)]
    all_to_all x1 -> x0, waiting for transfers between devices: 23 us -> none  [per_device(): sums = lax.all_to_all(parts, 'y', 0, 0, tiled=True)]
    all_to_all x1, starting transfers between devices: 17.1 us -> 5.91 us  [per_device(): back_all = lax.all_to_all(column, ('h', 'w'), 0, 0, tiled=True)]
    all_to_all x1, waiting for transfers between devices: 0.01 us -> 9.6 us  [per_device(): back_cols = lax.all_to_all(back, 'x', 0, 0, tiled=True)]
    ppermute x1, starting transfers between devices: 3.74 us -> 12.2 us  [per_device(): x_other = lax.ppermute(x_mine, 'c', swap)]
    unnamed x28 -> x18, local copies, waits for them, and re-layouts: 10 us -> 2.2 us
    all_to_all x1 -> x0, starting transfers between devices: 6.82 us -> none  [per_device(): sums = lax.all_to_all(parts, 'y', 0, 0, tiled=True)]
    all_to_all x1, waiting for transfers between devices: 7.59 us -> 1.36 us  [per_device(): back_all = lax.all_to_all(column, ('h', 'w'), 0, 0, tiled=True)]
  transfers between devices with their start and end apart: 20 -> 26, of which waited for: 9 -> 9; matrix products, arithmetic and copies ran while one was open for 5% -> 5% of each run, Pallas kernels for 1% -> 2%
where the time goes in v5:
time: 167 us; the launch traced here: 165 us
  starting transfers between devices  102 us (61%)
  waiting for transfers between devices  38.1 us (23%)
  Pallas kernels  12.1 us (7%)
  matrix products  8.42 us (5%)
  local copies, waits for them, and re-layouts  2.72 us (2%)
  between operations  2.34 us (1%)
    all_to_all x1, waiting for transfers between devices, per_device(): x_all = lax.all_to_all(copies, plane, 0, 0, tiled=True)  20.2 us
    ppermute x4, starting transfers between devices, ring_sum(): above = lax.ppermute(above, axis, down)  19.2 us
    ppermute x3, starting transfers between devices, ring(): above = lax.ppermute(above, axis, ahead)  15.3 us
    all_to_all x1, starting transfers between devices, per_device(): x_all = lax.all_to_all(copies, plane, 0, 0, tiled=True)  13.8 us
    ppermute x1, starting transfers between devices, per_device(): x_other = lax.ppermute(x_mine, 'c', swap)  12.2 us
    pallas_call x13, Pallas kernels, call(): pl.pallas_call(body, out_shape=[jax.ShapeDtypeStruct(s, t) for s, t in ou...  12.1 us
    all_to_all x1, waiting for transfers between devices, per_device(): back_cols = lax.all_to_all(back, 'x', 0, 0, tiled=True)  9.6 us
    all_to_all x1, starting transfers between devices, per_device(): back_all = lax.all_to_all(column, ('h', 'w'), 0, 0, tiled=True)  5.91 us
  transfers between devices with their start and end apart: 26, of which 9 were waited for; matrix products, arithmetic and copies ran while one was open for 5% of the time, Pallas kernels for 2%

profile of v5, /device:TPU:1, one launch (start us, length us, event | category | flops | bytes accessed | tf_op | source)
XLA Modules:
  0.0 165.4 jit_solution(1704100330738756533)
XLA Ops:
  0.6 0.8 copy.10.hist_ref
  1.4 0.8 copy-done.6
  2.1 1.2 shard_map.92
  3.3 13.8 %all-to-all-start = ((bf16[32,128,128]{2,1,0:T(8,128)(2,1)}), bf16[32,128,128]{2,1,0:T(8,128)(2,1)S(1)}, u32[]{:S(2)}, u32[]{:S(2)}) async-start(bf16[32,128,128]{2,1,0:T(8,128)(2,1)} %get-tuple-element.41), calls=%async_computation | async-start | bytes 2097152 | tf_op jit(solution)/shard_map/all_to_all | solution.py:239
  17.2 2.9 %collective-permute-start = (bf16[1024,256]{1,0:T(8,128)(2,1)S(1)}, bf16[1024,256]{1,0:T(8,128)(2,1)S(1)}, u32[]{:S(2)}, u32[]{:S(2)}) collective-permute-start(bf16[1024,256]{1,0:T(8,128)(2,1)S(1)} %copy-done), channel_id=1, source_target_pairs={{0,64},{64,0},{1,65},{65,1},{2,66},{66,2},{3,67},{67,3},{4,68},{68... | collective-permute-start | bytes 1572872 | tf_op jit(solution)/shard_map/ppermute | solution.py:240
  20.1 1.9 %collective-permute-start.1 = (bf16[1024,256]{1,0:T(8,128)(2,1)S(1)}, bf16[1024,256]{1,0:T(8,128)(2,1)S(1)}, u32[]{:S(2)}, u32[]{:S(2)}) collective-permute-start(bf16[1024,256]{1,0:T(8,128)(2,1)S(1)} %copy-done.1), channel_id=1, source_target_pairs={{0,64},{64,0},{1,65},{65,1},{2,66},{66,2},{3,67},{67,3},{4,68},{68... | collective-permute-start | bytes 1572872 | tf_op jit(solution)/shard_map/ppermute | solution.py:241
  22.0 0.7 collective-permute-start.2
  22.7 0.7 collective-permute-start.3
  23.4 0.1 pad_add_fusion.place_ref
  23.5 0.4 collective-permute-done.1.u1_ref.refs_11_
  23.9 20.2 %all-to-all-done.x_ref = bf16[32,128,128]{2,1,0:T(8,128)(2,1)S(1)} async-done(((bf16[32,128,128]{2,1,0:T(8,128)(2,1)}), bf16[32,128,128]{2,1,0:T(8,128)(2,1)S(1)}, u32[]{:S(2)}, u32[]{:S(2)}) %all-to-all-start) | async-done | bytes 1048608 | tf_op jit(solution)/shard_map/all_to_all | solution.py:239
  44.1 2.0 %shard_map.93 = (bf16[8,256,256]{2,1,0:T(8,128)(2,1)S(1)}, bf16[512,1024]{1,0:T(8,128)(2,1)}, bf16[256,256]{1,0:T(8,128)(2,1)S(1)}, bf16[256,256]{1,0:T(8,128)(2,1)S(1)}) custom-call(s32[3]{0:T(128)S(1)} %pad_add_fusion.place_ref, bf16[32,128,128]{2,1,0:T(8,128)(2,1)S(1)} %all-to-all-done.x_ref, bf16[1024,256]{1,0:T(8,128)(2,1)S(1)} %copy-done, ...), custom_call_target="tpu_custom_call" | custom-call | flops 1073741824 | bytes 6291456 | tf_op jit(solution)/shard_map/pallas_call | solution.py:22
  46.1 5.1 %collective-permute-start.4 = (bf16[256,256]{1,0:T(8,128)(2,1)S(1)}, bf16[256,256]{1,0:T(8,128)(2,1)S(1)}, u32[]{:S(2)}, u32[]{:S(2)}) collective-permute-start(bf16[256,256]{1,0:T(8,128)(2,1)S(1)} %get-tuple-element.45), channel_id=1, source_target_pairs={{0,7},{1,0},{2,1},{3,2},{4,3},{5,4},{6,5},{7,6},{8,15},{9,8},{10,9... | collective-permute-start | bytes 393224 | tf_op jit(solution)/shard_map/ppermute | solution.py:214
  51.2 1.9 %collective-permute-start.8 = (bf16[256,256]{1,0:T(8,128)(2,1)S(1)}, bf16[256,256]{1,0:T(8,128)(2,1)S(1)}, u32[]{:S(2)}, u32[]{:S(2)}) collective-permute-start(bf16[256,256]{1,0:T(8,128)(2,1)S(1)} %get-tuple-element.47), channel_id=1, source_target_pairs={{0,1},{1,2},{2,3},{3,4},{4,5},{5,6},{6,7},{7,0},{8,9},{9,10},{10,1... | collective-permute-start | bytes 393224 | tf_op jit(solution)/shard_map/ppermute | solution.py:216
  53.2 0.0 collective-permute-done.4.in_ref
  53.2 0.6 shard_map.94
  53.8 5.0 %collective-permute-start.5 = (bf16[256,256]{1,0:T(8,128)(2,1)S(1)}, bf16[256,256]{1,0:T(8,128)(2,1)S(1)}, u32[]{:S(2)}, u32[]{:S(2)}) collective-permute-start(bf16[256,256]{1,0:T(8,128)(2,1)S(1)} %shard_map.94), channel_id=1, source_target_pairs={{0,7},{1,0},{2,1},{3,2},{4,3},{5,4},{6,5},{7,6},{8,15},{9,8},{10,9... | collective-permute-start | bytes 393224 | tf_op jit(solution)/shard_map/ppermute | solution.py:214
  58.7 0.0 collective-permute-done.8.in_ref
  58.8 0.6 shard_map.97
  59.3 1.9 %collective-permute-start.9 = (bf16[256,256]{1,0:T(8,128)(2,1)S(1)}, bf16[256,256]{1,0:T(8,128)(2,1)S(1)}, u32[]{:S(2)}, u32[]{:S(2)}) collective-permute-start(bf16[256,256]{1,0:T(8,128)(2,1)S(1)} %shard_map.97), channel_id=1, source_target_pairs={{0,1},{1,2},{2,3},{3,4},{4,5},{5,6},{6,7},{7,0},{8,9},{9,10},{10,1... | collective-permute-start | bytes 393224 | tf_op jit(solution)/shard_map/ppermute | solution.py:216
  61.3 0.6 shard_map.95
  61.9 4.6 %collective-permute-start.6 = (bf16[256,256]{1,0:T(8,128)(2,1)S(1)}, bf16[256,256]{1,0:T(8,128)(2,1)S(1)}, u32[]{:S(2)}, u32[]{:S(2)}) collective-permute-start(bf16[256,256]{1,0:T(8,128)(2,1)S(1)} %shard_map.95), channel_id=1, source_target_pairs={{0,7},{1,0},{2,1},{3,2},{4,3},{5,4},{6,5},{7,6},{8,15},{9,8},{10,9... | collective-permute-start | bytes 393224 | tf_op jit(solution)/shard_map/ppermute | solution.py:214
  66.5 0.6 shard_map.98
  67.0 0.0 copy-start.3
  67.1 0.0 copy-start.5
  67.1 2.1 %collective-permute-start.10 = (bf16[256,256]{1,0:T(8,128)(2,1)S(1)}, bf16[256,256]{1,0:T(8,128)(2,1)S(1)}, u32[]{:S(2)}, u32[]{:S(2)}) collective-permute-start(bf16[256,256]{1,0:T(8,128)(2,1)S(1)} %shard_map.98), channel_id=1, source_target_pairs={{0,1},{1,2},{2,3},{3,4},{4,5},{5,6},{6,7},{7,0},{8,9},{9,10},{10,1... | collective-permute-start | bytes 393224 | tf_op jit(solution)/shard_map/ppermute | solution.py:216
  69.1 0.6 shard_map.96
  69.7 4.6 %collective-permute-start.7 = (bf16[256,256]{1,0:T(8,128)(2,1)S(1)}, bf16[256,256]{1,0:T(8,128)(2,1)S(1)}, u32[]{:S(2)}, u32[]{:S(2)}) collective-permute-start(bf16[256,256]{1,0:T(8,128)(2,1)S(1)} %shard_map.96), channel_id=1, source_target_pairs={{0,7},{1,0},{2,1},{3,2},{4,3},{5,4},{6,5},{7,6},{8,15},{9,8},{10,9... | collective-permute-start | bytes 393224 | tf_op jit(solution)/shard_map/ppermute | solution.py:214
  74.3 0.0 collective-permute-done.10.below_ref
  74.3 1.9 %collective-permute-done.7.above_ref = bf16[256,256]{1,0:T(8,128)(2,1)S(1)} collective-permute-done((bf16[256,256]{1,0:T(8,128)(2,1)S(1)}, bf16[256,256]{1,0:T(8,128)(2,1)S(1)}, u32[]{:S(2)}, u32[]{:S(2)}) %collective-permute-start.7) | collective-permute-done | bytes 131104 | tf_op jit(solution)/shard_map/ppermute | solution.py:214
  76.2 0.8 shard_map.99
  77.0 5.0 %collective-permute-start.11 = (bf16[264,256]{1,0:T(8,128)(2,1)S(1)}, bf16[264,256]{1,0:T(8,128)(2,1)S(1)}, u32[]{:S(2)}, u32[]{:S(2)}) collective-permute-start(bf16[264,256]{1,0:T(8,128)(2,1)S(1)} %get-tuple-element.56.refs_0_), channel_id=1, source_target_pairs={{0,7},{1,0},{2,1},{3,2},{4,3},{5,4},{6,5},{7,6},{8,15},{9,8},{10,9... | collective-permute-start | bytes 405512 | tf_op jit(solution)/shard_map/ppermute | solution.py:202
  82.0 1.9 %collective-permute-start.12 = (bf16[264,256]{1,0:T(8,128)(2,1)S(1)}, bf16[264,256]{1,0:T(8,128)(2,1)S(1)}, u32[]{:S(2)}, u32[]{:S(2)}) collective-permute-start(bf16[264,256]{1,0:T(8,128)(2,1)S(1)} %get-tuple-element.56.refs_0_), channel_id=1, source_target_pairs={{0,1},{1,2},{2,3},{3,4},{4,5},{5,6},{6,7},{7,0},{8,9},{9,10},{10,1... | collective-permute-start | bytes 405512 | tf_op jit(solution)/shard_map/ppermute | solution.py:203
  83.9 0.0 collective-permute-done.11.refs_1_
  84.0 5.0 %collective-permute-start.13 = (bf16[264,256]{1,0:T(8,128)(2,1)S(1)}, bf16[264,256]{1,0:T(8,128)(2,1)S(1)}, u32[]{:S(2)}, u32[]{:S(2)}) collective-permute-start(bf16[264,256]{1,0:T(8,128)(2,1)S(1)} %collective-permute-done.11.refs_1_), channel_id=1, source_target_pairs={{0,7},{1,0},{2,1},{3,2},{4,3},{5,4},{6,5},{7,6},{8,15},{9,8},{10,9... | collective-permute-start | bytes 405512 | tf_op jit(solution)/shard_map/ppermute | solution.py:202
  89.0 0.0 collective-permute-done.12.refs_2_
  89.0 1.9 %collective-permute-start.14 = (bf16[264,256]{1,0:T(8,128)(2,1)S(1)}, bf16[264,256]{1,0:T(8,128)(2,1)S(1)}, u32[]{:S(2)}, u32[]{:S(2)}) collective-permute-start(bf16[264,256]{1,0:T(8,128)(2,1)S(1)} %collective-permute-done.12.refs_2_), channel_id=1, source_target_pairs={{0,1},{1,2},{2,3},{3,4},{4,5},{5,6},{6,7},{7,0},{8,9},{9,10},{10,1... | collective-permute-start | bytes 405512 | tf_op jit(solution)/shard_map/ppermute | solution.py:203
  90.9 1.3 collective-permute-done.13.refs_3_
  92.2 5.3 %collective-permute-start.15 = (bf16[264,256]{1,0:T(8,128)(2,1)S(1)}, bf16[264,256]{1,0:T(8,128)(2,1)S(1)}, u32[]{:S(2)}, u32[]{:S(2)}) collective-permute-start(bf16[264,256]{1,0:T(8,128)(2,1)S(1)} %collective-permute-done.13.refs_3_), channel_id=1, source_target_pairs={{0,7},{1,0},{2,1},{3,2},{4,3},{5,4},{6,5},{7,6},{8,15},{9,8},{10,9... | collective-permute-start | bytes 405512 | tf_op jit(solution)/shard_map/ppermute | solution.py:202
  97.6 1.9 %collective-permute-start.16 = (bf16[264,256]{1,0:T(8,128)(2,1)S(1)}, bf16[264,256]{1,0:T(8,128)(2,1)S(1)}, u32[]{:S(2)}, u32[]{:S(2)}) collective-permute-start(bf16[264,256]{1,0:T(8,128)(2,1)S(1)} %collective-permute-done.14.refs_4_), channel_id=1, source_target_pairs={{0,1},{1,2},{2,3},{3,4},{4,5},{5,6},{6,7},{7,0},{8,9},{9,10},{10,1... | collective-permute-start | bytes 405512 | tf_op jit(solution)/shard_map/ppermute | solution.py:203
  99.5 0.5 collective-permute-done.15.refs_5_
  99.9 5.3 %collective-permute-start.17 = (bf16[264,256]{1,0:T(8,128)(2,1)S(1)}, bf16[264,256]{1,0:T(8,128)(2,1)S(1)}, u32[]{:S(2)}, u32[]{:S(2)}) collective-permute-start(bf16[264,256]{1,0:T(8,128)(2,1)S(1)} %collective-permute-done.15.refs_5_), channel_id=1, source_target_pairs={{0,7},{1,0},{2,1},{3,2},{4,3},{5,4},{6,5},{7,6},{8,15},{9,8},{10,9... | collective-permute-start | bytes 405512 | tf_op jit(solution)/shard_map/ppermute | solution.py:205
  105.3 2.0 %collective-permute-done.17.refs_7_ = bf16[264,256]{1,0:T(8,128)(2,1)S(1)} collective-permute-done((bf16[264,256]{1,0:T(8,128)(2,1)S(1)}, bf16[264,256]{1,0:T(8,128)(2,1)S(1)}, u32[]{:S(2)}, u32[]{:S(2)}) %collective-permute-start.17) | collective-permute-done | bytes 135200 | tf_op jit(solution)/shard_map/ppermute | solution.py:205
  107.2 2.9 %shard_map.100 = bf16[4,1032,128]{2,1,0:T(8,128)(2,1)} custom-call(s32[3]{0:T(128)S(1)} %pad_add_fusion.place_ref, bf16[264,256]{1,0:T(8,128)(2,1)S(1)} %get-tuple-element.56.refs_0_, bf16[264,256]{1,0:T(8,128)(2,1)S(1)} %collective-permute-done.11.refs_1_, bf16[264,256]{1,0:T(8,128)(2,1)S(1)} %collective-permute-done.12.refs_2_, ...), custom_call_target="tpu_custom_call" | custom-call | flops 1073741824 | bytes 6291456 | tf_op jit(solution)/shard_map/pallas_call | solution.py:22
  110.1 12.2 %collective-permute-start.19 = (bf16[512,1024]{1,0:T(8,128)(2,1)}, bf16[512,1024]{1,0:T(8,128)(2,1)}, u32[]{:S(2)}, u32[]{:S(2)}) collective-permute-start(bf16[512,1024]{1,0:T(8,128)(2,1)} %get-tuple-element.55), channel_id=1, source_target_pairs={{0,64},{64,0},{1,65},{65,1},{2,66},{66,2},{3,67},{67,3},{4,68},{68... | collective-permute-start | bytes 3145736 | tf_op jit(solution)/shard_map/ppermute | solution.py:274
  122.3 4.0 %all-to-all-start.1 = ((bf16[4,1032,128]{2,1,0:T(8,128)(2,1)}), bf16[4,1032,128]{2,1,0:T(8,128)(2,1)S(1)}, u32[]{:S(2)}, u32[]{:S(2)}) async-start(bf16[4,1032,128]{2,1,0:T(8,128)(2,1)} %shard_map.100), calls=%async_computation.1 | async-start | bytes 2113536 | tf_op jit(solution)/shard_map/all_to_all | solution.py:272
  126.3 0.7 shard_map.101
  127.0 2.2 %collective-permute-start.20 = (bf16[2,512,256]{2,1,0:T(8,128)(2,1)S(1)}, bf16[2,512,256]{2,1,0:T(8,128)(2,1)S(1)}, u32[]{:S(2)}, u32[]{:S(2)}) collective-permute-start(bf16[2,512,256]{2,1,0:T(8,128)(2,1)S(1)} %get-tuple-element.64), channel_id=1, source_target_pairs={{0,64},{64,0},{1,65},{65,1},{2,66},{66,2},{3,67},{67,3},{4,68},{68... | collective-permute-start | bytes 1572872 | tf_op jit(solution)/shard_map/ppermute | solution.py:282
  129.2 0.7 collective-permute-start.18
  129.9 0.5 fusion.14
  131.7 9.6 %all-to-all-done.1.in_ref = bf16[4,1032,128]{2,1,0:T(8,128)(2,1)S(1)} async-done(((bf16[4,1032,128]{2,1,0:T(8,128)(2,1)}), bf16[4,1032,128]{2,1,0:T(8,128)(2,1)S(1)}, u32[]{:S(2)}, u32[]{:S(2)}) %all-to-all-start.1) | async-done | bytes 1056800 | tf_op jit(solution)/shard_map/all_to_all | solution.py:272
  141.3 0.9 shard_map.102
  142.2 5.9 %all-to-all-start.2 = ((bf16[8,136,128]{2,1,0:T(8,128)(2,1)}), bf16[8,136,128]{2,1,0:T(8,128)(2,1)S(1)}, u32[]{:S(2)}, u32[]{:S(2)}) async-start(bf16[8,136,128]{2,1,0:T(8,128)(2,1)} %shard_map.102), calls=%async_computation.2 | async-start | bytes 557056 | tf_op jit(solution)/shard_map/all_to_all | solution.py:285
  148.1 0.7 collective-permute-start.21
  148.8 1.7 %fusion.7 = f32[1024,256]{1,0:T(8,128)S(1)} fusion(bf16[512,1024]{1,0:T(8,128)(2,1)} %collective-permute-done.19, bf16[2,512,256]{2,1,0:T(8,128)(2,1)S(1)} %collective-permute-done.20), kind=kOutput, calls=%fused_computation.9 | convolution fusion | flops 268435456 | bytes 2359296 | tf_op jit(solution)/shard_map/dot_general | solution.py:290
  150.5 2.5 %fusion.2 = bf16[1024,256]{1,0:T(8,128)(2,1)} fusion(f32[1024,256]{1,0:T(8,128)S(1)} %fusion.7, bf16[512,1024]{1,0:T(8,128)(2,1)} %get-tuple-element.55, f32[]{:T(128)} %bitcast.5, bf16[2,512,256]{2,1,0:T(8,128)(2,1)S(1)} %get-tuple-element.67), kind=kOutput, calls=%fused_computation.4 | convolution fusion | flops 269221888 | bytes 2883588 | tf_op jit(solution)/shard_map/dot_general | solution.py:290
  153.0 1.7 %fusion.4 = f32[1024,256]{1,0:T(8,128)S(1)} fusion(bf16[512,1024]{1,0:T(8,128)(2,1)} %collective-permute-done.19, bf16[2,512,256]{2,1,0:T(8,128)(2,1)S(1)} %collective-permute-done.20), kind=kOutput, calls=%fused_computation.6 | convolution fusion | flops 268435456 | bytes 2359296 | tf_op jit(solution)/shard_map/dot_general | solution.py:290
  154.7 2.5 %fusion.3 = bf16[1024,256]{1,0:T(8,128)(2,1)} fusion(f32[1024,256]{1,0:T(8,128)S(1)} %fusion.4, bf16[512,1024]{1,0:T(8,128)(2,1)} %get-tuple-element.55, f32[]{:T(128)} %bitcast.5, bf16[2,512,256]{2,1,0:T(8,128)(2,1)S(1)} %get-tuple-element.67), kind=kOutput, calls=%fused_computation.5 | convolution fusion | flops 269221888 | bytes 2883588 | tf_op jit(solution)/shard_map/dot_general | solution.py:290
  157.2 1.4 all-to-all-done.2.in_ref
  158.6 0.7 shard_map.103
  159.3 4.6 %collective-permute-start.22 = (f32[8,128]{1,0:T(8,128)S(1)}, f32[8,128]{1,0:T(8,128)S(1)}, u32[]{:S(2)}, u32[]{:S(2)}) collective-permute-start(f32[8,128]{1,0:T(8,128)S(1)} %get-tuple-element.76.mine_ref), channel_id=1, source_target_pairs={{0,64},{64,0},{1,65},{65,1},{2,66},{66,2},{3,67},{67,3},{4,68},{68... | collective-permute-start | bytes 12296 | tf_op jit(solution)/shard_map/ppermute | solution.py:302
  163.9 0.8 collective-permute-done.22.other_ref
  164.7 0.1 shard_map.104
  164.8 0.7 copy.12
  (25 shorter events, 0.1 us)
Async XLA Ops:
  1.4 0.8 copy-start.6
  3.3 13.9 %copy-start = (bf16[1024,256]{1,0:T(8,128)(2,1)S(1)}, bf16[1024,256]{1,0:T(8,128)(2,1)}, u32[]{:S(2)}) copy-start(bf16[1024,256]{1,0:T(8,128)(2,1)} %refs_8_.1) | copy-start | bytes 1572868
  3.3 16.7 %copy-start.1 = (bf16[1024,256]{1,0:T(8,128)(2,1)S(1)}, bf16[1024,256]{1,0:T(8,128)(2,1)}, u32[]{:S(2)}) copy-start(bf16[1024,256]{1,0:T(8,128)(2,1)} %refs_9_.1) | copy-start | bytes 1572868
  3.3 18.7 %copy-start.7 = (bf16[128,256]{1,0:T(8,128)(2,1)S(1)}, bf16[128,256]{1,0:T(8,128)(2,1)}, u32[]{:S(2)}) copy-start(bf16[128,256]{1,0:T(8,128)(2,1)} %param.8) | copy-start | bytes 196612
  3.3 40.8 %all-to-all-start = ((bf16[32,128,128]{2,1,0:T(8,128)(2,1)}), bf16[32,128,128]{2,1,0:T(8,128)(2,1)S(1)}, u32[]{:S(2)}, u32[]{:S(2)}) async-start(bf16[32,128,128]{2,1,0:T(8,128)(2,1)} %get-tuple-element.41), calls=%async_computation | async-start | bytes 2097152 | tf_op jit(solution)/shard_map/all_to_all | solution.py:239
  17.2 6.3 %collective-permute-start = (bf16[1024,256]{1,0:T(8,128)(2,1)S(1)}, bf16[1024,256]{1,0:T(8,128)(2,1)S(1)}, u32[]{:S(2)}, u32[]{:S(2)}) collective-permute-start(bf16[1024,256]{1,0:T(8,128)(2,1)S(1)} %copy-done), channel_id=1, source_target_pairs={{0,64},{64,0},{1,65},{65,1},{2,66},{66,2},{3,67},{67,3},{4,68},{68... | collective-permute-start | bytes 1572872 | tf_op jit(solution)/shard_map/ppermute | solution.py:240
  20.1 3.8 %collective-permute-start.1 = (bf16[1024,256]{1,0:T(8,128)(2,1)S(1)}, bf16[1024,256]{1,0:T(8,128)(2,1)S(1)}, u32[]{:S(2)}, u32[]{:S(2)}) collective-permute-start(bf16[1024,256]{1,0:T(8,128)(2,1)S(1)} %copy-done.1), channel_id=1, source_target_pairs={{0,64},{64,0},{1,65},{65,1},{2,66},{66,2},{3,67},{67,3},{4,68},{68... | collective-permute-start | bytes 1572872 | tf_op jit(solution)/shard_map/ppermute | solution.py:241
  22.0 0.7 collective-permute-start.2
  22.7 0.8 collective-permute-start.3
  23.5 22.7 %copy-start.2 = (bf16[1024,256]{1,0:T(8,128)(2,1)}, bf16[1024,256]{1,0:T(8,128)(2,1)S(1)}, u32[]{:S(2)}) copy-start(bf16[1024,256]{1,0:T(8,128)(2,1)S(1)} %collective-permute-done.g1_ref.refs_10_) | copy-start | bytes 1572868
  23.9 22.3 %copy-start.4 = (bf16[1024,256]{1,0:T(8,128)(2,1)}, bf16[1024,256]{1,0:T(8,128)(2,1)S(1)}, u32[]{:S(2)}) copy-start(bf16[1024,256]{1,0:T(8,128)(2,1)S(1)} %collective-permute-done.1.u1_ref.refs_11_) | copy-start | bytes 1572868
  46.1 7.0 %collective-permute-start.4 = (bf16[256,256]{1,0:T(8,128)(2,1)S(1)}, bf16[256,256]{1,0:T(8,128)(2,1)S(1)}, u32[]{:S(2)}, u32[]{:S(2)}) collective-permute-start(bf16[256,256]{1,0:T(8,128)(2,1)S(1)} %get-tuple-element.45), channel_id=1, source_target_pairs={{0,7},{1,0},{2,1},{3,2},{4,3},{5,4},{6,5},{7,6},{8,15},{9,8},{10,9... | collective-permute-start | bytes 393224 | tf_op jit(solution)/shard_map/ppermute | solution.py:214
  51.2 7.5 %collective-permute-start.8 = (bf16[256,256]{1,0:T(8,128)(2,1)S(1)}, bf16[256,256]{1,0:T(8,128)(2,1)S(1)}, u32[]{:S(2)}, u32[]{:S(2)}) collective-permute-start(bf16[256,256]{1,0:T(8,128)(2,1)S(1)} %get-tuple-element.47), channel_id=1, source_target_pairs={{0,1},{1,2},{2,3},{3,4},{4,5},{5,6},{6,7},{7,0},{8,9},{9,10},{10,1... | collective-permute-start | bytes 393224 | tf_op jit(solution)/shard_map/ppermute | solution.py:216
  53.8 7.5 %collective-permute-start.5 = (bf16[256,256]{1,0:T(8,128)(2,1)S(1)}, bf16[256,256]{1,0:T(8,128)(2,1)S(1)}, u32[]{:S(2)}, u32[]{:S(2)}) collective-permute-start(bf16[256,256]{1,0:T(8,128)(2,1)S(1)} %shard_map.94), channel_id=1, source_target_pairs={{0,7},{1,0},{2,1},{3,2},{4,3},{5,4},{6,5},{7,6},{8,15},{9,8},{10,9... | collective-permute-start | bytes 393224 | tf_op jit(solution)/shard_map/ppermute | solution.py:214
  59.3 7.1 %collective-permute-start.9 = (bf16[256,256]{1,0:T(8,128)(2,1)S(1)}, bf16[256,256]{1,0:T(8,128)(2,1)S(1)}, u32[]{:S(2)}, u32[]{:S(2)}) collective-permute-start(bf16[256,256]{1,0:T(8,128)(2,1)S(1)} %shard_map.97), channel_id=1, source_target_pairs={{0,1},{1,2},{2,3},{3,4},{4,5},{5,6},{6,7},{7,0},{8,9},{9,10},{10,1... | collective-permute-start | bytes 393224 | tf_op jit(solution)/shard_map/ppermute | solution.py:216
  61.9 7.3 %collective-permute-start.6 = (bf16[256,256]{1,0:T(8,128)(2,1)S(1)}, bf16[256,256]{1,0:T(8,128)(2,1)S(1)}, u32[]{:S(2)}, u32[]{:S(2)}) collective-permute-start(bf16[256,256]{1,0:T(8,128)(2,1)S(1)} %shard_map.95), channel_id=1, source_target_pairs={{0,7},{1,0},{2,1},{3,2},{4,3},{5,4},{6,5},{7,6},{8,15},{9,8},{10,9... | collective-permute-start | bytes 393224 | tf_op jit(solution)/shard_map/ppermute | solution.py:214
  67.0 40.2 %copy-start.3 = (bf16[1024,256]{1,0:T(8,128)(2,1)S(1)}, bf16[1024,256]{1,0:T(8,128)(2,1)}, u32[]{:S(2)}) copy-start(bf16[1024,256]{1,0:T(8,128)(2,1)} %copy-done.2) | copy-start | bytes 1572868
  67.1 40.2 %copy-start.5 = (bf16[1024,256]{1,0:T(8,128)(2,1)S(1)}, bf16[1024,256]{1,0:T(8,128)(2,1)}, u32[]{:S(2)}) copy-start(bf16[1024,256]{1,0:T(8,128)(2,1)} %copy-done.4) | copy-start | bytes 1572868
  67.1 7.2 %collective-permute-start.10 = (bf16[256,256]{1,0:T(8,128)(2,1)S(1)}, bf16[256,256]{1,0:T(8,128)(2,1)S(1)}, u32[]{:S(2)}, u32[]{:S(2)}) collective-permute-start(bf16[256,256]{1,0:T(8,128)(2,1)S(1)} %shard_map.98), channel_id=1, source_target_pairs={{0,1},{1,2},{2,3},{3,4},{4,5},{5,6},{6,7},{7,0},{8,9},{9,10},{10,1... | collective-permute-start | bytes 393224 | tf_op jit(solution)/shard_map/ppermute | solution.py:216
  69.7 6.5 %collective-permute-start.7 = (bf16[256,256]{1,0:T(8,128)(2,1)S(1)}, bf16[256,256]{1,0:T(8,128)(2,1)S(1)}, u32[]{:S(2)}, u32[]{:S(2)}) collective-permute-start(bf16[256,256]{1,0:T(8,128)(2,1)S(1)} %shard_map.96), channel_id=1, source_target_pairs={{0,7},{1,0},{2,1},{3,2},{4,3},{5,4},{6,5},{7,6},{8,15},{9,8},{10,9... | collective-permute-start | bytes 393224 | tf_op jit(solution)/shard_map/ppermute | solution.py:214
  77.0 7.0 %collective-permute-start.11 = (bf16[264,256]{1,0:T(8,128)(2,1)S(1)}, bf16[264,256]{1,0:T(8,128)(2,1)S(1)}, u32[]{:S(2)}, u32[]{:S(2)}) collective-permute-start(bf16[264,256]{1,0:T(8,128)(2,1)S(1)} %get-tuple-element.56.refs_0_), channel_id=1, source_target_pairs={{0,7},{1,0},{2,1},{3,2},{4,3},{5,4},{6,5},{7,6},{8,15},{9,8},{10,9... | collective-permute-start | bytes 405512 | tf_op jit(solution)/shard_map/ppermute | solution.py:202
  82.0 7.0 %collective-permute-start.12 = (bf16[264,256]{1,0:T(8,128)(2,1)S(1)}, bf16[264,256]{1,0:T(8,128)(2,1)S(1)}, u32[]{:S(2)}, u32[]{:S(2)}) collective-permute-start(bf16[264,256]{1,0:T(8,128)(2,1)S(1)} %get-tuple-element.56.refs_0_), channel_id=1, source_target_pairs={{0,1},{1,2},{2,3},{3,4},{4,5},{5,6},{6,7},{7,0},{8,9},{9,10},{10,1... | collective-permute-start | bytes 405512 | tf_op jit(solution)/shard_map/ppermute | solution.py:203
  84.0 8.2 %collective-permute-start.13 = (bf16[264,256]{1,0:T(8,128)(2,1)S(1)}, bf16[264,256]{1,0:T(8,128)(2,1)S(1)}, u32[]{:S(2)}, u32[]{:S(2)}) collective-permute-start(bf16[264,256]{1,0:T(8,128)(2,1)S(1)} %collective-permute-done.11.refs_1_), channel_id=1, source_target_pairs={{0,7},{1,0},{2,1},{3,2},{4,3},{5,4},{6,5},{7,6},{8,15},{9,8},{10,9... | collective-permute-start | bytes 405512 | tf_op jit(solution)/shard_map/ppermute | solution.py:202
  89.0 8.6 %collective-permute-start.14 = (bf16[264,256]{1,0:T(8,128)(2,1)S(1)}, bf16[264,256]{1,0:T(8,128)(2,1)S(1)}, u32[]{:S(2)}, u32[]{:S(2)}) collective-permute-start(bf16[264,256]{1,0:T(8,128)(2,1)S(1)} %collective-permute-done.12.refs_2_), channel_id=1, source_target_pairs={{0,1},{1,2},{2,3},{3,4},{4,5},{5,6},{6,7},{7,0},{8,9},{9,10},{10,1... | collective-permute-start | bytes 405512 | tf_op jit(solution)/shard_map/ppermute | solution.py:203
  92.2 7.7 %collective-permute-start.15 = (bf16[264,256]{1,0:T(8,128)(2,1)S(1)}, bf16[264,256]{1,0:T(8,128)(2,1)S(1)}, u32[]{:S(2)}, u32[]{:S(2)}) collective-permute-start(bf16[264,256]{1,0:T(8,128)(2,1)S(1)} %collective-permute-done.13.refs_3_), channel_id=1, source_target_pairs={{0,7},{1,0},{2,1},{3,2},{4,3},{5,4},{6,5},{7,6},{8,15},{9,8},{10,9... | collective-permute-start | bytes 405512 | tf_op jit(solution)/shard_map/ppermute | solution.py:202
  97.6 7.7 %collective-permute-start.16 = (bf16[264,256]{1,0:T(8,128)(2,1)S(1)}, bf16[264,256]{1,0:T(8,128)(2,1)S(1)}, u32[]{:S(2)}, u32[]{:S(2)}) collective-permute-start(bf16[264,256]{1,0:T(8,128)(2,1)S(1)} %collective-permute-done.14.refs_4_), channel_id=1, source_target_pairs={{0,1},{1,2},{2,3},{3,4},{4,5},{5,6},{6,7},{7,0},{8,9},{9,10},{10,1... | collective-permute-start | bytes 405512 | tf_op jit(solution)/shard_map/ppermute | solution.py:203
  99.9 7.3 %collective-permute-start.17 = (bf16[264,256]{1,0:T(8,128)(2,1)S(1)}, bf16[264,256]{1,0:T(8,128)(2,1)S(1)}, u32[]{:S(2)}, u32[]{:S(2)}) collective-permute-start(bf16[264,256]{1,0:T(8,128)(2,1)S(1)} %collective-permute-done.15.refs_5_), channel_id=1, source_target_pairs={{0,7},{1,0},{2,1},{3,2},{4,3},{5,4},{6,5},{7,6},{8,15},{9,8},{10,9... | collective-permute-start | bytes 405512 | tf_op jit(solution)/shard_map/ppermute | solution.py:205
  110.1 31.3 %collective-permute-start.19 = (bf16[512,1024]{1,0:T(8,128)(2,1)}, bf16[512,1024]{1,0:T(8,128)(2,1)}, u32[]{:S(2)}, u32[]{:S(2)}) collective-permute-start(bf16[512,1024]{1,0:T(8,128)(2,1)} %get-tuple-element.55), channel_id=1, source_target_pairs={{0,64},{64,0},{1,65},{65,1},{2,66},{66,2},{3,67},{67,3},{4,68},{68... | collective-permute-start | bytes 3145736 | tf_op jit(solution)/shard_map/ppermute | solution.py:274
  122.3 19.0 %all-to-all-start.1 = ((bf16[4,1032,128]{2,1,0:T(8,128)(2,1)}), bf16[4,1032,128]{2,1,0:T(8,128)(2,1)S(1)}, u32[]{:S(2)}, u32[]{:S(2)}) async-start(bf16[4,1032,128]{2,1,0:T(8,128)(2,1)} %shard_map.100), calls=%async_computation.1 | async-start | bytes 2113536 | tf_op jit(solution)/shard_map/all_to_all | solution.py:272
  127.0 4.7 %collective-permute-start.20 = (bf16[2,512,256]{2,1,0:T(8,128)(2,1)S(1)}, bf16[2,512,256]{2,1,0:T(8,128)(2,1)S(1)}, u32[]{:S(2)}, u32[]{:S(2)}) collective-permute-start(bf16[2,512,256]{2,1,0:T(8,128)(2,1)S(1)} %get-tuple-element.64), channel_id=1, source_target_pairs={{0,64},{64,0},{1,65},{65,1},{2,66},{66,2},{3,67},{67,3},{4,68},{68... | collective-permute-start | bytes 1572872 | tf_op jit(solution)/shard_map/ppermute | solution.py:282
  129.2 2.5 %collective-permute-start.18 = (bf16[128,256]{1,0:T(8,128)(2,1)S(1)}, bf16[128,256]{1,0:T(8,128)(2,1)S(1)}, u32[]{:S(2)}, u32[]{:S(2)}) collective-permute-start(bf16[128,256]{1,0:T(8,128)(2,1)S(1)} %get-tuple-element.54), channel_id=1, source_target_pairs={{0,0},{1,1},{2,130},{3,131},{4,260},{5,261},{6,390},{7,391},{128,3... | collective-permute-start | bytes 196616 | tf_op jit(solution)/shard_map/ppermute | solution.py:273
  142.2 16.4 %all-to-all-start.2 = ((bf16[8,136,128]{2,1,0:T(8,128)(2,1)}), bf16[8,136,128]{2,1,0:T(8,128)(2,1)S(1)}, u32[]{:S(2)}, u32[]{:S(2)}) async-start(bf16[8,136,128]{2,1,0:T(8,128)(2,1)} %shard_map.102), calls=%async_computation.2 | async-start | bytes 557056 | tf_op jit(solution)/shard_map/all_to_all | solution.py:285
  148.1 9.1 %collective-permute-start.21 = (bf16[128,256]{1,0:T(8,128)(2,1)S(1)}, bf16[128,256]{1,0:T(8,128)(2,1)S(1)}, u32[]{:S(2)}, u32[]{:S(2)}) collective-permute-start(bf16[128,256]{1,0:T(8,128)(2,1)S(1)} %collective-permute-done.18), channel_id=1, source_target_pairs={{0,0},{1,1},{2,2},{3,3},{4,4},{5,5},{6,6},{7,7},{130,128},{131,129... | collective-permute-start | bytes 196616 | tf_op jit(solution)/shard_map/ppermute | solution.py:294
  159.3 5.4 %collective-permute-start.22 = (f32[8,128]{1,0:T(8,128)S(1)}, f32[8,128]{1,0:T(8,128)S(1)}, u32[]{:S(2)}, u32[]{:S(2)}) collective-permute-start(f32[8,128]{1,0:T(8,128)S(1)} %get-tuple-element.76.mine_ref), channel_id=1, source_target_pairs={{0,64},{64,0},{1,65},{65,1},{2,66},{66,2},{3,67},{67,3},{4,68},{68... | collective-permute-start | bytes 12296 | tf_op jit(solution)/shard_map/ppermute | solution.py:302

commit v6 on v1

v6 whole, which is shorter than its diff:
```python
import jax
import jax.numpy as jnp
from jax import lax
from jax.experimental import pallas as pl
from jax.experimental.pallas import tpu as pltpu
from jax.sharding import Mesh
from jax.sharding import PartitionSpec as P

F32 = jnp.float32
BF16 = jnp.bfloat16
VMEM = pl.BlockSpec(memory_space=pltpu.VMEM)
SMEM = pl.BlockSpec(memory_space=pltpu.SMEM)


def params():
    return pltpu.CompilerParams(vmem_limit_bytes=28 * 1024 * 1024)


def call(body, outs, args, flops=0, moved=0, scratch=()):
    return pl.pallas_call(
        body,
        out_shape=[jax.ShapeDtypeStruct(s, t) for s, t in outs],
        in_specs=[SMEM if a.dtype == jnp.int32 else VMEM for a in args],
        out_specs=[VMEM] * len(outs),
        scratch_shapes=list(scratch),
        compiler_params=params(),
        cost_estimate=pl.CostEstimate(flops=flops, bytes_accessed=moved, transcendentals=0),
    )(*args)


def top(values):
    return jnp.max(jnp.max(values, axis=0, keepdims=True), axis=1, keepdims=True)


def rows_of(*values):
    row = lax.broadcasted_iota(jnp.int32, (8, 128), 0)
    tile = jnp.zeros((8, 128), F32)
    for i, v in enumerate(values):
        tile = jnp.where(row == i, v, tile)
    return tile


def pack_peaks(peak_in, peak_hidden, peak_grad):
    high = peak_grad.astype(BF16).astype(F32)
    rest = peak_grad - high
    mid = rest.astype(BF16).astype(F32)
    return rows_of(peak_in, peak_hidden, high, mid, rest - mid).astype(BF16)


def unpack_peaks(packed):
    grads = packed[:, 2, :] + packed[:, 3, :] + packed[:, 4, :]
    return top(packed[:, 0, :]), top(packed[:, 1, :]), top(grads)


def scale_body(hist_ref, tok_ref, out_ref, scal_ref):
    tops = jnp.max(hist_ref[...], axis=0, keepdims=True)
    scale_in = 448.0 / tops[:, 0:1]
    scale_grad = 448.0 / tops[:, 2:3]
    tok = tok_ref[...].astype(F32)
    quant = jnp.clip(tok * scale_in, -448.0, 448.0).astype(BF16)
    part = out_ref.shape[1]
    for i in range(out_ref.shape[0]):
        out_ref[i] = quant[i % 2 * part : (i % 2 + 1) * part]
    scal_ref[...] = rows_of(scale_in, scale_grad, top(jnp.abs(tok)))


def forward_body(place_ref, x_ref, *refs):
    w_refs, (out_ref, near_ref, far_ref) = refs[:8], refs[8:]
    groups, rows = out_ref.shape[0], x_ref.shape[1]
    cols = x_ref.shape[0] // (2 * groups)
    core, turned, side = place_ref[0], place_ref[1], place_ref[3]
    for g in range(groups):
        spot = pl.ds(pl.multiple_of(lax.rem(turned + g, groups) * rows, rows), rows)
        for k in range(cols):
            lanes = slice(k * 128, (k + 1) * 128)
            near_ref[spot, lanes] = x_ref[2 * (g * cols + k) + side]
            far_ref[spot, lanes] = x_ref[2 * (g * cols + k) + 1 - side]
    near, far = near_ref[...], far_ref[...]
    for i in range(4):
        place = core if i < 2 else 1 - core
        part = jnp.dot(near, w_refs[i][...], preferred_element_type=F32)
        part = (part + jnp.dot(far, w_refs[4 + i][...], preferred_element_type=F32)).astype(BF16)
        spot = pl.ds(pl.multiple_of((2 * place + i % 2) * rows, rows), rows)
        for g in range(groups):
            out_ref[g, spot, :] = part[g * rows : (g + 1) * rows]


def middle_body(place_ref, in_ref, up_ref, up_got_ref, scal_ref, keep_ref, send_ref, q_ref):
    rows = up_ref.shape[0]
    side = place_ref[3]
    scale_in = scal_ref[0:1, 0:1]
    scale_grad = scal_ref[1:2, 0:1]
    sums = jnp.sum(in_ref[...].astype(F32), axis=0)
    peak_hidden = peak_grad = jnp.zeros((1, 1), F32)
    hiddens = []
    for place in range(2):
        base = 2 * place * rows
        gate_sum = sums[base : base + rows] / scale_in
        lift_sum = sums[base + rows : base + 2 * rows] / scale_in
        sigmoid_gate = 1.0 / (1.0 + jnp.exp(-gate_sum))
        activated = gate_sum * sigmoid_gate
        hidden = (activated * lift_sum).astype(BF16)
        hiddens.append(hidden.astype(F32))
        grad_in = jnp.where(side == place, up_ref[...].astype(F32), up_got_ref[...].astype(F32))
        grad_gate = grad_in * lift_sum * sigmoid_gate * (1.0 + gate_sum * (1.0 - sigmoid_gate))
        grad_lift = grad_in * activated
        quant_gate = jnp.clip(grad_gate * scale_grad, -448.0, 448.0).astype(BF16)
        quant_lift = jnp.clip(grad_lift * scale_grad, -448.0, 448.0).astype(BF16)
        peak_grad = jnp.maximum(peak_grad, jnp.maximum(top(jnp.abs(grad_gate)), top(jnp.abs(grad_lift))))
        peak_hidden = jnp.maximum(peak_hidden, top(jnp.abs(hiddens[-1])))
        for i in range(q_ref.shape[0]):
            q_ref[i, base : base + rows, :] = quant_gate
            q_ref[i, base + rows : base + 2 * rows, :] = quant_lift
    keep_ref[...] = jnp.where(side == 0, hiddens[0], hiddens[1]).astype(BF16)
    send_ref[...] = jnp.where(side == 0, hiddens[1], hiddens[0]).astype(BF16)
    peaks = pack_peaks(scal_ref[2:3, 0:1], peak_hidden, peak_grad)
    wide = jnp.concatenate([peaks, peaks], axis=1)
    for i in range(q_ref.shape[0]):
        q_ref[i, 4 * rows :, :] = wide


def pick(place_ref, q_ref, kept_ref):
    rows = (q_ref.shape[1] - 8) // 4
    for i in range(4):
        place = place_ref[0] if i < 2 else 1 - place_ref[0]
        spot = pl.ds(pl.multiple_of((2 * place + i % 2) * rows, rows), rows)
        for g in range(q_ref.shape[0]):
            kept_ref[i, g * rows : (g + 1) * rows, :] = q_ref[g, spot, :]


def backward_body(place_ref, q_ref, *refs):
    w_refs, (out_ref, kept_ref) = refs[:8], refs[8:]
    groups, rows = q_ref.shape[0], (q_ref.shape[1] - 8) // 4
    cols = out_ref.shape[0]
    fine = (out_ref.shape[1] - 8) // (2 * groups * rows)
    turned, side = place_ref[1], place_ref[3]
    contract = (((1,), (1,)), ((), ()))
    pick(place_ref, q_ref, kept_ref)
    packed = pack_peaks(*unpack_peaks(q_ref[:, 4 * rows :, 0:128].astype(F32)))
    for away in range(2):
        total = None
        for i in range(4):
            part = lax.dot_general(kept_ref[i], w_refs[4 * away + i][...], contract, preferred_element_type=F32)
            total = part if total is None else total + part
        target = side if away == 0 else 1 - side
        for k in range(cols):
            for g in range(groups):
                first = lax.rem(groups + g - turned, groups) * fine
                for j in range(fine):
                    lane = (k * fine + j) * 128
                    spot = pl.ds(pl.multiple_of((2 * (first + j) + target) * rows, rows), rows)
                    out_ref[k, spot, :] = total[g * rows : (g + 1) * rows, lane : lane + 128].astype(BF16)
    for k in range(cols):
        out_ref[k, 2 * groups * fine * rows :, :] = packed


def pick_body(place_ref, q_ref, mine_ref, other_ref, kept_ref):
    pick(place_ref, q_ref, kept_ref)
    mine_ref[...] = kept_ref[0:2]
    other_ref[...] = kept_ref[2:4]


def column_body(in_ref, out_ref):
    blocks, rows = out_ref.shape[0], out_ref.shape[1] - 8
    packed = pack_peaks(*unpack_peaks(in_ref[:, blocks * rows :, :].astype(F32)))
    for i in range(blocks):
        part = jnp.sum(in_ref[:, i * rows : (i + 1) * rows, :].astype(F32), axis=0)
        out_ref[i, :rows, :] = part.astype(BF16)
        out_ref[i, rows:, :] = packed


def last_body(in_ref, scal_ref, hidden_ref, out_ref, peaks_ref, hidden_out_ref):
    rows = in_ref.shape[1] - 8
    for side in range(2):
        total = in_ref[side, :rows, :].astype(F32)
        for i in range(1, in_ref.shape[0] // 2):
            total = total + in_ref[2 * i + side, :rows, :].astype(F32)
        out_ref[side * rows : (side + 1) * rows, :] = (total / scal_ref[1:2, 0:1]).astype(BF16)
    peaks_ref[...] = rows_of(*unpack_peaks(in_ref[:, rows:, :].astype(F32)))
    hidden_out_ref[...] = hidden_ref[...]


def history_body(hist_ref, mine_ref, other_ref, out_ref):
    peaks = jnp.maximum(mine_ref[...], other_ref[...])
    col = lax.broadcasted_iota(jnp.int32, (1, 3), 1)
    row = jnp.where(col == 0, peaks[0:1, 0:1], jnp.where(col == 1, peaks[1:2, 0:1], peaks[2:3, 0:1]))
    past = hist_ref.shape[0] - 1
    out_ref[0:past, :] = hist_ref[1:, :]
    out_ref[past:, :] = row


def per_device(sizes, tokens, w_gate, w_up, upstream, history):
    nh, nx, nw, np = (sizes[a] for a in "hxwp")
    plane, last_stage, column_axis = ("h", "x", "w", "t"), ("h", "w", "t"), ("h", "p", "t")
    rows, width = tokens.shape
    rows = rows // 2
    depth, units = w_gate.shape
    swap = [(0, 1), (1, 0)]
    spots = [(h, a, b) for h in range(nh) for a in range(np) for b in range(2)]
    at = lambda h, a, b: (h * np + a % np) * 2 + b
    along_y = [(at(h, a, b), at(h, a + h, b)) for h, a, b in spots]
    along_z = [(at(h, a, b), at((a - h) % nh, a, b)) for h, a, b in spots]
    back_y = [(j, i) for i, j in along_y]
    side = lax.axis_index("t")
    place = jnp.stack([lax.axis_index("c"), lax.axis_index("h"), lax.axis_index("p"), side])

    copies, scal = call(scale_body, [((2 * nh * nx * nw, rows, width), BF16), ((8, 128), F32)], (history, tokens))
    x_all = lax.all_to_all(copies, plane, 0, 0, tiled=True)
    near = [w_gate, w_up]
    far = [lax.ppermute(w, "t", swap) for w in near]
    near += [lax.ppermute(w, "c", swap) for w in near]
    far += [lax.ppermute(w, "c", swap) for w in far]
    up = lax.ppermute(upstream, column_axis, along_y)
    up = lax.ppermute(up, column_axis, along_z).reshape(2, rows, units)
    up_got = lax.ppermute(lax.dynamic_index_in_dim(up, 1 - side, 0, keepdims=False), "t", swap)
    up = lax.dynamic_index_in_dim(up, side, 0, keepdims=False)
    x_all, up, up_got, *weights = lax.optimization_barrier((x_all, up, up_got, *near, *far))

    work = 16 * nh * rows * depth * units * 2
    parts, x_near, x_far = call(
        forward_body,
        [((np, 4 * rows, units), BF16), ((nh * rows, depth), BF16), ((nh * rows, depth), BF16)],
        (place, x_all, *weights),
        flops=work,
        moved=8 * 2**20,
    )
    sums = lax.all_to_all(parts, "p", 0, 0, tiled=True)
    keep, send, quants = call(
        middle_body,
        [((rows, units), BF16), ((rows, units), BF16), ((np, 4 * rows + 8, units), BF16)],
        (place, sums, up, up_got, scal),
        moved=2**20,
    )
    q_all = lax.all_to_all(quants, "p", 0, 0, tiled=True)
    (back,) = call(
        backward_body,
        [((nx, 2 * nh * nw * rows + 8, width), BF16)],
        (place, q_all, *weights),
        flops=work,
        moved=8 * 2**20,
        scratch=[pltpu.VMEM((4, nh * rows, units), BF16)],
    )
    q_all, back, keep, send, x_near, x_far = lax.optimization_barrier((q_all, back, keep, send, x_near, x_far))
    back_cols = lax.all_to_all(back, "x", 0, 0, tiled=True)
    x_side = lax.ppermute(x_far, "t", swap)
    q_mine, q_send = call(
        pick_body,
        [((2, nh * rows, units), BF16)] * 2,
        (place, q_all),
        moved=2**21,
        scratch=[pltpu.VMEM((4, nh * rows, units), BF16)],
    )
    got = lax.ppermute(send, "t", swap)
    hidden = jnp.where(side == 0, jnp.concatenate([keep, got]), jnp.concatenate([got, keep]))
    hidden = lax.ppermute(hidden, column_axis, along_z)
    q_side = lax.ppermute(q_mine, "t", swap)
    q_send_side = lax.ppermute(q_send, "t", swap)
    x_other = lax.ppermute(x_near, "c", swap)
    q_other = lax.ppermute(q_send, "c", swap)
    back_cols, hidden, x_near, x_side, x_other, q_mine, q_side, q_other, q_send_side = lax.optimization_barrier(
        (back_cols, hidden, x_near, x_side, x_other, q_mine, q_side, q_other, q_send_side)
    )
    (column,) = call(column_body, [((2 * nh * nw, rows + 8, width), BF16)], (back_cols,), moved=2**20)
    back_all = lax.all_to_all(column, last_stage, 0, 0, tiled=True)
    hidden = lax.ppermute(hidden, column_axis, back_y)
    xs = [x_near, x_side, x_other, lax.ppermute(x_side, "c", swap)]
    qs = [q_mine, q_side, q_other, lax.ppermute(q_send_side, "c", swap)]
    divisor = scal[0, 0] * scal[1, 0] * (4 * nh * rows)
    contract = (((0,), (0,)), ((), ()))
    grads = []
    for i in range(2):
        total = sum(lax.dot_general(x, q[i], contract, preferred_element_type=F32) for x, q in zip(xs, qs))
        grads.append((total / divisor).astype(BF16))
    back_all, hidden, *grads = lax.optimization_barrier((back_all, hidden, *grads))
    input_grad, peaks, hidden = call(
        last_body,
        [((2 * rows, width), BF16), ((8, 128), F32), ((2 * rows, units), BF16)],
        (back_all, scal, hidden),
        moved=2**20,
    )
    peaks_other = lax.ppermute(peaks, "c", swap)
    (new_history,) = call(history_body, [(history.shape, F32)], (history, peaks, peaks_other))
    return (hidden, input_grad, grads[0], grads[1], new_history)


def solution(mesh):
    sizes = dict(h=mesh.shape["row"] // 2, c=2, x=mesh.shape["col"] // 2, w=2, p=mesh.shape["dep"] // 2, t=2)
    fine = Mesh(mesh.devices.reshape(tuple(sizes.values())), tuple(sizes))
    row, col, dep = ("h", "c"), ("x", "w"), ("p", "t")
    placed = (P(row, dep + col), P(dep, col + row), P(dep, col + row), P(row, col + dep), P())

    def step(*args):
        return per_device(sizes, *args)

    return jax.shard_map(
        step,
        mesh=fine,
        in_specs=placed,
        out_specs=(P(row, col + dep), P(row, dep + col), P(dep, col + row), P(dep, col + row), P()),
        check_vma=False,
    )
```

time: 167 us -> 200 us (1.20); the launches traced: 165 us -> 196 us
  waiting for transfers between devices: 63.2 us -> 29.6 us
  starting transfers between devices: 50.4 us -> 81.9 us
  blocking collectives: 29.5 us -> 53.1 us
  matrix products: 4.51 us -> 10.6 us
  Pallas kernels: 6.98 us -> 11.3 us
    all_to_all x2, waiting for transfers between devices: 42.6 us -> 0.01 us  [the longest x1 0.01 us: per_device(): back_cols = lax.all_to_all(back, 'x', 0, 0, tiled=True)]
    ppermute x5 -> x18, starting transfers between devices: 11.1 us -> 45.6 us  [the longest x2 8.99 us: per_device(): far += [lax.ppermute(w, 'c', swap) for w in far]]
    ppermute x5 -> x18, waiting for transfers between devices: 1.08 us -> 28.7 us  [the longest x2 18 us: per_device(): far = [lax.ppermute(w, 't', swap) for w in near]]
    all_to_all x1 -> x2, blocking collectives: 29.5 us -> 53.1 us  [the longest x1 35.6 us: per_device(): sums = lax.all_to_all(parts, 'p', 0, 0, tiled=True)]
    all_to_all x1, waiting for transfers between devices: 19.4 us -> 0.01 us  [per_device(): x_all = lax.all_to_all(copies, plane, 0, 0, tiled=True)]
    dot_general x4 -> x8, matrix products: 4.51 us -> 10.6 us  [per_device(): lax.dot_general(x, q[i], contract, preferred_element_type=F32)]
    pallas_call x6 -> x8, Pallas kernels: 6.98 us -> 11.3 us  [call(): pl.pallas_call(body, out_shape=[jax.ShapeDtypeStruct(s, t) for s, t in ou...]
    all_to_all x2, starting transfers between devices: 18.2 us -> 14 us  [the longest x1 9.39 us: per_device(): back_all = lax.all_to_all(column, last_stage, 0, 0, tiled=True)]
  transfers between devices with their start and end apart: 10 -> 23, of which waited for: 4 -> 6; matrix products, arithmetic and copies ran while one was open for 3% -> 3% of each run, Pallas kernels for 0% -> 0%
where the time goes in v6:
time: 200 us; the launch traced here: 196 us
  starting transfers between devices  81.9 us (41%)
  blocking collectives  53.1 us (27%)
  waiting for transfers between devices  29.6 us (15%)
  Pallas kernels  11.3 us (6%)
  matrix products  10.6 us (5%)
  local copies, waits for them, and re-layouts  7.03 us (4%)
  between operations  2.33 us (1%)
    all_to_all x1, blocking collectives, per_device(): sums = lax.all_to_all(parts, 'p', 0, 0, tiled=True)  35.6 us
    ppermute x2, waiting for transfers between devices, per_device(): far = [lax.ppermute(w, 't', swap) for w in near]  18 us
    all_to_all x1, blocking collectives, per_device(): q_all = lax.all_to_all(quants, 'p', 0, 0, tiled=True)  17.4 us
    all_to_all x1, starting transfers between devices, per_device(): x_all = lax.all_to_all(copies, plane, 0, 0, tiled=True)  15.5 us
    pallas_call x8, Pallas kernels, call(): pl.pallas_call(body, out_shape=[jax.ShapeDtypeStruct(s, t) for s, t in ou...  11.3 us
    dot_general x8, matrix products, per_device(): lax.dot_general(x, q[i], contract, preferred_element_type=F32)  10.6 us
    all_to_all x1, starting transfers between devices, per_device(): back_all = lax.all_to_all(column, last_stage, 0, 0, tiled=True)  9.39 us
    ppermute x2, starting transfers between devices, per_device(): far += [lax.ppermute(w, 'c', swap) for w in far]  8.99 us
  transfers between devices with their start and end apart: 23, of which 6 were waited for; matrix products, arithmetic and copies ran while one was open for 3% of the time, Pallas kernels for 0%

profile of v6, /device:TPU:1, one launch (start us, length us, event | category | flops | bytes accessed | tf_op | source)
XLA Modules:
  0.0 195.8 jit_solution(8804784950376742946)
XLA Ops:
  0.6 0.8 copy.10.hist_ref
  1.4 0.8 copy-done
  2.1 1.2 shard_map.92
  3.3 15.5 %all-to-all-start = ((bf16[64,64,128]{2,1,0:T(8,128)(2,1)}), bf16[64,64,128]{2,1,0:T(8,128)(2,1)S(1)}, u32[]{:S(2)}, u32[]{:S(2)}) async-start(bf16[64,64,128]{2,1,0:T(8,128)(2,1)} %get-tuple-element.48), calls=%async_computation | async-start | bytes 2097152 | tf_op jit(solution)/shard_map/all_to_all | solution.py:208
  18.8 2.9 %collective-permute-start.5 = (bf16[1024,256]{1,0:T(8,128)(2,1)S(1)}, bf16[1024,256]{1,0:T(8,128)(2,1)S(1)}, u32[]{:S(2)}, u32[]{:S(2)}) collective-permute-start(bf16[1024,256]{1,0:T(8,128)(2,1)S(1)} %copy-done.1), channel_id=1, source_target_pairs={{0,1},{1,0},{2,3},{3,2},{4,5},{5,4},{6,7},{7,6},{8,9},{9,8},{10,11... | collective-permute-start | bytes 1572872 | tf_op jit(solution)/shard_map/ppermute | solution.py:210
  21.7 2.4 %collective-permute-start.6 = (bf16[1024,256]{1,0:T(8,128)(2,1)S(1)}, bf16[1024,256]{1,0:T(8,128)(2,1)}, u32[]{:S(2)}, u32[]{:S(2)}) collective-permute-start(bf16[1024,256]{1,0:T(8,128)(2,1)S(1)} %copy-done.2), channel_id=1, source_target_pairs={{0,1},{1,0},{2,3},{3,2},{4,5},{5,4},{6,7},{7,6},{8,9},{9,8},{10,11... | collective-permute-start | bytes 1572872 | tf_op jit(solution)/shard_map/ppermute | solution.py:210
  24.1 3.4 %collective-permute-start.3 = (bf16[1024,256]{1,0:T(8,128)(2,1)S(1)}, bf16[1024,256]{1,0:T(8,128)(2,1)}, u32[]{:S(2)}, u32[]{:S(2)}) collective-permute-start(bf16[1024,256]{1,0:T(8,128)(2,1)S(1)} %copy-done.1), channel_id=1, source_target_pairs={{0,64},{64,0},{1,65},{65,1},{2,66},{66,2},{3,67},{67,3},{4,68},{68... | collective-permute-start | bytes 1572872 | tf_op jit(solution)/shard_map/ppermute | solution.py:211
  27.6 1.9 collective-permute-start.4
  29.5 12.7 %collective-permute-done.5.refs_4_ = bf16[1024,256]{1,0:T(8,128)(2,1)S(1)} collective-permute-done((bf16[1024,256]{1,0:T(8,128)(2,1)S(1)}, bf16[1024,256]{1,0:T(8,128)(2,1)S(1)}, u32[]{:S(2)}, u32[]{:S(2)}) %collective-permute-start.5) | collective-permute-done | bytes 524320 | tf_op jit(solution)/shard_map/ppermute | solution.py:210
  42.2 5.2 %collective-permute-start.7 = (bf16[1024,256]{1,0:T(8,128)(2,1)S(1)}, bf16[1024,256]{1,0:T(8,128)(2,1)}, u32[]{:S(2)}, u32[]{:S(2)}) collective-permute-start(bf16[1024,256]{1,0:T(8,128)(2,1)S(1)} %collective-permute-done.5.refs_4_), channel_id=1, source_target_pairs={{0,64},{64,0},{1,65},{65,1},{2,66},{66,2},{3,67},{67,3},{4,68},{68... | collective-permute-start | bytes 1572872 | tf_op jit(solution)/shard_map/ppermute | solution.py:212
  47.4 0.0 copy-start.3
  47.4 0.8 copy-done.3
  48.2 5.3 %collective-permute-done.6.refs_5_ = bf16[1024,256]{1,0:T(8,128)(2,1)} collective-permute-done((bf16[1024,256]{1,0:T(8,128)(2,1)S(1)}, bf16[1024,256]{1,0:T(8,128)(2,1)}, u32[]{:S(2)}, u32[]{:S(2)}) %collective-permute-start.6) | collective-permute-done | bytes 524320 | tf_op jit(solution)/shard_map/ppermute | solution.py:210
  53.5 3.8 %collective-permute-start.8 = (bf16[1024,256]{1,0:T(8,128)(2,1)}, bf16[1024,256]{1,0:T(8,128)(2,1)}, u32[]{:S(2)}, u32[]{:S(2)}) collective-permute-start(bf16[1024,256]{1,0:T(8,128)(2,1)} %collective-permute-done.6.refs_5_), channel_id=1, source_target_pairs={{0,64},{64,0},{1,65},{65,1},{2,66},{66,2},{3,67},{67,3},{4,68},{68... | collective-permute-start | bytes 1572872 | tf_op jit(solution)/shard_map/ppermute | solution.py:212
  57.3 0.7 collective-permute-start
  58.0 0.7 collective-permute-start.1
  58.6 0.0 collective-permute-done.1
  58.7 2.0 %collective-permute-start.2 = (bf16[64,256]{1,0:T(8,128)(2,1)S(1)}, bf16[64,256]{1,0:T(8,128)(2,1)S(1)}, u32[]{:S(2)}, u32[]{:S(2)}) collective-permute-start(bf16[64,256]{1,0:T(8,128)(2,1)S(1)} %get-tuple-element.96), channel_id=1, source_target_pairs={{0,1},{1,0},{2,3},{3,2},{4,5},{5,4},{6,7},{7,6},{8,9},{9,8},{10,11... | collective-permute-start | bytes 98312 | tf_op jit(solution)/shard_map/ppermute | solution.py:215
  60.7 0.1 pad_add_fusion.place_ref
  60.7 2.6 %collective-permute-done.2.up_got_ref = bf16[64,256]{1,0:T(8,128)(2,1)S(1)} collective-permute-done((bf16[64,256]{1,0:T(8,128)(2,1)S(1)}, bf16[64,256]{1,0:T(8,128)(2,1)S(1)}, u32[]{:S(2)}, u32[]{:S(2)}) %collective-permute-start.2) | collective-permute-done | bytes 32800 | tf_op jit(solution)/shard_map/ppermute | solution.py:215
  63.3 0.0 collective-permute-done.8.refs_7_
  63.4 0.0 copy-start.4
  63.4 1.0 copy-done.4
  64.4 3.1 %shard_map.93 = (bf16[4,256,256]{2,1,0:T(8,128)(2,1)S(1)}, bf16[256,1024]{1,0:T(8,128)(2,1)S(1)}, bf16[256,1024]{1,0:T(8,128)(2,1)S(1)}) custom-call(s32[4]{0:T(128)S(1)} %pad_add_fusion.place_ref, bf16[64,64,128]{2,1,0:T(8,128)(2,1)S(1)} %all-to-all-done.x_ref, bf16[1024,256]{1,0:T(8,128)(2,1)S(1)} %copy-done.1, bf16[1024,256]{1,0:T(8,128)(2,1)S(1)} %copy-done.2, ...), custom_call_target="tpu_custom_call" | custom-call | flops 2147483648 | bytes 8388608 | tf_op jit(solution)/shard_map/pallas_call | solution.py:20
  67.5 0.0 copy-start.6
  67.5 0.8 copy-done.6
  68.3 35.6 %all_to_all.25.in_ref = bf16[4,256,256]{2,1,0:T(8,128)(2,1)S(1)} all-to-all(bf16[4,256,256]{2,1,0:T(8,128)(2,1)S(1)} %get-tuple-element.58), channel_id=1, replica_groups=mesh['h'=4,'c'=2,'x'=4,'w'=2,'p'=4,'t'=2] {'p'}, dimensions={0} | all-to-all | bytes 1048576 | tf_op jit(solution)/shard_map/all_to_all | solution.py:227
  103.9 0.8 shard_map.94
  104.8 17.4 %all_to_all.26.q_ref = bf16[4,264,256]{2,1,0:T(8,128)(2,1)S(1)} all-to-all(bf16[4,264,256]{2,1,0:T(8,128)(2,1)S(1)} %get-tuple-element.62), channel_id=1, replica_groups=mesh['h'=4,'c'=2,'x'=4,'w'=2,'p'=4,'t'=2] {'p'}, dimensions={0} | all-to-all | bytes 1081344 | tf_op jit(solution)/shard_map/all_to_all | solution.py:234
  122.2 4.0 %shard_map.95 = bf16[4,1032,128]{2,1,0:T(8,128)(2,1)} custom-call(s32[4]{0:T(128)S(1)} %pad_add_fusion.place_ref, bf16[4,264,256]{2,1,0:T(8,128)(2,1)S(1)} %all_to_all.26.q_ref, bf16[1024,256]{1,0:T(8,128)(2,1)S(1)} %copy-done.1, bf16[1024,256]{1,0:T(8,128)(2,1)S(1)} %copy-done.2, bf16[1024,256]{1,0:T(8,128)(2,1)} %collective-permute-done.3.refs_2_, ...), custom_call_target="tpu_custom_call" | custom-call | flops 2147483648 | bytes 8388608 | tf_op jit(solution)/shard_map/pallas_call | solution.py:20
  126.2 4.6 %all-to-all-start.3 = ((bf16[4,1032,128]{2,1,0:T(8,128)(2,1)}), bf16[4,1032,128]{2,1,0:T(8,128)(2,1)S(1)}, u32[]{:S(2)}, u32[]{:S(2)}) async-start(bf16[4,1032,128]{2,1,0:T(8,128)(2,1)} %shard_map.95), calls=%async_computation.3 | async-start | bytes 2113536 | tf_op jit(solution)/shard_map/all_to_all | solution.py:244
  130.8 1.9 collective-permute-start.11
  132.7 7.3 %collective-permute-start.12 = (bf16[256,1024]{1,0:T(8,128)(2,1)S(1)}, bf16[256,1024]{1,0:T(8,128)(2,1)}, u32[]{:S(2)}, u32[]{:S(2)}) collective-permute-start(bf16[256,1024]{1,0:T(8,128)(2,1)S(1)} %get-tuple-element.77), channel_id=1, source_target_pairs={{0,64},{64,0},{1,65},{65,1},{2,66},{66,2},{3,67},{67,3},{4,68},{68... | collective-permute-start | bytes 1572872 | tf_op jit(solution)/shard_map/ppermute | solution.py:258
  140.0 1.9 collective-permute-start.9
  142.0 3.5 %collective-permute-done.9 = bf16[64,256]{1,0:T(8,128)(2,1)S(1)} collective-permute-done((bf16[64,256]{1,0:T(8,128)(2,1)S(1)}, bf16[64,256]{1,0:T(8,128)(2,1)S(1)}, u32[]{:S(2)}, u32[]{:S(2)}) %collective-permute-start.9) | collective-permute-done | bytes 32800 | tf_op jit(solution)/shard_map/ppermute | solution.py:253
  145.5 0.7 collective-permute-start.10
  146.2 0.6 shard_map.96
  146.8 1.9 collective-permute-start.13
  148.7 4.4 %collective-permute-start.14 = (bf16[2,256,256]{2,1,0:T(8,128)(2,1)S(1)}, bf16[2,256,256]{2,1,0:T(8,128)(2,1)S(1)}, u32[]{:S(2)}, u32[]{:S(2)}) collective-permute-start(bf16[2,256,256]{2,1,0:T(8,128)(2,1)S(1)} %get-tuple-element.74), channel_id=1, source_target_pairs={{0,64},{64,0},{1,65},{65,1},{2,66},{66,2},{3,67},{67,3},{4,68},{68... | collective-permute-start | bytes 786440 | tf_op jit(solution)/shard_map/ppermute | solution.py:259
  153.2 0.0 collective-permute-done.10
  153.2 3.4 %collective-permute-start.15 = (bf16[2,256,256]{2,1,0:T(8,128)(2,1)S(1)}, bf16[2,256,256]{2,1,0:T(8,128)(2,1)S(1)}, u32[]{:S(2)}, u32[]{:S(2)}) collective-permute-start(bf16[2,256,256]{2,1,0:T(8,128)(2,1)S(1)} %get-tuple-element.74), channel_id=1, source_target_pairs={{0,1},{1,0},{2,3},{3,2},{4,5},{5,4},{6,7},{7,6},{8,9},{9,8},{10,11... | collective-permute-start | bytes 786440 | tf_op jit(solution)/shard_map/ppermute | solution.py:257
  156.5 0.5 fusion.26
  158.4 0.0 collective-permute-done.14
  158.4 4.6 %collective-permute-done.15 = bf16[2,256,256]{2,1,0:T(8,128)(2,1)S(1)} collective-permute-done((bf16[2,256,256]{2,1,0:T(8,128)(2,1)S(1)}, bf16[2,256,256]{2,1,0:T(8,128)(2,1)S(1)}, u32[]{:S(2)}, u32[]{:S(2)}) %collective-permute-start.15) | collective-permute-done | bytes 262176 | tf_op jit(solution)/shard_map/ppermute | solution.py:257
  163.0 2.4 %fusion.15 = f32[1024,256]{1,0:T(8,128)} fusion(bf16[256,1024]{1,0:T(8,128)(2,1)} %collective-permute-done.12, bf16[2,256,256]{2,1,0:T(8,128)(2,1)S(1)} %collective-permute-done.14), kind=kOutput, calls=%fused_computation.19 | convolution fusion | flops 134217728 | bytes 1703936 | tf_op jit(solution)/shard_map/dot_general | solution.py:272
  165.4 2.4 %fusion.10 = f32[1024,256]{1,0:T(8,128)} fusion(bf16[256,1024]{1,0:T(8,128)(2,1)} %collective-permute-done.12, bf16[2,256,256]{2,1,0:T(8,128)(2,1)S(1)} %collective-permute-done.14), kind=kOutput, calls=%fused_computation.14 | convolution fusion | flops 134217728 | bytes 1703936 | tf_op jit(solution)/shard_map/dot_general | solution.py:272
  167.8 0.9 shard_map.97
  168.6 9.4 %all-to-all-start.4 = ((bf16[16,72,128]{2,1,0:T(8,128)(2,1)}), bf16[16,72,128]{2,1,0:T(8,128)(2,1)S(1)}, u32[]{:S(2)}, u32[]{:S(2)}) async-start(bf16[16,72,128]{2,1,0:T(8,128)(2,1)} %shard_map.97), calls=%async_computation.4 | async-start | bytes 589824 | tf_op jit(solution)/shard_map/all_to_all | solution.py:264
  178.0 0.7 collective-permute-start.16
  178.7 3.0 %collective-permute-start.17 = (bf16[256,1024]{1,0:T(8,128)(2,1)}, bf16[256,1024]{1,0:T(8,128)(2,1)S(1)}, u32[]{:S(2)}, u32[]{:S(2)}) collective-permute-start(bf16[256,1024]{1,0:T(8,128)(2,1)} %collective-permute-done.11), channel_id=1, source_target_pairs={{0,64},{64,0},{1,65},{65,1},{2,66},{66,2},{3,67},{67,3},{4,68},{68... | collective-permute-start | bytes 1572872 | tf_op jit(solution)/shard_map/ppermute | solution.py:266
  181.7 1.9 collective-permute-start.18
  183.6 1.4 fusion.17
  185.0 1.4 fusion.12
  186.5 0.4 fusion.9
  186.8 0.8 copy-done.9
  187.7 1.2 fusion.6
  188.8 0.4 fusion.8
  189.2 0.9 copy-done.8
  190.0 1.2 fusion.7
  191.2 0.7 shard_map.98
  191.9 2.4 %collective-permute-start.19 = (f32[8,128]{1,0:T(8,128)S(1)}, f32[8,128]{1,0:T(8,128)S(1)}, u32[]{:S(2)}, u32[]{:S(2)}) collective-permute-start(f32[8,128]{1,0:T(8,128)S(1)} %get-tuple-element.90.mine_ref), channel_id=1, source_target_pairs={{0,64},{64,0},{1,65},{65,1},{2,66},{66,2},{3,67},{67,3},{4,68},{68... | collective-permute-start | bytes 12296 | tf_op jit(solution)/shard_map/ppermute | solution.py:281
  194.3 0.8 collective-permute-done.19.other_ref
  195.1 0.1 shard_map.99
  195.2 0.7 copy.12
  (28 shorter events, 0.1 us)
Async XLA Ops:
  1.4 0.8 copy-start
  3.3 15.5 %copy-start.1 = (bf16[1024,256]{1,0:T(8,128)(2,1)S(1)}, bf16[1024,256]{1,0:T(8,128)(2,1)}, u32[]{:S(2)}) copy-start(bf16[1024,256]{1,0:T(8,128)(2,1)} %refs_0_.1) | copy-start | bytes 1572868
  3.3 18.4 %copy-start.2 = (bf16[1024,256]{1,0:T(8,128)(2,1)S(1)}, bf16[1024,256]{1,0:T(8,128)(2,1)}, u32[]{:S(2)}) copy-start(bf16[1024,256]{1,0:T(8,128)(2,1)} %refs_1_.1) | copy-start | bytes 1572868
  3.3 54.0 %copy-start.10 = (bf16[128,256]{1,0:T(8,128)(2,1)S(1)}, bf16[128,256]{1,0:T(8,128)(2,1)}, u32[]{:S(2)}) copy-start(bf16[128,256]{1,0:T(8,128)(2,1)} %param.8) | copy-start | bytes 196612
  3.3 60.0 %all-to-all-start = ((bf16[64,64,128]{2,1,0:T(8,128)(2,1)}), bf16[64,64,128]{2,1,0:T(8,128)(2,1)S(1)}, u32[]{:S(2)}, u32[]{:S(2)}) async-start(bf16[64,64,128]{2,1,0:T(8,128)(2,1)} %get-tuple-element.48), calls=%async_computation | async-start | bytes 2097152 | tf_op jit(solution)/shard_map/all_to_all | solution.py:208
  18.8 23.3 %collective-permute-start.5 = (bf16[1024,256]{1,0:T(8,128)(2,1)S(1)}, bf16[1024,256]{1,0:T(8,128)(2,1)S(1)}, u32[]{:S(2)}, u32[]{:S(2)}) collective-permute-start(bf16[1024,256]{1,0:T(8,128)(2,1)S(1)} %copy-done.1), channel_id=1, source_target_pairs={{0,1},{1,0},{2,3},{3,2},{4,5},{5,4},{6,7},{7,6},{8,9},{9,8},{10,11... | collective-permute-start | bytes 1572872 | tf_op jit(solution)/shard_map/ppermute | solution.py:210
  21.7 31.7 %collective-permute-start.6 = (bf16[1024,256]{1,0:T(8,128)(2,1)S(1)}, bf16[1024,256]{1,0:T(8,128)(2,1)}, u32[]{:S(2)}, u32[]{:S(2)}) collective-permute-start(bf16[1024,256]{1,0:T(8,128)(2,1)S(1)} %copy-done.2), channel_id=1, source_target_pairs={{0,1},{1,0},{2,3},{3,2},{4,5},{5,4},{6,7},{7,6},{8,9},{9,8},{10,11... | collective-permute-start | bytes 1572872 | tf_op jit(solution)/shard_map/ppermute | solution.py:210
  24.1 39.2 %collective-permute-start.3 = (bf16[1024,256]{1,0:T(8,128)(2,1)S(1)}, bf16[1024,256]{1,0:T(8,128)(2,1)}, u32[]{:S(2)}, u32[]{:S(2)}) collective-permute-start(bf16[1024,256]{1,0:T(8,128)(2,1)S(1)} %copy-done.1), channel_id=1, source_target_pairs={{0,64},{64,0},{1,65},{65,1},{2,66},{66,2},{3,67},{67,3},{4,68},{68... | collective-permute-start | bytes 1572872 | tf_op jit(solution)/shard_map/ppermute | solution.py:211
  27.6 35.8 %collective-permute-start.4 = (bf16[1024,256]{1,0:T(8,128)(2,1)S(1)}, bf16[1024,256]{1,0:T(8,128)(2,1)}, u32[]{:S(2)}, u32[]{:S(2)}) collective-permute-start(bf16[1024,256]{1,0:T(8,128)(2,1)S(1)} %copy-done.2), channel_id=1, source_target_pairs={{0,64},{64,0},{1,65},{65,1},{2,66},{66,2},{3,67},{67,3},{4,68},{68... | collective-permute-start | bytes 1572872 | tf_op jit(solution)/shard_map/ppermute | solution.py:211
  42.2 21.2 %collective-permute-start.7 = (bf16[1024,256]{1,0:T(8,128)(2,1)S(1)}, bf16[1024,256]{1,0:T(8,128)(2,1)}, u32[]{:S(2)}, u32[]{:S(2)}) collective-permute-start(bf16[1024,256]{1,0:T(8,128)(2,1)S(1)} %collective-permute-done.5.refs_4_), channel_id=1, source_target_pairs={{0,64},{64,0},{1,65},{65,1},{2,66},{66,2},{3,67},{67,3},{4,68},{68... | collective-permute-start | bytes 1572872 | tf_op jit(solution)/shard_map/ppermute | solution.py:212
  47.4 0.8 copy-start.3
  53.5 9.9 %collective-permute-start.8 = (bf16[1024,256]{1,0:T(8,128)(2,1)}, bf16[1024,256]{1,0:T(8,128)(2,1)}, u32[]{:S(2)}, u32[]{:S(2)}) collective-permute-start(bf16[1024,256]{1,0:T(8,128)(2,1)} %collective-permute-done.6.refs_5_), channel_id=1, source_target_pairs={{0,64},{64,0},{1,65},{65,1},{2,66},{66,2},{3,67},{67,3},{4,68},{68... | collective-permute-start | bytes 1572872 | tf_op jit(solution)/shard_map/ppermute | solution.py:212
  57.3 0.7 collective-permute-start
  58.0 0.7 collective-permute-start.1
  58.7 4.7 %collective-permute-start.2 = (bf16[64,256]{1,0:T(8,128)(2,1)S(1)}, bf16[64,256]{1,0:T(8,128)(2,1)S(1)}, u32[]{:S(2)}, u32[]{:S(2)}) collective-permute-start(bf16[64,256]{1,0:T(8,128)(2,1)S(1)} %get-tuple-element.96), channel_id=1, source_target_pairs={{0,1},{1,0},{2,3},{3,2},{4,5},{5,4},{6,7},{7,6},{8,9},{9,8},{10,11... | collective-permute-start | bytes 98312 | tf_op jit(solution)/shard_map/ppermute | solution.py:215
  63.4 1.0 copy-start.4
  67.5 0.8 copy-start.6
  103.9 18.3 %copy-start.5 = (bf16[1024,256]{1,0:T(8,128)(2,1)S(1)}, bf16[1024,256]{1,0:T(8,128)(2,1)}, u32[]{:S(2)}) copy-start(bf16[1024,256]{1,0:T(8,128)(2,1)} %copy-done.3) | copy-start | bytes 1572868
  126.2 4.6 %copy-start.7 = (bf16[256,1024]{1,0:T(8,128)(2,1)S(1)}, bf16[256,1024]{1,0:T(8,128)(2,1)}, u32[]{:S(2)}) copy-start(bf16[256,1024]{1,0:T(8,128)(2,1)} %copy-done.6) | copy-start | bytes 1572868
  126.2 36.8 %all-to-all-start.3 = ((bf16[4,1032,128]{2,1,0:T(8,128)(2,1)}), bf16[4,1032,128]{2,1,0:T(8,128)(2,1)S(1)}, u32[]{:S(2)}, u32[]{:S(2)}) async-start(bf16[4,1032,128]{2,1,0:T(8,128)(2,1)} %shard_map.95), calls=%async_computation.3 | async-start | bytes 2113536 | tf_op jit(solution)/shard_map/all_to_all | solution.py:244
  130.8 32.2 %collective-permute-start.11 = (bf16[256,1024]{1,0:T(8,128)(2,1)S(1)}, bf16[256,1024]{1,0:T(8,128)(2,1)}, u32[]{:S(2)}, u32[]{:S(2)}) collective-permute-start(bf16[256,1024]{1,0:T(8,128)(2,1)S(1)} %copy-done.7), channel_id=1, source_target_pairs={{0,1},{1,0},{2,3},{3,2},{4,5},{5,4},{6,7},{7,6},{8,9},{9,8},{10,11... | collective-permute-start | bytes 1572872 | tf_op jit(solution)/shard_map/ppermute | solution.py:245
  132.7 30.2 %collective-permute-start.12 = (bf16[256,1024]{1,0:T(8,128)(2,1)S(1)}, bf16[256,1024]{1,0:T(8,128)(2,1)}, u32[]{:S(2)}, u32[]{:S(2)}) collective-permute-start(bf16[256,1024]{1,0:T(8,128)(2,1)S(1)} %get-tuple-element.77), channel_id=1, source_target_pairs={{0,64},{64,0},{1,65},{65,1},{2,66},{66,2},{3,67},{67,3},{4,68},{68... | collective-permute-start | bytes 1572872 | tf_op jit(solution)/shard_map/ppermute | solution.py:258
  140.0 5.5 %collective-permute-start.9 = (bf16[64,256]{1,0:T(8,128)(2,1)S(1)}, bf16[64,256]{1,0:T(8,128)(2,1)S(1)}, u32[]{:S(2)}, u32[]{:S(2)}) collective-permute-start(bf16[64,256]{1,0:T(8,128)(2,1)S(1)} %get-tuple-element.69), channel_id=1, source_target_pairs={{0,1},{1,0},{2,3},{3,2},{4,5},{5,4},{6,7},{7,6},{8,9},{9,8},{10,11... | collective-permute-start | bytes 98312 | tf_op jit(solution)/shard_map/ppermute | solution.py:253
  145.5 7.6 %collective-permute-start.10 = (bf16[128,256]{1,0:T(8,128)(2,1)S(1)}, bf16[128,256]{1,0:T(8,128)(2,1)S(1)}, u32[]{:S(2)}, u32[]{:S(2)}) collective-permute-start(bf16[128,256]{1,0:T(8,128)(2,1)S(1)} %maximum_select_fusion), channel_id=1, source_target_pairs={{0,0},{1,1},{2,130},{3,131},{4,260},{5,261},{6,390},{7,391},{128,3... | collective-permute-start | bytes 196616 | tf_op jit(solution)/shard_map/ppermute | solution.py:255
  146.8 11.6 %collective-permute-start.13 = (bf16[2,256,256]{2,1,0:T(8,128)(2,1)S(1)}, bf16[2,256,256]{2,1,0:T(8,128)(2,1)S(1)}, u32[]{:S(2)}, u32[]{:S(2)}) collective-permute-start(bf16[2,256,256]{2,1,0:T(8,128)(2,1)S(1)} %get-tuple-element.78), channel_id=1, source_target_pairs={{0,1},{1,0},{2,3},{3,2},{4,5},{5,4},{6,7},{7,6},{8,9},{9,8},{10,11... | collective-permute-start | bytes 786440 | tf_op jit(solution)/shard_map/ppermute | solution.py:256
  148.7 9.7 %collective-permute-start.14 = (bf16[2,256,256]{2,1,0:T(8,128)(2,1)S(1)}, bf16[2,256,256]{2,1,0:T(8,128)(2,1)S(1)}, u32[]{:S(2)}, u32[]{:S(2)}) collective-permute-start(bf16[2,256,256]{2,1,0:T(8,128)(2,1)S(1)} %get-tuple-element.74), channel_id=1, source_target_pairs={{0,64},{64,0},{1,65},{65,1},{2,66},{66,2},{3,67},{67,3},{4,68},{68... | collective-permute-start | bytes 786440 | tf_op jit(solution)/shard_map/ppermute | solution.py:259
  153.2 9.8 %collective-permute-start.15 = (bf16[2,256,256]{2,1,0:T(8,128)(2,1)S(1)}, bf16[2,256,256]{2,1,0:T(8,128)(2,1)S(1)}, u32[]{:S(2)}, u32[]{:S(2)}) collective-permute-start(bf16[2,256,256]{2,1,0:T(8,128)(2,1)S(1)} %get-tuple-element.74), channel_id=1, source_target_pairs={{0,1},{1,0},{2,3},{3,2},{4,5},{5,4},{6,7},{7,6},{8,9},{9,8},{10,11... | collective-permute-start | bytes 786440 | tf_op jit(solution)/shard_map/ppermute | solution.py:257
  168.6 22.6 %all-to-all-start.4 = ((bf16[16,72,128]{2,1,0:T(8,128)(2,1)}), bf16[16,72,128]{2,1,0:T(8,128)(2,1)S(1)}, u32[]{:S(2)}, u32[]{:S(2)}) async-start(bf16[16,72,128]{2,1,0:T(8,128)(2,1)} %shard_map.97), calls=%async_computation.4 | async-start | bytes 589824 | tf_op jit(solution)/shard_map/all_to_all | solution.py:264
  178.0 13.2 %collective-permute-start.16 = (bf16[128,256]{1,0:T(8,128)(2,1)S(1)}, bf16[128,256]{1,0:T(8,128)(2,1)S(1)}, u32[]{:S(2)}, u32[]{:S(2)}) collective-permute-start(bf16[128,256]{1,0:T(8,128)(2,1)S(1)} %collective-permute-done.10), channel_id=1, source_target_pairs={{0,0},{1,1},{2,2},{3,3},{4,4},{5,5},{6,6},{7,7},{130,128},{131,129... | collective-permute-start | bytes 196616 | tf_op jit(solution)/shard_map/ppermute | solution.py:265
  178.7 7.8 %collective-permute-start.17 = (bf16[256,1024]{1,0:T(8,128)(2,1)}, bf16[256,1024]{1,0:T(8,128)(2,1)S(1)}, u32[]{:S(2)}, u32[]{:S(2)}) collective-permute-start(bf16[256,1024]{1,0:T(8,128)(2,1)} %collective-permute-done.11), channel_id=1, source_target_pairs={{0,64},{64,0},{1,65},{65,1},{2,66},{66,2},{3,67},{67,3},{4,68},{68... | collective-permute-start | bytes 1572872 | tf_op jit(solution)/shard_map/ppermute | solution.py:266
  181.7 4.7 %collective-permute-start.18 = (bf16[2,256,256]{2,1,0:T(8,128)(2,1)S(1)}, bf16[2,256,256]{2,1,0:T(8,128)(2,1)S(1)}, u32[]{:S(2)}, u32[]{:S(2)}) collective-permute-start(bf16[2,256,256]{2,1,0:T(8,128)(2,1)S(1)} %collective-permute-done.15), channel_id=1, source_target_pairs={{0,64},{64,0},{1,65},{65,1},{2,66},{66,2},{3,67},{67,3},{4,68},{68... | collective-permute-start | bytes 786440 | tf_op jit(solution)/shard_map/ppermute | solution.py:267
  186.4 1.2 copy-start.9
  188.8 1.2 copy-start.8
  191.9 3.2 %collective-permute-start.19 = (f32[8,128]{1,0:T(8,128)S(1)}, f32[8,128]{1,0:T(8,128)S(1)}, u32[]{:S(2)}, u32[]{:S(2)}) collective-permute-start(f32[8,128]{1,0:T(8,128)S(1)} %get-tuple-element.90.mine_ref), channel_id=1, source_target_pairs={{0,64},{64,0},{1,65},{65,1},{2,66},{66,2},{3,67},{67,3},{4,68},{68... | collective-permute-start | bytes 12296 | tf_op jit(solution)/shard_map/ppermute | solution.py:281

commit v7 on v6

--- a/solution.py
+++ b/solution.py
@@ -85,7 +85,7 @@
             out_ref[g, spot, :] = part[g * rows : (g + 1) * rows]
 
 
-def middle_body(place_ref, in_ref, up_ref, up_got_ref, scal_ref, keep_ref, send_ref, q_ref):
+def middle_body(place_ref, in_ref, up_ref, up_got_ref, scal_ref, hidden_ref, q_ref):
     rows = up_ref.shape[0]
     side = place_ref[3]
     scale_in = scal_ref[0:1, 0:1]
@@ -111,8 +111,8 @@
         for i in range(q_ref.shape[0]):
             q_ref[i, base : base + rows, :] = quant_gate
             q_ref[i, base + rows : base + 2 * rows, :] = quant_lift
-    keep_ref[...] = jnp.where(side == 0, hiddens[0], hiddens[1]).astype(BF16)
-    send_ref[...] = jnp.where(side == 0, hiddens[1], hiddens[0]).astype(BF16)
+    hidden_ref[0] = jnp.where(side == 0, hiddens[0], hiddens[1]).astype(BF16)
+    hidden_ref[1] = jnp.where(side == 0, hiddens[1], hiddens[0]).astype(BF16)
     peaks = pack_peaks(scal_ref[2:3, 0:1], peak_hidden, peak_grad)
     wide = jnp.concatenate([peaks, peaks], axis=1)
     for i in range(q_ref.shape[0]):
@@ -154,10 +154,21 @@
         out_ref[k, 2 * groups * fine * rows :, :] = packed
 
 
-def pick_body(place_ref, q_ref, mine_ref, other_ref, kept_ref):
+def pick_body(place_ref, q_ref, kept_ref, other_ref):
     pick(place_ref, q_ref, kept_ref)
-    mine_ref[...] = kept_ref[0:2]
     other_ref[...] = kept_ref[2:4]
+
+
+def weights_body(*refs):
+    x_refs, q_refs, scal_ref, out_refs = refs[:4], refs[4:8], refs[8], refs[9:]
+    divisor = scal_ref[0:1, 0:1] * scal_ref[1:2, 0:1] * float(4 * x_refs[0].shape[0])
+    contract = (((0,), (0,)), ((), ()))
+    for i, out_ref in enumerate(out_refs):
+        total = None
+        for x_ref, q_ref in zip(x_refs, q_refs):
+            part = lax.dot_general(x_ref[...], q_ref[i], contract, preferred_element_type=F32)
+            total = part if total is None else total + part
+        out_ref[...] = (total / divisor).astype(BF16)
 
 
 def column_body(in_ref, out_ref):
@@ -169,7 +180,7 @@
         out_ref[i, rows:, :] = packed
 
 
-def last_body(in_ref, scal_ref, hidden_ref, out_ref, peaks_ref, hidden_out_ref):
+def last_body(place_ref, in_ref, scal_ref, hidden_ref, got_ref, out_ref, peaks_ref, hidden_out_ref):
     rows = in_ref.shape[1] - 8
     for side in range(2):
         total = in_ref[side, :rows, :].astype(F32)
@@ -177,7 +188,9 @@
             total = total + in_ref[2 * i + side, :rows, :].astype(F32)
         out_ref[side * rows : (side + 1) * rows, :] = (total / scal_ref[1:2, 0:1]).astype(BF16)
     peaks_ref[...] = rows_of(*unpack_peaks(in_ref[:, rows:, :].astype(F32)))
-    hidden_out_ref[...] = hidden_ref[...]
+    for away, ref in enumerate((hidden_ref.at[0], got_ref)):
+        half = place_ref[3] if away == 0 else 1 - place_ref[3]
+        hidden_out_ref[pl.ds(pl.multiple_of(half * rows, rows), rows), :] = ref[...]
 
 
 def history_body(hist_ref, mine_ref, other_ref, out_ref):
@@ -208,13 +221,14 @@
     x_all = lax.all_to_all(copies, plane, 0, 0, tiled=True)
     near = [w_gate, w_up]
     far = [lax.ppermute(w, "t", swap) for w in near]
-    near += [lax.ppermute(w, "c", swap) for w in near]
-    far += [lax.ppermute(w, "c", swap) for w in far]
     up = lax.ppermute(upstream, column_axis, along_y)
     up = lax.ppermute(up, column_axis, along_z).reshape(2, rows, units)
     up_got = lax.ppermute(lax.dynamic_index_in_dim(up, 1 - side, 0, keepdims=False), "t", swap)
     up = lax.dynamic_index_in_dim(up, side, 0, keepdims=False)
-    x_all, up, up_got, *weights = lax.optimization_barrier((x_all, up, up_got, *near, *far))
+    near += [lax.ppermute(w, "c", swap) for w in near]
+    up, up_got, *far = lax.optimization_barrier((up, up_got, *far))
+    far += [lax.ppermute(w, "c", swap) for w in far]
+    x_all, *weights = lax.optimization_barrier((x_all, *near, *far))
 
     work = 16 * nh * rows * depth * units * 2
     parts, x_near, x_far = call(
@@ -225,13 +239,14 @@
         moved=8 * 2**20,
     )
     sums = lax.all_to_all(parts, "p", 0, 0, tiled=True)
-    keep, send, quants = call(
+    hidden, quants = call(
         middle_body,
-        [((rows, units), BF16), ((rows, units), BF16), ((np, 4 * rows + 8, units), BF16)],
+        [((2, rows, units), BF16), ((np, 4 * rows + 8, units), BF16)],
         (place, sums, up, up_got, scal),
         moved=2**20,
     )
     q_all = lax.all_to_all(quants, "p", 0, 0, tiled=True)
+    hidden = lax.ppermute(hidden, column_axis, along_z)
     (back,) = call(
         backward_body,
         [((nx, 2 * nh * nw * rows + 8, width), BF16)],
@@ -240,42 +255,31 @@
         moved=8 * 2**20,
         scratch=[pltpu.VMEM((4, nh * rows, units), BF16)],
     )
-    q_all, back, keep, send, x_near, x_far = lax.optimization_barrier((q_all, back, keep, send, x_near, x_far))
+    q_all, back, hidden, x_near, x_far = lax.optimization_barrier((q_all, back, hidden, x_near, x_far))
     back_cols = lax.all_to_all(back, "x", 0, 0, tiled=True)
-    x_side = lax.ppermute(x_far, "t", swap)
     q_mine, q_send = call(
         pick_body,
-        [((2, nh * rows, units), BF16)] * 2,
+        [((4, nh * rows, units), BF16), ((2, nh * rows, units), BF16)],
         (place, q_all),
-        moved=2**21,
-        scratch=[pltpu.VMEM((4, nh * rows, units), BF16)],
-    )
-    got = lax.ppermute(send, "t", swap)
-    hidden = jnp.where(side == 0, jnp.concatenate([keep, got]), jnp.concatenate([got, keep]))
-    hidden = lax.ppermute(hidden, column_axis, along_z)
+        moved=2**20,
+    )
+    x_side = lax.ppermute(x_far, "t", swap)
     q_side = lax.ppermute(q_mine, "t", swap)
-    q_send_side = lax.ppermute(q_send, "t", swap)
     x_other = lax.ppermute(x_near, "c", swap)
     q_other = lax.ppermute(q_send, "c", swap)
-    back_cols, hidden, x_near, x_side, x_other, q_mine, q_side, q_other, q_send_side = lax.optimization_barrier(
-        (back_cols, hidden, x_near, x_side, x_other, q_mine, q_side, q_other, q_send_side)
-    )
+    back_cols, x_other, q_other = lax.optimization_barrier((back_cols, x_other, q_other))
     (column,) = call(column_body, [((2 * nh * nw, rows + 8, width), BF16)], (back_cols,), moved=2**20)
     back_all = lax.all_to_all(column, last_stage, 0, 0, tiled=True)
     hidden = lax.ppermute(hidden, column_axis, back_y)
-    xs = [x_near, x_side, x_other, lax.ppermute(x_side, "c", swap)]
-    qs = [q_mine, q_side, q_other, lax.ppermute(q_send_side, "c", swap)]
-    divisor = scal[0, 0] * scal[1, 0] * (4 * nh * rows)
-    contract = (((0,), (0,)), ((), ()))
-    grads = []
-    for i in range(2):
-        total = sum(lax.dot_general(x, q[i], contract, preferred_element_type=F32) for x, q in zip(xs, qs))
-        grads.append((total / divisor).astype(BF16))
-    back_all, hidden, *grads = lax.optimization_barrier((back_all, hidden, *grads))
+    hidden_got = lax.ppermute(hidden[1], "t", swap)
+    xs = (x_near, x_side, x_other, lax.ppermute(x_side, "c", swap))
+    qs = (q_mine, q_side, q_other, lax.ppermute(q_side[2:], "c", swap))
+    grads = call(weights_body, [((depth, units), BF16)] * 2, (*xs, *qs, scal), flops=work, moved=2**22)
+    back_all, hidden, hidden_got, *grads = lax.optimization_barrier((back_all, hidden, hidden_got, *grads))
     input_grad, peaks, hidden = call(
         last_body,
         [((2 * rows, width), BF16), ((8, 128), F32), ((2 * rows, units), BF16)],
-        (back_all, scal, hidden),
+        (place, back_all, scal, hidden, hidden_got),
         moved=2**20,
     )
     peaks_other = lax.ppermute(peaks, "c", swap)

time: 200 us -> 181 us (0.905); the launches traced: 196 us -> 179 us
  blocking collectives: 53.1 us -> 39.1 us
  matrix products: 10.6 us -> 0 us
  waiting for transfers between devices: 29.6 us -> 38.9 us
  Pallas kernels: 11.3 us -> 16.9 us
  local copies, waits for them, and re-layouts: 7.03 us -> 2.23 us
    ppermute x2, waiting for transfers between devices: 18 us -> 0.01 us  [per_device(): far = [lax.ppermute(w, 't', swap) for w in near]]
    all_to_all x1 -> x0, blocking collectives: 17.4 us -> none  [per_device(): q_all = lax.all_to_all(quants, 'p', 0, 0, tiled=True)]
    ppermute x1, waiting for transfers between devices: 2.58 us -> 19.8 us  [per_device(): lax.ppermute(lax.dynamic_index_in_dim(up, 1 - side, 0, keepdims=False), '...]
    all_to_all x0 -> x1, waiting for transfers between devices: none -> 14.2 us  [per_device(): q_all = lax.all_to_all(quants, 'p', 0, 0, tiled=True)]
    dot_general x8 -> x0, matrix products: 10.6 us -> none  [per_device(): lax.dot_general(x, q[i], contract, preferred_element_type=F32)]
    ppermute x4 -> x3, waiting for transfers between devices: 8.15 us -> 0.01 us  [the longest x1 0.01 us: per_device(): qs = (q_mine, q_side, q_other, lax.ppermute(q_side[2:], 'c', swap))]
    pallas_call x8 -> x9, Pallas kernels: 11.3 us -> 16.9 us  [call(): pl.pallas_call(body, out_shape=[jax.ShapeDtypeStruct(s, t) for s, t in ou...]
    unnamed x24 -> x14, local copies, waits for them, and re-layouts: 6.5 us -> 2.19 us
  transfers between devices with their start and end apart: 23 -> 23, of which waited for: 6 -> 6; matrix products, arithmetic and copies ran while one was open for 3% -> 0% of each run, Pallas kernels for 0% -> 5%
where the time goes in v7:
time: 181 us; the launch traced here: 179 us
  starting transfers between devices  81 us (45%)
  blocking collectives  39.1 us (22%)
  waiting for transfers between devices  38.9 us (21%)
  Pallas kernels  16.9 us (9%)
  local copies, waits for them, and re-layouts  2.23 us (1%)
    all_to_all x1, blocking collectives, per_device(): sums = lax.all_to_all(parts, 'p', 0, 0, tiled=True)  39.1 us
    ppermute x1, waiting for transfers between devices, per_device(): lax.ppermute(lax.dynamic_index_in_dim(up, 1 - side, 0, keepdims=False), '...  19.8 us
    pallas_call x9, Pallas kernels, call(): pl.pallas_call(body, out_shape=[jax.ShapeDtypeStruct(s, t) for s, t in ou...  16.9 us
    all_to_all x1, starting transfers between devices, per_device(): x_all = lax.all_to_all(copies, plane, 0, 0, tiled=True)  15.5 us
    all_to_all x1, waiting for transfers between devices, per_device(): q_all = lax.all_to_all(quants, 'p', 0, 0, tiled=True)  14.2 us
    all_to_all x1, starting transfers between devices, per_device(): back_all = lax.all_to_all(column, last_stage, 0, 0, tiled=True)  7.02 us
    ppermute x1, starting transfers between devices, per_device(): xs = (x_near, x_side, x_other, lax.ppermute(x_side, 'c', swap))  6.91 us
    ppermute x2, starting transfers between devices, per_device(): near += [lax.ppermute(w, 'c', swap) for w in near]  5.91 us
  transfers between devices with their start and end apart: 23, of which 6 were waited for; matrix products, arithmetic and copies ran while one was open for 0% of the time, Pallas kernels for 5%

profile of v7, /device:TPU:1, one launch (start us, length us, event | category | flops | bytes accessed | tf_op | source)
XLA Modules:
  0.0 179.1 jit_solution(2781795116214982220)
XLA Ops:
  0.6 0.8 copy.10.hist_ref
  1.4 0.8 copy-done
  2.1 1.2 shard_map.92
  3.3 15.5 %all-to-all-start = ((bf16[64,64,128]{2,1,0:T(8,128)(2,1)}), bf16[64,64,128]{2,1,0:T(8,128)(2,1)S(1)}, u32[]{:S(2)}, u32[]{:S(2)}) async-start(bf16[64,64,128]{2,1,0:T(8,128)(2,1)} %get-tuple-element.45), calls=%async_computation | async-start | bytes 2097152 | tf_op jit(solution)/shard_map/all_to_all | solution.py:221
  18.8 0.0 copy-done.1
  18.8 2.9 %collective-permute-start.5 = (bf16[1024,256]{1,0:T(8,128)(2,1)S(1)}, bf16[1024,256]{1,0:T(8,128)(2,1)S(1)}, u32[]{:S(2)}, u32[]{:S(2)}) collective-permute-start(bf16[1024,256]{1,0:T(8,128)(2,1)S(1)} %copy-done.1), channel_id=1, source_target_pairs={{0,1},{1,0},{2,3},{3,2},{4,5},{5,4},{6,7},{7,6},{8,9},{9,8},{10,11... | collective-permute-start | bytes 1572872 | tf_op jit(solution)/shard_map/ppermute | solution.py:223
  21.7 0.0 copy-done.2
  21.7 2.4 %collective-permute-start.6 = (bf16[1024,256]{1,0:T(8,128)(2,1)S(1)}, bf16[1024,256]{1,0:T(8,128)(2,1)}, u32[]{:S(2)}, u32[]{:S(2)}) collective-permute-start(bf16[1024,256]{1,0:T(8,128)(2,1)S(1)} %copy-done.2), channel_id=1, source_target_pairs={{0,1},{1,0},{2,3},{3,2},{4,5},{5,4},{6,7},{7,6},{8,9},{9,8},{10,11... | collective-permute-start | bytes 1572872 | tf_op jit(solution)/shard_map/ppermute | solution.py:223
  24.1 0.0 copy-done.5
  24.1 0.7 collective-permute-start.2
  24.8 0.0 collective-permute-done.2
  24.8 0.7 collective-permute-start.3
  25.5 0.0 collective-permute-done.3
  25.5 2.9 %collective-permute-start.4 = (bf16[64,256]{1,0:T(8,128)(2,1)S(1)}, bf16[64,256]{1,0:T(8,128)(2,1)S(1)}, u32[]{:S(2)}, u32[]{:S(2)}) collective-permute-start(bf16[64,256]{1,0:T(8,128)(2,1)S(1)} %get-tuple-element.90), channel_id=1, source_target_pairs={{0,1},{1,0},{2,3},{3,2},{4,5},{5,4},{6,7},{7,6},{8,9},{9,8},{10,11... | collective-permute-start | bytes 98312 | tf_op jit(solution)/shard_map/ppermute | solution.py:226
  28.4 4.0 %collective-permute-start = (bf16[1024,256]{1,0:T(8,128)(2,1)S(1)}, bf16[1024,256]{1,0:T(8,128)(2,1)}, u32[]{:S(2)}, u32[]{:S(2)}) collective-permute-start(bf16[1024,256]{1,0:T(8,128)(2,1)S(1)} %copy-done.1), channel_id=1, source_target_pairs={{0,64},{64,0},{1,65},{65,1},{2,66},{66,2},{3,67},{67,3},{4,68},{68... | collective-permute-start | bytes 1572872 | tf_op jit(solution)/shard_map/ppermute | solution.py:228
  32.4 1.9 %collective-permute-start.1 = (bf16[1024,256]{1,0:T(8,128)(2,1)S(1)}, bf16[1024,256]{1,0:T(8,128)(2,1)}, u32[]{:S(2)}, u32[]{:S(2)}) collective-permute-start(bf16[1024,256]{1,0:T(8,128)(2,1)S(1)} %copy-done.2), channel_id=1, source_target_pairs={{0,64},{64,0},{1,65},{65,1},{2,66},{66,2},{3,67},{67,3},{4,68},{68... | collective-permute-start | bytes 1572872 | tf_op jit(solution)/shard_map/ppermute | solution.py:228
  34.4 19.8 %collective-permute-done.4.up_got_ref = bf16[64,256]{1,0:T(8,128)(2,1)S(1)} collective-permute-done((bf16[64,256]{1,0:T(8,128)(2,1)S(1)}, bf16[64,256]{1,0:T(8,128)(2,1)S(1)}, u32[]{:S(2)}, u32[]{:S(2)}) %collective-permute-start.4) | collective-permute-done | bytes 32800 | tf_op jit(solution)/shard_map/ppermute | solution.py:226
  54.2 0.0 collective-permute-done.5.refs_4_
  54.2 0.0 collective-permute-done.6.refs_5_
  54.2 3.7 %collective-permute-start.7 = (bf16[1024,256]{1,0:T(8,128)(2,1)S(1)}, bf16[1024,256]{1,0:T(8,128)(2,1)}, u32[]{:S(2)}, u32[]{:S(2)}) collective-permute-start(bf16[1024,256]{1,0:T(8,128)(2,1)S(1)} %collective-permute-done.5.refs_4_), channel_id=1, source_target_pairs={{0,64},{64,0},{1,65},{65,1},{2,66},{66,2},{3,67},{67,3},{4,68},{68... | collective-permute-start | bytes 1572872 | tf_op jit(solution)/shard_map/ppermute | solution.py:230
  57.9 1.9 %collective-permute-start.8 = (bf16[1024,256]{1,0:T(8,128)(2,1)}, bf16[1024,256]{1,0:T(8,128)(2,1)}, u32[]{:S(2)}, u32[]{:S(2)}) collective-permute-start(bf16[1024,256]{1,0:T(8,128)(2,1)} %collective-permute-done.6.refs_5_), channel_id=1, source_target_pairs={{0,64},{64,0},{1,65},{65,1},{2,66},{66,2},{3,67},{67,3},{4,68},{68... | collective-permute-start | bytes 1572872 | tf_op jit(solution)/shard_map/ppermute | solution.py:230
  59.8 0.1 pad_add_fusion.place_ref
  59.9 0.0 collective-permute-done.refs_2_
  59.9 0.0 collective-permute-done.1.refs_3_
  59.9 0.0 collective-permute-done.7.refs_6_
  59.9 2.1 %collective-permute-done.8.refs_7_ = bf16[1024,256]{1,0:T(8,128)(2,1)} collective-permute-done((bf16[1024,256]{1,0:T(8,128)(2,1)}, bf16[1024,256]{1,0:T(8,128)(2,1)}, u32[]{:S(2)}, u32[]{:S(2)}) %collective-permute-start.8) | collective-permute-done | bytes 524320 | tf_op jit(solution)/shard_map/ppermute | solution.py:230
  62.0 0.0 all-to-all-done.x_ref
  62.0 3.1 %shard_map.93 = (bf16[4,256,256]{2,1,0:T(8,128)(2,1)S(1)}, bf16[256,1024]{1,0:T(8,128)(2,1)S(1)}, bf16[256,1024]{1,0:T(8,128)(2,1)}) custom-call(s32[4]{0:T(128)S(1)} %pad_add_fusion.place_ref, bf16[64,64,128]{2,1,0:T(8,128)(2,1)S(1)} %all-to-all-done.x_ref, bf16[1024,256]{1,0:T(8,128)(2,1)S(1)} %copy-done.1, bf16[1024,256]{1,0:T(8,128)(2,1)S(1)} %copy-done.2, ...), custom_call_target="tpu_custom_call" | custom-call | flops 2147483648 | bytes 8388608 | tf_op jit(solution)/shard_map/pallas_call | solution.py:20
  65.1 0.0 copy-start.3
  65.1 39.1 %all_to_all.25.in_ref = bf16[4,256,256]{2,1,0:T(8,128)(2,1)S(1)} all-to-all(bf16[4,256,256]{2,1,0:T(8,128)(2,1)S(1)} %get-tuple-element.57), channel_id=1, replica_groups=mesh['h'=4,'c'=2,'x'=4,'w'=2,'p'=4,'t'=2] {'p'}, dimensions={0} | all-to-all | bytes 1048576 | tf_op jit(solution)/shard_map/all_to_all | solution.py:241
  104.2 1.6 shard_map.94
  105.9 3.6 %all-to-all-start.2 = ((bf16[4,264,256]{2,1,0:T(8,128)(2,1)}), bf16[4,264,256]{2,1,0:T(8,128)(2,1)S(1)}, u32[]{:S(2)}, u32[]{:S(2)}) async-start(bf16[4,264,256]{2,1,0:T(8,128)(2,1)} %get-tuple-element.61), calls=%async_computation.2 | async-start | bytes 1081344 | tf_op jit(solution)/shard_map/all_to_all | solution.py:248
  109.4 0.7 collective-permute-start.9
  110.1 14.2 %all-to-all-done.2.q_ref = bf16[4,264,256]{2,1,0:T(8,128)(2,1)S(1)} async-done(((bf16[4,264,256]{2,1,0:T(8,128)(2,1)}), bf16[4,264,256]{2,1,0:T(8,128)(2,1)S(1)}, u32[]{:S(2)}, u32[]{:S(2)}) %all-to-all-start.2) | async-done | bytes 540704 | tf_op jit(solution)/shard_map/all_to_all | solution.py:248
  124.3 4.0 %shard_map.95 = bf16[4,1032,128]{2,1,0:T(8,128)(2,1)} custom-call(s32[4]{0:T(128)S(1)} %pad_add_fusion.place_ref, bf16[4,264,256]{2,1,0:T(8,128)(2,1)S(1)} %all-to-all-done.2.q_ref, bf16[1024,256]{1,0:T(8,128)(2,1)S(1)} %copy-done.1, bf16[1024,256]{1,0:T(8,128)(2,1)S(1)} %copy-done.2, bf16[1024,256]{1,0:T(8,128)(2,1)} %collective-permute-done.refs_2_, ...), custom_call_target="tpu_custom_call" | custom-call | flops 2147483648 | bytes 8388608 | tf_op jit(solution)/shard_map/pallas_call | solution.py:20
  128.3 0.0 collective-permute-done.9
  128.3 4.6 %all-to-all-start.3 = ((bf16[4,1032,128]{2,1,0:T(8,128)(2,1)}), bf16[4,1032,128]{2,1,0:T(8,128)(2,1)S(1)}, u32[]{:S(2)}, u32[]{:S(2)}) async-start(bf16[4,1032,128]{2,1,0:T(8,128)(2,1)} %shard_map.95), calls=%async_computation.3 | async-start | bytes 2113536 | tf_op jit(solution)/shard_map/all_to_all | solution.py:259
  132.8 1.9 %collective-permute-start.14 = (bf16[256,1024]{1,0:T(8,128)(2,1)}, bf16[256,1024]{1,0:T(8,128)(2,1)S(1)}, u32[]{:S(2)}, u32[]{:S(2)}) collective-permute-start(bf16[256,1024]{1,0:T(8,128)(2,1)} %get-tuple-element.71), channel_id=1, source_target_pairs={{0,1},{1,0},{2,3},{3,2},{4,5},{5,4},{6,7},{7,6},{8,9},{9,8},{10,11... | collective-permute-start | bytes 1572872 | tf_op jit(solution)/shard_map/ppermute | solution.py:266
  134.8 3.7 %collective-permute-start.10 = (bf16[256,1024]{1,0:T(8,128)(2,1)S(1)}, bf16[256,1024]{1,0:T(8,128)(2,1)S(1)}, u32[]{:S(2)}, u32[]{:S(2)}) collective-permute-start(bf16[256,1024]{1,0:T(8,128)(2,1)S(1)} %copy-done.4), channel_id=1, source_target_pairs={{0,64},{64,0},{1,65},{65,1},{2,66},{66,2},{3,67},{67,3},{4,68},{68... | collective-permute-start | bytes 1572872 | tf_op jit(solution)/shard_map/ppermute | solution.py:268
  138.5 1.4 shard_map.96
  139.9 3.6 %collective-permute-start.16 = (bf16[4,256,256]{2,1,0:T(8,128)(2,1)}, bf16[4,256,256]{2,1,0:T(8,128)(2,1)S(1)}, u32[]{:S(2)}, u32[]{:S(2)}) collective-permute-start(bf16[4,256,256]{2,1,0:T(8,128)(2,1)} %get-tuple-element.73.refs_4_), channel_id=1, source_target_pairs={{0,1},{1,0},{2,3},{3,2},{4,5},{5,4},{6,7},{7,6},{8,9},{9,8},{10,11... | collective-permute-start | bytes 1572872 | tf_op jit(solution)/shard_map/ppermute | solution.py:267
  143.5 2.2 %collective-permute-start.11 = (bf16[2,256,256]{2,1,0:T(8,128)(2,1)S(1)}, bf16[2,256,256]{2,1,0:T(8,128)(2,1)S(1)}, u32[]{:S(2)}, u32[]{:S(2)}) collective-permute-start(bf16[2,256,256]{2,1,0:T(8,128)(2,1)S(1)} %get-tuple-element.68), channel_id=1, source_target_pairs={{0,64},{64,0},{1,65},{65,1},{2,66},{66,2},{3,67},{67,3},{4,68},{68... | collective-permute-start | bytes 786440 | tf_op jit(solution)/shard_map/ppermute | solution.py:269
  145.7 0.8 collective-permute-done.14.refs_1_
  146.6 6.9 %collective-permute-start.15 = (bf16[256,1024]{1,0:T(8,128)(2,1)S(1)}, bf16[256,1024]{1,0:T(8,128)(2,1)}, u32[]{:S(2)}, u32[]{:S(2)}) collective-permute-start(bf16[256,1024]{1,0:T(8,128)(2,1)S(1)} %collective-permute-done.14.refs_1_), channel_id=1, source_target_pairs={{0,64},{64,0},{1,65},{65,1},{2,66},{66,2},{3,67},{67,3},{4,68},{68... | collective-permute-start | bytes 1572872 | tf_op jit(solution)/shard_map/ppermute | solution.py:275
  153.5 0.0 collective-permute-done.11.refs_6_
  153.5 0.0 collective-permute-done.10.refs_2_
  153.5 0.0 all-to-all-done.3.in_ref
  153.5 0.9 shard_map.97
  154.4 7.0 %all-to-all-start.4 = ((bf16[16,72,128]{2,1,0:T(8,128)(2,1)}), bf16[16,72,128]{2,1,0:T(8,128)(2,1)S(1)}, u32[]{:S(2)}, u32[]{:S(2)}) async-start(bf16[16,72,128]{2,1,0:T(8,128)(2,1)} %shard_map.97), calls=%async_computation.4 | async-start | bytes 589824 | tf_op jit(solution)/shard_map/all_to_all | solution.py:272
  161.4 0.7 collective-permute-start.12
  162.1 0.0 collective-permute-done.16.refs_5_
  162.1 2.2 %collective-permute-start.17 = (bf16[2,256,256]{2,1,0:T(8,128)(2,1)S(1)}, bf16[2,256,256]{2,1,0:T(8,128)(2,1)S(1)}, u32[]{:S(2)}, u32[]{:S(2)}) collective-permute-start(bf16[2,256,256]{2,1,0:T(8,128)(2,1)S(1)} %slice.9), channel_id=1, source_target_pairs={{0,64},{64,0},{1,65},{65,1},{2,66},{66,2},{3,67},{67,3},{4,68},{68... | collective-permute-start | bytes 786440 | tf_op jit(solution)/shard_map/ppermute | solution.py:276
  164.3 0.0 collective-permute-done.12.hidden_ref
  164.3 3.5 %collective-permute-start.13 = (bf16[64,256]{1,0:T(8,128)(2,1)S(1)}, bf16[64,256]{1,0:T(8,128)(2,1)S(1)}, u32[]{:S(2)}, u32[]{:S(2)}) collective-permute-start(bf16[64,256]{1,0:T(8,128)(2,1)S(1)} %slice_bitcast_fusion), channel_id=1, source_target_pairs={{0,1},{1,0},{2,3},{3,2},{4,5},{5,4},{6,7},{7,6},{8,9},{9,8},{10,11... | collective-permute-start | bytes 98312 | tf_op jit(solution)/shard_map/ppermute | solution.py:274
  167.9 0.0 collective-permute-done.17.refs_7_
  167.9 0.0 collective-permute-done.15.refs_3_
  167.9 3.5 %shard_map.98 = (bf16[1024,256]{1,0:T(8,128)(2,1)}, bf16[1024,256]{1,0:T(8,128)(2,1)}) custom-call(bf16[256,1024]{1,0:T(8,128)(2,1)S(1)} %copy-done.4, bf16[256,1024]{1,0:T(8,128)(2,1)S(1)} %collective-permute-done.14.refs_1_, bf16[256,1024]{1,0:T(8,128)(2,1)S(1)} %collective-permute-done.10.refs_2_, bf16[256,1024]{1,0:T(8,128)(2,1)} %collective-permute-done.15.refs_3_, ...), custom_call_target="tpu_custom_call" | custom-call | flops 2147483648 | bytes 4194304 | tf_op jit(solution)/shard_map/pallas_call | solution.py:20
  171.4 0.0 collective-permute-done.13.got_ref
  171.4 1.0 all-to-all-done.4.in_ref
  172.4 1.2 shard_map.99
  173.6 4.0 %collective-permute-start.18 = (f32[8,128]{1,0:T(8,128)S(1)}, f32[8,128]{1,0:T(8,128)S(1)}, u32[]{:S(2)}, u32[]{:S(2)}) collective-permute-start(f32[8,128]{1,0:T(8,128)S(1)} %get-tuple-element.84.mine_ref), channel_id=1, source_target_pairs={{0,64},{64,0},{1,65},{65,1},{2,66},{66,2},{3,67},{67,3},{4,68},{68... | collective-permute-start | bytes 12296 | tf_op jit(solution)/shard_map/ppermute | solution.py:285
  177.6 0.8 collective-permute-done.18.other_ref
  178.4 0.1 shard_map.100
  178.5 0.7 copy.12
  (10 shorter events, 0.0 us)
Async XLA Ops:
  1.4 0.8 copy-start
  3.3 15.5 %copy-start.1 = (bf16[1024,256]{1,0:T(8,128)(2,1)S(1)}, bf16[1024,256]{1,0:T(8,128)(2,1)}, u32[]{:S(2)}) copy-start(bf16[1024,256]{1,0:T(8,128)(2,1)} %refs_0_.1) | copy-start | bytes 1572868
  3.3 18.4 %copy-start.2 = (bf16[1024,256]{1,0:T(8,128)(2,1)S(1)}, bf16[1024,256]{1,0:T(8,128)(2,1)}, u32[]{:S(2)}) copy-start(bf16[1024,256]{1,0:T(8,128)(2,1)} %refs_1_.1) | copy-start | bytes 1572868
  3.3 20.8 %copy-start.5 = (bf16[128,256]{1,0:T(8,128)(2,1)S(1)}, bf16[128,256]{1,0:T(8,128)(2,1)}, u32[]{:S(2)}) copy-start(bf16[128,256]{1,0:T(8,128)(2,1)} %param.8) | copy-start | bytes 196612
  3.3 58.7 %all-to-all-start = ((bf16[64,64,128]{2,1,0:T(8,128)(2,1)}), bf16[64,64,128]{2,1,0:T(8,128)(2,1)S(1)}, u32[]{:S(2)}, u32[]{:S(2)}) async-start(bf16[64,64,128]{2,1,0:T(8,128)(2,1)} %get-tuple-element.45), calls=%async_computation | async-start | bytes 2097152 | tf_op jit(solution)/shard_map/all_to_all | solution.py:221
  18.8 35.4 %collective-permute-start.5 = (bf16[1024,256]{1,0:T(8,128)(2,1)S(1)}, bf16[1024,256]{1,0:T(8,128)(2,1)S(1)}, u32[]{:S(2)}, u32[]{:S(2)}) collective-permute-start(bf16[1024,256]{1,0:T(8,128)(2,1)S(1)} %copy-done.1), channel_id=1, source_target_pairs={{0,1},{1,0},{2,3},{3,2},{4,5},{5,4},{6,7},{7,6},{8,9},{9,8},{10,11... | collective-permute-start | bytes 1572872 | tf_op jit(solution)/shard_map/ppermute | solution.py:223
  21.7 32.5 %collective-permute-start.6 = (bf16[1024,256]{1,0:T(8,128)(2,1)S(1)}, bf16[1024,256]{1,0:T(8,128)(2,1)}, u32[]{:S(2)}, u32[]{:S(2)}) collective-permute-start(bf16[1024,256]{1,0:T(8,128)(2,1)S(1)} %copy-done.2), channel_id=1, source_target_pairs={{0,1},{1,0},{2,3},{3,2},{4,5},{5,4},{6,7},{7,6},{8,9},{9,8},{10,11... | collective-permute-start | bytes 1572872 | tf_op jit(solution)/shard_map/ppermute | solution.py:223
  24.1 0.7 collective-permute-start.2
  24.8 0.7 collective-permute-start.3
  25.5 28.7 %collective-permute-start.4 = (bf16[64,256]{1,0:T(8,128)(2,1)S(1)}, bf16[64,256]{1,0:T(8,128)(2,1)S(1)}, u32[]{:S(2)}, u32[]{:S(2)}) collective-permute-start(bf16[64,256]{1,0:T(8,128)(2,1)S(1)} %get-tuple-element.90), channel_id=1, source_target_pairs={{0,1},{1,0},{2,3},{3,2},{4,5},{5,4},{6,7},{7,6},{8,9},{9,8},{10,11... | collective-permute-start | bytes 98312 | tf_op jit(solution)/shard_map/ppermute | solution.py:226
  28.4 31.4 %collective-permute-start = (bf16[1024,256]{1,0:T(8,128)(2,1)S(1)}, bf16[1024,256]{1,0:T(8,128)(2,1)}, u32[]{:S(2)}, u32[]{:S(2)}) collective-permute-start(bf16[1024,256]{1,0:T(8,128)(2,1)S(1)} %copy-done.1), channel_id=1, source_target_pairs={{0,64},{64,0},{1,65},{65,1},{2,66},{66,2},{3,67},{67,3},{4,68},{68... | collective-permute-start | bytes 1572872 | tf_op jit(solution)/shard_map/ppermute | solution.py:228
  32.4 27.4 %collective-permute-start.1 = (bf16[1024,256]{1,0:T(8,128)(2,1)S(1)}, bf16[1024,256]{1,0:T(8,128)(2,1)}, u32[]{:S(2)}, u32[]{:S(2)}) collective-permute-start(bf16[1024,256]{1,0:T(8,128)(2,1)S(1)} %copy-done.2), channel_id=1, source_target_pairs={{0,64},{64,0},{1,65},{65,1},{2,66},{66,2},{3,67},{67,3},{4,68},{68... | collective-permute-start | bytes 1572872 | tf_op jit(solution)/shard_map/ppermute | solution.py:228
  54.2 5.7 %collective-permute-start.7 = (bf16[1024,256]{1,0:T(8,128)(2,1)S(1)}, bf16[1024,256]{1,0:T(8,128)(2,1)}, u32[]{:S(2)}, u32[]{:S(2)}) collective-permute-start(bf16[1024,256]{1,0:T(8,128)(2,1)S(1)} %collective-permute-done.5.refs_4_), channel_id=1, source_target_pairs={{0,64},{64,0},{1,65},{65,1},{2,66},{66,2},{3,67},{67,3},{4,68},{68... | collective-permute-start | bytes 1572872 | tf_op jit(solution)/shard_map/ppermute | solution.py:230
  57.9 4.1 %collective-permute-start.8 = (bf16[1024,256]{1,0:T(8,128)(2,1)}, bf16[1024,256]{1,0:T(8,128)(2,1)}, u32[]{:S(2)}, u32[]{:S(2)}) collective-permute-start(bf16[1024,256]{1,0:T(8,128)(2,1)} %collective-permute-done.6.refs_5_), channel_id=1, source_target_pairs={{0,64},{64,0},{1,65},{65,1},{2,66},{66,2},{3,67},{67,3},{4,68},{68... | collective-permute-start | bytes 1572872 | tf_op jit(solution)/shard_map/ppermute | solution.py:230
  65.1 40.8 %copy-start.3 = (bf16[256,1024]{1,0:T(8,128)(2,1)}, bf16[256,1024]{1,0:T(8,128)(2,1)S(1)}, u32[]{:S(2)}) copy-start(bf16[256,1024]{1,0:T(8,128)(2,1)S(1)} %get-tuple-element.66.refs_0_) | copy-start | bytes 1572868
  105.9 18.4 %all-to-all-start.2 = ((bf16[4,264,256]{2,1,0:T(8,128)(2,1)}), bf16[4,264,256]{2,1,0:T(8,128)(2,1)S(1)}, u32[]{:S(2)}, u32[]{:S(2)}) async-start(bf16[4,264,256]{2,1,0:T(8,128)(2,1)} %get-tuple-element.61), calls=%async_computation.2 | async-start | bytes 1081344 | tf_op jit(solution)/shard_map/all_to_all | solution.py:248
  109.4 18.8 %collective-permute-start.9 = (bf16[2,64,256]{2,1,0:T(8,128)(2,1)S(1)}, bf16[2,64,256]{2,1,0:T(8,128)(2,1)S(1)}, u32[]{:S(2)}, u32[]{:S(2)}) collective-permute-start(bf16[2,64,256]{2,1,0:T(8,128)(2,1)S(1)} %get-tuple-element.62), channel_id=1, source_target_pairs={{0,0},{1,1},{2,130},{3,131},{4,260},{5,261},{6,390},{7,391},{128,3... | collective-permute-start | bytes 196616 | tf_op jit(solution)/shard_map/ppermute | solution.py:249
  128.3 6.5 %copy-start.4 = (bf16[256,1024]{1,0:T(8,128)(2,1)S(1)}, bf16[256,1024]{1,0:T(8,128)(2,1)}, u32[]{:S(2)}) copy-start(bf16[256,1024]{1,0:T(8,128)(2,1)} %copy-done.3) | copy-start | bytes 1572868
  128.3 25.2 %all-to-all-start.3 = ((bf16[4,1032,128]{2,1,0:T(8,128)(2,1)}), bf16[4,1032,128]{2,1,0:T(8,128)(2,1)S(1)}, u32[]{:S(2)}, u32[]{:S(2)}) async-start(bf16[4,1032,128]{2,1,0:T(8,128)(2,1)} %shard_map.95), calls=%async_computation.3 | async-start | bytes 2113536 | tf_op jit(solution)/shard_map/all_to_all | solution.py:259
  132.8 13.7 %collective-permute-start.14 = (bf16[256,1024]{1,0:T(8,128)(2,1)}, bf16[256,1024]{1,0:T(8,128)(2,1)S(1)}, u32[]{:S(2)}, u32[]{:S(2)}) collective-permute-start(bf16[256,1024]{1,0:T(8,128)(2,1)} %get-tuple-element.71), channel_id=1, source_target_pairs={{0,1},{1,0},{2,3},{3,2},{4,5},{5,4},{6,7},{7,6},{8,9},{9,8},{10,11... | collective-permute-start | bytes 1572872 | tf_op jit(solution)/shard_map/ppermute | solution.py:266
  134.8 18.7 %collective-permute-start.10 = (bf16[256,1024]{1,0:T(8,128)(2,1)S(1)}, bf16[256,1024]{1,0:T(8,128)(2,1)S(1)}, u32[]{:S(2)}, u32[]{:S(2)}) collective-permute-start(bf16[256,1024]{1,0:T(8,128)(2,1)S(1)} %copy-done.4), channel_id=1, source_target_pairs={{0,64},{64,0},{1,65},{65,1},{2,66},{66,2},{3,67},{67,3},{4,68},{68... | collective-permute-start | bytes 1572872 | tf_op jit(solution)/shard_map/ppermute | solution.py:268
  139.9 22.2 %collective-permute-start.16 = (bf16[4,256,256]{2,1,0:T(8,128)(2,1)}, bf16[4,256,256]{2,1,0:T(8,128)(2,1)S(1)}, u32[]{:S(2)}, u32[]{:S(2)}) collective-permute-start(bf16[4,256,256]{2,1,0:T(8,128)(2,1)} %get-tuple-element.73.refs_4_), channel_id=1, source_target_pairs={{0,1},{1,0},{2,3},{3,2},{4,5},{5,4},{6,7},{7,6},{8,9},{9,8},{10,11... | collective-permute-start | bytes 1572872 | tf_op jit(solution)/shard_map/ppermute | solution.py:267
  143.5 10.0 %collective-permute-start.11 = (bf16[2,256,256]{2,1,0:T(8,128)(2,1)S(1)}, bf16[2,256,256]{2,1,0:T(8,128)(2,1)S(1)}, u32[]{:S(2)}, u32[]{:S(2)}) collective-permute-start(bf16[2,256,256]{2,1,0:T(8,128)(2,1)S(1)} %get-tuple-element.68), channel_id=1, source_target_pairs={{0,64},{64,0},{1,65},{65,1},{2,66},{66,2},{3,67},{67,3},{4,68},{68... | collective-permute-start | bytes 786440 | tf_op jit(solution)/shard_map/ppermute | solution.py:269
  146.6 21.3 %collective-permute-start.15 = (bf16[256,1024]{1,0:T(8,128)(2,1)S(1)}, bf16[256,1024]{1,0:T(8,128)(2,1)}, u32[]{:S(2)}, u32[]{:S(2)}) collective-permute-start(bf16[256,1024]{1,0:T(8,128)(2,1)S(1)} %collective-permute-done.14.refs_1_), channel_id=1, source_target_pairs={{0,64},{64,0},{1,65},{65,1},{2,66},{66,2},{3,67},{67,3},{4,68},{68... | collective-permute-start | bytes 1572872 | tf_op jit(solution)/shard_map/ppermute | solution.py:275
  154.4 18.0 %all-to-all-start.4 = ((bf16[16,72,128]{2,1,0:T(8,128)(2,1)}), bf16[16,72,128]{2,1,0:T(8,128)(2,1)S(1)}, u32[]{:S(2)}, u32[]{:S(2)}) async-start(bf16[16,72,128]{2,1,0:T(8,128)(2,1)} %shard_map.97), calls=%async_computation.4 | async-start | bytes 589824 | tf_op jit(solution)/shard_map/all_to_all | solution.py:272
  161.4 2.9 %collective-permute-start.12 = (bf16[2,64,256]{2,1,0:T(8,128)(2,1)S(1)}, bf16[2,64,256]{2,1,0:T(8,128)(2,1)S(1)}, u32[]{:S(2)}, u32[]{:S(2)}) collective-permute-start(bf16[2,64,256]{2,1,0:T(8,128)(2,1)S(1)} %collective-permute-done.9), channel_id=1, source_target_pairs={{0,0},{1,1},{2,2},{3,3},{4,4},{5,5},{6,6},{7,7},{130,128},{131,129... | collective-permute-start | bytes 196616 | tf_op jit(solution)/shard_map/ppermute | solution.py:273
  162.1 5.8 %collective-permute-start.17 = (bf16[2,256,256]{2,1,0:T(8,128)(2,1)S(1)}, bf16[2,256,256]{2,1,0:T(8,128)(2,1)S(1)}, u32[]{:S(2)}, u32[]{:S(2)}) collective-permute-start(bf16[2,256,256]{2,1,0:T(8,128)(2,1)S(1)} %slice.9), channel_id=1, source_target_pairs={{0,64},{64,0},{1,65},{65,1},{2,66},{66,2},{3,67},{67,3},{4,68},{68... | collective-permute-start | bytes 786440 | tf_op jit(solution)/shard_map/ppermute | solution.py:276
  164.3 7.1 %collective-permute-start.13 = (bf16[64,256]{1,0:T(8,128)(2,1)S(1)}, bf16[64,256]{1,0:T(8,128)(2,1)S(1)}, u32[]{:S(2)}, u32[]{:S(2)}) collective-permute-start(bf16[64,256]{1,0:T(8,128)(2,1)S(1)} %slice_bitcast_fusion), channel_id=1, source_target_pairs={{0,1},{1,0},{2,3},{3,2},{4,5},{5,4},{6,7},{7,6},{8,9},{9,8},{10,11... | collective-permute-start | bytes 98312 | tf_op jit(solution)/shard_map/ppermute | solution.py:274
  173.6 4.8 %collective-permute-start.18 = (f32[8,128]{1,0:T(8,128)S(1)}, f32[8,128]{1,0:T(8,128)S(1)}, u32[]{:S(2)}, u32[]{:S(2)}) collective-permute-start(f32[8,128]{1,0:T(8,128)S(1)} %get-tuple-element.84.mine_ref), channel_id=1, source_target_pairs={{0,64},{64,0},{1,65},{65,1},{2,66},{66,2},{3,67},{67,3},{4,68},{68... | collective-permute-start | bytes 12296 | tf_op jit(solution)/shard_map/ppermute | solution.py:285

commit v8 on v7

--- a/solution.py
+++ b/solution.py
@@ -218,15 +218,12 @@
     place = jnp.stack([lax.axis_index("c"), lax.axis_index("h"), lax.axis_index("p"), side])
 
     copies, scal = call(scale_body, [((2 * nh * nx * nw, rows, width), BF16), ((8, 128), F32)], (history, tokens))
+    up = lax.ppermute(upstream, column_axis, along_y)
+    copies, up = lax.optimization_barrier((copies, up))
     x_all = lax.all_to_all(copies, plane, 0, 0, tiled=True)
     near = [w_gate, w_up]
     far = [lax.ppermute(w, "t", swap) for w in near]
-    up = lax.ppermute(upstream, column_axis, along_y)
-    up = lax.ppermute(up, column_axis, along_z).reshape(2, rows, units)
-    up_got = lax.ppermute(lax.dynamic_index_in_dim(up, 1 - side, 0, keepdims=False), "t", swap)
-    up = lax.dynamic_index_in_dim(up, side, 0, keepdims=False)
     near += [lax.ppermute(w, "c", swap) for w in near]
-    up, up_got, *far = lax.optimization_barrier((up, up_got, *far))
     far += [lax.ppermute(w, "c", swap) for w in far]
     x_all, *weights = lax.optimization_barrier((x_all, *near, *far))
 
@@ -238,7 +235,12 @@
         flops=work,
         moved=8 * 2**20,
     )
+    parts, up = lax.optimization_barrier((parts, up))
     sums = lax.all_to_all(parts, "p", 0, 0, tiled=True)
+    up = lax.ppermute(up, column_axis, along_z).reshape(2, rows, units)
+    up_got = lax.ppermute(lax.dynamic_index_in_dim(up, 1 - side, 0, keepdims=False), "t", swap)
+    up = lax.dynamic_index_in_dim(up, side, 0, keepdims=False)
+    sums, up, up_got = lax.optimization_barrier((sums, up, up_got))
     hidden, quants = call(
         middle_body,
         [((2, rows, units), BF16), ((np, 4 * rows + 8, units), BF16)],
@@ -263,6 +265,8 @@
         (place, q_all),
         moved=2**20,
     )
+    hidden = lax.ppermute(hidden, column_axis, back_y)
+    x_far, q_mine, hidden = lax.optimization_barrier((x_far, q_mine, hidden))
     x_side = lax.ppermute(x_far, "t", swap)
     q_side = lax.ppermute(q_mine, "t", swap)
     x_other = lax.ppermute(x_near, "c", swap)
@@ -270,17 +274,16 @@
     back_cols, x_other, q_other = lax.optimization_barrier((back_cols, x_other, q_other))
     (column,) = call(column_body, [((2 * nh * nw, rows + 8, width), BF16)], (back_cols,), moved=2**20)
     back_all = lax.all_to_all(column, last_stage, 0, 0, tiled=True)
-    hidden = lax.ppermute(hidden, column_axis, back_y)
     hidden_got = lax.ppermute(hidden[1], "t", swap)
     xs = (x_near, x_side, x_other, lax.ppermute(x_side, "c", swap))
     qs = (q_mine, q_side, q_other, lax.ppermute(q_side[2:], "c", swap))
-    grads = call(weights_body, [((depth, units), BF16)] * 2, (*xs, *qs, scal), flops=work, moved=2**22)
+    grads = call(weights_body, [((depth, units), BF16)] * 2, (*xs, *qs, scal))
     back_all, hidden, hidden_got, *grads = lax.optimization_barrier((back_all, hidden, hidden_got, *grads))
     input_grad, peaks, hidden = call(
         last_body,
         [((2 * rows, width), BF16), ((8, 128), F32), ((2 * rows, units), BF16)],
         (place, back_all, scal, hidden, hidden_got),
-        moved=2**20,
+        moved=2**28,
     )
     peaks_other = lax.ppermute(peaks, "c", swap)
     (new_history,) = call(history_body, [(history.shape, F32)], (history, peaks, peaks_other))

time: 181 us -> 174 us (0.961)
  blocking collectives: 39.1 us -> 0 us
  starting transfers between devices: 81 us -> 107 us
  local copies, waits for them, and re-layouts: 2.23 us -> 6.92 us
  waiting for transfers between devices: 38.9 us -> 41.4 us
    all_to_all x1 -> x0, blocking collectives: 39.1 us -> none  [per_device(): sums = lax.all_to_all(parts, 'p', 0, 0, tiled=True)]
    ppermute x2, waiting for transfers between devices: 0.01 us -> 14.7 us  [per_device(): far = [lax.ppermute(w, 't', swap) for w in near]]
    ppermute x1, waiting for transfers between devices: 19.8 us -> 7.51 us  [per_device(): lax.ppermute(lax.dynamic_index_in_dim(up, 1 - side, 0, keepdims=False), '...]
    all_to_all x1, starting transfers between devices: 7.02 us -> 14.5 us  [per_device(): back_all = lax.all_to_all(column, last_stage, 0, 0, tiled=True)]
    all_to_all x0 -> x1, starting transfers between devices: none -> 6.4 us  [per_device(): sums = lax.all_to_all(parts, 'p', 0, 0, tiled=True)]
    ppermute x2, starting transfers between devices: 5.58 us -> 11.8 us  [per_device(): far += [lax.ppermute(w, 'c', swap) for w in far]]
    all_to_all x1, starting transfers between devices: 15.5 us -> 20.5 us  [per_device(): x_all = lax.all_to_all(copies, plane, 0, 0, tiled=True)]
    unnamed x14 -> x20, local copies, waits for them, and re-layouts: 2.19 us -> 6.89 us
  transfers between devices with their start and end apart: 23 -> 24, of which waited for: 6 -> 8; matrix products, arithmetic and copies ran while one was open for 0% -> 1% of each run, Pallas kernels for 5% -> 6%
where the time goes in v8:
time: 174 us; the launch traced here: 173 us
  starting transfers between devices  107 us (61%)
  waiting for transfers between devices  41.4 us (24%)
  Pallas kernels  16.4 us (9%)
  local copies, waits for them, and re-layouts  6.92 us (4%)
    all_to_all x1, starting transfers between devices, per_device(): x_all = lax.all_to_all(copies, plane, 0, 0, tiled=True)  20.5 us
    pallas_call x9, Pallas kernels, call(): pl.pallas_call(body, out_shape=[jax.ShapeDtypeStruct(s, t) for s, t in ou...  16.4 us
    ppermute x2, waiting for transfers between devices, per_device(): far = [lax.ppermute(w, 't', swap) for w in near]  14.7 us
    all_to_all x1, starting transfers between devices, per_device(): back_all = lax.all_to_all(column, last_stage, 0, 0, tiled=True)  14.5 us
    all_to_all x1, waiting for transfers between devices, per_device(): q_all = lax.all_to_all(quants, 'p', 0, 0, tiled=True)  12.2 us
    ppermute x2, starting transfers between devices, per_device(): far += [lax.ppermute(w, 'c', swap) for w in far]  11.8 us
    ppermute x1, waiting for transfers between devices, per_device(): lax.ppermute(lax.dynamic_index_in_dim(up, 1 - side, 0, keepdims=False), '...  7.51 us
    unnamed x20, local copies, waits for them, and re-layouts  6.89 us
  transfers between devices with their start and end apart: 24, of which 8 were waited for; matrix products, arithmetic and copies ran while one was open for 1% of the time, Pallas kernels for 6%

profile of v8, /device:TPU:1, one launch (start us, length us, event | category | flops | bytes accessed | tf_op | source)
XLA Modules:
  0.0 172.6 jit_solution(10886861457518504071)
XLA Ops:
  0.6 1.5 collective-permute-start
  2.1 0.8 copy.10.hist_ref
  2.9 0.8 copy-done
  3.6 1.1 shard_map.92
  4.8 0.0 collective-permute-done
  4.8 20.5 %all-to-all-start = ((bf16[64,64,128]{2,1,0:T(8,128)(2,1)}), bf16[64,64,128]{2,1,0:T(8,128)(2,1)S(1)}, u32[]{:S(2)}, u32[]{:S(2)}) async-start(bf16[64,64,128]{2,1,0:T(8,128)(2,1)} %get-tuple-element.52), calls=%async_computation | async-start | bytes 2097152 | tf_op jit(solution)/shard_map/all_to_all | solution.py:223
  25.3 2.9 %collective-permute-start.3 = (bf16[1024,256]{1,0:T(8,128)(2,1)S(1)}, bf16[1024,256]{1,0:T(8,128)(2,1)S(1)}, u32[]{:S(2)}, u32[]{:S(2)}) collective-permute-start(bf16[1024,256]{1,0:T(8,128)(2,1)S(1)} %copy-done.1), channel_id=1, source_target_pairs={{0,1},{1,0},{2,3},{3,2},{4,5},{5,4},{6,7},{7,6},{8,9},{9,8},{10,11... | collective-permute-start | bytes 1572872 | tf_op jit(solution)/shard_map/ppermute | solution.py:225
  28.3 2.4 %collective-permute-start.4 = (bf16[1024,256]{1,0:T(8,128)(2,1)S(1)}, bf16[1024,256]{1,0:T(8,128)(2,1)S(1)}, u32[]{:S(2)}, u32[]{:S(2)}) collective-permute-start(bf16[1024,256]{1,0:T(8,128)(2,1)S(1)} %copy-done.2), channel_id=1, source_target_pairs={{0,1},{1,0},{2,3},{3,2},{4,5},{5,4},{6,7},{7,6},{8,9},{9,8},{10,11... | collective-permute-start | bytes 1572872 | tf_op jit(solution)/shard_map/ppermute | solution.py:225
  30.7 4.3 %collective-permute-start.1 = (bf16[1024,256]{1,0:T(8,128)(2,1)S(1)}, bf16[1024,256]{1,0:T(8,128)(2,1)}, u32[]{:S(2)}, u32[]{:S(2)}) collective-permute-start(bf16[1024,256]{1,0:T(8,128)(2,1)S(1)} %copy-done.1), channel_id=1, source_target_pairs={{0,64},{64,0},{1,65},{65,1},{2,66},{66,2},{3,67},{67,3},{4,68},{68... | collective-permute-start | bytes 1572872 | tf_op jit(solution)/shard_map/ppermute | solution.py:226
  35.0 1.9 %collective-permute-start.2 = (bf16[1024,256]{1,0:T(8,128)(2,1)S(1)}, bf16[1024,256]{1,0:T(8,128)(2,1)}, u32[]{:S(2)}, u32[]{:S(2)}) collective-permute-start(bf16[1024,256]{1,0:T(8,128)(2,1)S(1)} %copy-done.2), channel_id=1, source_target_pairs={{0,64},{64,0},{1,65},{65,1},{2,66},{66,2},{3,67},{67,3},{4,68},{68... | collective-permute-start | bytes 1572872 | tf_op jit(solution)/shard_map/ppermute | solution.py:226
  36.9 10.6 %collective-permute-done.3.refs_4_ = bf16[1024,256]{1,0:T(8,128)(2,1)S(1)} collective-permute-done((bf16[1024,256]{1,0:T(8,128)(2,1)S(1)}, bf16[1024,256]{1,0:T(8,128)(2,1)S(1)}, u32[]{:S(2)}, u32[]{:S(2)}) %collective-permute-start.3) | collective-permute-done | bytes 524320 | tf_op jit(solution)/shard_map/ppermute | solution.py:225
  47.5 7.1 %collective-permute-start.5 = (bf16[1024,256]{1,0:T(8,128)(2,1)S(1)}, bf16[1024,256]{1,0:T(8,128)(2,1)}, u32[]{:S(2)}, u32[]{:S(2)}) collective-permute-start(bf16[1024,256]{1,0:T(8,128)(2,1)S(1)} %collective-permute-done.3.refs_4_), channel_id=1, source_target_pairs={{0,64},{64,0},{1,65},{65,1},{2,66},{66,2},{3,67},{67,3},{4,68},{68... | collective-permute-start | bytes 1572872 | tf_op jit(solution)/shard_map/ppermute | solution.py:227
  54.6 4.1 %collective-permute-done.4.refs_5_ = bf16[1024,256]{1,0:T(8,128)(2,1)S(1)} collective-permute-done((bf16[1024,256]{1,0:T(8,128)(2,1)S(1)}, bf16[1024,256]{1,0:T(8,128)(2,1)S(1)}, u32[]{:S(2)}, u32[]{:S(2)}) %collective-permute-start.4) | collective-permute-done | bytes 524320 | tf_op jit(solution)/shard_map/ppermute | solution.py:225
  58.7 4.7 %collective-permute-start.6 = (bf16[1024,256]{1,0:T(8,128)(2,1)S(1)}, bf16[1024,256]{1,0:T(8,128)(2,1)}, u32[]{:S(2)}, u32[]{:S(2)}) collective-permute-start(bf16[1024,256]{1,0:T(8,128)(2,1)S(1)} %collective-permute-done.4.refs_5_), channel_id=1, source_target_pairs={{0,64},{64,0},{1,65},{65,1},{2,66},{66,2},{3,67},{67,3},{4,68},{68... | collective-permute-start | bytes 1572872 | tf_op jit(solution)/shard_map/ppermute | solution.py:227
  63.4 0.0 copy-start.5
  63.4 0.8 copy-done.5
  64.2 0.1 pad_add_fusion.place_ref
  64.3 0.0 collective-permute-done.1.refs_2_
  64.3 0.0 collective-permute-done.2.refs_3_
  64.3 0.0 collective-permute-done.5.refs_6_
  64.3 0.8 collective-permute-done.6.refs_7_
  65.1 0.0 all-to-all-done.x_ref
  65.1 1.0 copy-done.6
  66.1 3.7 %shard_map.93 = (bf16[4,256,256]{2,1,0:T(8,128)(2,1)}, bf16[256,1024]{1,0:T(8,128)(2,1)S(1)}, bf16[256,1024]{1,0:T(8,128)(2,1)S(1)}) custom-call(s32[4]{0:T(128)S(1)} %pad_add_fusion.place_ref, bf16[64,64,128]{2,1,0:T(8,128)(2,1)S(1)} %all-to-all-done.x_ref, bf16[1024,256]{1,0:T(8,128)(2,1)S(1)} %copy-done.1, bf16[1024,256]{1,0:T(8,128)(2,1)S(1)} %copy-done.2, ...), custom_call_target="tpu_custom_call" | custom-call | flops 2147483648 | bytes 8388608 | tf_op jit(solution)/shard_map/pallas_call | solution.py:20
  69.9 0.8 copy-done.8
  70.6 6.4 %all-to-all-start.1 = ((bf16[4,256,256]{2,1,0:T(8,128)(2,1)}), bf16[4,256,256]{2,1,0:T(8,128)(2,1)S(1)}, u32[]{:S(2)}, u32[]{:S(2)}) async-start(bf16[4,256,256]{2,1,0:T(8,128)(2,1)} %get-tuple-element.64), calls=%async_computation.1 | async-start | bytes 1048576 | tf_op jit(solution)/shard_map/all_to_all | solution.py:239
  77.0 0.7 collective-permute-start.7
  77.7 0.0 collective-permute-done.7
  77.7 1.9 %collective-permute-start.8 = (bf16[64,256]{1,0:T(8,128)(2,1)S(1)}, bf16[64,256]{1,0:T(8,128)(2,1)S(1)}, u32[]{:S(2)}, u32[]{:S(2)}) collective-permute-start(bf16[64,256]{1,0:T(8,128)(2,1)S(1)} %get-tuple-element.102), channel_id=1, source_target_pairs={{0,1},{1,0},{2,3},{3,2},{4,5},{5,4},{6,7},{7,6},{8,9},{9,8},{10,11... | collective-permute-start | bytes 98312 | tf_op jit(solution)/shard_map/ppermute | solution.py:241
  79.7 7.5 %collective-permute-done.8.up_got_ref = bf16[64,256]{1,0:T(8,128)(2,1)S(1)} collective-permute-done((bf16[64,256]{1,0:T(8,128)(2,1)S(1)}, bf16[64,256]{1,0:T(8,128)(2,1)S(1)}, u32[]{:S(2)}, u32[]{:S(2)}) %collective-permute-start.8) | collective-permute-done | bytes 32800 | tf_op jit(solution)/shard_map/ppermute | solution.py:241
  87.2 3.9 %all-to-all-done.1.in_ref = bf16[4,256,256]{2,1,0:T(8,128)(2,1)S(1)} async-done(((bf16[4,256,256]{2,1,0:T(8,128)(2,1)}), bf16[4,256,256]{2,1,0:T(8,128)(2,1)S(1)}, u32[]{:S(2)}, u32[]{:S(2)}) %all-to-all-start.1) | async-done | bytes 524320 | tf_op jit(solution)/shard_map/all_to_all | solution.py:239
  91.1 1.6 shard_map.94
  92.7 6.5 %all-to-all-start.2 = ((bf16[4,264,256]{2,1,0:T(8,128)(2,1)}), bf16[4,264,256]{2,1,0:T(8,128)(2,1)S(1)}, u32[]{:S(2)}, u32[]{:S(2)}) async-start(bf16[4,264,256]{2,1,0:T(8,128)(2,1)} %get-tuple-element.70), calls=%async_computation.2 | async-start | bytes 1081344 | tf_op jit(solution)/shard_map/all_to_all | solution.py:250
  99.2 0.7 collective-permute-start.9
  99.8 12.2 %all-to-all-done.2.q_ref = bf16[4,264,256]{2,1,0:T(8,128)(2,1)S(1)} async-done(((bf16[4,264,256]{2,1,0:T(8,128)(2,1)}), bf16[4,264,256]{2,1,0:T(8,128)(2,1)S(1)}, u32[]{:S(2)}, u32[]{:S(2)}) %all-to-all-start.2) | async-done | bytes 540704 | tf_op jit(solution)/shard_map/all_to_all | solution.py:250
  112.0 1.0 copy-done.4
  113.1 1.0 copy-done.7
  114.1 3.8 %shard_map.95 = bf16[4,1032,128]{2,1,0:T(8,128)(2,1)} custom-call(s32[4]{0:T(128)S(1)} %pad_add_fusion.place_ref, bf16[4,264,256]{2,1,0:T(8,128)(2,1)S(1)} %all-to-all-done.2.q_ref, bf16[1024,256]{1,0:T(8,128)(2,1)S(1)} %copy-done.1, bf16[1024,256]{1,0:T(8,128)(2,1)S(1)} %copy-done.2, bf16[1024,256]{1,0:T(8,128)(2,1)} %collective-permute-done.1.refs_2_, ...), custom_call_target="tpu_custom_call" | custom-call | flops 2147483648 | bytes 8388608 | tf_op jit(solution)/shard_map/pallas_call | solution.py:20
  117.9 0.0 collective-permute-done.9
  117.9 4.3 %all-to-all-start.3 = ((bf16[4,1032,128]{2,1,0:T(8,128)(2,1)}), bf16[4,1032,128]{2,1,0:T(8,128)(2,1)S(1)}, u32[]{:S(2)}, u32[]{:S(2)}) async-start(bf16[4,1032,128]{2,1,0:T(8,128)(2,1)} %shard_map.95), calls=%async_computation.3 | async-start | bytes 2113536 | tf_op jit(solution)/shard_map/all_to_all | solution.py:261
  122.3 0.7 collective-permute-start.12
  122.9 6.7 %collective-permute-start.10 = (bf16[256,1024]{1,0:T(8,128)(2,1)S(1)}, bf16[256,1024]{1,0:T(8,128)(2,1)S(1)}, u32[]{:S(2)}, u32[]{:S(2)}) collective-permute-start(bf16[256,1024]{1,0:T(8,128)(2,1)S(1)} %get-tuple-element.75.refs_0_), channel_id=1, source_target_pairs={{0,64},{64,0},{1,65},{65,1},{2,66},{66,2},{3,67},{67,3},{4,68},{68... | collective-permute-start | bytes 1572872 | tf_op jit(solution)/shard_map/ppermute | solution.py:272
  129.7 0.6 shard_map.96
  130.3 0.0 collective-permute-done.12.hidden_ref
  130.3 1.9 %collective-permute-start.14 = (bf16[256,1024]{1,0:T(8,128)(2,1)}, bf16[256,1024]{1,0:T(8,128)(2,1)}, u32[]{:S(2)}, u32[]{:S(2)}) collective-permute-start(bf16[256,1024]{1,0:T(8,128)(2,1)} %copy-done.8), channel_id=1, source_target_pairs={{0,1},{1,0},{2,3},{3,2},{4,5},{5,4},{6,7},{7,6},{8,9},{9,8},{10,11... | collective-permute-start | bytes 1572872 | tf_op jit(solution)/shard_map/ppermute | solution.py:270
  132.2 1.9 %collective-permute-start.11 = (bf16[2,256,256]{2,1,0:T(8,128)(2,1)S(1)}, bf16[2,256,256]{2,1,0:T(8,128)(2,1)S(1)}, u32[]{:S(2)}, u32[]{:S(2)}) collective-permute-start(bf16[2,256,256]{2,1,0:T(8,128)(2,1)S(1)} %get-tuple-element.77), channel_id=1, source_target_pairs={{0,64},{64,0},{1,65},{65,1},{2,66},{66,2},{3,67},{67,3},{4,68},{68... | collective-permute-start | bytes 786440 | tf_op jit(solution)/shard_map/ppermute | solution.py:273
  134.2 3.6 %collective-permute-start.16 = (bf16[4,256,256]{2,1,0:T(8,128)(2,1)S(1)}, bf16[4,256,256]{2,1,0:T(8,128)(2,1)S(1)}, u32[]{:S(2)}, u32[]{:S(2)}) collective-permute-start(bf16[4,256,256]{2,1,0:T(8,128)(2,1)S(1)} %get-tuple-element.85.refs_4_), channel_id=1, source_target_pairs={{0,1},{1,0},{2,3},{3,2},{4,5},{5,4},{6,7},{7,6},{8,9},{9,8},{10,11... | collective-permute-start | bytes 1572872 | tf_op jit(solution)/shard_map/ppermute | solution.py:271
  137.8 0.0 collective-permute-done.10.refs_2_
  137.8 0.0 all-to-all-done.3.in_ref
  137.8 0.9 shard_map.97
  138.7 14.5 %all-to-all-start.4 = ((bf16[16,72,128]{2,1,0:T(8,128)(2,1)}), bf16[16,72,128]{2,1,0:T(8,128)(2,1)S(1)}, u32[]{:S(2)}, u32[]{:S(2)}) async-start(bf16[16,72,128]{2,1,0:T(8,128)(2,1)} %shard_map.97), calls=%async_computation.4 | async-start | bytes 589824 | tf_op jit(solution)/shard_map/all_to_all | solution.py:276
  153.3 2.5 %collective-permute-start.15 = (bf16[256,1024]{1,0:T(8,128)(2,1)}, bf16[256,1024]{1,0:T(8,128)(2,1)S(1)}, u32[]{:S(2)}, u32[]{:S(2)}) collective-permute-start(bf16[256,1024]{1,0:T(8,128)(2,1)} %collective-permute-done.14.refs_1_), channel_id=1, source_target_pairs={{0,64},{64,0},{1,65},{65,1},{2,66},{66,2},{3,67},{67,3},{4,68},{68... | collective-permute-start | bytes 1572872 | tf_op jit(solution)/shard_map/ppermute | solution.py:278
  155.7 1.4 collective-permute-done.16.refs_5_
  157.2 3.1 %collective-permute-start.17 = (bf16[2,256,256]{2,1,0:T(8,128)(2,1)S(1)}, bf16[2,256,256]{2,1,0:T(8,128)(2,1)S(1)}, u32[]{:S(2)}, u32[]{:S(2)}) collective-permute-start(bf16[2,256,256]{2,1,0:T(8,128)(2,1)S(1)} %slice.8), channel_id=1, source_target_pairs={{0,64},{64,0},{1,65},{65,1},{2,66},{66,2},{3,67},{67,3},{4,68},{68... | collective-permute-start | bytes 786440 | tf_op jit(solution)/shard_map/ppermute | solution.py:279
  160.3 1.9 %collective-permute-start.13 = (bf16[64,256]{1,0:T(8,128)(2,1)S(1)}, bf16[64,256]{1,0:T(8,128)(2,1)S(1)}, u32[]{:S(2)}, u32[]{:S(2)}) collective-permute-start(bf16[64,256]{1,0:T(8,128)(2,1)S(1)} %slice_bitcast_fusion), channel_id=1, source_target_pairs={{0,1},{1,0},{2,3},{3,2},{4,5},{5,4},{6,7},{7,6},{8,9},{9,8},{10,11... | collective-permute-start | bytes 98312 | tf_op jit(solution)/shard_map/ppermute | solution.py:277
  162.3 0.0 collective-permute-done.15.refs_3_
  162.3 3.3 %shard_map.98 = (bf16[1024,256]{1,0:T(8,128)(2,1)}, bf16[1024,256]{1,0:T(8,128)(2,1)}) custom-call(bf16[256,1024]{1,0:T(8,128)(2,1)S(1)} %get-tuple-element.75.refs_0_, bf16[256,1024]{1,0:T(8,128)(2,1)} %collective-permute-done.14.refs_1_, bf16[256,1024]{1,0:T(8,128)(2,1)S(1)} %collective-permute-done.10.refs_2_, ...), custom_call_target="tpu_custom_call" | custom-call | tf_op jit(solution)/shard_map/pallas_call | solution.py:20
  165.6 0.0 collective-permute-done.13.got_ref
  165.6 0.0 all-to-all-done.4.in_ref
  165.6 1.2 shard_map.99
  166.9 4.2 %collective-permute-start.18 = (f32[8,128]{1,0:T(8,128)S(1)}, f32[8,128]{1,0:T(8,128)S(1)}, u32[]{:S(2)}, u32[]{:S(2)}) collective-permute-start(f32[8,128]{1,0:T(8,128)S(1)} %get-tuple-element.96.mine_ref), channel_id=1, source_target_pairs={{0,64},{64,0},{1,65},{65,1},{2,66},{66,2},{3,67},{67,3},{4,68},{68... | collective-permute-start | bytes 12296 | tf_op jit(solution)/shard_map/ppermute | solution.py:288
  171.1 0.8 collective-permute-done.18.other_ref
  171.9 0.1 shard_map.100
  172.0 0.7 copy.12
  (17 shorter events, 0.1 us)
Async XLA Ops:
  0.6 4.2 %collective-permute-start = (bf16[128,256]{1,0:T(8,128)(2,1)}, bf16[128,256]{1,0:T(8,128)(2,1)S(1)}, u32[]{:S(2)}, u32[]{:S(2)}) collective-permute-start(bf16[128,256]{1,0:T(8,128)(2,1)} %param.8), channel_id=1, source_target_pairs={{0,0},{1,1},{2,2},{3,3},{4,4},{5,5},{6,6},{7,7},{128,130},{129,131... | collective-permute-start | bytes 196616 | tf_op jit(solution)/shard_map/ppermute | solution.py:221
  2.9 0.8 copy-start
  4.8 20.5 %copy-start.1 = (bf16[1024,256]{1,0:T(8,128)(2,1)S(1)}, bf16[1024,256]{1,0:T(8,128)(2,1)}, u32[]{:S(2)}) copy-start(bf16[1024,256]{1,0:T(8,128)(2,1)} %refs_0_.1) | copy-start | bytes 1572868
  4.8 23.5 %copy-start.2 = (bf16[1024,256]{1,0:T(8,128)(2,1)S(1)}, bf16[1024,256]{1,0:T(8,128)(2,1)}, u32[]{:S(2)}) copy-start(bf16[1024,256]{1,0:T(8,128)(2,1)} %refs_1_.1) | copy-start | bytes 1572868
  4.8 60.3 %all-to-all-start = ((bf16[64,64,128]{2,1,0:T(8,128)(2,1)}), bf16[64,64,128]{2,1,0:T(8,128)(2,1)S(1)}, u32[]{:S(2)}, u32[]{:S(2)}) async-start(bf16[64,64,128]{2,1,0:T(8,128)(2,1)} %get-tuple-element.52), calls=%async_computation | async-start | bytes 2097152 | tf_op jit(solution)/shard_map/all_to_all | solution.py:223
  25.3 22.2 %collective-permute-start.3 = (bf16[1024,256]{1,0:T(8,128)(2,1)S(1)}, bf16[1024,256]{1,0:T(8,128)(2,1)S(1)}, u32[]{:S(2)}, u32[]{:S(2)}) collective-permute-start(bf16[1024,256]{1,0:T(8,128)(2,1)S(1)} %copy-done.1), channel_id=1, source_target_pairs={{0,1},{1,0},{2,3},{3,2},{4,5},{5,4},{6,7},{7,6},{8,9},{9,8},{10,11... | collective-permute-start | bytes 1572872 | tf_op jit(solution)/shard_map/ppermute | solution.py:225
  28.3 30.5 %collective-permute-start.4 = (bf16[1024,256]{1,0:T(8,128)(2,1)S(1)}, bf16[1024,256]{1,0:T(8,128)(2,1)S(1)}, u32[]{:S(2)}, u32[]{:S(2)}) collective-permute-start(bf16[1024,256]{1,0:T(8,128)(2,1)S(1)} %copy-done.2), channel_id=1, source_target_pairs={{0,1},{1,0},{2,3},{3,2},{4,5},{5,4},{6,7},{7,6},{8,9},{9,8},{10,11... | collective-permute-start | bytes 1572872 | tf_op jit(solution)/shard_map/ppermute | solution.py:225
  30.7 33.7 %collective-permute-start.1 = (bf16[1024,256]{1,0:T(8,128)(2,1)S(1)}, bf16[1024,256]{1,0:T(8,128)(2,1)}, u32[]{:S(2)}, u32[]{:S(2)}) collective-permute-start(bf16[1024,256]{1,0:T(8,128)(2,1)S(1)} %copy-done.1), channel_id=1, source_target_pairs={{0,64},{64,0},{1,65},{65,1},{2,66},{66,2},{3,67},{67,3},{4,68},{68... | collective-permute-start | bytes 1572872 | tf_op jit(solution)/shard_map/ppermute | solution.py:226
  35.0 29.3 %collective-permute-start.2 = (bf16[1024,256]{1,0:T(8,128)(2,1)S(1)}, bf16[1024,256]{1,0:T(8,128)(2,1)}, u32[]{:S(2)}, u32[]{:S(2)}) collective-permute-start(bf16[1024,256]{1,0:T(8,128)(2,1)S(1)} %copy-done.2), channel_id=1, source_target_pairs={{0,64},{64,0},{1,65},{65,1},{2,66},{66,2},{3,67},{67,3},{4,68},{68... | collective-permute-start | bytes 1572872 | tf_op jit(solution)/shard_map/ppermute | solution.py:226
  47.5 22.3 %copy-start.3 = (bf16[1024,256]{1,0:T(8,128)(2,1)}, bf16[1024,256]{1,0:T(8,128)(2,1)S(1)}, u32[]{:S(2)}) copy-start(bf16[1024,256]{1,0:T(8,128)(2,1)S(1)} %collective-permute-done.3.refs_4_) | copy-start | bytes 1572868
  47.5 16.8 %collective-permute-start.5 = (bf16[1024,256]{1,0:T(8,128)(2,1)S(1)}, bf16[1024,256]{1,0:T(8,128)(2,1)}, u32[]{:S(2)}, u32[]{:S(2)}) collective-permute-start(bf16[1024,256]{1,0:T(8,128)(2,1)S(1)} %collective-permute-done.3.refs_4_), channel_id=1, source_target_pairs={{0,64},{64,0},{1,65},{65,1},{2,66},{66,2},{3,67},{67,3},{4,68},{68... | collective-permute-start | bytes 1572872 | tf_op jit(solution)/shard_map/ppermute | solution.py:227
  58.7 6.3 %collective-permute-start.6 = (bf16[1024,256]{1,0:T(8,128)(2,1)S(1)}, bf16[1024,256]{1,0:T(8,128)(2,1)}, u32[]{:S(2)}, u32[]{:S(2)}) collective-permute-start(bf16[1024,256]{1,0:T(8,128)(2,1)S(1)} %collective-permute-done.4.refs_5_), channel_id=1, source_target_pairs={{0,64},{64,0},{1,65},{65,1},{2,66},{66,2},{3,67},{67,3},{4,68},{68... | collective-permute-start | bytes 1572872 | tf_op jit(solution)/shard_map/ppermute | solution.py:227
  63.4 0.8 copy-start.5
  65.1 1.0 copy-start.6
  69.8 0.8 copy-start.8
  70.6 20.4 %all-to-all-start.1 = ((bf16[4,256,256]{2,1,0:T(8,128)(2,1)}), bf16[4,256,256]{2,1,0:T(8,128)(2,1)S(1)}, u32[]{:S(2)}, u32[]{:S(2)}) async-start(bf16[4,256,256]{2,1,0:T(8,128)(2,1)} %get-tuple-element.64), calls=%async_computation.1 | async-start | bytes 1048576 | tf_op jit(solution)/shard_map/all_to_all | solution.py:239
  77.0 0.7 collective-permute-start.7
  77.7 9.4 %collective-permute-start.8 = (bf16[64,256]{1,0:T(8,128)(2,1)S(1)}, bf16[64,256]{1,0:T(8,128)(2,1)S(1)}, u32[]{:S(2)}, u32[]{:S(2)}) collective-permute-start(bf16[64,256]{1,0:T(8,128)(2,1)S(1)} %get-tuple-element.102), channel_id=1, source_target_pairs={{0,1},{1,0},{2,3},{3,2},{4,5},{5,4},{6,7},{7,6},{8,9},{9,8},{10,11... | collective-permute-start | bytes 98312 | tf_op jit(solution)/shard_map/ppermute | solution.py:241
  92.7 19.3 %all-to-all-start.2 = ((bf16[4,264,256]{2,1,0:T(8,128)(2,1)}), bf16[4,264,256]{2,1,0:T(8,128)(2,1)S(1)}, u32[]{:S(2)}, u32[]{:S(2)}) async-start(bf16[4,264,256]{2,1,0:T(8,128)(2,1)} %get-tuple-element.70), calls=%async_computation.2 | async-start | bytes 1081344 | tf_op jit(solution)/shard_map/all_to_all | solution.py:250
  99.2 18.8 %collective-permute-start.9 = (bf16[2,64,256]{2,1,0:T(8,128)(2,1)S(1)}, bf16[2,64,256]{2,1,0:T(8,128)(2,1)S(1)}, u32[]{:S(2)}, u32[]{:S(2)}) collective-permute-start(bf16[2,64,256]{2,1,0:T(8,128)(2,1)S(1)} %get-tuple-element.71), channel_id=1, source_target_pairs={{0,0},{1,1},{2,130},{3,131},{4,260},{5,261},{6,390},{7,391},{128,3... | collective-permute-start | bytes 196616 | tf_op jit(solution)/shard_map/ppermute | solution.py:251
  112.0 1.0 copy-start.4
  113.1 1.0 copy-start.7
  117.9 19.9 %all-to-all-start.3 = ((bf16[4,1032,128]{2,1,0:T(8,128)(2,1)}), bf16[4,1032,128]{2,1,0:T(8,128)(2,1)S(1)}, u32[]{:S(2)}, u32[]{:S(2)}) async-start(bf16[4,1032,128]{2,1,0:T(8,128)(2,1)} %shard_map.95), calls=%async_computation.3 | async-start | bytes 2113536 | tf_op jit(solution)/shard_map/all_to_all | solution.py:261
  122.3 8.0 %collective-permute-start.12 = (bf16[2,64,256]{2,1,0:T(8,128)(2,1)S(1)}, bf16[2,64,256]{2,1,0:T(8,128)(2,1)S(1)}, u32[]{:S(2)}, u32[]{:S(2)}) collective-permute-start(bf16[2,64,256]{2,1,0:T(8,128)(2,1)S(1)} %collective-permute-done.9), channel_id=1, source_target_pairs={{0,0},{1,1},{2,2},{3,3},{4,4},{5,5},{6,6},{7,7},{130,128},{131,129... | collective-permute-start | bytes 196616 | tf_op jit(solution)/shard_map/ppermute | solution.py:268
  122.9 14.9 %collective-permute-start.10 = (bf16[256,1024]{1,0:T(8,128)(2,1)S(1)}, bf16[256,1024]{1,0:T(8,128)(2,1)S(1)}, u32[]{:S(2)}, u32[]{:S(2)}) collective-permute-start(bf16[256,1024]{1,0:T(8,128)(2,1)S(1)} %get-tuple-element.75.refs_0_), channel_id=1, source_target_pairs={{0,64},{64,0},{1,65},{65,1},{2,66},{66,2},{3,67},{67,3},{4,68},{68... | collective-permute-start | bytes 1572872 | tf_op jit(solution)/shard_map/ppermute | solution.py:272
  130.3 22.9 %collective-permute-start.14 = (bf16[256,1024]{1,0:T(8,128)(2,1)}, bf16[256,1024]{1,0:T(8,128)(2,1)}, u32[]{:S(2)}, u32[]{:S(2)}) collective-permute-start(bf16[256,1024]{1,0:T(8,128)(2,1)} %copy-done.8), channel_id=1, source_target_pairs={{0,1},{1,0},{2,3},{3,2},{4,5},{5,4},{6,7},{7,6},{8,9},{9,8},{10,11... | collective-permute-start | bytes 1572872 | tf_op jit(solution)/shard_map/ppermute | solution.py:270
  132.2 5.6 %collective-permute-start.11 = (bf16[2,256,256]{2,1,0:T(8,128)(2,1)S(1)}, bf16[2,256,256]{2,1,0:T(8,128)(2,1)S(1)}, u32[]{:S(2)}, u32[]{:S(2)}) collective-permute-start(bf16[2,256,256]{2,1,0:T(8,128)(2,1)S(1)} %get-tuple-element.77), channel_id=1, source_target_pairs={{0,64},{64,0},{1,65},{65,1},{2,66},{66,2},{3,67},{67,3},{4,68},{68... | collective-permute-start | bytes 786440 | tf_op jit(solution)/shard_map/ppermute | solution.py:273
  134.2 23.0 %collective-permute-start.16 = (bf16[4,256,256]{2,1,0:T(8,128)(2,1)S(1)}, bf16[4,256,256]{2,1,0:T(8,128)(2,1)S(1)}, u32[]{:S(2)}, u32[]{:S(2)}) collective-permute-start(bf16[4,256,256]{2,1,0:T(8,128)(2,1)S(1)} %get-tuple-element.85.refs_4_), channel_id=1, source_target_pairs={{0,1},{1,0},{2,3},{3,2},{4,5},{5,4},{6,7},{7,6},{8,9},{9,8},{10,11... | collective-permute-start | bytes 1572872 | tf_op jit(solution)/shard_map/ppermute | solution.py:271
  138.7 26.9 %all-to-all-start.4 = ((bf16[16,72,128]{2,1,0:T(8,128)(2,1)}), bf16[16,72,128]{2,1,0:T(8,128)(2,1)S(1)}, u32[]{:S(2)}, u32[]{:S(2)}) async-start(bf16[16,72,128]{2,1,0:T(8,128)(2,1)} %shard_map.97), calls=%async_computation.4 | async-start | bytes 589824 | tf_op jit(solution)/shard_map/all_to_all | solution.py:276
  153.3 9.0 %collective-permute-start.15 = (bf16[256,1024]{1,0:T(8,128)(2,1)}, bf16[256,1024]{1,0:T(8,128)(2,1)S(1)}, u32[]{:S(2)}, u32[]{:S(2)}) collective-permute-start(bf16[256,1024]{1,0:T(8,128)(2,1)} %collective-permute-done.14.refs_1_), channel_id=1, source_target_pairs={{0,64},{64,0},{1,65},{65,1},{2,66},{66,2},{3,67},{67,3},{4,68},{68... | collective-permute-start | bytes 1572872 | tf_op jit(solution)/shard_map/ppermute | solution.py:278
  157.2 5.0 %collective-permute-start.17 = (bf16[2,256,256]{2,1,0:T(8,128)(2,1)S(1)}, bf16[2,256,256]{2,1,0:T(8,128)(2,1)S(1)}, u32[]{:S(2)}, u32[]{:S(2)}) collective-permute-start(bf16[2,256,256]{2,1,0:T(8,128)(2,1)S(1)} %slice.8), channel_id=1, source_target_pairs={{0,64},{64,0},{1,65},{65,1},{2,66},{66,2},{3,67},{67,3},{4,68},{68... | collective-permute-start | bytes 786440 | tf_op jit(solution)/shard_map/ppermute | solution.py:279
  160.3 5.3 %collective-permute-start.13 = (bf16[64,256]{1,0:T(8,128)(2,1)S(1)}, bf16[64,256]{1,0:T(8,128)(2,1)S(1)}, u32[]{:S(2)}, u32[]{:S(2)}) collective-permute-start(bf16[64,256]{1,0:T(8,128)(2,1)S(1)} %slice_bitcast_fusion), channel_id=1, source_target_pairs={{0,1},{1,0},{2,3},{3,2},{4,5},{5,4},{6,7},{7,6},{8,9},{9,8},{10,11... | collective-permute-start | bytes 98312 | tf_op jit(solution)/shard_map/ppermute | solution.py:277
  166.9 5.1 %collective-permute-start.18 = (f32[8,128]{1,0:T(8,128)S(1)}, f32[8,128]{1,0:T(8,128)S(1)}, u32[]{:S(2)}, u32[]{:S(2)}) collective-permute-start(f32[8,128]{1,0:T(8,128)S(1)} %get-tuple-element.96.mine_ref), channel_id=1, source_target_pairs={{0,64},{64,0},{1,65},{65,1},{2,66},{66,2},{3,67},{67,3},{4,68},{68... | collective-permute-start | bytes 12296 | tf_op jit(solution)/shard_map/ppermute | solution.py:288

commit v9 on v3

--- a/solution.py
+++ b/solution.py
@@ -8,22 +8,20 @@
 
 F32 = jnp.float32
 BF16 = jnp.bfloat16
+STASH = 64
+ANY = pl.BlockSpec(memory_space=pl.ANY)
 VMEM = pl.BlockSpec(memory_space=pltpu.VMEM)
 SMEM = pl.BlockSpec(memory_space=pltpu.SMEM)
 
 
-def params():
-    return pltpu.CompilerParams(vmem_limit_bytes=16 * 1024 * 1024)
-
-
-def call(body, outs, args, flops=0, moved=0, scratch=()):
+def call(body, outs, args, flops=0, moved=0, scratch=(), vmem=48, far=(), far_outs=()):
     return pl.pallas_call(
         body,
         out_shape=[jax.ShapeDtypeStruct(s, t) for s, t in outs],
-        in_specs=[SMEM if a.dtype == jnp.int32 else VMEM for a in args],
-        out_specs=[VMEM] * len(outs),
+        in_specs=[SMEM if a.dtype == jnp.int32 else ANY if i in far else VMEM for i, a in enumerate(args)],
+        out_specs=[ANY if i in far_outs else VMEM for i in range(len(outs))],
         scratch_shapes=list(scratch),
-        compiler_params=params(),
+        compiler_params=pltpu.CompilerParams(vmem_limit_bytes=vmem * 2**20),
         cost_estimate=pl.CostEstimate(flops=flops, bytes_accessed=moved, transcendentals=0),
     )(*args)
 
@@ -63,7 +61,22 @@
     scal_ref[...] = rows_of(scale_in, scale_grad, top(jnp.abs(tok)))
 
 
-def forward_body(place_ref, x_ref, g0_ref, u0_ref, g1_ref, u1_ref, out_ref, xh_ref):
+def copies_of(source, target, sems):
+    return [pltpu.make_async_copy(source(i), target(i), sems.at[i]) for i in range(2)]
+
+
+def stash_body(g_ref, u_ref, out_ref, sems):
+    copies = copies_of(lambda i: (g_ref, u_ref)[i], lambda i: out_ref.at[i], sems)
+    for copy in copies:
+        copy.start()
+    for copy in copies:
+        copy.wait()
+
+
+def forward_body(place_ref, x_ref, g0_ref, u0_ref, stash_ref, out_ref, xh_ref, held_ref, sems):
+    copies = copies_of(lambda i: stash_ref.at[i], lambda i: held_ref.at[i], sems)
+    for copy in copies:
+        copy.start()
     groups, cols, rows = out_ref.shape[0] // 2, x_ref.shape[0] // (out_ref.shape[0] // 2), x_ref.shape[1]
     core, turned = place_ref[0], place_ref[1]
     for g in range(groups):
@@ -71,9 +84,11 @@
         for k in range(cols):
             xh_ref[spot, k * 128 : (k + 1) * 128] = x_ref[g * cols + k]
     x = xh_ref[...]
-    for which, pair in enumerate(((g0_ref, u0_ref), (g1_ref, u1_ref))):
+    for which, pair in enumerate(((g0_ref, u0_ref), (held_ref.at[0], held_ref.at[1]))):
         place = core if which == 0 else 1 - core
         for half, w_ref in enumerate(pair):
+            if which == 1:
+                copies[half].wait()
             part = jnp.dot(x, w_ref[...], preferred_element_type=F32).astype(BF16)
             for g in range(groups):
                 out_ref[2 * g + place, half * rows : (half + 1) * rows, :] = part[g * rows : (g + 1) * rows]
@@ -103,16 +118,21 @@
         q_ref[i, 2 * rows :, :] = wide
 
 
-def backward_body(place_ref, q_ref, g0_ref, u0_ref, g1_ref, u1_ref, out_ref, kept_ref):
+def backward_body(place_ref, q_ref, g0_ref, u0_ref, stash_ref, out_ref, kept_ref, held_ref, sems):
+    copies = copies_of(lambda i: stash_ref.at[i], lambda i: held_ref.at[i], sems)
+    for copy in copies:
+        copy.start()
     groups = q_ref.shape[0] // 2
     rows = (q_ref.shape[1] - 8) // 2
     cols = out_ref.shape[0] // groups
     core, turned = place_ref[0], place_ref[1]
     contract = (((1,), (1,)), ((), ()))
     total = None
-    for which, pair in enumerate(((g0_ref, u0_ref), (g1_ref, u1_ref))):
+    for which, pair in enumerate(((g0_ref, u0_ref), (held_ref.at[0], held_ref.at[1]))):
         place = core if which == 0 else 1 - core
         for half, w_ref in enumerate(pair):
+            if which == 1:
+                copies[half].wait()
             for g in range(groups):
                 kept_ref[g * rows : (g + 1) * rows, :] = q_ref[2 * g + place, half * rows : (half + 1) * rows, :]
             part = lax.dot_general(kept_ref[...], w_ref[...], contract, preferred_element_type=F32)
@@ -130,15 +150,6 @@
     out_ref[...] = (jnp.sum(in_ref[:, :rows, :].astype(F32), axis=0) / scal_ref[1:2, 0:1]).astype(BF16)
     peaks_ref[...] = rows_of(*unpack_peaks(in_ref[:, rows:, :].astype(F32)))
     hidden_out_ref[...] = hidden_ref[...]
-
-
-def history_body(hist_ref, mine_ref, other_ref, out_ref):
-    peaks = jnp.maximum(mine_ref[...], other_ref[...])
-    col = lax.broadcasted_iota(jnp.int32, (1, 3), 1)
-    row = jnp.where(col == 0, peaks[0:1, 0:1], jnp.where(col == 1, peaks[1:2, 0:1], peaks[2:3, 0:1]))
-    past = hist_ref.shape[0] - 1
-    out_ref[0:past, :] = hist_ref[1:, :]
-    out_ref[past:, :] = row
 
 
 def per_device(sizes, tokens, w_gate, w_up, upstream, history):
@@ -160,16 +171,28 @@
     x_all = lax.all_to_all(copies, plane, 0, 0, tiled=True)
     gate_other = lax.ppermute(w_gate, "c", swap)
     lift_other = lax.ppermute(w_up, "c", swap)
+    (stash,) = call(
+        stash_body,
+        [((STASH, depth, units), BF16)],
+        (gate_other, lift_other),
+        scratch=[pltpu.SemaphoreType.DMA((2,))],
+        far=(0, 1),
+        far_outs=(0,),
+    )
+    held = [pltpu.VMEM((2, depth, units), BF16), pltpu.SemaphoreType.DMA((2,))]
     up = lax.ppermute(upstream, ("h", "y"), along_y)
-    x_all, gate_other, lift_other, up = lax.optimization_barrier((x_all, gate_other, lift_other, up))
+    x_all, stash, up = lax.optimization_barrier((x_all, stash, up))
 
     work = 8 * nh * rows * depth * units
     parts, x_mine = call(
         forward_body,
         [((ny, 2 * rows, units), BF16), ((nh * rows, depth), BF16)],
-        (place, x_all, w_gate, w_up, gate_other, lift_other),
+        (place, x_all, w_gate, w_up, stash),
         flops=work,
         moved=6 * 2**20,
+        scratch=held,
+        vmem=48,
+        far=(4,),
     )
     parts, x_mine, up = lax.optimization_barrier((parts, x_mine, up))
     sums = lax.all_to_all(parts, "y", 0, 0, tiled=True)
@@ -186,10 +209,12 @@
     (back,) = call(
         backward_body,
         [((count, rows + 8, width), BF16)],
-        (place, q_all, w_gate, w_up, gate_other, lift_other),
+        (place, q_all, w_gate, w_up, stash),
         flops=work,
         moved=6 * 2**20,
-        scratch=[pltpu.VMEM((nh * rows, units), BF16)],
+        scratch=[pltpu.VMEM((nh * rows, units), BF16)] + held,
+        vmem=48,
+        far=(4,),
     )
     back, q_all, hidden = lax.optimization_barrier((back, q_all, hidden))
     back_all = lax.all_to_all(back, plane, 0, 0, tiled=True)
@@ -218,7 +243,9 @@
         moved=2**21,
     )
     peaks_other = lax.ppermute(peaks, "c", swap)
-    (new_history,) = call(history_body, [(history.shape, F32)], (history, peaks, peaks_other))
+    row = jnp.maximum(peaks, peaks_other)[:3, 0]
+    last = lax.broadcasted_iota(jnp.int32, history.shape, 0) == history.shape[0] - 1
+    new_history = jnp.where(last, row[None, :], jnp.roll(history, -1, axis=0))
     return (hidden, input_grad, grads[0], grads[1], new_history)
 
 

time: 166 us -> 164 us (0.988)
  local copies, waits for them, and re-layouts: 8.78 us -> 4.54 us
  Pallas kernels: 9.13 us -> 10.9 us
    unnamed x22 -> x15, local copies, waits for them, and re-layouts: 8.02 us -> 3.59 us
    pallas_call x6, Pallas kernels: 9.13 us -> 10.9 us  [call(): pl.pallas_call(body, out_shape=[jax.ShapeDtypeStruct(s, t) for s, t in ou...]
  transfers between devices with their start and end apart: 13 -> 13, of which waited for: 8 -> 7; matrix products, arithmetic and copies ran while one was open for 4% -> 4% of each run, Pallas kernels for 0% -> 1%
where the time goes in v9:
time: 164 us; the launch traced here: 163 us
  waiting for transfers between devices  93.3 us (57%)
  starting transfers between devices  45.8 us (28%)
  Pallas kernels  10.9 us (7%)
  matrix products  5.97 us (4%)
  local copies, waits for them, and re-layouts  4.54 us (3%)
  between operations  2.21 us (1%)
    all_to_all x1, waiting for transfers between devices, per_device(): sums = lax.all_to_all(parts, 'y', 0, 0, tiled=True)  28.5 us
    all_to_all x1, waiting for transfers between devices, per_device(): q_all = lax.all_to_all(quants, 'y', 0, 0, tiled=True)  25.1 us
    all_to_all x1, waiting for transfers between devices, per_device(): x_all = lax.all_to_all(copies, plane, 0, 0, tiled=True)  19.2 us
    all_to_all x1, waiting for transfers between devices, per_device(): back_all = lax.all_to_all(back, plane, 0, 0, tiled=True)  16.9 us
    all_to_all x1, starting transfers between devices, per_device(): x_all = lax.all_to_all(copies, plane, 0, 0, tiled=True)  13.7 us
    pallas_call x6, Pallas kernels, call(): pl.pallas_call(body, out_shape=[jax.ShapeDtypeStruct(s, t) for s, t in ou...  10.9 us
    all_to_all x1, starting transfers between devices, per_device(): sums = lax.all_to_all(parts, 'y', 0, 0, tiled=True)  6.84 us
    all_to_all x1, starting transfers between devices, per_device(): back_all = lax.all_to_all(back, plane, 0, 0, tiled=True)  5.8 us
  transfers between devices with their start and end apart: 13, of which 7 were waited for; matrix products, arithmetic and copies ran while one was open for 4% of the time, Pallas kernels for 1%

profile of v9, /device:TPU:1, one launch (start us, length us, event | category | flops | bytes accessed | tf_op | source)
XLA Modules:
  0.0 163.4 jit_solution(11917425653377455990)
XLA Ops:
  0.6 0.0 copy-start
  0.6 0.0 copy-start.1
  0.7 0.8 copy.11.hist_ref
  1.5 0.0 copy-start.4
  1.5 0.8 copy-done.4
  2.3 0.0 copy-start.6
  2.3 1.2 shard_map.92
  3.4 13.7 %all-to-all-start = ((bf16[32,128,128]{2,1,0:T(8,128)(2,1)}), bf16[32,128,128]{2,1,0:T(8,128)(2,1)S(1)}, u32[]{:S(2)}, u32[]{:S(2)}) async-start(bf16[32,128,128]{2,1,0:T(8,128)(2,1)} %get-tuple-element.34), calls=%async_computation | async-start | bytes 2097152 | tf_op jit(solution)/shard_map/all_to_all | solution.py:171
  17.1 0.0 copy-done
  17.1 2.9 %collective-permute-start = (bf16[1024,256]{1,0:T(8,128)(2,1)S(1)}, bf16[1024,256]{1,0:T(8,128)(2,1)S(1)}, u32[]{:S(2)}, u32[]{:S(2)}) collective-permute-start(bf16[1024,256]{1,0:T(8,128)(2,1)S(1)} %copy-done), channel_id=1, source_target_pairs={{0,64},{64,0},{1,65},{65,1},{2,66},{66,2},{3,67},{67,3},{4,68},{68... | collective-permute-start | bytes 1572872 | tf_op jit(solution)/shard_map/ppermute | solution.py:172
  20.0 0.0 copy-done.1
  20.0 1.9 %collective-permute-start.1 = (bf16[1024,256]{1,0:T(8,128)(2,1)S(1)}, bf16[1024,256]{1,0:T(8,128)(2,1)S(1)}, u32[]{:S(2)}, u32[]{:S(2)}) collective-permute-start(bf16[1024,256]{1,0:T(8,128)(2,1)S(1)} %copy-done.1), channel_id=1, source_target_pairs={{0,64},{64,0},{1,65},{65,1},{2,66},{66,2},{3,67},{67,3},{4,68},{68... | collective-permute-start | bytes 1572872 | tf_op jit(solution)/shard_map/ppermute | solution.py:173
  22.0 0.0 copy-done.6
  22.0 0.7 collective-permute-start.2
  22.6 0.1 pad_add_fusion.place_ref
  22.7 0.0 collective-permute-done.g_ref
  22.7 1.1 collective-permute-done.1.u_ref
  23.8 1.0 shard_map.93.stash_ref
  24.9 0.0 collective-permute-done.2
  24.9 19.2 %all-to-all-done.x_ref = bf16[32,128,128]{2,1,0:T(8,128)(2,1)S(1)} async-done(((bf16[32,128,128]{2,1,0:T(8,128)(2,1)}), bf16[32,128,128]{2,1,0:T(8,128)(2,1)S(1)}, u32[]{:S(2)}, u32[]{:S(2)}) %all-to-all-start) | async-done | bytes 1048608 | tf_op jit(solution)/shard_map/all_to_all | solution.py:171
  44.1 3.6 %shard_map.94 = (bf16[8,256,256]{2,1,0:T(8,128)(2,1)S(1)}, bf16[512,1024]{1,0:T(8,128)(2,1)S(1)}) custom-call(s32[2]{0:T(128)S(1)} %pad_add_fusion.place_ref, bf16[32,128,128]{2,1,0:T(8,128)(2,1)S(1)} %all-to-all-done.x_ref, bf16[1024,256]{1,0:T(8,128)(2,1)S(1)} %copy-done, bf16[1024,256]{1,0:T(8,128)(2,1)S(1)} %copy-done.1, ...), custom_call_target="tpu_custom_call" | custom-call | flops 1073741824 | bytes 6291456 | tf_op jit(solution)/shard_map/pallas_call | solution.py:18
  47.7 0.0 copy-start.3
  47.7 1.0 copy-done.3
  48.7 6.8 %all-to-all-start.1 = ((bf16[8,256,256]{2,1,0:T(8,128)(2,1)}), bf16[8,256,256]{2,1,0:T(8,128)(2,1)S(1)}, u32[]{:S(2)}, u32[]{:S(2)}) async-start(bf16[8,256,256]{2,1,0:T(8,128)(2,1)} %copy-done.3), calls=%async_computation.1 | async-start | bytes 2097152 | tf_op jit(solution)/shard_map/all_to_all | solution.py:198
  55.5 0.7 collective-permute-start.3
  56.2 0.0 collective-permute-done.3.up_ref
  56.2 28.5 %all-to-all-done.1.in_ref = bf16[8,256,256]{2,1,0:T(8,128)(2,1)S(1)} async-done(((bf16[8,256,256]{2,1,0:T(8,128)(2,1)}), bf16[8,256,256]{2,1,0:T(8,128)(2,1)S(1)}, u32[]{:S(2)}, u32[]{:S(2)}) %all-to-all-start.1) | async-done | bytes 1048608 | tf_op jit(solution)/shard_map/all_to_all | solution.py:198
  84.7 0.4 shard_map.95
  85.1 0.0 copy-start.2
  85.1 1.0 copy-done.2
  86.1 3.6 %all-to-all-start.2 = ((bf16[8,264,256]{2,1,0:T(8,128)(2,1)}), bf16[8,264,256]{2,1,0:T(8,128)(2,1)S(1)}, u32[]{:S(2)}, u32[]{:S(2)}) async-start(bf16[8,264,256]{2,1,0:T(8,128)(2,1)} %copy-done.2), calls=%async_computation.2 | async-start | bytes 2162688 | tf_op jit(solution)/shard_map/all_to_all | solution.py:205
  89.6 2.4 %collective-permute-start.5 = (bf16[512,1024]{1,0:T(8,128)(2,1)S(1)}, bf16[512,1024]{1,0:T(8,128)(2,1)}, u32[]{:S(2)}, u32[]{:S(2)}) collective-permute-start(bf16[512,1024]{1,0:T(8,128)(2,1)S(1)} %get-tuple-element.49), channel_id=1, source_target_pairs={{0,64},{64,0},{1,65},{65,1},{2,66},{66,2},{3,67},{67,3},{4,68},{68... | collective-permute-start | bytes 3145736 | tf_op jit(solution)/shard_map/ppermute | solution.py:207
  92.1 0.7 collective-permute-start.4
  92.7 0.0 collective-permute-done.4
  92.7 1.7 %collective-permute-done.5 = bf16[512,1024]{1,0:T(8,128)(2,1)} collective-permute-done((bf16[512,1024]{1,0:T(8,128)(2,1)S(1)}, bf16[512,1024]{1,0:T(8,128)(2,1)}, u32[]{:S(2)}, u32[]{:S(2)}) %collective-permute-start.5) | collective-permute-done | bytes 1048608 | tf_op jit(solution)/shard_map/ppermute | solution.py:207
  94.5 25.1 %all-to-all-done.2.q_ref = bf16[8,264,256]{2,1,0:T(8,128)(2,1)S(1)} async-done(((bf16[8,264,256]{2,1,0:T(8,128)(2,1)}), bf16[8,264,256]{2,1,0:T(8,128)(2,1)S(1)}, u32[]{:S(2)}, u32[]{:S(2)}) %all-to-all-start.2) | async-done | bytes 1081376 | tf_op jit(solution)/shard_map/all_to_all | solution.py:205
  119.5 3.8 %shard_map.96 = bf16[32,136,128]{2,1,0:T(8,128)(2,1)} custom-call(s32[2]{0:T(128)S(1)} %pad_add_fusion.place_ref, bf16[8,264,256]{2,1,0:T(8,128)(2,1)S(1)} %all-to-all-done.2.q_ref, bf16[1024,256]{1,0:T(8,128)(2,1)S(1)} %copy-done, bf16[1024,256]{1,0:T(8,128)(2,1)S(1)} %copy-done.1, bf16[64,1024,256]{2,1,0:T(8,128)(2,1)} %shard_map.93.stash_ref), custom_call_target="tpu_custom_call" | custom-call | flops 1073741824 | bytes 6291456 | tf_op jit(solution)/shard_map/pallas_call | solution.py:18
  123.4 5.8 %all-to-all-start.3 = ((bf16[32,136,128]{2,1,0:T(8,128)(2,1)}), bf16[32,136,128]{2,1,0:T(8,128)(2,1)S(1)}, u32[]{:S(2)}, u32[]{:S(2)}) async-start(bf16[32,136,128]{2,1,0:T(8,128)(2,1)} %shard_map.96), calls=%async_computation.3 | async-start | bytes 2228224 | tf_op jit(solution)/shard_map/all_to_all | solution.py:220
  129.2 0.5 fusion.5
  131.0 0.1 slice.34
  131.1 0.1 constant_dynamic-slice_fusion
  131.3 2.7 %collective-permute-start.6 = (bf16[2,512,256]{2,1,0:T(8,128)(2,1)S(1)}, bf16[2,512,256]{2,1,0:T(8,128)(2,1)S(1)}, u32[]{:S(2)}, u32[]{:S(2)}) collective-permute-start(bf16[2,512,256]{2,1,0:T(8,128)(2,1)S(1)} %bitcast.31), channel_id=1, source_target_pairs={{0,64},{64,0},{1,65},{65,1},{2,66},{66,2},{3,67},{67,3},{4,68},{68... | collective-permute-start | bytes 1572872 | tf_op jit(solution)/shard_map/ppermute | solution.py:228
  133.9 0.7 collective-permute-start.7
  134.7 0.5 fusion.7
  135.1 0.5 fusion.6
  135.6 0.0 collective-permute-done.6
  135.6 2.5 %fusion.3 = bf16[1024,256]{1,0:T(8,128)(2,1)} fusion(f32[1024,256]{1,0:T(8,128)S(1)} %fusion.7, bf16[512,1024]{1,0:T(8,128)(2,1)} %collective-permute-done.5, f32[]{:T(128)} %bitcast.10, bf16[2,512,256]{2,1,0:T(8,128)(2,1)S(1)} %collective-permute-done.6), kind=kOutput, calls=%fused_computation.5 | convolution fusion | flops 269221888 | bytes 2883588 | tf_op jit(solution)/shard_map/dot_general | solution.py:234
  138.1 2.5 %fusion.2 = bf16[1024,256]{1,0:T(8,128)(2,1)} fusion(f32[1024,256]{1,0:T(8,128)S(1)} %fusion.6, bf16[512,1024]{1,0:T(8,128)(2,1)} %collective-permute-done.5, f32[]{:T(128)} %bitcast.10, bf16[2,512,256]{2,1,0:T(8,128)(2,1)S(1)} %collective-permute-done.6), kind=kOutput, calls=%fused_computation.4 | convolution fusion | flops 269221888 | bytes 2883588 | tf_op jit(solution)/shard_map/dot_general | solution.py:234
  140.7 0.0 copy-start.5
  140.7 0.0 collective-permute-done.7.hidden_ref
  140.7 16.9 %all-to-all-done.3.in_ref = bf16[32,136,128]{2,1,0:T(8,128)(2,1)S(1)} async-done(((bf16[32,136,128]{2,1,0:T(8,128)(2,1)}), bf16[32,136,128]{2,1,0:T(8,128)(2,1)S(1)}, u32[]{:S(2)}, u32[]{:S(2)}) %all-to-all-start.3) | async-done | bytes 1114144 | tf_op jit(solution)/shard_map/all_to_all | solution.py:220
  157.6 0.9 shard_map.97
  158.4 3.4 %collective-permute-start.8 = (f32[8,128]{1,0:T(8,128)S(1)}, f32[8,128]{1,0:T(8,128)S(1)}, u32[]{:S(2)}, u32[]{:S(2)}) collective-permute-start(f32[8,128]{1,0:T(8,128)S(1)} %get-tuple-element.62), channel_id=1, source_target_pairs={{0,64},{64,0},{1,65},{65,1},{2,66},{66,2},{3,67},{67,3},{4,68},{68... | collective-permute-start | bytes 12296 | tf_op jit(solution)/shard_map/ppermute | solution.py:245
  161.8 0.0 copy-done.5
  161.8 0.1 slice.42
  161.9 0.7 collective-permute-done.8
  162.6 0.1 slice_reduce_fusion
  162.7 0.7 maximum_select_fusion
  (4 shorter events, 0.1 us)
Async XLA Ops:
  0.6 16.5 %copy-start = (bf16[1024,256]{1,0:T(8,128)(2,1)S(1)}, bf16[1024,256]{1,0:T(8,128)(2,1)}, u32[]{:S(2)}) copy-start(bf16[1024,256]{1,0:T(8,128)(2,1)} %g0_ref.3) | copy-start | bytes 1572868
  0.6 19.4 %copy-start.1 = (bf16[1024,256]{1,0:T(8,128)(2,1)S(1)}, bf16[1024,256]{1,0:T(8,128)(2,1)}, u32[]{:S(2)}) copy-start(bf16[1024,256]{1,0:T(8,128)(2,1)} %u0_ref.3) | copy-start | bytes 1572868
  1.5 0.8 copy-start.4
  2.3 19.7 %copy-start.6 = (bf16[128,256]{1,0:T(8,128)(2,1)S(1)}, bf16[128,256]{1,0:T(8,128)(2,1)}, u32[]{:S(2)}) copy-start(bf16[128,256]{1,0:T(8,128)(2,1)} %param.8) | copy-start | bytes 196612
  3.4 40.6 %all-to-all-start = ((bf16[32,128,128]{2,1,0:T(8,128)(2,1)}), bf16[32,128,128]{2,1,0:T(8,128)(2,1)S(1)}, u32[]{:S(2)}, u32[]{:S(2)}) async-start(bf16[32,128,128]{2,1,0:T(8,128)(2,1)} %get-tuple-element.34), calls=%async_computation | async-start | bytes 2097152 | tf_op jit(solution)/shard_map/all_to_all | solution.py:171
  17.1 5.6 %collective-permute-start = (bf16[1024,256]{1,0:T(8,128)(2,1)S(1)}, bf16[1024,256]{1,0:T(8,128)(2,1)S(1)}, u32[]{:S(2)}, u32[]{:S(2)}) collective-permute-start(bf16[1024,256]{1,0:T(8,128)(2,1)S(1)} %copy-done), channel_id=1, source_target_pairs={{0,64},{64,0},{1,65},{65,1},{2,66},{66,2},{3,67},{67,3},{4,68},{68... | collective-permute-start | bytes 1572872 | tf_op jit(solution)/shard_map/ppermute | solution.py:172
  20.0 3.8 %collective-permute-start.1 = (bf16[1024,256]{1,0:T(8,128)(2,1)S(1)}, bf16[1024,256]{1,0:T(8,128)(2,1)S(1)}, u32[]{:S(2)}, u32[]{:S(2)}) collective-permute-start(bf16[1024,256]{1,0:T(8,128)(2,1)S(1)} %copy-done.1), channel_id=1, source_target_pairs={{0,64},{64,0},{1,65},{65,1},{2,66},{66,2},{3,67},{67,3},{4,68},{68... | collective-permute-start | bytes 1572872 | tf_op jit(solution)/shard_map/ppermute | solution.py:173
  22.0 2.9 %collective-permute-start.2 = (bf16[128,256]{1,0:T(8,128)(2,1)S(1)}, bf16[128,256]{1,0:T(8,128)(2,1)S(1)}, u32[]{:S(2)}, u32[]{:S(2)}) collective-permute-start(bf16[128,256]{1,0:T(8,128)(2,1)S(1)} %copy-done.6), channel_id=1, source_target_pairs={{0,0},{1,1},{2,2},{3,3},{4,4},{5,5},{6,6},{7,7},{128,130},{129,131... | collective-permute-start | bytes 196616 | tf_op jit(solution)/shard_map/ppermute | solution.py:183
  47.7 1.0 copy-start.3
  48.7 36.0 %all-to-all-start.1 = ((bf16[8,256,256]{2,1,0:T(8,128)(2,1)}), bf16[8,256,256]{2,1,0:T(8,128)(2,1)S(1)}, u32[]{:S(2)}, u32[]{:S(2)}) async-start(bf16[8,256,256]{2,1,0:T(8,128)(2,1)} %copy-done.3), calls=%async_computation.1 | async-start | bytes 2097152 | tf_op jit(solution)/shard_map/all_to_all | solution.py:198
  55.5 0.7 collective-permute-start.3
  85.1 1.0 copy-start.2
  86.1 33.5 %all-to-all-start.2 = ((bf16[8,264,256]{2,1,0:T(8,128)(2,1)}), bf16[8,264,256]{2,1,0:T(8,128)(2,1)S(1)}, u32[]{:S(2)}, u32[]{:S(2)}) async-start(bf16[8,264,256]{2,1,0:T(8,128)(2,1)} %copy-done.2), calls=%async_computation.2 | async-start | bytes 2162688 | tf_op jit(solution)/shard_map/all_to_all | solution.py:205
  89.6 4.8 %collective-permute-start.5 = (bf16[512,1024]{1,0:T(8,128)(2,1)S(1)}, bf16[512,1024]{1,0:T(8,128)(2,1)}, u32[]{:S(2)}, u32[]{:S(2)}) collective-permute-start(bf16[512,1024]{1,0:T(8,128)(2,1)S(1)} %get-tuple-element.49), channel_id=1, source_target_pairs={{0,64},{64,0},{1,65},{65,1},{2,66},{66,2},{3,67},{67,3},{4,68},{68... | collective-permute-start | bytes 3145736 | tf_op jit(solution)/shard_map/ppermute | solution.py:207
  92.1 0.7 collective-permute-start.4
  123.4 34.2 %all-to-all-start.3 = ((bf16[32,136,128]{2,1,0:T(8,128)(2,1)}), bf16[32,136,128]{2,1,0:T(8,128)(2,1)S(1)}, u32[]{:S(2)}, u32[]{:S(2)}) async-start(bf16[32,136,128]{2,1,0:T(8,128)(2,1)} %shard_map.96), calls=%async_computation.3 | async-start | bytes 2228224 | tf_op jit(solution)/shard_map/all_to_all | solution.py:220
  131.3 4.4 %collective-permute-start.6 = (bf16[2,512,256]{2,1,0:T(8,128)(2,1)S(1)}, bf16[2,512,256]{2,1,0:T(8,128)(2,1)S(1)}, u32[]{:S(2)}, u32[]{:S(2)}) collective-permute-start(bf16[2,512,256]{2,1,0:T(8,128)(2,1)S(1)} %bitcast.31), channel_id=1, source_target_pairs={{0,64},{64,0},{1,65},{65,1},{2,66},{66,2},{3,67},{67,3},{4,68},{68... | collective-permute-start | bytes 1572872 | tf_op jit(solution)/shard_map/ppermute | solution.py:228
  133.9 6.7 %collective-permute-start.7 = (bf16[128,256]{1,0:T(8,128)(2,1)S(1)}, bf16[128,256]{1,0:T(8,128)(2,1)S(1)}, u32[]{:S(2)}, u32[]{:S(2)}) collective-permute-start(bf16[128,256]{1,0:T(8,128)(2,1)S(1)} %collective-permute-done.4), channel_id=1, source_target_pairs={{0,0},{1,1},{2,2},{3,3},{4,4},{5,5},{6,6},{7,7},{130,128},{131,129... | collective-permute-start | bytes 196616 | tf_op jit(solution)/shard_map/ppermute | solution.py:221
  140.7 21.2 %copy-start.5 = (f32[16,3]{0,1:T(4,128)S(1)}, f32[16,3]{0,1:T(4,128)}, u32[]{:S(2)}) copy-start(f32[16,3]{0,1:T(4,128)} %param.9) | copy-start | bytes 580
  158.4 4.2 %collective-permute-start.8 = (f32[8,128]{1,0:T(8,128)S(1)}, f32[8,128]{1,0:T(8,128)S(1)}, u32[]{:S(2)}, u32[]{:S(2)}) collective-permute-start(f32[8,128]{1,0:T(8,128)S(1)} %get-tuple-element.62), channel_id=1, source_target_pairs={{0,64},{64,0},{1,65},{65,1},{2,66},{66,2},{3,67},{67,3},{4,68},{68... | collective-permute-start | bytes 12296 | tf_op jit(solution)/shard_map/ppermute | solution.py:245

commit v10 on v9

--- a/solution.py
+++ b/solution.py
@@ -62,7 +62,14 @@
 
 
 def copies_of(source, target, sems):
-    return [pltpu.make_async_copy(source(i), target(i), sems.at[i]) for i in range(2)]
+    cut = source(0).shape[0] // sems.shape[1]
+    return [
+        pltpu.make_async_copy(
+            source(i).at[pl.ds(j * cut, cut)], target(i).at[pl.ds(j * cut, cut)], sems.at[i, j]
+        )
+        for i in range(2)
+        for j in range(sems.shape[1])
+    ]
 
 
 def stash_body(g_ref, u_ref, out_ref, sems):
@@ -88,7 +95,8 @@
         place = core if which == 0 else 1 - core
         for half, w_ref in enumerate(pair):
             if which == 1:
-                copies[half].wait()
+                for copy in copies[half * len(copies) // 2 : (half + 1) * len(copies) // 2]:
+                    copy.wait()
             part = jnp.dot(x, w_ref[...], preferred_element_type=F32).astype(BF16)
             for g in range(groups):
                 out_ref[2 * g + place, half * rows : (half + 1) * rows, :] = part[g * rows : (g + 1) * rows]
@@ -132,7 +140,8 @@
         place = core if which == 0 else 1 - core
         for half, w_ref in enumerate(pair):
             if which == 1:
-                copies[half].wait()
+                for copy in copies[half * len(copies) // 2 : (half + 1) * len(copies) // 2]:
+                    copy.wait()
             for g in range(groups):
                 kept_ref[g * rows : (g + 1) * rows, :] = q_ref[2 * g + place, half * rows : (half + 1) * rows, :]
             part = lax.dot_general(kept_ref[...], w_ref[...], contract, preferred_element_type=F32)
@@ -175,11 +184,11 @@
         stash_body,
         [((STASH, depth, units), BF16)],
         (gate_other, lift_other),
-        scratch=[pltpu.SemaphoreType.DMA((2,))],
+        scratch=[pltpu.SemaphoreType.DMA((2, 4))],
         far=(0, 1),
         far_outs=(0,),
     )
-    held = [pltpu.VMEM((2, depth, units), BF16), pltpu.SemaphoreType.DMA((2,))]
+    held = [pltpu.VMEM((2, depth, units), BF16), pltpu.SemaphoreType.DMA((2, 4))]
     up = lax.ppermute(upstream, ("h", "y"), along_y)
     x_all, stash, up = lax.optimization_barrier((x_all, stash, up))
 

time: 164 us -> 164 us (level)
  no operation moved by 1% of the time
where the time goes in v10:
time: 164 us
  waiting for transfers between devices  93.2 us (57%)
  starting transfers between devices  45.8 us (28%)
  Pallas kernels  11.2 us (7%)
  matrix products  5.96 us (4%)
  local copies, waits for them, and re-layouts  4.54 us (3%)
  between operations  2.21 us (1%)
    all_to_all x1, waiting for transfers between devices, per_device(): sums = lax.all_to_all(parts, 'y', 0, 0, tiled=True)  28.5 us
    all_to_all x1, waiting for transfers between devices, per_device(): q_all = lax.all_to_all(quants, 'y', 0, 0, tiled=True)  25.1 us
    all_to_all x1, waiting for transfers between devices, per_device(): x_all = lax.all_to_all(copies, plane, 0, 0, tiled=True)  19.1 us
    all_to_all x1, waiting for transfers between devices, per_device(): back_all = lax.all_to_all(back, plane, 0, 0, tiled=True)  16.9 us
    all_to_all x1, starting transfers between devices, per_device(): x_all = lax.all_to_all(copies, plane, 0, 0, tiled=True)  13.7 us
    pallas_call x6, Pallas kernels, call(): pl.pallas_call(body, out_shape=[jax.ShapeDtypeStruct(s, t) for s, t in ou...  11.2 us
    all_to_all x1, starting transfers between devices, per_device(): sums = lax.all_to_all(parts, 'y', 0, 0, tiled=True)  6.84 us
    all_to_all x1, starting transfers between devices, per_device(): back_all = lax.all_to_all(back, plane, 0, 0, tiled=True)  5.8 us
  transfers between devices with their start and end apart: 13, of which 7 were waited for; matrix products, arithmetic and copies ran while one was open for 4% of the time, Pallas kernels for 1%

profile of v10, /device:TPU:1, one launch (start us, length us, event | category | flops | bytes accessed | tf_op | source)
XLA Modules:
  0.0 163.6 jit_solution(5546222592977421618)
XLA Ops:
  0.6 0.0 copy-start
  0.6 0.0 copy-start.1
  0.7 0.8 copy.11.hist_ref
  1.5 0.0 copy-start.4
  1.5 0.8 copy-done.4
  2.3 0.0 copy-start.6
  2.3 1.2 shard_map.92
  3.4 13.7 %all-to-all-start = ((bf16[32,128,128]{2,1,0:T(8,128)(2,1)}), bf16[32,128,128]{2,1,0:T(8,128)(2,1)S(1)}, u32[]{:S(2)}, u32[]{:S(2)}) async-start(bf16[32,128,128]{2,1,0:T(8,128)(2,1)} %get-tuple-element.34), calls=%async_computation | async-start | bytes 2097152 | tf_op jit(solution)/shard_map/all_to_all | solution.py:180
  17.1 0.0 copy-done
  17.1 2.9 %collective-permute-start = (bf16[1024,256]{1,0:T(8,128)(2,1)S(1)}, bf16[1024,256]{1,0:T(8,128)(2,1)S(1)}, u32[]{:S(2)}, u32[]{:S(2)}) collective-permute-start(bf16[1024,256]{1,0:T(8,128)(2,1)S(1)} %copy-done), channel_id=1, source_target_pairs={{0,64},{64,0},{1,65},{65,1},{2,66},{66,2},{3,67},{67,3},{4,68},{68... | collective-permute-start | bytes 1572872 | tf_op jit(solution)/shard_map/ppermute | solution.py:181
  20.0 0.0 copy-done.1
  20.0 1.9 %collective-permute-start.1 = (bf16[1024,256]{1,0:T(8,128)(2,1)S(1)}, bf16[1024,256]{1,0:T(8,128)(2,1)S(1)}, u32[]{:S(2)}, u32[]{:S(2)}) collective-permute-start(bf16[1024,256]{1,0:T(8,128)(2,1)S(1)} %copy-done.1), channel_id=1, source_target_pairs={{0,64},{64,0},{1,65},{65,1},{2,66},{66,2},{3,67},{67,3},{4,68},{68... | collective-permute-start | bytes 1572872 | tf_op jit(solution)/shard_map/ppermute | solution.py:182
  22.0 0.0 copy-done.6
  22.0 0.7 collective-permute-start.2
  22.6 0.1 pad_add_fusion.place_ref
  22.7 0.0 collective-permute-done.g_ref
  22.7 1.1 collective-permute-done.1.u_ref
  23.8 1.1 shard_map.93.stash_ref
  24.9 0.0 collective-permute-done.2
  24.9 19.1 %all-to-all-done.x_ref = bf16[32,128,128]{2,1,0:T(8,128)(2,1)S(1)} async-done(((bf16[32,128,128]{2,1,0:T(8,128)(2,1)}), bf16[32,128,128]{2,1,0:T(8,128)(2,1)S(1)}, u32[]{:S(2)}, u32[]{:S(2)}) %all-to-all-start) | async-done | bytes 1048608 | tf_op jit(solution)/shard_map/all_to_all | solution.py:180
  44.1 3.7 %shard_map.94 = (bf16[8,256,256]{2,1,0:T(8,128)(2,1)S(1)}, bf16[512,1024]{1,0:T(8,128)(2,1)S(1)}) custom-call(s32[2]{0:T(128)S(1)} %pad_add_fusion.place_ref, bf16[32,128,128]{2,1,0:T(8,128)(2,1)S(1)} %all-to-all-done.x_ref, bf16[1024,256]{1,0:T(8,128)(2,1)S(1)} %copy-done, bf16[1024,256]{1,0:T(8,128)(2,1)S(1)} %copy-done.1, ...), custom_call_target="tpu_custom_call" | custom-call | flops 1073741824 | bytes 6291456 | tf_op jit(solution)/shard_map/pallas_call | solution.py:18
  47.8 0.0 copy-start.3
  47.8 1.0 copy-done.3
  48.8 6.8 %all-to-all-start.1 = ((bf16[8,256,256]{2,1,0:T(8,128)(2,1)}), bf16[8,256,256]{2,1,0:T(8,128)(2,1)S(1)}, u32[]{:S(2)}, u32[]{:S(2)}) async-start(bf16[8,256,256]{2,1,0:T(8,128)(2,1)} %copy-done.3), calls=%async_computation.1 | async-start | bytes 2097152 | tf_op jit(solution)/shard_map/all_to_all | solution.py:207
  55.6 0.7 collective-permute-start.3
  56.3 0.0 collective-permute-done.3.up_ref
  56.3 28.5 %all-to-all-done.1.in_ref = bf16[8,256,256]{2,1,0:T(8,128)(2,1)S(1)} async-done(((bf16[8,256,256]{2,1,0:T(8,128)(2,1)}), bf16[8,256,256]{2,1,0:T(8,128)(2,1)S(1)}, u32[]{:S(2)}, u32[]{:S(2)}) %all-to-all-start.1) | async-done | bytes 1048608 | tf_op jit(solution)/shard_map/all_to_all | solution.py:207
  84.8 0.4 shard_map.95
  85.2 0.0 copy-start.2
  85.2 1.0 copy-done.2
  86.2 3.6 %all-to-all-start.2 = ((bf16[8,264,256]{2,1,0:T(8,128)(2,1)}), bf16[8,264,256]{2,1,0:T(8,128)(2,1)S(1)}, u32[]{:S(2)}, u32[]{:S(2)}) async-start(bf16[8,264,256]{2,1,0:T(8,128)(2,1)} %copy-done.2), calls=%async_computation.2 | async-start | bytes 2162688 | tf_op jit(solution)/shard_map/all_to_all | solution.py:214
  89.8 2.4 %collective-permute-start.5 = (bf16[512,1024]{1,0:T(8,128)(2,1)S(1)}, bf16[512,1024]{1,0:T(8,128)(2,1)}, u32[]{:S(2)}, u32[]{:S(2)}) collective-permute-start(bf16[512,1024]{1,0:T(8,128)(2,1)S(1)} %get-tuple-element.49), channel_id=1, source_target_pairs={{0,64},{64,0},{1,65},{65,1},{2,66},{66,2},{3,67},{67,3},{4,68},{68... | collective-permute-start | bytes 3145736 | tf_op jit(solution)/shard_map/ppermute | solution.py:216
  92.2 0.7 collective-permute-start.4
  92.8 0.0 collective-permute-done.4
  92.9 1.7 %collective-permute-done.5 = bf16[512,1024]{1,0:T(8,128)(2,1)} collective-permute-done((bf16[512,1024]{1,0:T(8,128)(2,1)S(1)}, bf16[512,1024]{1,0:T(8,128)(2,1)}, u32[]{:S(2)}, u32[]{:S(2)}) %collective-permute-start.5) | collective-permute-done | bytes 1048608 | tf_op jit(solution)/shard_map/ppermute | solution.py:216
  94.6 25.1 %all-to-all-done.2.q_ref = bf16[8,264,256]{2,1,0:T(8,128)(2,1)S(1)} async-done(((bf16[8,264,256]{2,1,0:T(8,128)(2,1)}), bf16[8,264,256]{2,1,0:T(8,128)(2,1)S(1)}, u32[]{:S(2)}, u32[]{:S(2)}) %all-to-all-start.2) | async-done | bytes 1081376 | tf_op jit(solution)/shard_map/all_to_all | solution.py:214
  119.7 4.0 %shard_map.96 = bf16[32,136,128]{2,1,0:T(8,128)(2,1)} custom-call(s32[2]{0:T(128)S(1)} %pad_add_fusion.place_ref, bf16[8,264,256]{2,1,0:T(8,128)(2,1)S(1)} %all-to-all-done.2.q_ref, bf16[1024,256]{1,0:T(8,128)(2,1)S(1)} %copy-done, bf16[1024,256]{1,0:T(8,128)(2,1)S(1)} %copy-done.1, bf16[64,1024,256]{2,1,0:T(8,128)(2,1)} %shard_map.93.stash_ref), custom_call_target="tpu_custom_call" | custom-call | flops 1073741824 | bytes 6291456 | tf_op jit(solution)/shard_map/pallas_call | solution.py:18
  123.6 5.8 %all-to-all-start.3 = ((bf16[32,136,128]{2,1,0:T(8,128)(2,1)}), bf16[32,136,128]{2,1,0:T(8,128)(2,1)S(1)}, u32[]{:S(2)}, u32[]{:S(2)}) async-start(bf16[32,136,128]{2,1,0:T(8,128)(2,1)} %shard_map.96), calls=%async_computation.3 | async-start | bytes 2228224 | tf_op jit(solution)/shard_map/all_to_all | solution.py:229
  129.4 0.5 fusion.5
  131.2 0.1 slice.34
  131.3 0.1 constant_dynamic-slice_fusion
  131.5 2.7 %collective-permute-start.6 = (bf16[2,512,256]{2,1,0:T(8,128)(2,1)S(1)}, bf16[2,512,256]{2,1,0:T(8,128)(2,1)S(1)}, u32[]{:S(2)}, u32[]{:S(2)}) collective-permute-start(bf16[2,512,256]{2,1,0:T(8,128)(2,1)S(1)} %bitcast.31), channel_id=1, source_target_pairs={{0,64},{64,0},{1,65},{65,1},{2,66},{66,2},{3,67},{67,3},{4,68},{68... | collective-permute-start | bytes 1572872 | tf_op jit(solution)/shard_map/ppermute | solution.py:237
  134.2 0.7 collective-permute-start.7
  134.9 0.5 fusion.7
  135.4 0.5 fusion.6
  135.8 0.0 collective-permute-done.6
  135.8 2.5 %fusion.3 = bf16[1024,256]{1,0:T(8,128)(2,1)} fusion(f32[1024,256]{1,0:T(8,128)S(1)} %fusion.7, bf16[512,1024]{1,0:T(8,128)(2,1)} %collective-permute-done.5, f32[]{:T(128)} %bitcast.10, bf16[2,512,256]{2,1,0:T(8,128)(2,1)S(1)} %collective-permute-done.6), kind=kOutput, calls=%fused_computation.5 | convolution fusion | flops 269221888 | bytes 2883588 | tf_op jit(solution)/shard_map/dot_general | solution.py:243
  138.4 2.5 %fusion.2 = bf16[1024,256]{1,0:T(8,128)(2,1)} fusion(f32[1024,256]{1,0:T(8,128)S(1)} %fusion.6, bf16[512,1024]{1,0:T(8,128)(2,1)} %collective-permute-done.5, f32[]{:T(128)} %bitcast.10, bf16[2,512,256]{2,1,0:T(8,128)(2,1)S(1)} %collective-permute-done.6), kind=kOutput, calls=%fused_computation.4 | convolution fusion | flops 269221888 | bytes 2883588 | tf_op jit(solution)/shard_map/dot_general | solution.py:243
  140.9 0.0 copy-start.5
  140.9 0.0 collective-permute-done.7.hidden_ref
  140.9 16.9 %all-to-all-done.3.in_ref = bf16[32,136,128]{2,1,0:T(8,128)(2,1)S(1)} async-done(((bf16[32,136,128]{2,1,0:T(8,128)(2,1)}), bf16[32,136,128]{2,1,0:T(8,128)(2,1)S(1)}, u32[]{:S(2)}, u32[]{:S(2)}) %all-to-all-start.3) | async-done | bytes 1114144 | tf_op jit(solution)/shard_map/all_to_all | solution.py:229
  157.8 0.9 shard_map.97
  158.7 3.4 %collective-permute-start.8 = (f32[8,128]{1,0:T(8,128)S(1)}, f32[8,128]{1,0:T(8,128)S(1)}, u32[]{:S(2)}, u32[]{:S(2)}) collective-permute-start(f32[8,128]{1,0:T(8,128)S(1)} %get-tuple-element.62), channel_id=1, source_target_pairs={{0,64},{64,0},{1,65},{65,1},{2,66},{66,2},{3,67},{67,3},{4,68},{68... | collective-permute-start | bytes 12296 | tf_op jit(solution)/shard_map/ppermute | solution.py:254
  162.0 0.0 copy-done.5
  162.0 0.1 slice.42
  162.1 0.7 collective-permute-done.8
  162.8 0.1 slice_reduce_fusion
  162.9 0.7 maximum_select_fusion
  (4 shorter events, 0.1 us)
Async XLA Ops:
  0.6 16.5 %copy-start = (bf16[1024,256]{1,0:T(8,128)(2,1)S(1)}, bf16[1024,256]{1,0:T(8,128)(2,1)}, u32[]{:S(2)}) copy-start(bf16[1024,256]{1,0:T(8,128)(2,1)} %g0_ref.3) | copy-start | bytes 1572868
  0.6 19.4 %copy-start.1 = (bf16[1024,256]{1,0:T(8,128)(2,1)S(1)}, bf16[1024,256]{1,0:T(8,128)(2,1)}, u32[]{:S(2)}) copy-start(bf16[1024,256]{1,0:T(8,128)(2,1)} %u0_ref.3) | copy-start | bytes 1572868
  1.5 0.8 copy-start.4
  2.3 19.7 %copy-start.6 = (bf16[128,256]{1,0:T(8,128)(2,1)S(1)}, bf16[128,256]{1,0:T(8,128)(2,1)}, u32[]{:S(2)}) copy-start(bf16[128,256]{1,0:T(8,128)(2,1)} %param.8) | copy-start | bytes 196612
  3.4 40.6 %all-to-all-start = ((bf16[32,128,128]{2,1,0:T(8,128)(2,1)}), bf16[32,128,128]{2,1,0:T(8,128)(2,1)S(1)}, u32[]{:S(2)}, u32[]{:S(2)}) async-start(bf16[32,128,128]{2,1,0:T(8,128)(2,1)} %get-tuple-element.34), calls=%async_computation | async-start | bytes 2097152 | tf_op jit(solution)/shard_map/all_to_all | solution.py:180
  17.1 5.6 %collective-permute-start = (bf16[1024,256]{1,0:T(8,128)(2,1)S(1)}, bf16[1024,256]{1,0:T(8,128)(2,1)S(1)}, u32[]{:S(2)}, u32[]{:S(2)}) collective-permute-start(bf16[1024,256]{1,0:T(8,128)(2,1)S(1)} %copy-done), channel_id=1, source_target_pairs={{0,64},{64,0},{1,65},{65,1},{2,66},{66,2},{3,67},{67,3},{4,68},{68... | collective-permute-start | bytes 1572872 | tf_op jit(solution)/shard_map/ppermute | solution.py:181
  20.0 3.8 %collective-permute-start.1 = (bf16[1024,256]{1,0:T(8,128)(2,1)S(1)}, bf16[1024,256]{1,0:T(8,128)(2,1)S(1)}, u32[]{:S(2)}, u32[]{:S(2)}) collective-permute-start(bf16[1024,256]{1,0:T(8,128)(2,1)S(1)} %copy-done.1), channel_id=1, source_target_pairs={{0,64},{64,0},{1,65},{65,1},{2,66},{66,2},{3,67},{67,3},{4,68},{68... | collective-permute-start | bytes 1572872 | tf_op jit(solution)/shard_map/ppermute | solution.py:182
  22.0 3.0 %collective-permute-start.2 = (bf16[128,256]{1,0:T(8,128)(2,1)S(1)}, bf16[128,256]{1,0:T(8,128)(2,1)S(1)}, u32[]{:S(2)}, u32[]{:S(2)}) collective-permute-start(bf16[128,256]{1,0:T(8,128)(2,1)S(1)} %copy-done.6), channel_id=1, source_target_pairs={{0,0},{1,1},{2,2},{3,3},{4,4},{5,5},{6,6},{7,7},{128,130},{129,131... | collective-permute-start | bytes 196616 | tf_op jit(solution)/shard_map/ppermute | solution.py:192
  47.8 1.0 copy-start.3
  48.8 36.0 %all-to-all-start.1 = ((bf16[8,256,256]{2,1,0:T(8,128)(2,1)}), bf16[8,256,256]{2,1,0:T(8,128)(2,1)S(1)}, u32[]{:S(2)}, u32[]{:S(2)}) async-start(bf16[8,256,256]{2,1,0:T(8,128)(2,1)} %copy-done.3), calls=%async_computation.1 | async-start | bytes 2097152 | tf_op jit(solution)/shard_map/all_to_all | solution.py:207
  55.6 0.7 collective-permute-start.3
  85.2 1.0 copy-start.2
  86.2 33.5 %all-to-all-start.2 = ((bf16[8,264,256]{2,1,0:T(8,128)(2,1)}), bf16[8,264,256]{2,1,0:T(8,128)(2,1)S(1)}, u32[]{:S(2)}, u32[]{:S(2)}) async-start(bf16[8,264,256]{2,1,0:T(8,128)(2,1)} %copy-done.2), calls=%async_computation.2 | async-start | bytes 2162688 | tf_op jit(solution)/shard_map/all_to_all | solution.py:214
  89.8 4.8 %collective-permute-start.5 = (bf16[512,1024]{1,0:T(8,128)(2,1)S(1)}, bf16[512,1024]{1,0:T(8,128)(2,1)}, u32[]{:S(2)}, u32[]{:S(2)}) collective-permute-start(bf16[512,1024]{1,0:T(8,128)(2,1)S(1)} %get-tuple-element.49), channel_id=1, source_target_pairs={{0,64},{64,0},{1,65},{65,1},{2,66},{66,2},{3,67},{67,3},{4,68},{68... | collective-permute-start | bytes 3145736 | tf_op jit(solution)/shard_map/ppermute | solution.py:216
  92.2 0.7 collective-permute-start.4
  123.6 34.2 %all-to-all-start.3 = ((bf16[32,136,128]{2,1,0:T(8,128)(2,1)}), bf16[32,136,128]{2,1,0:T(8,128)(2,1)S(1)}, u32[]{:S(2)}, u32[]{:S(2)}) async-start(bf16[32,136,128]{2,1,0:T(8,128)(2,1)} %shard_map.96), calls=%async_computation.3 | async-start | bytes 2228224 | tf_op jit(solution)/shard_map/all_to_all | solution.py:229
  131.5 4.4 %collective-permute-start.6 = (bf16[2,512,256]{2,1,0:T(8,128)(2,1)S(1)}, bf16[2,512,256]{2,1,0:T(8,128)(2,1)S(1)}, u32[]{:S(2)}, u32[]{:S(2)}) collective-permute-start(bf16[2,512,256]{2,1,0:T(8,128)(2,1)S(1)} %bitcast.31), channel_id=1, source_target_pairs={{0,64},{64,0},{1,65},{65,1},{2,66},{66,2},{3,67},{67,3},{4,68},{68... | collective-permute-start | bytes 1572872 | tf_op jit(solution)/shard_map/ppermute | solution.py:237
  134.2 6.7 %collective-permute-start.7 = (bf16[128,256]{1,0:T(8,128)(2,1)S(1)}, bf16[128,256]{1,0:T(8,128)(2,1)S(1)}, u32[]{:S(2)}, u32[]{:S(2)}) collective-permute-start(bf16[128,256]{1,0:T(8,128)(2,1)S(1)} %collective-permute-done.4), channel_id=1, source_target_pairs={{0,0},{1,1},{2,2},{3,3},{4,4},{5,5},{6,6},{7,7},{130,128},{131,129... | collective-permute-start | bytes 196616 | tf_op jit(solution)/shard_map/ppermute | solution.py:230
  140.9 21.2 %copy-start.5 = (f32[16,3]{0,1:T(4,128)S(1)}, f32[16,3]{0,1:T(4,128)}, u32[]{:S(2)}) copy-start(f32[16,3]{0,1:T(4,128)} %param.9) | copy-start | bytes 580
  158.7 4.2 %collective-permute-start.8 = (f32[8,128]{1,0:T(8,128)S(1)}, f32[8,128]{1,0:T(8,128)S(1)}, u32[]{:S(2)}, u32[]{:S(2)}) collective-permute-start(f32[8,128]{1,0:T(8,128)S(1)} %get-tuple-element.62), channel_id=1, source_target_pairs={{0,64},{64,0},{1,65},{65,1},{2,66},{66,2},{3,67},{67,3},{4,68},{68... | collective-permute-start | bytes 12296 | tf_op jit(solution)/shard_map/ppermute | solution.py:254

commit v11 on v9

--- a/solution.py
+++ b/solution.py
@@ -14,11 +14,16 @@
 SMEM = pl.BlockSpec(memory_space=pltpu.SMEM)
 
 
-def call(body, outs, args, flops=0, moved=0, scratch=(), vmem=48, far=(), far_outs=()):
+def window(array, block):
+    return pl.BlockSpec((1,) + array.shape[1:], lambda i: (block, 0, 0))
+
+
+def call(body, outs, args, flops=0, moved=0, scratch=(), vmem=48, far=(), far_outs=(), windows=()):
     return pl.pallas_call(
         body,
+        grid=(1,) if windows else (),
         out_shape=[jax.ShapeDtypeStruct(s, t) for s, t in outs],
-        in_specs=[SMEM if a.dtype == jnp.int32 else ANY if i in far else VMEM for i, a in enumerate(args)],
+        in_specs=[window(args[i], windows.index(i)) if i in windows else SMEM if a.dtype == jnp.int32 else ANY if i in far else VMEM for i, a in enumerate(args)],
         out_specs=[ANY if i in far_outs else VMEM for i in range(len(outs))],
         scratch_shapes=list(scratch),
         compiler_params=pltpu.CompilerParams(vmem_limit_bytes=vmem * 2**20),
@@ -73,10 +78,7 @@
         copy.wait()
 
 
-def forward_body(place_ref, x_ref, g0_ref, u0_ref, stash_ref, out_ref, xh_ref, held_ref, sems):
-    copies = copies_of(lambda i: stash_ref.at[i], lambda i: held_ref.at[i], sems)
-    for copy in copies:
-        copy.start()
+def forward_body(place_ref, x_ref, g0_ref, u0_ref, g1_ref, u1_ref, out_ref, xh_ref):
     groups, cols, rows = out_ref.shape[0] // 2, x_ref.shape[0] // (out_ref.shape[0] // 2), x_ref.shape[1]
     core, turned = place_ref[0], place_ref[1]
     for g in range(groups):
@@ -84,11 +86,9 @@
         for k in range(cols):
             xh_ref[spot, k * 128 : (k + 1) * 128] = x_ref[g * cols + k]
     x = xh_ref[...]
-    for which, pair in enumerate(((g0_ref, u0_ref), (held_ref.at[0], held_ref.at[1]))):
+    for which, pair in enumerate(((g0_ref, u0_ref), (g1_ref.at[0], u1_ref.at[0]))):
         place = core if which == 0 else 1 - core
         for half, w_ref in enumerate(pair):
-            if which == 1:
-                copies[half].wait()
             part = jnp.dot(x, w_ref[...], preferred_element_type=F32).astype(BF16)
             for g in range(groups):
                 out_ref[2 * g + place, half * rows : (half + 1) * rows, :] = part[g * rows : (g + 1) * rows]
@@ -118,21 +118,16 @@
         q_ref[i, 2 * rows :, :] = wide
 
 
-def backward_body(place_ref, q_ref, g0_ref, u0_ref, stash_ref, out_ref, kept_ref, held_ref, sems):
-    copies = copies_of(lambda i: stash_ref.at[i], lambda i: held_ref.at[i], sems)
-    for copy in copies:
-        copy.start()
+def backward_body(place_ref, q_ref, g0_ref, u0_ref, g1_ref, u1_ref, out_ref, kept_ref):
     groups = q_ref.shape[0] // 2
     rows = (q_ref.shape[1] - 8) // 2
     cols = out_ref.shape[0] // groups
     core, turned = place_ref[0], place_ref[1]
     contract = (((1,), (1,)), ((), ()))
     total = None
-    for which, pair in enumerate(((g0_ref, u0_ref), (held_ref.at[0], held_ref.at[1]))):
+    for which, pair in enumerate(((g0_ref, u0_ref), (g1_ref.at[0], u1_ref.at[0]))):
         place = core if which == 0 else 1 - core
         for half, w_ref in enumerate(pair):
-            if which == 1:
-                copies[half].wait()
             for g in range(groups):
                 kept_ref[g * rows : (g + 1) * rows, :] = q_ref[2 * g + place, half * rows : (half + 1) * rows, :]
             part = lax.dot_general(kept_ref[...], w_ref[...], contract, preferred_element_type=F32)
@@ -179,7 +174,6 @@
         far=(0, 1),
         far_outs=(0,),
     )
-    held = [pltpu.VMEM((2, depth, units), BF16), pltpu.SemaphoreType.DMA((2,))]
     up = lax.ppermute(upstream, ("h", "y"), along_y)
     x_all, stash, up = lax.optimization_barrier((x_all, stash, up))
 
@@ -187,12 +181,11 @@
     parts, x_mine = call(
         forward_body,
         [((ny, 2 * rows, units), BF16), ((nh * rows, depth), BF16)],
-        (place, x_all, w_gate, w_up, stash),
+        (place, x_all, w_gate, w_up, stash, stash),
         flops=work,
         moved=6 * 2**20,
-        scratch=held,
         vmem=48,
-        far=(4,),
+        windows=(4, 5),
     )
     parts, x_mine, up = lax.optimization_barrier((parts, x_mine, up))
     sums = lax.all_to_all(parts, "y", 0, 0, tiled=True)
@@ -209,12 +202,12 @@
     (back,) = call(
         backward_body,
         [((count, rows + 8, width), BF16)],
-        (place, q_all, w_gate, w_up, stash),
+        (place, q_all, w_gate, w_up, stash, stash),
         flops=work,
         moved=6 * 2**20,
-        scratch=[pltpu.VMEM((nh * rows, units), BF16)] + held,
+        scratch=[pltpu.VMEM((nh * rows, units), BF16)],
         vmem=48,
-        far=(4,),
+        windows=(4, 5),
     )
     back, q_all, hidden = lax.optimization_barrier((back, q_all, hidden))
     back_all = lax.all_to_all(back, plane, 0, 0, tiled=True)

time: 164 us -> 163 us (level)
  no operation moved by 1% of the time
where the time goes in v11:
time: 163 us; the launch traced here: 162 us
  waiting for transfers between devices  93.3 us (57%)
  starting transfers between devices  45.7 us (28%)
  Pallas kernels  9.46 us (6%)
  matrix products  5.96 us (4%)
  local copies, waits for them, and re-layouts  4.54 us (3%)
  between operations  2.2 us (1%)
    all_to_all x1, waiting for transfers between devices, per_device(): sums = lax.all_to_all(parts, 'y', 0, 0, tiled=True)  28.5 us
    all_to_all x1, waiting for transfers between devices, per_device(): q_all = lax.all_to_all(quants, 'y', 0, 0, tiled=True)  25.1 us
    all_to_all x1, waiting for transfers between devices, per_device(): x_all = lax.all_to_all(copies, plane, 0, 0, tiled=True)  19.2 us
    all_to_all x1, waiting for transfers between devices, per_device(): back_all = lax.all_to_all(back, plane, 0, 0, tiled=True)  16.9 us
    all_to_all x1, starting transfers between devices, per_device(): x_all = lax.all_to_all(copies, plane, 0, 0, tiled=True)  13.7 us
    pallas_call x6, Pallas kernels, call(): pl.pallas_call(body, grid=(1,) if windows else (), out_shape=[jax.ShapeDt...  9.46 us
    all_to_all x1, starting transfers between devices, per_device(): sums = lax.all_to_all(parts, 'y', 0, 0, tiled=True)  6.83 us
    all_to_all x1, starting transfers between devices, per_device(): back_all = lax.all_to_all(back, plane, 0, 0, tiled=True)  5.77 us
  transfers between devices with their start and end apart: 13, of which 7 were waited for; matrix products, arithmetic and copies ran while one was open for 4% of the time, Pallas kernels for 1%

profile of v11, /device:TPU:1, one launch (start us, length us, event | category | flops | bytes accessed | tf_op | source)
XLA Modules:
  0.0 161.9 jit_solution(3232097473227933888)
XLA Ops:
  0.6 0.0 copy-start
  0.6 0.0 copy-start.1
  0.7 0.8 copy.11.hist_ref
  1.5 0.0 copy-start.4
  1.5 0.8 copy-done.4
  2.3 0.0 copy-start.6
  2.3 1.2 shard_map.92
  3.4 13.7 %all-to-all-start = ((bf16[32,128,128]{2,1,0:T(8,128)(2,1)}), bf16[32,128,128]{2,1,0:T(8,128)(2,1)S(1)}, u32[]{:S(2)}, u32[]{:S(2)}) async-start(bf16[32,128,128]{2,1,0:T(8,128)(2,1)} %get-tuple-element.34), calls=%async_computation | async-start | bytes 2097152 | tf_op jit(solution)/shard_map/all_to_all | solution.py:166
  17.1 0.0 copy-done
  17.1 2.9 %collective-permute-start = (bf16[1024,256]{1,0:T(8,128)(2,1)S(1)}, bf16[1024,256]{1,0:T(8,128)(2,1)S(1)}, u32[]{:S(2)}, u32[]{:S(2)}) collective-permute-start(bf16[1024,256]{1,0:T(8,128)(2,1)S(1)} %copy-done), channel_id=1, source_target_pairs={{0,64},{64,0},{1,65},{65,1},{2,66},{66,2},{3,67},{67,3},{4,68},{68... | collective-permute-start | bytes 1572872 | tf_op jit(solution)/shard_map/ppermute | solution.py:167
  20.0 0.0 copy-done.1
  20.0 1.9 %collective-permute-start.1 = (bf16[1024,256]{1,0:T(8,128)(2,1)S(1)}, bf16[1024,256]{1,0:T(8,128)(2,1)S(1)}, u32[]{:S(2)}, u32[]{:S(2)}) collective-permute-start(bf16[1024,256]{1,0:T(8,128)(2,1)S(1)} %copy-done.1), channel_id=1, source_target_pairs={{0,64},{64,0},{1,65},{65,1},{2,66},{66,2},{3,67},{67,3},{4,68},{68... | collective-permute-start | bytes 1572872 | tf_op jit(solution)/shard_map/ppermute | solution.py:168
  22.0 0.0 copy-done.6
  22.0 0.7 collective-permute-start.2
  22.6 0.1 pad_add_fusion.place_ref
  22.7 0.0 collective-permute-done.g_ref
  22.7 1.1 collective-permute-done.1.u_ref
  23.8 1.0 shard_map.93.g1_ref.u1_ref
  24.9 0.0 collective-permute-done.2
  24.9 19.2 %all-to-all-done.x_ref = bf16[32,128,128]{2,1,0:T(8,128)(2,1)S(1)} async-done(((bf16[32,128,128]{2,1,0:T(8,128)(2,1)}), bf16[32,128,128]{2,1,0:T(8,128)(2,1)S(1)}, u32[]{:S(2)}, u32[]{:S(2)}) %all-to-all-start) | async-done | bytes 1048608 | tf_op jit(solution)/shard_map/all_to_all | solution.py:166
  44.1 2.6 %shard_map.94 = (bf16[8,256,256]{2,1,0:T(8,128)(2,1)S(1)}, bf16[512,1024]{1,0:T(8,128)(2,1)S(1)}) custom-call(s32[2]{0:T(128)S(1)} %pad_add_fusion.place_ref, bf16[32,128,128]{2,1,0:T(8,128)(2,1)S(1)} %all-to-all-done.x_ref, bf16[1024,256]{1,0:T(8,128)(2,1)S(1)} %copy-done, bf16[1024,256]{1,0:T(8,128)(2,1)S(1)} %copy-done.1, ...), custom_call_target="tpu_custom_call" | custom-call | flops 1073741824 | bytes 6291456 | tf_op jit(solution)/shard_map/pallas_call | solution.py:22
  46.6 0.0 copy-start.3
  46.6 1.0 copy-done.3
  47.6 6.8 %all-to-all-start.1 = ((bf16[8,256,256]{2,1,0:T(8,128)(2,1)}), bf16[8,256,256]{2,1,0:T(8,128)(2,1)S(1)}, u32[]{:S(2)}, u32[]{:S(2)}) async-start(bf16[8,256,256]{2,1,0:T(8,128)(2,1)} %copy-done.3), calls=%async_computation.1 | async-start | bytes 2097152 | tf_op jit(solution)/shard_map/all_to_all | solution.py:191
  54.4 0.7 collective-permute-start.3
  55.1 0.0 collective-permute-done.3.up_ref
  55.1 28.5 %all-to-all-done.1.in_ref = bf16[8,256,256]{2,1,0:T(8,128)(2,1)S(1)} async-done(((bf16[8,256,256]{2,1,0:T(8,128)(2,1)}), bf16[8,256,256]{2,1,0:T(8,128)(2,1)S(1)}, u32[]{:S(2)}, u32[]{:S(2)}) %all-to-all-start.1) | async-done | bytes 1048608 | tf_op jit(solution)/shard_map/all_to_all | solution.py:191
  83.6 0.4 shard_map.95
  84.0 0.0 copy-start.2
  84.0 1.0 copy-done.2
  85.0 3.6 %all-to-all-start.2 = ((bf16[8,264,256]{2,1,0:T(8,128)(2,1)}), bf16[8,264,256]{2,1,0:T(8,128)(2,1)S(1)}, u32[]{:S(2)}, u32[]{:S(2)}) async-start(bf16[8,264,256]{2,1,0:T(8,128)(2,1)} %copy-done.2), calls=%async_computation.2 | async-start | bytes 2162688 | tf_op jit(solution)/shard_map/all_to_all | solution.py:198
  88.6 2.4 %collective-permute-start.5 = (bf16[512,1024]{1,0:T(8,128)(2,1)S(1)}, bf16[512,1024]{1,0:T(8,128)(2,1)}, u32[]{:S(2)}, u32[]{:S(2)}) collective-permute-start(bf16[512,1024]{1,0:T(8,128)(2,1)S(1)} %get-tuple-element.49), channel_id=1, source_target_pairs={{0,64},{64,0},{1,65},{65,1},{2,66},{66,2},{3,67},{67,3},{4,68},{68... | collective-permute-start | bytes 3145736 | tf_op jit(solution)/shard_map/ppermute | solution.py:200
  91.0 0.7 collective-permute-start.4
  91.6 0.0 collective-permute-done.4
  91.7 1.7 %collective-permute-done.5 = bf16[512,1024]{1,0:T(8,128)(2,1)} collective-permute-done((bf16[512,1024]{1,0:T(8,128)(2,1)S(1)}, bf16[512,1024]{1,0:T(8,128)(2,1)}, u32[]{:S(2)}, u32[]{:S(2)}) %collective-permute-start.5) | collective-permute-done | bytes 1048608 | tf_op jit(solution)/shard_map/ppermute | solution.py:200
  93.4 25.1 %all-to-all-done.2.q_ref = bf16[8,264,256]{2,1,0:T(8,128)(2,1)S(1)} async-done(((bf16[8,264,256]{2,1,0:T(8,128)(2,1)}), bf16[8,264,256]{2,1,0:T(8,128)(2,1)S(1)}, u32[]{:S(2)}, u32[]{:S(2)}) %all-to-all-start.2) | async-done | bytes 1081376 | tf_op jit(solution)/shard_map/all_to_all | solution.py:198
  118.5 3.5 %shard_map.96 = bf16[32,136,128]{2,1,0:T(8,128)(2,1)} custom-call(s32[2]{0:T(128)S(1)} %pad_add_fusion.place_ref, bf16[8,264,256]{2,1,0:T(8,128)(2,1)S(1)} %all-to-all-done.2.q_ref, bf16[1024,256]{1,0:T(8,128)(2,1)S(1)} %copy-done, bf16[1024,256]{1,0:T(8,128)(2,1)S(1)} %copy-done.1, bf16[64,1024,256]{2,1,0:T(8,128)(2,1)} %shard_map.93.g1_ref.u1_ref, ...), custom_call_target="tpu_custom_call" | custom-call | flops 1073741824 | bytes 6291456 | tf_op jit(solution)/shard_map/pallas_call | solution.py:22
  122.0 5.8 %all-to-all-start.3 = ((bf16[32,136,128]{2,1,0:T(8,128)(2,1)}), bf16[32,136,128]{2,1,0:T(8,128)(2,1)S(1)}, u32[]{:S(2)}, u32[]{:S(2)}) async-start(bf16[32,136,128]{2,1,0:T(8,128)(2,1)} %shard_map.96), calls=%async_computation.3 | async-start | bytes 2228224 | tf_op jit(solution)/shard_map/all_to_all | solution.py:213
  127.7 0.5 fusion.5
  129.6 0.1 slice.34
  129.6 0.1 constant_dynamic-slice_fusion
  129.8 2.7 %collective-permute-start.6 = (bf16[2,512,256]{2,1,0:T(8,128)(2,1)S(1)}, bf16[2,512,256]{2,1,0:T(8,128)(2,1)S(1)}, u32[]{:S(2)}, u32[]{:S(2)}) collective-permute-start(bf16[2,512,256]{2,1,0:T(8,128)(2,1)S(1)} %bitcast.31), channel_id=1, source_target_pairs={{0,64},{64,0},{1,65},{65,1},{2,66},{66,2},{3,67},{67,3},{4,68},{68... | collective-permute-start | bytes 1572872 | tf_op jit(solution)/shard_map/ppermute | solution.py:221
  132.5 0.7 collective-permute-start.7
  133.2 0.5 fusion.7
  133.7 0.5 fusion.6
  134.1 0.0 collective-permute-done.6
  134.2 2.5 %fusion.3 = bf16[1024,256]{1,0:T(8,128)(2,1)} fusion(f32[1024,256]{1,0:T(8,128)S(1)} %fusion.7, bf16[512,1024]{1,0:T(8,128)(2,1)} %collective-permute-done.5, f32[]{:T(128)} %bitcast.10, bf16[2,512,256]{2,1,0:T(8,128)(2,1)S(1)} %collective-permute-done.6), kind=kOutput, calls=%fused_computation.5 | convolution fusion | flops 269221888 | bytes 2883588 | tf_op jit(solution)/shard_map/dot_general | solution.py:227
  136.7 2.5 %fusion.2 = bf16[1024,256]{1,0:T(8,128)(2,1)} fusion(f32[1024,256]{1,0:T(8,128)S(1)} %fusion.6, bf16[512,1024]{1,0:T(8,128)(2,1)} %collective-permute-done.5, f32[]{:T(128)} %bitcast.10, bf16[2,512,256]{2,1,0:T(8,128)(2,1)S(1)} %collective-permute-done.6), kind=kOutput, calls=%fused_computation.4 | convolution fusion | flops 269221888 | bytes 2883588 | tf_op jit(solution)/shard_map/dot_general | solution.py:227
  139.2 0.0 copy-start.5
  139.2 0.0 collective-permute-done.7.hidden_ref
  139.2 16.9 %all-to-all-done.3.in_ref = bf16[32,136,128]{2,1,0:T(8,128)(2,1)S(1)} async-done(((bf16[32,136,128]{2,1,0:T(8,128)(2,1)}), bf16[32,136,128]{2,1,0:T(8,128)(2,1)S(1)}, u32[]{:S(2)}, u32[]{:S(2)}) %all-to-all-start.3) | async-done | bytes 1114144 | tf_op jit(solution)/shard_map/all_to_all | solution.py:213
  156.1 0.9 shard_map.97
  157.0 3.3 %collective-permute-start.8 = (f32[8,128]{1,0:T(8,128)S(1)}, f32[8,128]{1,0:T(8,128)S(1)}, u32[]{:S(2)}, u32[]{:S(2)}) collective-permute-start(f32[8,128]{1,0:T(8,128)S(1)} %get-tuple-element.62), channel_id=1, source_target_pairs={{0,64},{64,0},{1,65},{65,1},{2,66},{66,2},{3,67},{67,3},{4,68},{68... | collective-permute-start | bytes 12296 | tf_op jit(solution)/shard_map/ppermute | solution.py:238
  160.3 0.0 copy-done.5
  160.4 0.1 slice.42
  160.4 0.7 collective-permute-done.8
  161.1 0.1 slice_reduce_fusion
  161.3 0.7 maximum_select_fusion
  (4 shorter events, 0.1 us)
Async XLA Ops:
  0.6 16.5 %copy-start = (bf16[1024,256]{1,0:T(8,128)(2,1)S(1)}, bf16[1024,256]{1,0:T(8,128)(2,1)}, u32[]{:S(2)}) copy-start(bf16[1024,256]{1,0:T(8,128)(2,1)} %g0_ref.3) | copy-start | bytes 1572868
  0.6 19.4 %copy-start.1 = (bf16[1024,256]{1,0:T(8,128)(2,1)S(1)}, bf16[1024,256]{1,0:T(8,128)(2,1)}, u32[]{:S(2)}) copy-start(bf16[1024,256]{1,0:T(8,128)(2,1)} %u0_ref.3) | copy-start | bytes 1572868
  1.5 0.8 copy-start.4
  2.3 19.7 %copy-start.6 = (bf16[128,256]{1,0:T(8,128)(2,1)S(1)}, bf16[128,256]{1,0:T(8,128)(2,1)}, u32[]{:S(2)}) copy-start(bf16[128,256]{1,0:T(8,128)(2,1)} %param.8) | copy-start | bytes 196612
  3.4 40.6 %all-to-all-start = ((bf16[32,128,128]{2,1,0:T(8,128)(2,1)}), bf16[32,128,128]{2,1,0:T(8,128)(2,1)S(1)}, u32[]{:S(2)}, u32[]{:S(2)}) async-start(bf16[32,128,128]{2,1,0:T(8,128)(2,1)} %get-tuple-element.34), calls=%async_computation | async-start | bytes 2097152 | tf_op jit(solution)/shard_map/all_to_all | solution.py:166
  17.1 5.6 %collective-permute-start = (bf16[1024,256]{1,0:T(8,128)(2,1)S(1)}, bf16[1024,256]{1,0:T(8,128)(2,1)S(1)}, u32[]{:S(2)}, u32[]{:S(2)}) collective-permute-start(bf16[1024,256]{1,0:T(8,128)(2,1)S(1)} %copy-done), channel_id=1, source_target_pairs={{0,64},{64,0},{1,65},{65,1},{2,66},{66,2},{3,67},{67,3},{4,68},{68... | collective-permute-start | bytes 1572872 | tf_op jit(solution)/shard_map/ppermute | solution.py:167
  20.0 3.8 %collective-permute-start.1 = (bf16[1024,256]{1,0:T(8,128)(2,1)S(1)}, bf16[1024,256]{1,0:T(8,128)(2,1)S(1)}, u32[]{:S(2)}, u32[]{:S(2)}) collective-permute-start(bf16[1024,256]{1,0:T(8,128)(2,1)S(1)} %copy-done.1), channel_id=1, source_target_pairs={{0,64},{64,0},{1,65},{65,1},{2,66},{66,2},{3,67},{67,3},{4,68},{68... | collective-permute-start | bytes 1572872 | tf_op jit(solution)/shard_map/ppermute | solution.py:168
  22.0 2.9 %collective-permute-start.2 = (bf16[128,256]{1,0:T(8,128)(2,1)S(1)}, bf16[128,256]{1,0:T(8,128)(2,1)S(1)}, u32[]{:S(2)}, u32[]{:S(2)}) collective-permute-start(bf16[128,256]{1,0:T(8,128)(2,1)S(1)} %copy-done.6), channel_id=1, source_target_pairs={{0,0},{1,1},{2,2},{3,3},{4,4},{5,5},{6,6},{7,7},{128,130},{129,131... | collective-permute-start | bytes 196616 | tf_op jit(solution)/shard_map/ppermute | solution.py:177
  46.6 1.0 copy-start.3
  47.6 36.0 %all-to-all-start.1 = ((bf16[8,256,256]{2,1,0:T(8,128)(2,1)}), bf16[8,256,256]{2,1,0:T(8,128)(2,1)S(1)}, u32[]{:S(2)}, u32[]{:S(2)}) async-start(bf16[8,256,256]{2,1,0:T(8,128)(2,1)} %copy-done.3), calls=%async_computation.1 | async-start | bytes 2097152 | tf_op jit(solution)/shard_map/all_to_all | solution.py:191
  54.4 0.7 collective-permute-start.3
  84.0 1.0 copy-start.2
  85.0 33.5 %all-to-all-start.2 = ((bf16[8,264,256]{2,1,0:T(8,128)(2,1)}), bf16[8,264,256]{2,1,0:T(8,128)(2,1)S(1)}, u32[]{:S(2)}, u32[]{:S(2)}) async-start(bf16[8,264,256]{2,1,0:T(8,128)(2,1)} %copy-done.2), calls=%async_computation.2 | async-start | bytes 2162688 | tf_op jit(solution)/shard_map/all_to_all | solution.py:198
  88.6 4.8 %collective-permute-start.5 = (bf16[512,1024]{1,0:T(8,128)(2,1)S(1)}, bf16[512,1024]{1,0:T(8,128)(2,1)}, u32[]{:S(2)}, u32[]{:S(2)}) collective-permute-start(bf16[512,1024]{1,0:T(8,128)(2,1)S(1)} %get-tuple-element.49), channel_id=1, source_target_pairs={{0,64},{64,0},{1,65},{65,1},{2,66},{66,2},{3,67},{67,3},{4,68},{68... | collective-permute-start | bytes 3145736 | tf_op jit(solution)/shard_map/ppermute | solution.py:200
  91.0 0.7 collective-permute-start.4
  122.0 34.2 %all-to-all-start.3 = ((bf16[32,136,128]{2,1,0:T(8,128)(2,1)}), bf16[32,136,128]{2,1,0:T(8,128)(2,1)S(1)}, u32[]{:S(2)}, u32[]{:S(2)}) async-start(bf16[32,136,128]{2,1,0:T(8,128)(2,1)} %shard_map.96), calls=%async_computation.3 | async-start | bytes 2228224 | tf_op jit(solution)/shard_map/all_to_all | solution.py:213
  129.8 4.4 %collective-permute-start.6 = (bf16[2,512,256]{2,1,0:T(8,128)(2,1)S(1)}, bf16[2,512,256]{2,1,0:T(8,128)(2,1)S(1)}, u32[]{:S(2)}, u32[]{:S(2)}) collective-permute-start(bf16[2,512,256]{2,1,0:T(8,128)(2,1)S(1)} %bitcast.31), channel_id=1, source_target_pairs={{0,64},{64,0},{1,65},{65,1},{2,66},{66,2},{3,67},{67,3},{4,68},{68... | collective-permute-start | bytes 1572872 | tf_op jit(solution)/shard_map/ppermute | solution.py:221
  132.5 6.7 %collective-permute-start.7 = (bf16[128,256]{1,0:T(8,128)(2,1)S(1)}, bf16[128,256]{1,0:T(8,128)(2,1)S(1)}, u32[]{:S(2)}, u32[]{:S(2)}) collective-permute-start(bf16[128,256]{1,0:T(8,128)(2,1)S(1)} %collective-permute-done.4), channel_id=1, source_target_pairs={{0,0},{1,1},{2,2},{3,3},{4,4},{5,5},{6,6},{7,7},{130,128},{131,129... | collective-permute-start | bytes 196616 | tf_op jit(solution)/shard_map/ppermute | solution.py:214
  139.2 21.2 %copy-start.5 = (f32[16,3]{0,1:T(4,128)S(1)}, f32[16,3]{0,1:T(4,128)}, u32[]{:S(2)}) copy-start(f32[16,3]{0,1:T(4,128)} %param.9) | copy-start | bytes 580
  157.0 4.2 %collective-permute-start.8 = (f32[8,128]{1,0:T(8,128)S(1)}, f32[8,128]{1,0:T(8,128)S(1)}, u32[]{:S(2)}, u32[]{:S(2)}) collective-permute-start(f32[8,128]{1,0:T(8,128)S(1)} %get-tuple-element.62), channel_id=1, source_target_pairs={{0,64},{64,0},{1,65},{65,1},{2,66},{66,2},{3,67},{67,3},{4,68},{68... | collective-permute-start | bytes 12296 | tf_op jit(solution)/shard_map/ppermute | solution.py:238

commit v12 on v11

--- a/solution.py
+++ b/solution.py
@@ -140,10 +140,13 @@
             out_ref[first + k, rows:, :] = packed
 
 
-def last_body(in_ref, scal_ref, hidden_ref, out_ref, peaks_ref, hidden_out_ref):
+def peaks_body(in_ref, peaks_ref):
+    peaks_ref[...] = rows_of(*unpack_peaks(in_ref[:, in_ref.shape[1] - 8 :, :].astype(F32)))
+
+
+def last_body(in_ref, scal_ref, hidden_ref, out_ref, hidden_out_ref):
     rows = out_ref.shape[0]
     out_ref[...] = (jnp.sum(in_ref[:, :rows, :].astype(F32), axis=0) / scal_ref[1:2, 0:1]).astype(BF16)
-    peaks_ref[...] = rows_of(*unpack_peaks(in_ref[:, rows:, :].astype(F32)))
     hidden_out_ref[...] = hidden_ref[...]
 
 
@@ -229,9 +232,10 @@
         )
         grads.append((total / divisor).astype(BF16))
     back_all, grads, hidden = lax.optimization_barrier((back_all, grads, hidden))
-    input_grad, peaks, hidden = call(
+    (peaks,) = call(peaks_body, [((8, 128), F32)], (back_all,))
+    input_grad, hidden = call(
         last_body,
-        [((rows, width), BF16), ((8, 128), F32), ((rows, units), BF16)],
+        [((rows, width), BF16), ((rows, units), BF16)],
         (back_all, scal, hidden),
         moved=2**21,
     )

time: 163 us -> 162 us (level)
    pallas_call x6 -> x7, Pallas kernels: 9.46 us -> 9.53 us  [call(): pl.pallas_call(body, grid=(1,) if windows else (), out_shape=[jax.ShapeDt...]
    unnamed x15 -> x19, local copies, waits for them, and re-layouts: 3.59 us -> 3.6 us
  transfers between devices with their start and end apart: 13 -> 13, of which waited for: 7 -> 6; matrix products, arithmetic and copies ran while one was open for 4% -> 4% of each run, Pallas kernels for 1% -> 1%
where the time goes in v12:
time: 162 us; the launch traced here: 161 us
  waiting for transfers between devices  92.6 us (57%)
  starting transfers between devices  45.9 us (28%)
  Pallas kernels  9.53 us (6%)
  matrix products  5.97 us (4%)
  local copies, waits for them, and re-layouts  4.55 us (3%)
  between operations  2.21 us (1%)
    all_to_all x1, waiting for transfers between devices, per_device(): sums = lax.all_to_all(parts, 'y', 0, 0, tiled=True)  28.5 us
    all_to_all x1, waiting for transfers between devices, per_device(): q_all = lax.all_to_all(quants, 'y', 0, 0, tiled=True)  25.1 us
    all_to_all x1, waiting for transfers between devices, per_device(): x_all = lax.all_to_all(copies, plane, 0, 0, tiled=True)  19.2 us
    all_to_all x1, waiting for transfers between devices, per_device(): back_all = lax.all_to_all(back, plane, 0, 0, tiled=True)  16.9 us
    all_to_all x1, starting transfers between devices, per_device(): x_all = lax.all_to_all(copies, plane, 0, 0, tiled=True)  13.7 us
    pallas_call x7, Pallas kernels, call(): pl.pallas_call(body, grid=(1,) if windows else (), out_shape=[jax.ShapeDt...  9.53 us
    all_to_all x1, starting transfers between devices, per_device(): sums = lax.all_to_all(parts, 'y', 0, 0, tiled=True)  6.8 us
    all_to_all x1, starting transfers between devices, per_device(): back_all = lax.all_to_all(back, plane, 0, 0, tiled=True)  5.8 us
  transfers between devices with their start and end apart: 13, of which 6 were waited for; matrix products, arithmetic and copies ran while one was open for 4% of the time, Pallas kernels for 1%

profile of v12, /device:TPU:1, one launch (start us, length us, event | category | flops | bytes accessed | tf_op | source)
XLA Modules:
  0.0 161.5 jit_solution(8304989111412399724)
XLA Ops:
  0.6 0.0 copy-start
  0.6 0.0 copy-start.2
  0.7 0.8 copy.11.hist_ref
  1.5 0.0 copy-start.6
  1.5 0.8 copy-done.6
  2.3 0.0 copy-start.8
  2.3 1.1 shard_map.92
  3.4 13.7 %all-to-all-start = ((bf16[32,128,128]{2,1,0:T(8,128)(2,1)}), bf16[32,128,128]{2,1,0:T(8,128)(2,1)S(1)}, u32[]{:S(2)}, u32[]{:S(2)}) async-start(bf16[32,128,128]{2,1,0:T(8,128)(2,1)} %get-tuple-element.33), calls=%async_computation | async-start | bytes 2097152 | tf_op jit(solution)/shard_map/all_to_all | solution.py:169
  17.1 0.0 copy-done
  17.1 2.9 %collective-permute-start = (bf16[1024,256]{1,0:T(8,128)(2,1)S(1)}, bf16[1024,256]{1,0:T(8,128)(2,1)S(1)}, u32[]{:S(2)}, u32[]{:S(2)}) collective-permute-start(bf16[1024,256]{1,0:T(8,128)(2,1)S(1)} %copy-done), channel_id=1, source_target_pairs={{0,64},{64,0},{1,65},{65,1},{2,66},{66,2},{3,67},{67,3},{4,68},{68... | collective-permute-start | bytes 1572872 | tf_op jit(solution)/shard_map/ppermute | solution.py:170
  20.0 0.0 copy-done.2
  20.0 1.9 %collective-permute-start.1 = (bf16[1024,256]{1,0:T(8,128)(2,1)S(1)}, bf16[1024,256]{1,0:T(8,128)(2,1)S(1)}, u32[]{:S(2)}, u32[]{:S(2)}) collective-permute-start(bf16[1024,256]{1,0:T(8,128)(2,1)S(1)} %copy-done.2), channel_id=1, source_target_pairs={{0,64},{64,0},{1,65},{65,1},{2,66},{66,2},{3,67},{67,3},{4,68},{68... | collective-permute-start | bytes 1572872 | tf_op jit(solution)/shard_map/ppermute | solution.py:171
  22.0 0.0 copy-done.8
  22.0 0.7 collective-permute-start.2
  22.6 0.1 pad_add_fusion.place_ref
  22.7 0.0 collective-permute-done.g_ref
  22.7 1.1 collective-permute-done.1.u_ref
  23.8 1.0 shard_map.93.g1_ref.u1_ref
  24.8 0.0 collective-permute-done.2
  24.9 19.2 %all-to-all-done.x_ref = bf16[32,128,128]{2,1,0:T(8,128)(2,1)S(1)} async-done(((bf16[32,128,128]{2,1,0:T(8,128)(2,1)}), bf16[32,128,128]{2,1,0:T(8,128)(2,1)S(1)}, u32[]{:S(2)}, u32[]{:S(2)}) %all-to-all-start) | async-done | bytes 1048608 | tf_op jit(solution)/shard_map/all_to_all | solution.py:169
  44.0 2.6 %shard_map.94 = (bf16[8,256,256]{2,1,0:T(8,128)(2,1)S(1)}, bf16[512,1024]{1,0:T(8,128)(2,1)S(1)}) custom-call(s32[2]{0:T(128)S(1)} %pad_add_fusion.place_ref, bf16[32,128,128]{2,1,0:T(8,128)(2,1)S(1)} %all-to-all-done.x_ref, bf16[1024,256]{1,0:T(8,128)(2,1)S(1)} %copy-done, bf16[1024,256]{1,0:T(8,128)(2,1)S(1)} %copy-done.2, ...), custom_call_target="tpu_custom_call" | custom-call | flops 1073741824 | bytes 6291456 | tf_op jit(solution)/shard_map/pallas_call | solution.py:22
  46.6 0.0 copy-start.5
  46.6 1.0 copy-done.5
  47.6 6.8 %all-to-all-start.1 = ((bf16[8,256,256]{2,1,0:T(8,128)(2,1)}), bf16[8,256,256]{2,1,0:T(8,128)(2,1)S(1)}, u32[]{:S(2)}, u32[]{:S(2)}) async-start(bf16[8,256,256]{2,1,0:T(8,128)(2,1)} %copy-done.5), calls=%async_computation.1 | async-start | bytes 2097152 | tf_op jit(solution)/shard_map/all_to_all | solution.py:194
  54.4 0.7 collective-permute-start.3
  55.1 0.0 collective-permute-done.3.up_ref
  55.1 28.5 %all-to-all-done.1.in_ref = bf16[8,256,256]{2,1,0:T(8,128)(2,1)S(1)} async-done(((bf16[8,256,256]{2,1,0:T(8,128)(2,1)}), bf16[8,256,256]{2,1,0:T(8,128)(2,1)S(1)}, u32[]{:S(2)}, u32[]{:S(2)}) %all-to-all-start.1) | async-done | bytes 1048608 | tf_op jit(solution)/shard_map/all_to_all | solution.py:194
  83.6 0.4 shard_map.95
  84.0 0.0 copy-start.4
  84.0 1.0 copy-done.4
  85.0 0.0 copy-start.1
  85.0 0.0 copy-start.3
  85.0 3.7 %all-to-all-start.2 = ((bf16[8,264,256]{2,1,0:T(8,128)(2,1)}), bf16[8,264,256]{2,1,0:T(8,128)(2,1)S(1)}, u32[]{:S(2)}, u32[]{:S(2)}) async-start(bf16[8,264,256]{2,1,0:T(8,128)(2,1)} %copy-done.4), calls=%async_computation.2 | async-start | bytes 2162688 | tf_op jit(solution)/shard_map/all_to_all | solution.py:201
  88.7 2.4 %collective-permute-start.5 = (bf16[512,1024]{1,0:T(8,128)(2,1)S(1)}, bf16[512,1024]{1,0:T(8,128)(2,1)}, u32[]{:S(2)}, u32[]{:S(2)}) collective-permute-start(bf16[512,1024]{1,0:T(8,128)(2,1)S(1)} %get-tuple-element.48), channel_id=1, source_target_pairs={{0,64},{64,0},{1,65},{65,1},{2,66},{66,2},{3,67},{67,3},{4,68},{68... | collective-permute-start | bytes 3145736 | tf_op jit(solution)/shard_map/ppermute | solution.py:203
  91.1 0.7 collective-permute-start.4
  91.8 0.0 collective-permute-done.4
  91.8 1.7 %collective-permute-done.5 = bf16[512,1024]{1,0:T(8,128)(2,1)} collective-permute-done((bf16[512,1024]{1,0:T(8,128)(2,1)S(1)}, bf16[512,1024]{1,0:T(8,128)(2,1)}, u32[]{:S(2)}, u32[]{:S(2)}) %collective-permute-start.5) | collective-permute-done | bytes 1048608 | tf_op jit(solution)/shard_map/ppermute | solution.py:203
  93.5 25.1 %all-to-all-done.2.q_ref = bf16[8,264,256]{2,1,0:T(8,128)(2,1)S(1)} async-done(((bf16[8,264,256]{2,1,0:T(8,128)(2,1)}), bf16[8,264,256]{2,1,0:T(8,128)(2,1)S(1)}, u32[]{:S(2)}, u32[]{:S(2)}) %all-to-all-start.2) | async-done | bytes 1081376 | tf_op jit(solution)/shard_map/all_to_all | solution.py:201
  118.6 0.0 copy-done.1
  118.6 0.0 copy-done.3
  118.6 3.5 %shard_map.96 = bf16[32,136,128]{2,1,0:T(8,128)(2,1)} custom-call(s32[2]{0:T(128)S(1)} %pad_add_fusion.place_ref, bf16[8,264,256]{2,1,0:T(8,128)(2,1)S(1)} %all-to-all-done.2.q_ref, bf16[1024,256]{1,0:T(8,128)(2,1)S(1)} %copy-done.1, bf16[1024,256]{1,0:T(8,128)(2,1)S(1)} %copy-done.3, bf16[64,1024,256]{2,1,0:T(8,128)(2,1)} %shard_map.93.g1_ref.u1_ref, ...), custom_call_target="tpu_custom_call" | custom-call | flops 1073741824 | bytes 6291456 | tf_op jit(solution)/shard_map/pallas_call | solution.py:22
  122.1 5.8 %all-to-all-start.3 = ((bf16[32,136,128]{2,1,0:T(8,128)(2,1)}), bf16[32,136,128]{2,1,0:T(8,128)(2,1)S(1)}, u32[]{:S(2)}, u32[]{:S(2)}) async-start(bf16[32,136,128]{2,1,0:T(8,128)(2,1)} %shard_map.96), calls=%async_computation.3 | async-start | bytes 2228224 | tf_op jit(solution)/shard_map/all_to_all | solution.py:216
  127.9 0.5 fusion.5
  129.7 0.1 slice.34
  129.8 0.1 constant_dynamic-slice_fusion
  129.9 2.7 %collective-permute-start.6 = (bf16[2,512,256]{2,1,0:T(8,128)(2,1)S(1)}, bf16[2,512,256]{2,1,0:T(8,128)(2,1)S(1)}, u32[]{:S(2)}, u32[]{:S(2)}) collective-permute-start(bf16[2,512,256]{2,1,0:T(8,128)(2,1)S(1)} %bitcast.31), channel_id=1, source_target_pairs={{0,64},{64,0},{1,65},{65,1},{2,66},{66,2},{3,67},{67,3},{4,68},{68... | collective-permute-start | bytes 1572872 | tf_op jit(solution)/shard_map/ppermute | solution.py:224
  132.6 0.7 collective-permute-start.7
  133.3 0.5 fusion.7
  133.8 0.5 fusion.6
  134.3 0.0 collective-permute-done.6
  134.3 2.5 %fusion.3 = bf16[1024,256]{1,0:T(8,128)(2,1)} fusion(f32[1024,256]{1,0:T(8,128)S(1)} %fusion.7, bf16[512,1024]{1,0:T(8,128)(2,1)} %collective-permute-done.5, f32[]{:T(128)} %bitcast.10, bf16[2,512,256]{2,1,0:T(8,128)(2,1)S(1)} %collective-permute-done.6), kind=kOutput, calls=%fused_computation.5 | convolution fusion | flops 269221888 | bytes 2883588 | tf_op jit(solution)/shard_map/dot_general | solution.py:230
  136.8 2.5 %fusion.2 = bf16[1024,256]{1,0:T(8,128)(2,1)} fusion(f32[1024,256]{1,0:T(8,128)S(1)} %fusion.6, bf16[512,1024]{1,0:T(8,128)(2,1)} %collective-permute-done.5, f32[]{:T(128)} %bitcast.10, bf16[2,512,256]{2,1,0:T(8,128)(2,1)S(1)} %collective-permute-done.6), kind=kOutput, calls=%fused_computation.4 | convolution fusion | flops 269221888 | bytes 2883588 | tf_op jit(solution)/shard_map/dot_general | solution.py:230
  139.3 0.0 copy-start.7
  139.3 0.0 collective-permute-done.7.hidden_ref
  139.3 16.9 %all-to-all-done.3.in_ref = bf16[32,136,128]{2,1,0:T(8,128)(2,1)S(1)} async-done(((bf16[32,136,128]{2,1,0:T(8,128)(2,1)}), bf16[32,136,128]{2,1,0:T(8,128)(2,1)S(1)}, u32[]{:S(2)}, u32[]{:S(2)}) %all-to-all-start.3) | async-done | bytes 1114144 | tf_op jit(solution)/shard_map/all_to_all | solution.py:216
  156.3 0.1 shard_map.98
  156.4 3.4 %collective-permute-start.8 = (f32[8,128]{1,0:T(8,128)S(1)}, f32[8,128]{1,0:T(8,128)S(1)}, u32[]{:S(2)}, u32[]{:S(2)}) collective-permute-start(f32[8,128]{1,0:T(8,128)S(1)} %shard_map.98), channel_id=1, source_target_pairs={{0,64},{64,0},{1,65},{65,1},{2,66},{66,2},{3,67},{67,3},{4,68},{68... | collective-permute-start | bytes 12296 | tf_op jit(solution)/shard_map/ppermute | solution.py:242
  159.8 0.0 copy-done.7
  159.8 0.1 slice.42
  159.9 0.8 shard_map.97
  160.7 0.0 collective-permute-done.8
  160.7 0.1 slice_reduce_fusion
  160.8 0.7 maximum_select_fusion
  (4 shorter events, 0.1 us)
Async XLA Ops:
  0.6 16.5 %copy-start = (bf16[1024,256]{1,0:T(8,128)(2,1)S(1)}, bf16[1024,256]{1,0:T(8,128)(2,1)}, u32[]{:S(2)}) copy-start(bf16[1024,256]{1,0:T(8,128)(2,1)} %g0_ref.3) | copy-start | bytes 1572868
  0.6 19.4 %copy-start.2 = (bf16[1024,256]{1,0:T(8,128)(2,1)S(1)}, bf16[1024,256]{1,0:T(8,128)(2,1)}, u32[]{:S(2)}) copy-start(bf16[1024,256]{1,0:T(8,128)(2,1)} %u0_ref.3) | copy-start | bytes 1572868
  1.5 0.8 copy-start.6
  2.3 19.7 %copy-start.8 = (bf16[128,256]{1,0:T(8,128)(2,1)S(1)}, bf16[128,256]{1,0:T(8,128)(2,1)}, u32[]{:S(2)}) copy-start(bf16[128,256]{1,0:T(8,128)(2,1)} %param.8) | copy-start | bytes 196612
  3.4 40.6 %all-to-all-start = ((bf16[32,128,128]{2,1,0:T(8,128)(2,1)}), bf16[32,128,128]{2,1,0:T(8,128)(2,1)S(1)}, u32[]{:S(2)}, u32[]{:S(2)}) async-start(bf16[32,128,128]{2,1,0:T(8,128)(2,1)} %get-tuple-element.33), calls=%async_computation | async-start | bytes 2097152 | tf_op jit(solution)/shard_map/all_to_all | solution.py:169
  17.1 5.6 %collective-permute-start = (bf16[1024,256]{1,0:T(8,128)(2,1)S(1)}, bf16[1024,256]{1,0:T(8,128)(2,1)S(1)}, u32[]{:S(2)}, u32[]{:S(2)}) collective-permute-start(bf16[1024,256]{1,0:T(8,128)(2,1)S(1)} %copy-done), channel_id=1, source_target_pairs={{0,64},{64,0},{1,65},{65,1},{2,66},{66,2},{3,67},{67,3},{4,68},{68... | collective-permute-start | bytes 1572872 | tf_op jit(solution)/shard_map/ppermute | solution.py:170
  20.0 3.8 %collective-permute-start.1 = (bf16[1024,256]{1,0:T(8,128)(2,1)S(1)}, bf16[1024,256]{1,0:T(8,128)(2,1)S(1)}, u32[]{:S(2)}, u32[]{:S(2)}) collective-permute-start(bf16[1024,256]{1,0:T(8,128)(2,1)S(1)} %copy-done.2), channel_id=1, source_target_pairs={{0,64},{64,0},{1,65},{65,1},{2,66},{66,2},{3,67},{67,3},{4,68},{68... | collective-permute-start | bytes 1572872 | tf_op jit(solution)/shard_map/ppermute | solution.py:171
  22.0 2.9 %collective-permute-start.2 = (bf16[128,256]{1,0:T(8,128)(2,1)S(1)}, bf16[128,256]{1,0:T(8,128)(2,1)S(1)}, u32[]{:S(2)}, u32[]{:S(2)}) collective-permute-start(bf16[128,256]{1,0:T(8,128)(2,1)S(1)} %copy-done.8), channel_id=1, source_target_pairs={{0,0},{1,1},{2,2},{3,3},{4,4},{5,5},{6,6},{7,7},{128,130},{129,131... | collective-permute-start | bytes 196616 | tf_op jit(solution)/shard_map/ppermute | solution.py:180
  46.6 1.0 copy-start.5
  47.6 36.0 %all-to-all-start.1 = ((bf16[8,256,256]{2,1,0:T(8,128)(2,1)}), bf16[8,256,256]{2,1,0:T(8,128)(2,1)S(1)}, u32[]{:S(2)}, u32[]{:S(2)}) async-start(bf16[8,256,256]{2,1,0:T(8,128)(2,1)} %copy-done.5), calls=%async_computation.1 | async-start | bytes 2097152 | tf_op jit(solution)/shard_map/all_to_all | solution.py:194
  54.4 0.7 collective-permute-start.3
  84.0 1.0 copy-start.4
  85.0 33.6 %copy-start.1 = (bf16[1024,256]{1,0:T(8,128)(2,1)S(1)}, bf16[1024,256]{1,0:T(8,128)(2,1)}, u32[]{:S(2)}) copy-start(bf16[1024,256]{1,0:T(8,128)(2,1)} %g0_ref.3) | copy-start | bytes 1572868
  85.0 33.6 %copy-start.3 = (bf16[1024,256]{1,0:T(8,128)(2,1)S(1)}, bf16[1024,256]{1,0:T(8,128)(2,1)}, u32[]{:S(2)}) copy-start(bf16[1024,256]{1,0:T(8,128)(2,1)} %u0_ref.3) | copy-start | bytes 1572868
  85.0 33.6 %all-to-all-start.2 = ((bf16[8,264,256]{2,1,0:T(8,128)(2,1)}), bf16[8,264,256]{2,1,0:T(8,128)(2,1)S(1)}, u32[]{:S(2)}, u32[]{:S(2)}) async-start(bf16[8,264,256]{2,1,0:T(8,128)(2,1)} %copy-done.4), calls=%async_computation.2 | async-start | bytes 2162688 | tf_op jit(solution)/shard_map/all_to_all | solution.py:201
  88.7 4.8 %collective-permute-start.5 = (bf16[512,1024]{1,0:T(8,128)(2,1)S(1)}, bf16[512,1024]{1,0:T(8,128)(2,1)}, u32[]{:S(2)}, u32[]{:S(2)}) collective-permute-start(bf16[512,1024]{1,0:T(8,128)(2,1)S(1)} %get-tuple-element.48), channel_id=1, source_target_pairs={{0,64},{64,0},{1,65},{65,1},{2,66},{66,2},{3,67},{67,3},{4,68},{68... | collective-permute-start | bytes 3145736 | tf_op jit(solution)/shard_map/ppermute | solution.py:203
  91.1 0.7 collective-permute-start.4
  122.1 34.2 %all-to-all-start.3 = ((bf16[32,136,128]{2,1,0:T(8,128)(2,1)}), bf16[32,136,128]{2,1,0:T(8,128)(2,1)S(1)}, u32[]{:S(2)}, u32[]{:S(2)}) async-start(bf16[32,136,128]{2,1,0:T(8,128)(2,1)} %shard_map.96), calls=%async_computation.3 | async-start | bytes 2228224 | tf_op jit(solution)/shard_map/all_to_all | solution.py:216
  129.9 4.4 %collective-permute-start.6 = (bf16[2,512,256]{2,1,0:T(8,128)(2,1)S(1)}, bf16[2,512,256]{2,1,0:T(8,128)(2,1)S(1)}, u32[]{:S(2)}, u32[]{:S(2)}) collective-permute-start(bf16[2,512,256]{2,1,0:T(8,128)(2,1)S(1)} %bitcast.31), channel_id=1, source_target_pairs={{0,64},{64,0},{1,65},{65,1},{2,66},{66,2},{3,67},{67,3},{4,68},{68... | collective-permute-start | bytes 1572872 | tf_op jit(solution)/shard_map/ppermute | solution.py:224
  132.6 6.7 %collective-permute-start.7 = (bf16[128,256]{1,0:T(8,128)(2,1)S(1)}, bf16[128,256]{1,0:T(8,128)(2,1)S(1)}, u32[]{:S(2)}, u32[]{:S(2)}) collective-permute-start(bf16[128,256]{1,0:T(8,128)(2,1)S(1)} %collective-permute-done.4), channel_id=1, source_target_pairs={{0,0},{1,1},{2,2},{3,3},{4,4},{5,5},{6,6},{7,7},{130,128},{131,129... | collective-permute-start | bytes 196616 | tf_op jit(solution)/shard_map/ppermute | solution.py:217
  139.3 20.4 %copy-start.7 = (f32[16,3]{0,1:T(4,128)S(1)}, f32[16,3]{0,1:T(4,128)}, u32[]{:S(2)}) copy-start(f32[16,3]{0,1:T(4,128)} %param.9) | copy-start | bytes 580
  156.4 4.3 %collective-permute-start.8 = (f32[8,128]{1,0:T(8,128)S(1)}, f32[8,128]{1,0:T(8,128)S(1)}, u32[]{:S(2)}, u32[]{:S(2)}) collective-permute-start(f32[8,128]{1,0:T(8,128)S(1)} %shard_map.98), channel_id=1, source_target_pairs={{0,64},{64,0},{1,65},{65,1},{2,66},{66,2},{3,67},{67,3},{4,68},{68... | collective-permute-start | bytes 12296 | tf_op jit(solution)/shard_map/ppermute | solution.py:242
